TPU v7x, 32 devices: a whole 2x2x4 slice. The times are simulated.
32 devices in a mesh: section: 4 (over y, x), dp: 2 (over core), tensor: 4 (over z).
Axes of the slice: x: 2, y: 2, z: 4, core: 2. Of those that a mesh axis runs over, the one named last changes fastest.
Arguments:
- queries: bfloat16 [1024, 2048], P(('section', 'dp'), 'tensor'), may hold values from -6 to 6
- images: bfloat16 [2, 800, 8192], P('dp', 'section', 'tensor'), may hold values from -6 to 6
- kv_weight: bfloat16 [2, 8192, 256], P(None, 'tensor', 'dp'), may hold values from -0.0625 to 0.0625
- q_gain: float32 [128], replicated, may hold values from 1 to 10
- k_gain: float32 [128], replicated, may hold values from 0.1 to 1.9
- tile_mask: int32 [1024, 4], P(('section', 'dp')), may hold values 0 or 1
Outputs:
- context: bfloat16 [1024, 2048], P(('section', 'dp'), 'tensor')
All inputs are finite; a program needn't handle non-finite values. No bound on the sum of `tile_mask` on one device may be relied on, other than what follows from the above.
Results may differ from a plain program's by a relative error of at most 0.04.
Values may be sent and summed in bfloat16 or wider, within the bound.
No kernel may reach another device: no remote copies, remote signals or barrier semaphores. Data moves between devices by JAX's collectives and lax.ppermute only.
A program may use at most 64 MiB of HBM per device.

v0:
```python
import functools

import jax
import jax.numpy as jnp
from jax import lax
from jax.experimental import pallas as pl
from jax.experimental.pallas import tpu as pltpu
from jax.sharding import PartitionSpec as P

EPSILON = 1e-05
MASKED_SCORE = -1e30
TOP_FLOOR = -1e29
VMEM = pl.BlockSpec(memory_space=pltpu.VMEM)
HBM = pl.BlockSpec(memory_space=pltpu.HBM)
F32 = jnp.float32
MIB = 1024 * 1024
LIMIT = 24 * MIB
BF16 = jnp.bfloat16


def shape_of(dims, dtype=BF16):
    return jax.ShapeDtypeStruct(dims, dtype)


def call(
    kernel, outs, n_in, name, flops=0, size=0, exps=0, in_specs=None, scratch=(), aliases=None
):
    many = isinstance(outs, list)
    return pl.pallas_call(
        kernel,
        out_shape=outs,
        in_specs=in_specs or [VMEM] * n_in,
        out_specs=[VMEM] * len(outs) if many else VMEM,
        scratch_shapes=scratch,
        input_output_aliases=aliases or {},
        compiler_params=pltpu.CompilerParams(vmem_limit_bytes=LIMIT),
        cost_estimate=pl.CostEstimate(flops=flops, bytes_accessed=size, transcendentals=exps),
        name=name,
    )


def normalize(values, gain_vec):
    mean_sq = jnp.mean(values * values, axis=-1, keepdims=True)
    return values * lax.rsqrt(mean_sq + EPSILON) * gain_vec


def project(x, w):
    return jnp.dot(
        x, jnp.concatenate([w[0], w[1]], axis=1), preferred_element_type=F32
    ).astype(BF16)


def store_heads(ref, base, both, head_dim):
    width = both.shape[1] // 2
    for head in range(width // head_dim):
        lo = head * head_dim
        ref[base + head, 0] = both[:, lo : lo + head_dim]
        ref[base + head, 1] = both[:, width + lo : width + lo + head_dim]


def prepare_queries(hbm, vmem, sems, qt_ref, bias_ref):
    copies = [pltpu.make_async_copy(a, b, sems.at[i]) for i, (a, b) in enumerate(zip(hbm, vmem))]
    for copy in copies:
        copy.start()
    for copy in copies:
        copy.wait()
    q_ref, q_gain_ref, mask_ref = vmem
    tokens = q_ref.shape[0]
    head_dim = q_gain_ref.shape[1]
    bias = jnp.where(mask_ref[...] > 0, 0.0, MASKED_SCORE).astype(F32)
    for head in range(q_ref.shape[1] // head_dim):
        rows = q_ref[:, head * head_dim : (head + 1) * head_dim].astype(F32)
        normed = normalize(rows, q_gain_ref[...]) * head_dim ** (-0.5)
        qt_ref[:, head * tokens : (head + 1) * tokens] = normed.T.astype(BF16)
        bias_ref[:, head * tokens : (head + 1) * tokens] = bias


def own_kernel(
    head_dim, x_hbm, w_hbm, k_gain_hbm, own_ref, x_ref, k_gain_ref, w_ref, sems
):
    moves = [(k_gain_hbm, k_gain_ref), (x_hbm, x_ref), (w_hbm, w_ref)]
    copies = [pltpu.make_async_copy(a, b, sems.at[i]) for i, (a, b) in enumerate(moves)]
    for copy in copies:
        copy.start()
    for copy in copies:
        copy.wait()
    store_heads(own_ref, 0, project(x_ref[0], w_ref[...]), head_dim)


def split_half(held, send_ref, keep_ref, partner_heads, own_heads):
    for i in range(send_ref.shape[0]):
        send_ref[i] = held[partner_heads + i]
        keep_ref[i] = held[own_heads + i]


def other_kernel(head_dim, n_dp, n_tensor, x_ref, own_ref, *refs):
    w_refs, refs = refs[: n_dp - 1], refs[n_dp - 1 :]
    query_hbm, (send_ref, keep_ref, qt_ref, bias_ref) = refs[:3], refs[3:7]
    held, query_vmem, sems = refs[7], refs[8:11], refs[11]
    d = lax.axis_index("dp")
    t = lax.axis_index("tensor")
    own_heads = own_ref.shape[0]
    held[pl.ds(d * own_heads, own_heads)] = own_ref[...]
    for k in range(1, n_dp):
        store_heads(held, (d ^ k) * own_heads, project(x_ref[0], w_refs[k - 1][...]), head_dim)
    half = send_ref.shape[0]
    upper = t // (n_tensor // 2)
    split_half(held, send_ref, keep_ref, (1 - upper) * half, upper * half)

    @pl.when(d % 2 == 0)
    def _():
        prepare_queries(query_hbm, query_vmem, sems, qt_ref, bias_ref)


def late_kernel(*refs):
    query_hbm, (qt_ref, bias_ref) = refs[2:5], refs[5:7]
    query_vmem, sems = refs[7:10], refs[10]

    @pl.when(lax.axis_index("dp") % 2 == 1)
    def _():
        prepare_queries(query_hbm, query_vmem, sems, qt_ref, bias_ref)


def add_kernel(bit, keep_ref, arrived_ref, send_ref, next_ref, held):
    held[...] = (keep_ref[...].astype(F32) + arrived_ref[...].astype(F32)).astype(BF16)
    half = send_ref.shape[0]
    upper = (lax.axis_index("tensor") // bit) % 2
    split_half(held, send_ref, next_ref, (1 - upper) * half, upper * half)


def add_last_kernel(keep_ref, arrived_ref, bias_ref, out_ref):
    out_ref[...] = (keep_ref[...].astype(F32) + arrived_ref[...].astype(F32)).astype(BF16)


def finish_rows(k_gain, one, two):
    keys = one[0].astype(F32) + two[0].astype(F32)
    values = one[1].astype(F32) + two[1].astype(F32)
    return normalize(keys, k_gain).astype(BF16), values.astype(BF16)


def norm_kernel(k_gain_ref, keep_ref, arrived_ref, kv_ref):
    kv_ref[0], kv_ref[1] = finish_rows(k_gain_ref[...], keep_ref.at[0], arrived_ref.at[0])


def attend_kernel(near, far, tile_len, first, last, head_dim, k_gain_ref, qt_ref, bias_ref, *refs):
    near_refs, refs = refs[: len(near)], refs[len(near) :]
    far_refs, refs = refs[: 2 * len(far)], refs[2 * len(far) :]
    if not first:
        top_in, sum_in, mixed_in = refs[:3]
        refs = refs[3:]
    s = lax.axis_index("section")
    qt = qt_ref[...]
    parts = [(part[0], part[1]) for part in near_refs]
    for one, two in zip(far_refs[::2], far_refs[1::2]):
        parts.append(finish_rows(k_gain_ref[...], one.at[0], two.at[0]))
    rows = parts[0][0].shape[0]
    scores, biases = [], []
    top = TOP_FLOOR if first else top_in[...]
    for step, (keys, _) in zip((*near, *far), parts):
        score = jnp.dot(keys, qt, preferred_element_type=F32)
        bias = bias_ref[pl.ds(((s ^ step) * rows) // tile_len, 1), :]
        scores.append(score)
        biases.append(bias)
        top = jnp.maximum(top, jnp.max(score, axis=0, keepdims=True) + bias)
    row_sum, mixed = 0.0, 0.0
    if not first:
        scale = jnp.exp(top_in[...] - top)
        row_sum = sum_in[...] * scale
        mixed = mixed_in[...] * scale
    for (_, values), score, bias in zip(parts, scores, biases):
        weights = jnp.exp(score + (bias - top))
        row_sum = row_sum + jnp.sum(weights, axis=0, keepdims=True)
        mixed = mixed + lax.dot_general(
            values, weights.astype(BF16), (((0,), (0,)), ((), ())), preferred_element_type=F32
        )
    if not last:
        top_out, sum_out, mixed_out = refs
        top_out[...] = top
        sum_out[...] = row_sum
        mixed_out[...] = mixed
        return
    (out,) = refs
    has_any = jnp.max(bias_ref[...], axis=0, keepdims=True) > -1.0
    inverse = jnp.where(has_any, 1.0 / jnp.where(has_any, row_sum, 1.0), 0.0)
    context = (mixed * inverse).astype(BF16)
    tokens = out.shape[0]
    for head in range(out.shape[1] // head_dim):
        out[:, head * head_dim : (head + 1) * head_dim] = context[
            :, head * tokens : (head + 1) * tokens
        ].T


def on_device(queries, images, kv_weight, q_gain, k_gain, tile_mask):
    n_section = lax.axis_size("section")
    n_dp = lax.axis_size("dp")
    n_tensor = lax.axis_size("tensor")
    head_dim = q_gain.shape[0]
    tokens, q_width = queries.shape
    rows, features = images.shape[1:]
    tiles = tile_mask.shape[1]
    own_heads = kv_weight.shape[2] // head_dim
    heads = own_heads * n_dp
    tile_len = rows * n_section // tiles
    assert heads * 2 == n_tensor and tile_len % rows == 0 and n_section >= 4
    pairs = tokens * (q_width // head_dim)
    work = 4 * rows * features * kv_weight.shape[2]

    def swap(value, axis, k):
        return lax.ppermute(value, axis, [(i, i ^ k) for i in range(lax.axis_size(axis))])

    others = [swap(kv_weight, "dp", k) for k in range(1, n_dp)]
    in_hbm = [
        pltpu.with_memory_space_constraint(value, pltpu.HBM)
        for value in (
            images, kv_weight, k_gain.reshape(1, -1), queries, q_gain.reshape(1, -1), tile_mask.T,
        )
    ]
    own, x, gain = call(
        functools.partial(own_kernel, head_dim),
        [
            shape_of((own_heads, 2, rows, head_dim)),
            shape_of(images.shape),
            shape_of((1, head_dim), F32),
        ],
        3,
        "own_head",
        flops=work,
        size=2 * (images.size + kv_weight.size),
        in_specs=[HBM] * 3,
        scratch=[pltpu.VMEM(kv_weight.shape, BF16), pltpu.SemaphoreType.DMA((3,))],
    )(*in_hbm[:3])
    half = shape_of((heads // 2, 2, rows, head_dim))
    prepared = [shape_of((head_dim, pairs)), shape_of((tiles, pairs), F32)]
    query_scratch = [
        pltpu.VMEM(queries.shape, BF16),
        pltpu.VMEM((1, head_dim), F32),
        pltpu.VMEM((tiles, tokens), jnp.int32),
        pltpu.SemaphoreType.DMA((3,)),
    ]
    send, keep, qt, bias = call(
        functools.partial(other_kernel, head_dim, n_dp, n_tensor),
        [half, half, *prepared],
        n_dp + 1,
        "other_heads",
        flops=work * (n_dp - 1),
        in_specs=[VMEM] * (n_dp + 1) + [HBM] * 3,
        scratch=[pltpu.VMEM((heads, 2, rows, head_dim), BF16), *query_scratch],
    )(x, own, *others, *in_hbm[3:])
    qt, bias = call(
        late_kernel,
        prepared,
        5,
        "late_queries",
        in_specs=[VMEM] * 2 + [HBM] * 3,
        scratch=query_scratch,
        aliases={0: 0, 1: 1},
        flops=work,
    )(qt, bias, *in_hbm[3:])
    bit = n_tensor // 2
    while bit > 1:
        arrived = swap(send, "tensor", bit)
        bit //= 2
        now = keep.shape
        if bit > 1:
            half = shape_of((now[0] // 2, *now[1:]))
            send, keep = call(
                functools.partial(add_kernel, bit),
                [half, half],
                2,
                "add_part",
                scratch=[pltpu.VMEM(now, BF16)],
            )(keep, arrived)
        else:
            send = keep = call(add_last_kernel, shape_of(now), 3, "add_pair")(keep, arrived, bias)
    far = [step for step in range(1, n_section) if step & (step - 1)]
    near = [step for step in range(1, n_section) if not step & (step - 1)]
    arrived = swap(send, "tensor", 1)
    halves = [swap(send, "section", step) for step in far]
    kv = call(norm_kernel, shape_of((2, rows, head_dim)), 3, "sum_norm")(gain, keep, arrived)
    finished = [swap(kv, "section", step) for step in near]
    both = []
    for value in halves:
        both += [value, swap(value, "tensor", 1)]
    state = []
    for here, there, operands in (
        ([0], [], [kv]),
        (near, [], finished),
        ([], far, both),
    ):
        first, last = here == [0], len(there) > 0
        outs = (
            shape_of((tokens, q_width))
            if last
            else [shape_of((1, pairs), F32), shape_of((1, pairs), F32), shape_of((head_dim, pairs), F32)]
        )
        parts = len(here) + len(there)
        state = call(
            functools.partial(attend_kernel, here, there, tile_len, first, last, head_dim),
            outs,
            3 + len(operands) + len(state),
            "attend",
            flops=4 * pairs * rows * head_dim * parts,
            exps=pairs * rows * parts,
        )(gain, qt, bias, *operands, *state)
    return state


def solution(mesh):
    in_specs = (
        P(("section", "dp"), "tensor"),
        P("dp", "section", "tensor"),
        P(None, "tensor", "dp"),
        P(),
        P(),
        P(("section", "dp"), None),
    )
    out_specs = P(("section", "dp"), "tensor")
    return jax.shard_map(
        on_device, mesh=mesh, in_specs=in_specs, out_specs=out_specs, check_vma=False
    )
```

profile of v0, /device:TPU:0, one launch (start us, length us, event | category | flops | bytes accessed | tf_op | source)
XLA Modules:
  0.0 26.8 jit_solution(4027467583078816255)
XLA Ops:
  0.0 0.5 %collective-permute-start = (bf16[2,2048,128]{2,1,0:T(8,128)(2,1)}, bf16[2,2048,128]{2,1,0:T(8,128)(2,1)S(1)}, u32[]{:S(2)}, u32[]{:S(2)}) collective-permute-start(bf16[2,2048,128]{2,1,0:T(8,128)(2,1)} %w_hbm.1), channel_id=1, source_target_pairs={{0,4},{4,0},{1,5},{5,1},{2,6},{6,2},{3,7},{7,3},{8,12},{12,8},{9,1... | collective-permute-start | bytes 3145736 | tf_op jit(solution)/shard_map/ppermute | solution.py:209
  0.5 1.9 %own_head.1 = (bf16[1,2,200,128]{3,2,1,0:T(8,128)(2,1)S(1)}, bf16[1,200,2048]{2,1,0:T(8,128)(2,1)S(1)}, f32[1,128]{1,0:T(1,128)S(1)}) custom-call(bf16[1,200,2048]{2,1,0:T(8,128)(2,1)} %x_hbm.1, bf16[2,2048,128]{2,1,0:T(8,128)(2,1)} %w_hbm.1, f32[1,128]{1,0:T(1,128)} %bitcast.5), custom_call_target="tpu_custom_call" | custom-call | flops 209715200 | bytes 1867776 | tf_op jit(solution)/shard_map/own_head/pallas_call | solution.py:218
  2.4 0.6 %collective-permute-done.refs_0_ = bf16[2,2048,128]{2,1,0:T(8,128)(2,1)S(1)} collective-permute-done((bf16[2,2048,128]{2,1,0:T(8,128)(2,1)}, bf16[2,2048,128]{2,1,0:T(8,128)(2,1)S(1)}, u32[]{:S(2)}, u32[]{:S(2)}) %collective-permute-start) | collective-permute-done | bytes 1048608 | tf_op jit(solution)/shard_map/ppermute | solution.py:209
  3.0 1.7 %other_heads.1 = (bf16[1,2,200,128]{3,2,1,0:T(8,128)(2,1)S(1)}, bf16[1,2,200,128]{3,2,1,0:T(8,128)(2,1)S(1)}, bf16[128,512]{1,0:T(8,128)(2,1)S(1)}, f32[4,512]{1,0:T(4,128)S(1)}) custom-call(bf16[1,200,2048]{2,1,0:T(8,128)(2,1)S(1)} %get-tuple-element.21.x_ref, bf16[1,2,200,128]{3,2,1,0:T(8,128)(2,1)S(1)} %get-tuple-element.22.own_ref, ...), custom_call_target="tpu_custom_call" | custom-call | flops 209715200 | tf_op jit(solution)/shard_map/other_heads/pallas_call | solution.py:240
  4.6 4.0 %collective-permute-start.1 = (bf16[1,2,200,128]{3,2,1,0:T(8,128)(2,1)S(1)}, bf16[1,2,200,128]{3,2,1,0:T(8,128)(2,1)S(1)}, u32[]{:S(2)}, u32[]{:S(2)}) collective-permute-start(bf16[1,2,200,128]{3,2,1,0:T(8,128)(2,1)S(1)} %get-tuple-element.28), channel_id=1, source_target_pairs={{0,2},{1,3},{2,0},{3,1},{4,6},{5,7},{6,4},{7,5},{8,10},{9,11},{10,... | collective-permute-start | bytes 307208 | tf_op jit(solution)/shard_map/ppermute | solution.py:209
  8.7 4.2 %collective-permute-done.1.arrived_ref = bf16[1,2,200,128]{3,2,1,0:T(8,128)(2,1)S(1)} collective-permute-done((bf16[1,2,200,128]{3,2,1,0:T(8,128)(2,1)S(1)}, bf16[1,2,200,128]{3,2,1,0:T(8,128)(2,1)S(1)}, u32[]{:S(2)}, u32[]{:S(2)}) %collective-permute-start.1) | collective-permute-done | bytes 102432 | tf_op jit(solution)/shard_map/ppermute | solution.py:209
  12.9 0.7 %collective-permute-start.4 = (bf16[1,2,200,128]{3,2,1,0:T(8,128)(2,1)S(1)}, bf16[1,2,200,128]{3,2,1,0:T(8,128)(2,1)S(1)}, u32[]{:S(2)}, u32[]{:S(2)}) collective-permute-start(bf16[1,2,200,128]{3,2,1,0:T(8,128)(2,1)S(1)} %add_pair.1.keep_ref), channel_id=1, source_target_pairs={{0,1},{1,0},{2,3},{3,2},{4,5},{5,4},{6,7},{7,6},{8,9},{9,8},{10,11... | collective-permute-start | bytes 307208 | tf_op jit(solution)/shard_map/ppermute | solution.py:209
  13.6 2.4 %collective-permute-start.2 = (bf16[1,2,200,128]{3,2,1,0:T(8,128)(2,1)S(1)}, bf16[1,2,200,128]{3,2,1,0:T(8,128)(2,1)S(1)}, u32[]{:S(2)}, u32[]{:S(2)}) collective-permute-start(bf16[1,2,200,128]{3,2,1,0:T(8,128)(2,1)S(1)} %add_pair.1.keep_ref), channel_id=1, source_target_pairs={{0,24},{8,16},{16,8},{24,0},{1,25},{9,17},{17,9},{25,1},{2,26},{10... | collective-permute-start | bytes 307208 | tf_op jit(solution)/shard_map/ppermute | solution.py:209
  16.1 1.6 %collective-permute-done.4.arrived_ref = bf16[1,2,200,128]{3,2,1,0:T(8,128)(2,1)S(1)} collective-permute-done((bf16[1,2,200,128]{3,2,1,0:T(8,128)(2,1)S(1)}, bf16[1,2,200,128]{3,2,1,0:T(8,128)(2,1)S(1)}, u32[]{:S(2)}, u32[]{:S(2)}) %collective-permute-start.4) | collective-permute-done | bytes 102432 | tf_op jit(solution)/shard_map/ppermute | solution.py:209
  17.7 0.1 sum_norm.1.refs_0_
  17.8 1.6 %collective-permute-start.6 = (bf16[2,200,128]{2,1,0:T(8,128)(2,1)S(1)}, bf16[2,200,128]{2,1,0:T(8,128)(2,1)S(1)}, u32[]{:S(2)}, u32[]{:S(2)}) collective-permute-start(bf16[2,200,128]{2,1,0:T(8,128)(2,1)S(1)} %sum_norm.1.refs_0_), channel_id=1, source_target_pairs={{0,16},{8,24},{16,0},{24,8},{1,17},{9,25},{17,1},{25,9},{2,18},{10... | collective-permute-start | bytes 307208 | tf_op jit(solution)/shard_map/ppermute | solution.py:209
  19.4 1.5 %collective-permute-start.5 = (bf16[2,200,128]{2,1,0:T(8,128)(2,1)S(1)}, bf16[2,200,128]{2,1,0:T(8,128)(2,1)S(1)}, u32[]{:S(2)}, u32[]{:S(2)}) collective-permute-start(bf16[2,200,128]{2,1,0:T(8,128)(2,1)S(1)} %sum_norm.1.refs_0_), channel_id=1, source_target_pairs={{0,8},{8,0},{16,24},{24,16},{1,9},{9,1},{17,25},{25,17},{2,10},{10... | collective-permute-start | bytes 307208 | tf_op jit(solution)/shard_map/ppermute | solution.py:209
  20.9 0.0 collective-permute-done.2.refs_0_
  20.9 0.6 %collective-permute-start.3 = (bf16[1,2,200,128]{3,2,1,0:T(8,128)(2,1)S(1)}, bf16[1,2,200,128]{3,2,1,0:T(8,128)(2,1)S(1)}, u32[]{:S(2)}, u32[]{:S(2)}) collective-permute-start(bf16[1,2,200,128]{3,2,1,0:T(8,128)(2,1)S(1)} %collective-permute-done.2.refs_0_), channel_id=1, source_target_pairs={{0,1},{1,0},{2,3},{3,2},{4,5},{5,4},{6,7},{7,6},{8,9},{9,8},{10,11... | collective-permute-start | bytes 307208 | tf_op jit(solution)/shard_map/ppermute | solution.py:209
  21.5 0.4 %attend.3 = (f32[1,512]{1,0:T(1,128)S(1)}, f32[1,512]{1,0:T(1,128)S(1)}, f32[128,512]{1,0:T(8,128)S(1)}) custom-call(f32[1,128]{1,0:T(1,128)S(1)} %get-tuple-element.20.k_gain_ref, bf16[128,512]{1,0:T(8,128)(2,1)S(1)} %get-tuple-element.25.qt_ref, f32[4,512]{1,0:T(4,128)S(1)} %get-tuple-element.26.bias_ref, bf16[2,200,128]{2,1,0:T(8,128)(2,1)S(1)} %sum_norm.1.refs_0_), custom_call_target="tpu_custom_call" | custom-call | flops 52428800 | tf_op jit(solution)/shard_map/attend/pallas_call | solution.py:297
  21.9 0.6 %collective-permute-done.6.refs_1_ = bf16[2,200,128]{2,1,0:T(8,128)(2,1)S(1)} collective-permute-done((bf16[2,200,128]{2,1,0:T(8,128)(2,1)S(1)}, bf16[2,200,128]{2,1,0:T(8,128)(2,1)S(1)}, u32[]{:S(2)}, u32[]{:S(2)}) %collective-permute-start.6) | collective-permute-done | bytes 102432 | tf_op jit(solution)/shard_map/ppermute | solution.py:209
  22.5 1.6 %collective-permute-done.5.refs_0_ = bf16[2,200,128]{2,1,0:T(8,128)(2,1)S(1)} collective-permute-done((bf16[2,200,128]{2,1,0:T(8,128)(2,1)S(1)}, bf16[2,200,128]{2,1,0:T(8,128)(2,1)S(1)}, u32[]{:S(2)}, u32[]{:S(2)}) %collective-permute-start.5) | collective-permute-done | bytes 102432 | tf_op jit(solution)/shard_map/ppermute | solution.py:209
  24.1 0.6 %attend.4 = (f32[1,512]{1,0:T(1,128)S(1)}, f32[1,512]{1,0:T(1,128)S(1)}, f32[128,512]{1,0:T(8,128)S(1)}) custom-call(f32[1,128]{1,0:T(1,128)S(1)} %get-tuple-element.20.k_gain_ref, bf16[128,512]{1,0:T(8,128)(2,1)S(1)} %get-tuple-element.25.qt_ref, f32[4,512]{1,0:T(4,128)S(1)} %get-tuple-element.26.bias_ref, ...), custom_call_target="tpu_custom_call" | custom-call | flops 104857600 | tf_op jit(solution)/shard_map/attend/pallas_call | solution.py:297
  24.7 0.9 %collective-permute-done.3.refs_1_ = bf16[1,2,200,128]{3,2,1,0:T(8,128)(2,1)S(1)} collective-permute-done((bf16[1,2,200,128]{3,2,1,0:T(8,128)(2,1)S(1)}, bf16[1,2,200,128]{3,2,1,0:T(8,128)(2,1)S(1)}, u32[]{:S(2)}, u32[]{:S(2)}) %collective-permute-start.3) | collective-permute-done | bytes 102432 | tf_op jit(solution)/shard_map/ppermute | solution.py:209
  25.6 1.3 %attend.5 = bf16[128,512]{1,0:T(8,128)(2,1)} custom-call(f32[1,128]{1,0:T(1,128)S(1)} %get-tuple-element.20.k_gain_ref, bf16[128,512]{1,0:T(8,128)(2,1)S(1)} %get-tuple-element.25.qt_ref, f32[4,512]{1,0:T(4,128)S(1)} %get-tuple-element.26.bias_ref, bf16[1,2,200,128]{3,2,1,0:T(8,128)(2,1)S(1)} %collective-permute-done.2.refs_0_, ...), custom_call_target="tpu_custom_call" | custom-call | flops 52428800 | tf_op jit(solution)/shard_map/attend/pallas_call | solution.py:297
  (2 shorter events, 0.1 us)
Async XLA Ops:
  0.0 3.0 %collective-permute-start = (bf16[2,2048,128]{2,1,0:T(8,128)(2,1)}, bf16[2,2048,128]{2,1,0:T(8,128)(2,1)S(1)}, u32[]{:S(2)}, u32[]{:S(2)}) collective-permute-start(bf16[2,2048,128]{2,1,0:T(8,128)(2,1)} %w_hbm.1), channel_id=1, source_target_pairs={{0,4},{4,0},{1,5},{5,1},{2,6},{6,2},{3,7},{7,3},{8,12},{12,8},{9,1... | collective-permute-start | bytes 3145736 | tf_op jit(solution)/shard_map/ppermute | solution.py:209
  4.6 8.3 %collective-permute-start.1 = (bf16[1,2,200,128]{3,2,1,0:T(8,128)(2,1)S(1)}, bf16[1,2,200,128]{3,2,1,0:T(8,128)(2,1)S(1)}, u32[]{:S(2)}, u32[]{:S(2)}) collective-permute-start(bf16[1,2,200,128]{3,2,1,0:T(8,128)(2,1)S(1)} %get-tuple-element.28), channel_id=1, source_target_pairs={{0,2},{1,3},{2,0},{3,1},{4,6},{5,7},{6,4},{7,5},{8,10},{9,11},{10,... | collective-permute-start | bytes 307208 | tf_op jit(solution)/shard_map/ppermute | solution.py:209
  12.9 4.7 %collective-permute-start.4 = (bf16[1,2,200,128]{3,2,1,0:T(8,128)(2,1)S(1)}, bf16[1,2,200,128]{3,2,1,0:T(8,128)(2,1)S(1)}, u32[]{:S(2)}, u32[]{:S(2)}) collective-permute-start(bf16[1,2,200,128]{3,2,1,0:T(8,128)(2,1)S(1)} %add_pair.1.keep_ref), channel_id=1, source_target_pairs={{0,1},{1,0},{2,3},{3,2},{4,5},{5,4},{6,7},{7,6},{8,9},{9,8},{10,11... | collective-permute-start | bytes 307208 | tf_op jit(solution)/shard_map/ppermute | solution.py:209
  13.6 7.3 %collective-permute-start.2 = (bf16[1,2,200,128]{3,2,1,0:T(8,128)(2,1)S(1)}, bf16[1,2,200,128]{3,2,1,0:T(8,128)(2,1)S(1)}, u32[]{:S(2)}, u32[]{:S(2)}) collective-permute-start(bf16[1,2,200,128]{3,2,1,0:T(8,128)(2,1)S(1)} %add_pair.1.keep_ref), channel_id=1, source_target_pairs={{0,24},{8,16},{16,8},{24,0},{1,25},{9,17},{17,9},{25,1},{2,26},{10... | collective-permute-start | bytes 307208 | tf_op jit(solution)/shard_map/ppermute | solution.py:209
  17.8 4.7 %collective-permute-start.6 = (bf16[2,200,128]{2,1,0:T(8,128)(2,1)S(1)}, bf16[2,200,128]{2,1,0:T(8,128)(2,1)S(1)}, u32[]{:S(2)}, u32[]{:S(2)}) collective-permute-start(bf16[2,200,128]{2,1,0:T(8,128)(2,1)S(1)} %sum_norm.1.refs_0_), channel_id=1, source_target_pairs={{0,16},{8,24},{16,0},{24,8},{1,17},{9,25},{17,1},{25,9},{2,18},{10... | collective-permute-start | bytes 307208 | tf_op jit(solution)/shard_map/ppermute | solution.py:209
  19.4 4.7 %collective-permute-start.5 = (bf16[2,200,128]{2,1,0:T(8,128)(2,1)S(1)}, bf16[2,200,128]{2,1,0:T(8,128)(2,1)S(1)}, u32[]{:S(2)}, u32[]{:S(2)}) collective-permute-start(bf16[2,200,128]{2,1,0:T(8,128)(2,1)S(1)} %sum_norm.1.refs_0_), channel_id=1, source_target_pairs={{0,8},{8,0},{16,24},{24,16},{1,9},{9,1},{17,25},{25,17},{2,10},{10... | collective-permute-start | bytes 307208 | tf_op jit(solution)/shard_map/ppermute | solution.py:209
  20.9 4.7 %collective-permute-start.3 = (bf16[1,2,200,128]{3,2,1,0:T(8,128)(2,1)S(1)}, bf16[1,2,200,128]{3,2,1,0:T(8,128)(2,1)S(1)}, u32[]{:S(2)}, u32[]{:S(2)}) collective-permute-start(bf16[1,2,200,128]{3,2,1,0:T(8,128)(2,1)S(1)} %collective-permute-done.2.refs_0_), channel_id=1, source_target_pairs={{0,1},{1,0},{2,3},{3,2},{4,5},{5,4},{6,7},{7,6},{8,9},{9,8},{10,11... | collective-permute-start | bytes 307208 | tf_op jit(solution)/shard_map/ppermute | solution.py:209
where the time goes:
time: 27 us; the launch traced here: 26.8 us
  starting transfers between devices  11.3 us (42%)
  waiting for transfers between devices  9.45 us (35%)
  Pallas kernels  6.04 us (22%)
    ppermute x7, starting transfers between devices, swap(): lax.ppermute(value, axis, [(i, i ^ k) for i in range(lax.axis_size(axis))])  11.3 us
    ppermute x7, waiting for transfers between devices, swap(): lax.ppermute(value, axis, [(i, i ^ k) for i in range(lax.axis_size(axis))])  9.45 us
    pallas_call x3, Pallas kernels, on_device(): call(functools.partial(attend_kernel, here, there, tile_len, first, last,...  2.26 us
    pallas_call x1, Pallas kernels, on_device(): call(functools.partial(own_kernel, head_dim), [shape_of((own_heads, 2, ro...  1.92 us
    pallas_call x1, Pallas kernels, on_device(): call(functools.partial(other_kernel, head_dim, n_dp, n_tensor), [half, ha...  1.68 us
  transfers between devices with their start and end apart: 7, of which 6 were waited for; matrix products, arithmetic and copies ran while one was open for 0% of the time, Pallas kernels for 11%

commit v1 on v0

--- a/solution.py
+++ b/solution.py
@@ -23,7 +23,7 @@
 
 
 def call(
-    kernel, outs, n_in, name, flops=0, size=0, exps=0, in_specs=None, scratch=(), aliases=None
+    kernel, outs, n_in, name, flops=0, size=0, exps=0, in_specs=None, scratch=()
 ):
     many = isinstance(outs, list)
     return pl.pallas_call(
@@ -32,7 +32,6 @@
         in_specs=in_specs or [VMEM] * n_in,
         out_specs=[VMEM] * len(outs) if many else VMEM,
         scratch_shapes=scratch,
-        input_output_aliases=aliases or {},
         compiler_params=pltpu.CompilerParams(vmem_limit_bytes=LIMIT),
         cost_estimate=pl.CostEstimate(flops=flops, bytes_accessed=size, transcendentals=exps),
         name=name,
@@ -93,32 +92,30 @@
         keep_ref[i] = held[own_heads + i]
 
 
-def other_kernel(head_dim, n_dp, n_tensor, x_ref, own_ref, *refs):
-    w_refs, refs = refs[: n_dp - 1], refs[n_dp - 1 :]
-    query_hbm, (send_ref, keep_ref, qt_ref, bias_ref) = refs[:3], refs[3:7]
-    held, query_vmem, sems = refs[7], refs[8:11], refs[11]
+def other_kernel(head_dim, x_ref, w_ref, other_ref):
+    store_heads(other_ref, 0, project(x_ref[0], w_ref[...]), head_dim)
+
+
+def spread_kernel(n_dp, n_tensor, own_ref, *refs):
+    others, (send_ref, keep_ref, held) = refs[: n_dp - 1], refs[n_dp - 1 :]
     d = lax.axis_index("dp")
-    t = lax.axis_index("tensor")
     own_heads = own_ref.shape[0]
-    held[pl.ds(d * own_heads, own_heads)] = own_ref[...]
-    for k in range(1, n_dp):
-        store_heads(held, (d ^ k) * own_heads, project(x_ref[0], w_refs[k - 1][...]), head_dim)
+    for k, ref in enumerate((own_ref, *others)):
+        held[pl.ds((d ^ k) * own_heads, own_heads)] = ref[...]
     half = send_ref.shape[0]
-    upper = t // (n_tensor // 2)
+    upper = lax.axis_index("tensor") // (n_tensor // 2)
     split_half(held, send_ref, keep_ref, (1 - upper) * half, upper * half)
 
-    @pl.when(d % 2 == 0)
-    def _():
-        prepare_queries(query_hbm, query_vmem, sems, qt_ref, bias_ref)
-
-
-def late_kernel(*refs):
-    query_hbm, (qt_ref, bias_ref) = refs[2:5], refs[5:7]
-    query_vmem, sems = refs[7:10], refs[10]
-
-    @pl.when(lax.axis_index("dp") % 2 == 1)
-    def _():
-        prepare_queries(query_hbm, query_vmem, sems, qt_ref, bias_ref)
+
+def query_kernel(*refs):
+    prepare_queries(refs[:3], refs[5:8], refs[8], *refs[3:5])
+
+
+def pair_kernel(own_ref, other_ref, first_ref, second_ref, bias_ref, out_ref):
+    mine = lax.axis_index("tensor") // 2 == lax.axis_index("dp")
+    keep = jnp.where(mine, own_ref[...], other_ref[...]).astype(F32)
+    arrived = jnp.where(mine, first_ref[...], second_ref[...]).astype(F32)
+    out_ref[...] = (keep + arrived).astype(BF16)
 
 
 def add_kernel(bit, keep_ref, arrived_ref, send_ref, next_ref, held):
@@ -128,7 +125,7 @@
     split_half(held, send_ref, next_ref, (1 - upper) * half, upper * half)
 
 
-def add_last_kernel(keep_ref, arrived_ref, bias_ref, out_ref):
+def add_last_kernel(keep_ref, arrived_ref, out_ref):
     out_ref[...] = (keep_ref[...].astype(F32) + arrived_ref[...].astype(F32)).astype(BF16)
 
 
@@ -190,6 +187,56 @@
         ].T
 
 
+def swap(value, axis, k):
+    return lax.ppermute(value, axis, [(i, i ^ k) for i in range(lax.axis_size(axis))])
+
+
+def sum_two_heads(own, other, bias):
+    devices = [(d, t) for d in range(2) for t in range(4)]
+
+    def exchange(value, senders):
+        hops = [
+            (4 * d + t, 4 * d + (t ^ 2) if (t // 2 == d) == senders else 4 * (1 - d) + t)
+            for d, t in devices
+        ]
+        return lax.ppermute(value, ("dp", "tensor"), hops)
+
+    first = exchange(own, False)
+    rest = other(1)
+    second = exchange(rest, True)
+    return call(pair_kernel, shape_of(own.shape), 5, "pair_sum")(own, rest, first, second, bias)
+
+
+def sum_many_heads(own, others):
+    n_dp, n_tensor = lax.axis_size("dp"), lax.axis_size("tensor")
+    heads = own.shape[0] * n_dp
+    half = shape_of((heads // 2, *own.shape[1:]))
+    send, keep = call(
+        functools.partial(spread_kernel, n_dp, n_tensor),
+        [half, half],
+        n_dp,
+        "spread",
+        scratch=[pltpu.VMEM((heads, *own.shape[1:]), BF16)],
+    )(own, *others)
+    bit = n_tensor // 2
+    while bit > 1:
+        arrived = swap(send, "tensor", bit)
+        bit //= 2
+        now = keep.shape
+        if bit > 1:
+            half = shape_of((now[0] // 2, *now[1:]))
+            send, keep = call(
+                functools.partial(add_kernel, bit),
+                [half, half],
+                2,
+                "add_part",
+                scratch=[pltpu.VMEM(now, BF16)],
+            )(keep, arrived)
+        else:
+            send = keep = call(add_last_kernel, shape_of(now), 2, "add_pair")(keep, arrived)
+    return send, keep
+
+
 def on_device(queries, images, kv_weight, q_gain, k_gain, tile_mask):
     n_section = lax.axis_size("section")
     n_dp = lax.axis_size("dp")
@@ -204,9 +251,6 @@
     assert heads * 2 == n_tensor and tile_len % rows == 0 and n_section >= 4
     pairs = tokens * (q_width // head_dim)
     work = 4 * rows * features * kv_weight.shape[2]
-
-    def swap(value, axis, k):
-        return lax.ppermute(value, axis, [(i, i ^ k) for i in range(lax.axis_size(axis))])
 
     others = [swap(kv_weight, "dp", k) for k in range(1, n_dp)]
     in_hbm = [
@@ -229,49 +273,29 @@
         in_specs=[HBM] * 3,
         scratch=[pltpu.VMEM(kv_weight.shape, BF16), pltpu.SemaphoreType.DMA((3,))],
     )(*in_hbm[:3])
-    half = shape_of((heads // 2, 2, rows, head_dim))
-    prepared = [shape_of((head_dim, pairs)), shape_of((tiles, pairs), F32)]
-    query_scratch = [
-        pltpu.VMEM(queries.shape, BF16),
-        pltpu.VMEM((1, head_dim), F32),
-        pltpu.VMEM((tiles, tokens), jnp.int32),
-        pltpu.SemaphoreType.DMA((3,)),
-    ]
-    send, keep, qt, bias = call(
-        functools.partial(other_kernel, head_dim, n_dp, n_tensor),
-        [half, half, *prepared],
-        n_dp + 1,
-        "other_heads",
-        flops=work * (n_dp - 1),
-        in_specs=[VMEM] * (n_dp + 1) + [HBM] * 3,
-        scratch=[pltpu.VMEM((heads, 2, rows, head_dim), BF16), *query_scratch],
-    )(x, own, *others, *in_hbm[3:])
     qt, bias = call(
-        late_kernel,
-        prepared,
-        5,
-        "late_queries",
-        in_specs=[VMEM] * 2 + [HBM] * 3,
-        scratch=query_scratch,
-        aliases={0: 0, 1: 1},
-        flops=work,
-    )(qt, bias, *in_hbm[3:])
-    bit = n_tensor // 2
-    while bit > 1:
-        arrived = swap(send, "tensor", bit)
-        bit //= 2
-        now = keep.shape
-        if bit > 1:
-            half = shape_of((now[0] // 2, *now[1:]))
-            send, keep = call(
-                functools.partial(add_kernel, bit),
-                [half, half],
-                2,
-                "add_part",
-                scratch=[pltpu.VMEM(now, BF16)],
-            )(keep, arrived)
-        else:
-            send = keep = call(add_last_kernel, shape_of(now), 3, "add_pair")(keep, arrived, bias)
+        query_kernel,
+        [shape_of((head_dim, pairs)), shape_of((tiles, pairs), F32)],
+        3,
+        "queries",
+        in_specs=[HBM] * 3,
+        scratch=[
+            pltpu.VMEM(queries.shape, BF16),
+            pltpu.VMEM((1, head_dim), F32),
+            pltpu.VMEM((tiles, tokens), jnp.int32),
+            pltpu.SemaphoreType.DMA((3,)),
+        ],
+    )(*in_hbm[3:])
+
+    def other(k):
+        return call(
+            functools.partial(other_kernel, head_dim), shape_of(own.shape), 2, "other_heads", flops=work
+        )(x, others[k - 1])
+
+    if n_dp == 2 and own_heads == 1:
+        send = keep = sum_two_heads(own, other, bias)
+    else:
+        send, keep = sum_many_heads(own, [other(k) for k in range(1, n_dp)])
     far = [step for step in range(1, n_section) if step & (step - 1)]
     near = [step for step in range(1, n_section) if not step & (step - 1)]
     arrived = swap(send, "tensor", 1)

time: 27 us -> 25.3 us (0.937)
  waiting for transfers between devices: 9.45 us -> 4.4 us
  starting transfers between devices: 11.3 us -> 14.7 us
    ppermute x7 -> x6, waiting for transfers between devices: 9.45 us -> 3.43 us  [swap(): lax.ppermute(value, axis, [(i, i ^ k) for i in range(lax.axis_size(axis))])]
    ppermute x0 -> x2, starting transfers between devices: none -> 4.14 us  [exchange(): return lax.ppermute(value, ('dp', 'tensor'), hops)]
    ppermute x0 -> x2, waiting for transfers between devices: none -> 0.97 us  [exchange(): return lax.ppermute(value, ('dp', 'tensor'), hops)]
    ppermute x7 -> x6, starting transfers between devices: 11.3 us -> 10.6 us  [swap(): lax.ppermute(value, axis, [(i, i ^ k) for i in range(lax.axis_size(axis))])]
  transfers between devices with their start and end apart: 7 -> 8, of which waited for: 6 -> 5; matrix products, arithmetic and copies ran while one was open for 0% -> 0% of each run, Pallas kernels for 11% -> 19%
where the time goes in v1:
time: 25.3 us; the launch traced here: 25.2 us
  starting transfers between devices  14.7 us (58%)
  Pallas kernels  6.01 us (24%)
  waiting for transfers between devices  4.4 us (17%)
    ppermute x6, starting transfers between devices, swap(): lax.ppermute(value, axis, [(i, i ^ k) for i in range(lax.axis_size(axis))])  10.6 us
    ppermute x2, starting transfers between devices, exchange(): return lax.ppermute(value, ('dp', 'tensor'), hops)  4.14 us
    ppermute x6, waiting for transfers between devices, swap(): lax.ppermute(value, axis, [(i, i ^ k) for i in range(lax.axis_size(axis))])  3.43 us
    pallas_call x3, Pallas kernels, on_device(): call(functools.partial(attend_kernel, here, there, tile_len, first, last,...  2.26 us
    pallas_call x1, Pallas kernels, on_device(): call(functools.partial(own_kernel, head_dim), [shape_of((own_heads, 2, ro...  1.92 us
    pallas_call x1, Pallas kernels, on_device(): call(query_kernel, [shape_of((head_dim, pairs)), shape_of((tiles, pairs),...  1.27 us
    ppermute x2, waiting for transfers between devices, exchange(): return lax.ppermute(value, ('dp', 'tensor'), hops)  0.97 us
  transfers between devices with their start and end apart: 8, of which 5 were waited for; matrix products, arithmetic and copies ran while one was open for 0% of the time, Pallas kernels for 19%

profile of v1, /device:TPU:0, one launch (start us, length us, event | category | flops | bytes accessed | tf_op | source)
XLA Modules:
  0.0 25.2 jit_solution(17329674333633154319)
XLA Ops:
  0.0 0.5 %collective-permute-start = (bf16[2,2048,128]{2,1,0:T(8,128)(2,1)}, bf16[2,2048,128]{2,1,0:T(8,128)(2,1)S(1)}, u32[]{:S(2)}, u32[]{:S(2)}) collective-permute-start(bf16[2,2048,128]{2,1,0:T(8,128)(2,1)} %w_hbm.1), channel_id=1, source_target_pairs={{0,4},{4,0},{1,5},{5,1},{2,6},{6,2},{3,7},{7,3},{8,12},{12,8},{9,1... | collective-permute-start | bytes 3145736 | tf_op jit(solution)/shard_map/ppermute | solution.py:191
  0.5 1.9 %own_head.1 = (bf16[1,2,200,128]{3,2,1,0:T(8,128)(2,1)S(1)}, bf16[1,200,2048]{2,1,0:T(8,128)(2,1)S(1)}, f32[1,128]{1,0:T(1,128)S(1)}) custom-call(bf16[1,200,2048]{2,1,0:T(8,128)(2,1)} %x_hbm.1, bf16[2,2048,128]{2,1,0:T(8,128)(2,1)} %w_hbm.1, f32[1,128]{1,0:T(1,128)} %bitcast.5), custom_call_target="tpu_custom_call" | custom-call | flops 209715200 | bytes 1867776 | tf_op jit(solution)/shard_map/own_head/pallas_call | solution.py:262
  2.4 0.1 collective-permute-start.1
  2.5 0.5 %collective-permute-done.w_ref = bf16[2,2048,128]{2,1,0:T(8,128)(2,1)S(1)} collective-permute-done((bf16[2,2048,128]{2,1,0:T(8,128)(2,1)}, bf16[2,2048,128]{2,1,0:T(8,128)(2,1)S(1)}, u32[]{:S(2)}, u32[]{:S(2)}) %collective-permute-start) | collective-permute-done | bytes 1048608 | tf_op jit(solution)/shard_map/ppermute | solution.py:191
  3.0 0.4 %other_heads.1.other_ref = bf16[1,2,200,128]{3,2,1,0:T(8,128)(2,1)S(1)} custom-call(bf16[1,200,2048]{2,1,0:T(8,128)(2,1)S(1)} %get-tuple-element.20.x_ref, bf16[2,2048,128]{2,1,0:T(8,128)(2,1)S(1)} %collective-permute-done.w_ref), custom_call_target="tpu_custom_call" | custom-call | flops 209715200 | tf_op jit(solution)/shard_map/other_heads/pallas_call | solution.py:291
  3.4 4.0 %collective-permute-start.2 = (bf16[1,2,200,128]{3,2,1,0:T(8,128)(2,1)S(1)}, bf16[1,2,200,128]{3,2,1,0:T(8,128)(2,1)S(1)}, u32[]{:S(2)}, u32[]{:S(2)}) collective-permute-start(bf16[1,2,200,128]{3,2,1,0:T(8,128)(2,1)S(1)} %other_heads.1.other_ref), channel_id=1, source_target_pairs={{0,2},{1,3},{2,6},{3,7},{4,0},{5,1},{6,4},{7,5},{8,10},{9,11},{10,... | collective-permute-start | bytes 307208 | tf_op jit(solution)/shard_map/ppermute | solution.py:202
  7.4 1.3 %queries.1 = (bf16[128,512]{1,0:T(8,128)(2,1)S(1)}, f32[4,512]{1,0:T(4,128)S(1)}) custom-call(bf16[128,512]{1,0:T(8,128)(2,1)} %refs_0_.1, f32[1,128]{1,0:T(1,128)} %bitcast.4, s32[4,128]{1,0:T(4,128)} %bitcast.3), custom_call_target="tpu_custom_call" | custom-call | tf_op jit(solution)/shard_map/queries/pallas_call | solution.py:276
  8.6 0.0 collective-permute-done.1.first_ref
  8.7 1.0 %collective-permute-done.2.second_ref = bf16[1,2,200,128]{3,2,1,0:T(8,128)(2,1)S(1)} collective-permute-done((bf16[1,2,200,128]{3,2,1,0:T(8,128)(2,1)S(1)}, bf16[1,2,200,128]{3,2,1,0:T(8,128)(2,1)S(1)}, u32[]{:S(2)}, u32[]{:S(2)}) %collective-permute-start.2) | collective-permute-done | bytes 102432 | tf_op jit(solution)/shard_map/ppermute | solution.py:202
  9.7 2.9 %collective-permute-start.5 = (bf16[1,2,200,128]{3,2,1,0:T(8,128)(2,1)S(1)}, bf16[1,2,200,128]{3,2,1,0:T(8,128)(2,1)S(1)}, u32[]{:S(2)}, u32[]{:S(2)}) collective-permute-start(bf16[1,2,200,128]{3,2,1,0:T(8,128)(2,1)S(1)} %pair_sum.1.keep_ref), channel_id=1, source_target_pairs={{0,1},{1,0},{2,3},{3,2},{4,5},{5,4},{6,7},{7,6},{8,9},{9,8},{10,11... | collective-permute-start | bytes 307208 | tf_op jit(solution)/shard_map/ppermute | solution.py:191
  12.6 2.4 %collective-permute-start.3 = (bf16[1,2,200,128]{3,2,1,0:T(8,128)(2,1)S(1)}, bf16[1,2,200,128]{3,2,1,0:T(8,128)(2,1)S(1)}, u32[]{:S(2)}, u32[]{:S(2)}) collective-permute-start(bf16[1,2,200,128]{3,2,1,0:T(8,128)(2,1)S(1)} %pair_sum.1.keep_ref), channel_id=1, source_target_pairs={{0,24},{8,16},{16,8},{24,0},{1,25},{9,17},{17,9},{25,1},{2,26},{10... | collective-permute-start | bytes 307208 | tf_op jit(solution)/shard_map/ppermute | solution.py:191
  15.1 1.0 %collective-permute-done.5.arrived_ref = bf16[1,2,200,128]{3,2,1,0:T(8,128)(2,1)S(1)} collective-permute-done((bf16[1,2,200,128]{3,2,1,0:T(8,128)(2,1)S(1)}, bf16[1,2,200,128]{3,2,1,0:T(8,128)(2,1)S(1)}, u32[]{:S(2)}, u32[]{:S(2)}) %collective-permute-start.5) | collective-permute-done | bytes 102432 | tf_op jit(solution)/shard_map/ppermute | solution.py:191
  16.1 0.1 sum_norm.1.refs_0_
  16.2 1.6 %collective-permute-start.6 = (bf16[2,200,128]{2,1,0:T(8,128)(2,1)S(1)}, bf16[2,200,128]{2,1,0:T(8,128)(2,1)S(1)}, u32[]{:S(2)}, u32[]{:S(2)}) collective-permute-start(bf16[2,200,128]{2,1,0:T(8,128)(2,1)S(1)} %sum_norm.1.refs_0_), channel_id=1, source_target_pairs={{0,8},{8,0},{16,24},{24,16},{1,9},{9,1},{17,25},{25,17},{2,10},{10... | collective-permute-start | bytes 307208 | tf_op jit(solution)/shard_map/ppermute | solution.py:191
  17.7 1.5 %collective-permute-start.7 = (bf16[2,200,128]{2,1,0:T(8,128)(2,1)S(1)}, bf16[2,200,128]{2,1,0:T(8,128)(2,1)S(1)}, u32[]{:S(2)}, u32[]{:S(2)}) collective-permute-start(bf16[2,200,128]{2,1,0:T(8,128)(2,1)S(1)} %sum_norm.1.refs_0_), channel_id=1, source_target_pairs={{0,16},{8,24},{16,0},{24,8},{1,17},{9,25},{17,1},{25,9},{2,18},{10... | collective-permute-start | bytes 307208 | tf_op jit(solution)/shard_map/ppermute | solution.py:191
  19.2 0.0 collective-permute-done.3.refs_0_
  19.2 1.7 %collective-permute-start.4 = (bf16[1,2,200,128]{3,2,1,0:T(8,128)(2,1)S(1)}, bf16[1,2,200,128]{3,2,1,0:T(8,128)(2,1)S(1)}, u32[]{:S(2)}, u32[]{:S(2)}) collective-permute-start(bf16[1,2,200,128]{3,2,1,0:T(8,128)(2,1)S(1)} %collective-permute-done.3.refs_0_), channel_id=1, source_target_pairs={{0,1},{1,0},{2,3},{3,2},{4,5},{5,4},{6,7},{7,6},{8,9},{9,8},{10,11... | collective-permute-start | bytes 307208 | tf_op jit(solution)/shard_map/ppermute | solution.py:191
  20.9 0.4 %attend.3 = (f32[1,512]{1,0:T(1,128)S(1)}, f32[1,512]{1,0:T(1,128)S(1)}, f32[128,512]{1,0:T(8,128)S(1)}) custom-call(f32[1,128]{1,0:T(1,128)S(1)} %get-tuple-element.16.k_gain_ref, bf16[128,512]{1,0:T(8,128)(2,1)S(1)} %get-tuple-element.17.qt_ref, f32[4,512]{1,0:T(4,128)S(1)} %get-tuple-element.18.bias_ref, bf16[2,200,128]{2,1,0:T(8,128)(2,1)S(1)} %sum_norm.1.refs_0_), custom_call_target="tpu_custom_call" | custom-call | flops 52428800 | tf_op jit(solution)/shard_map/attend/pallas_call | solution.py:321
  21.3 0.0 collective-permute-done.6.refs_0_
  21.3 1.0 %collective-permute-done.7.refs_1_ = bf16[2,200,128]{2,1,0:T(8,128)(2,1)S(1)} collective-permute-done((bf16[2,200,128]{2,1,0:T(8,128)(2,1)S(1)}, bf16[2,200,128]{2,1,0:T(8,128)(2,1)S(1)}, u32[]{:S(2)}, u32[]{:S(2)}) %collective-permute-start.7) | collective-permute-done | bytes 102432 | tf_op jit(solution)/shard_map/ppermute | solution.py:191
  22.4 0.6 %attend.4 = (f32[1,512]{1,0:T(1,128)S(1)}, f32[1,512]{1,0:T(1,128)S(1)}, f32[128,512]{1,0:T(8,128)S(1)}) custom-call(f32[1,128]{1,0:T(1,128)S(1)} %get-tuple-element.16.k_gain_ref, bf16[128,512]{1,0:T(8,128)(2,1)S(1)} %get-tuple-element.17.qt_ref, f32[4,512]{1,0:T(4,128)S(1)} %get-tuple-element.18.bias_ref, ...), custom_call_target="tpu_custom_call" | custom-call | flops 104857600 | tf_op jit(solution)/shard_map/attend/pallas_call | solution.py:321
  23.0 0.9 %collective-permute-done.4.refs_1_ = bf16[1,2,200,128]{3,2,1,0:T(8,128)(2,1)S(1)} collective-permute-done((bf16[1,2,200,128]{3,2,1,0:T(8,128)(2,1)S(1)}, bf16[1,2,200,128]{3,2,1,0:T(8,128)(2,1)S(1)}, u32[]{:S(2)}, u32[]{:S(2)}) %collective-permute-start.4) | collective-permute-done | bytes 102432 | tf_op jit(solution)/shard_map/ppermute | solution.py:191
  23.9 1.3 %attend.5 = bf16[128,512]{1,0:T(8,128)(2,1)} custom-call(f32[1,128]{1,0:T(1,128)S(1)} %get-tuple-element.16.k_gain_ref, bf16[128,512]{1,0:T(8,128)(2,1)S(1)} %get-tuple-element.17.qt_ref, f32[4,512]{1,0:T(4,128)S(1)} %get-tuple-element.18.bias_ref, bf16[1,2,200,128]{3,2,1,0:T(8,128)(2,1)S(1)} %collective-permute-done.3.refs_0_, ...), custom_call_target="tpu_custom_call" | custom-call | flops 52428800 | tf_op jit(solution)/shard_map/attend/pallas_call | solution.py:321
  (1 shorter events, 0.0 us)
Async XLA Ops:
  0.0 3.0 %collective-permute-start = (bf16[2,2048,128]{2,1,0:T(8,128)(2,1)}, bf16[2,2048,128]{2,1,0:T(8,128)(2,1)S(1)}, u32[]{:S(2)}, u32[]{:S(2)}) collective-permute-start(bf16[2,2048,128]{2,1,0:T(8,128)(2,1)} %w_hbm.1), channel_id=1, source_target_pairs={{0,4},{4,0},{1,5},{5,1},{2,6},{6,2},{3,7},{7,3},{8,12},{12,8},{9,1... | collective-permute-start | bytes 3145736 | tf_op jit(solution)/shard_map/ppermute | solution.py:191
  2.4 6.3 %collective-permute-start.1 = (bf16[1,2,200,128]{3,2,1,0:T(8,128)(2,1)S(1)}, bf16[1,2,200,128]{3,2,1,0:T(8,128)(2,1)S(1)}, u32[]{:S(2)}, u32[]{:S(2)}) collective-permute-start(bf16[1,2,200,128]{3,2,1,0:T(8,128)(2,1)S(1)} %get-tuple-element.19.own_ref), channel_id=1, source_target_pairs={{0,4},{1,5},{2,0},{3,1},{4,6},{5,7},{6,2},{7,3},{8,12},{9,13},{10,... | collective-permute-start | bytes 307208 | tf_op jit(solution)/shard_map/ppermute | solution.py:202
  3.4 6.3 %collective-permute-start.2 = (bf16[1,2,200,128]{3,2,1,0:T(8,128)(2,1)S(1)}, bf16[1,2,200,128]{3,2,1,0:T(8,128)(2,1)S(1)}, u32[]{:S(2)}, u32[]{:S(2)}) collective-permute-start(bf16[1,2,200,128]{3,2,1,0:T(8,128)(2,1)S(1)} %other_heads.1.other_ref), channel_id=1, source_target_pairs={{0,2},{1,3},{2,6},{3,7},{4,0},{5,1},{6,4},{7,5},{8,10},{9,11},{10,... | collective-permute-start | bytes 307208 | tf_op jit(solution)/shard_map/ppermute | solution.py:202
  9.7 6.4 %collective-permute-start.5 = (bf16[1,2,200,128]{3,2,1,0:T(8,128)(2,1)S(1)}, bf16[1,2,200,128]{3,2,1,0:T(8,128)(2,1)S(1)}, u32[]{:S(2)}, u32[]{:S(2)}) collective-permute-start(bf16[1,2,200,128]{3,2,1,0:T(8,128)(2,1)S(1)} %pair_sum.1.keep_ref), channel_id=1, source_target_pairs={{0,1},{1,0},{2,3},{3,2},{4,5},{5,4},{6,7},{7,6},{8,9},{9,8},{10,11... | collective-permute-start | bytes 307208 | tf_op jit(solution)/shard_map/ppermute | solution.py:191
  12.6 6.6 %collective-permute-start.3 = (bf16[1,2,200,128]{3,2,1,0:T(8,128)(2,1)S(1)}, bf16[1,2,200,128]{3,2,1,0:T(8,128)(2,1)S(1)}, u32[]{:S(2)}, u32[]{:S(2)}) collective-permute-start(bf16[1,2,200,128]{3,2,1,0:T(8,128)(2,1)S(1)} %pair_sum.1.keep_ref), channel_id=1, source_target_pairs={{0,24},{8,16},{16,8},{24,0},{1,25},{9,17},{17,9},{25,1},{2,26},{10... | collective-permute-start | bytes 307208 | tf_op jit(solution)/shard_map/ppermute | solution.py:191
  16.2 5.2 %collective-permute-start.6 = (bf16[2,200,128]{2,1,0:T(8,128)(2,1)S(1)}, bf16[2,200,128]{2,1,0:T(8,128)(2,1)S(1)}, u32[]{:S(2)}, u32[]{:S(2)}) collective-permute-start(bf16[2,200,128]{2,1,0:T(8,128)(2,1)S(1)} %sum_norm.1.refs_0_), channel_id=1, source_target_pairs={{0,8},{8,0},{16,24},{24,16},{1,9},{9,1},{17,25},{25,17},{2,10},{10... | collective-permute-start | bytes 307208 | tf_op jit(solution)/shard_map/ppermute | solution.py:191
  17.7 4.7 %collective-permute-start.7 = (bf16[2,200,128]{2,1,0:T(8,128)(2,1)S(1)}, bf16[2,200,128]{2,1,0:T(8,128)(2,1)S(1)}, u32[]{:S(2)}, u32[]{:S(2)}) collective-permute-start(bf16[2,200,128]{2,1,0:T(8,128)(2,1)S(1)} %sum_norm.1.refs_0_), channel_id=1, source_target_pairs={{0,16},{8,24},{16,0},{24,8},{1,17},{9,25},{17,1},{25,9},{2,18},{10... | collective-permute-start | bytes 307208 | tf_op jit(solution)/shard_map/ppermute | solution.py:191
  19.2 4.7 %collective-permute-start.4 = (bf16[1,2,200,128]{3,2,1,0:T(8,128)(2,1)S(1)}, bf16[1,2,200,128]{3,2,1,0:T(8,128)(2,1)S(1)}, u32[]{:S(2)}, u32[]{:S(2)}) collective-permute-start(bf16[1,2,200,128]{3,2,1,0:T(8,128)(2,1)S(1)} %collective-permute-done.3.refs_0_), channel_id=1, source_target_pairs={{0,1},{1,0},{2,3},{3,2},{4,5},{5,4},{6,7},{7,6},{8,9},{9,8},{10,11... | collective-permute-start | bytes 307208 | tf_op jit(solution)/shard_map/ppermute | solution.py:191

commit v2 on v1

--- a/solution.py
+++ b/solution.py
@@ -196,7 +196,7 @@
 
     def exchange(value, senders):
         hops = [
-            (4 * d + t, 4 * d + (t ^ 2) if (t // 2 == d) == senders else 4 * (1 - d) + t)
+            (4 * d + t, 4 * d + (t ^ 3) if (t // 2 == d) == senders else 4 * (1 - d) + t)
             for d, t in devices
         ]
         return lax.ppermute(value, ("dp", "tensor"), hops)

time: 25.3 us -> 25.5 us (level)
  starting transfers between devices: 14.7 us -> 15.4 us
  waiting for transfers between devices: 4.4 us -> 3.93 us
    ppermute x2, starting transfers between devices: 4.14 us -> 5.15 us  [exchange(): return lax.ppermute(value, ('dp', 'tensor'), hops)]
    ppermute x6, waiting for transfers between devices: 3.43 us -> 2.96 us  [swap(): lax.ppermute(value, axis, [(i, i ^ k) for i in range(lax.axis_size(axis))])]
    ppermute x6, starting transfers between devices: 10.6 us -> 10.2 us  [swap(): lax.ppermute(value, axis, [(i, i ^ k) for i in range(lax.axis_size(axis))])]
  transfers between devices with their start and end apart: 8 -> 8, of which waited for: 5 -> 6; matrix products, arithmetic and copies ran while one was open for 0% -> 0% of each run, Pallas kernels for 19% -> 19%
where the time goes in v2:
time: 25.5 us; the launch traced here: 25.4 us
  starting transfers between devices  15.4 us (60%)
  Pallas kernels  6.02 us (24%)
  waiting for transfers between devices  3.93 us (15%)
    ppermute x6, starting transfers between devices, swap(): lax.ppermute(value, axis, [(i, i ^ k) for i in range(lax.axis_size(axis))])  10.2 us
    ppermute x2, starting transfers between devices, exchange(): return lax.ppermute(value, ('dp', 'tensor'), hops)  5.15 us
    ppermute x6, waiting for transfers between devices, swap(): lax.ppermute(value, axis, [(i, i ^ k) for i in range(lax.axis_size(axis))])  2.96 us
    pallas_call x3, Pallas kernels, on_device(): call(functools.partial(attend_kernel, here, there, tile_len, first, last,...  2.27 us
    pallas_call x1, Pallas kernels, on_device(): call(functools.partial(own_kernel, head_dim), [shape_of((own_heads, 2, ro...  1.92 us
    pallas_call x1, Pallas kernels, on_device(): call(query_kernel, [shape_of((head_dim, pairs)), shape_of((tiles, pairs),...  1.27 us
    ppermute x2, waiting for transfers between devices, exchange(): return lax.ppermute(value, ('dp', 'tensor'), hops)  0.97 us
  transfers between devices with their start and end apart: 8, of which 6 were waited for; matrix products, arithmetic and copies ran while one was open for 0% of the time, Pallas kernels for 19%

profile of v2, /device:TPU:0, one launch (start us, length us, event | category | flops | bytes accessed | tf_op | source)
XLA Modules:
  0.0 25.4 jit_solution(6219328052843647783)
XLA Ops:
  0.0 0.5 %collective-permute-start = (bf16[2,2048,128]{2,1,0:T(8,128)(2,1)}, bf16[2,2048,128]{2,1,0:T(8,128)(2,1)S(1)}, u32[]{:S(2)}, u32[]{:S(2)}) collective-permute-start(bf16[2,2048,128]{2,1,0:T(8,128)(2,1)} %w_hbm.1), channel_id=1, source_target_pairs={{0,4},{4,0},{1,5},{5,1},{2,6},{6,2},{3,7},{7,3},{8,12},{12,8},{9,1... | collective-permute-start | bytes 3145736 | tf_op jit(solution)/shard_map/ppermute | solution.py:191
  0.5 1.9 %own_head.1 = (bf16[1,2,200,128]{3,2,1,0:T(8,128)(2,1)S(1)}, bf16[1,200,2048]{2,1,0:T(8,128)(2,1)S(1)}, f32[1,128]{1,0:T(1,128)S(1)}) custom-call(bf16[1,200,2048]{2,1,0:T(8,128)(2,1)} %x_hbm.1, bf16[2,2048,128]{2,1,0:T(8,128)(2,1)} %w_hbm.1, f32[1,128]{1,0:T(1,128)} %bitcast.5), custom_call_target="tpu_custom_call" | custom-call | flops 209715200 | bytes 1867776 | tf_op jit(solution)/shard_map/own_head/pallas_call | solution.py:262
  2.4 0.1 collective-permute-start.1
  2.5 0.5 %collective-permute-done.w_ref = bf16[2,2048,128]{2,1,0:T(8,128)(2,1)S(1)} collective-permute-done((bf16[2,2048,128]{2,1,0:T(8,128)(2,1)}, bf16[2,2048,128]{2,1,0:T(8,128)(2,1)S(1)}, u32[]{:S(2)}, u32[]{:S(2)}) %collective-permute-start) | collective-permute-done | bytes 1048608 | tf_op jit(solution)/shard_map/ppermute | solution.py:191
  3.0 0.4 %other_heads.1.other_ref = bf16[1,2,200,128]{3,2,1,0:T(8,128)(2,1)S(1)} custom-call(bf16[1,200,2048]{2,1,0:T(8,128)(2,1)S(1)} %get-tuple-element.20.x_ref, bf16[2,2048,128]{2,1,0:T(8,128)(2,1)S(1)} %collective-permute-done.w_ref), custom_call_target="tpu_custom_call" | custom-call | flops 209715200 | tf_op jit(solution)/shard_map/other_heads/pallas_call | solution.py:291
  3.4 5.0 %collective-permute-start.2 = (bf16[1,2,200,128]{3,2,1,0:T(8,128)(2,1)S(1)}, bf16[1,2,200,128]{3,2,1,0:T(8,128)(2,1)S(1)}, u32[]{:S(2)}, u32[]{:S(2)}) collective-permute-start(bf16[1,2,200,128]{3,2,1,0:T(8,128)(2,1)S(1)} %other_heads.1.other_ref), channel_id=1, source_target_pairs={{0,3},{1,2},{2,6},{3,7},{4,0},{5,1},{6,5},{7,4},{8,11},{9,10},{10,... | collective-permute-start | bytes 307208 | tf_op jit(solution)/shard_map/ppermute | solution.py:202
  8.4 1.3 %queries.1 = (bf16[128,512]{1,0:T(8,128)(2,1)S(1)}, f32[4,512]{1,0:T(4,128)S(1)}) custom-call(bf16[128,512]{1,0:T(8,128)(2,1)} %refs_0_.1, f32[1,128]{1,0:T(1,128)} %bitcast.4, s32[4,128]{1,0:T(4,128)} %bitcast.3), custom_call_target="tpu_custom_call" | custom-call | tf_op jit(solution)/shard_map/queries/pallas_call | solution.py:276
  9.7 0.1 collective-permute-done.1.first_ref
  9.8 0.8 %collective-permute-done.2.second_ref = bf16[1,2,200,128]{3,2,1,0:T(8,128)(2,1)S(1)} collective-permute-done((bf16[1,2,200,128]{3,2,1,0:T(8,128)(2,1)S(1)}, bf16[1,2,200,128]{3,2,1,0:T(8,128)(2,1)S(1)}, u32[]{:S(2)}, u32[]{:S(2)}) %collective-permute-start.2) | collective-permute-done | bytes 102432 | tf_op jit(solution)/shard_map/ppermute | solution.py:202
  10.7 1.8 %collective-permute-start.5 = (bf16[1,2,200,128]{3,2,1,0:T(8,128)(2,1)S(1)}, bf16[1,2,200,128]{3,2,1,0:T(8,128)(2,1)S(1)}, u32[]{:S(2)}, u32[]{:S(2)}) collective-permute-start(bf16[1,2,200,128]{3,2,1,0:T(8,128)(2,1)S(1)} %pair_sum.1.keep_ref), channel_id=1, source_target_pairs={{0,1},{1,0},{2,3},{3,2},{4,5},{5,4},{6,7},{7,6},{8,9},{9,8},{10,11... | collective-permute-start | bytes 307208 | tf_op jit(solution)/shard_map/ppermute | solution.py:191
  12.4 2.4 %collective-permute-start.3 = (bf16[1,2,200,128]{3,2,1,0:T(8,128)(2,1)S(1)}, bf16[1,2,200,128]{3,2,1,0:T(8,128)(2,1)S(1)}, u32[]{:S(2)}, u32[]{:S(2)}) collective-permute-start(bf16[1,2,200,128]{3,2,1,0:T(8,128)(2,1)S(1)} %pair_sum.1.keep_ref), channel_id=1, source_target_pairs={{0,24},{8,16},{16,8},{24,0},{1,25},{9,17},{17,9},{25,1},{2,26},{10... | collective-permute-start | bytes 307208 | tf_op jit(solution)/shard_map/ppermute | solution.py:191
  14.9 0.8 %collective-permute-done.5.arrived_ref = bf16[1,2,200,128]{3,2,1,0:T(8,128)(2,1)S(1)} collective-permute-done((bf16[1,2,200,128]{3,2,1,0:T(8,128)(2,1)S(1)}, bf16[1,2,200,128]{3,2,1,0:T(8,128)(2,1)S(1)}, u32[]{:S(2)}, u32[]{:S(2)}) %collective-permute-start.5) | collective-permute-done | bytes 102432 | tf_op jit(solution)/shard_map/ppermute | solution.py:191
  15.7 0.1 sum_norm.1.refs_0_
  15.8 1.6 %collective-permute-start.6 = (bf16[2,200,128]{2,1,0:T(8,128)(2,1)S(1)}, bf16[2,200,128]{2,1,0:T(8,128)(2,1)S(1)}, u32[]{:S(2)}, u32[]{:S(2)}) collective-permute-start(bf16[2,200,128]{2,1,0:T(8,128)(2,1)S(1)} %sum_norm.1.refs_0_), channel_id=1, source_target_pairs={{0,8},{8,0},{16,24},{24,16},{1,9},{9,1},{17,25},{25,17},{2,10},{10... | collective-permute-start | bytes 307208 | tf_op jit(solution)/shard_map/ppermute | solution.py:191
  17.4 1.5 %collective-permute-start.7 = (bf16[2,200,128]{2,1,0:T(8,128)(2,1)S(1)}, bf16[2,200,128]{2,1,0:T(8,128)(2,1)S(1)}, u32[]{:S(2)}, u32[]{:S(2)}) collective-permute-start(bf16[2,200,128]{2,1,0:T(8,128)(2,1)S(1)} %sum_norm.1.refs_0_), channel_id=1, source_target_pairs={{0,16},{8,24},{16,0},{24,8},{1,17},{9,25},{17,1},{25,9},{2,18},{10... | collective-permute-start | bytes 307208 | tf_op jit(solution)/shard_map/ppermute | solution.py:191
  18.9 0.0 collective-permute-done.3.refs_0_
  18.9 2.5 %collective-permute-start.4 = (bf16[1,2,200,128]{3,2,1,0:T(8,128)(2,1)S(1)}, bf16[1,2,200,128]{3,2,1,0:T(8,128)(2,1)S(1)}, u32[]{:S(2)}, u32[]{:S(2)}) collective-permute-start(bf16[1,2,200,128]{3,2,1,0:T(8,128)(2,1)S(1)} %collective-permute-done.3.refs_0_), channel_id=1, source_target_pairs={{0,1},{1,0},{2,3},{3,2},{4,5},{5,4},{6,7},{7,6},{8,9},{9,8},{10,11... | collective-permute-start | bytes 307208 | tf_op jit(solution)/shard_map/ppermute | solution.py:191
  21.4 0.4 %attend.3 = (f32[1,512]{1,0:T(1,128)S(1)}, f32[1,512]{1,0:T(1,128)S(1)}, f32[128,512]{1,0:T(8,128)S(1)}) custom-call(f32[1,128]{1,0:T(1,128)S(1)} %get-tuple-element.16.k_gain_ref, bf16[128,512]{1,0:T(8,128)(2,1)S(1)} %get-tuple-element.17.qt_ref, f32[4,512]{1,0:T(4,128)S(1)} %get-tuple-element.18.bias_ref, bf16[2,200,128]{2,1,0:T(8,128)(2,1)S(1)} %sum_norm.1.refs_0_), custom_call_target="tpu_custom_call" | custom-call | flops 52428800 | tf_op jit(solution)/shard_map/attend/pallas_call | solution.py:321
  21.8 0.0 collective-permute-done.6.refs_0_
  21.8 1.0 %collective-permute-done.7.refs_1_ = bf16[2,200,128]{2,1,0:T(8,128)(2,1)S(1)} collective-permute-done((bf16[2,200,128]{2,1,0:T(8,128)(2,1)S(1)}, bf16[2,200,128]{2,1,0:T(8,128)(2,1)S(1)}, u32[]{:S(2)}, u32[]{:S(2)}) %collective-permute-start.7) | collective-permute-done | bytes 102432 | tf_op jit(solution)/shard_map/ppermute | solution.py:191
  22.9 0.6 %attend.4 = (f32[1,512]{1,0:T(1,128)S(1)}, f32[1,512]{1,0:T(1,128)S(1)}, f32[128,512]{1,0:T(8,128)S(1)}) custom-call(f32[1,128]{1,0:T(1,128)S(1)} %get-tuple-element.16.k_gain_ref, bf16[128,512]{1,0:T(8,128)(2,1)S(1)} %get-tuple-element.17.qt_ref, f32[4,512]{1,0:T(4,128)S(1)} %get-tuple-element.18.bias_ref, ...), custom_call_target="tpu_custom_call" | custom-call | flops 104857600 | tf_op jit(solution)/shard_map/attend/pallas_call | solution.py:321
  23.4 0.7 %collective-permute-done.4.refs_1_ = bf16[1,2,200,128]{3,2,1,0:T(8,128)(2,1)S(1)} collective-permute-done((bf16[1,2,200,128]{3,2,1,0:T(8,128)(2,1)S(1)}, bf16[1,2,200,128]{3,2,1,0:T(8,128)(2,1)S(1)}, u32[]{:S(2)}, u32[]{:S(2)}) %collective-permute-start.4) | collective-permute-done | bytes 102432 | tf_op jit(solution)/shard_map/ppermute | solution.py:191
  24.1 1.3 %attend.5 = bf16[128,512]{1,0:T(8,128)(2,1)} custom-call(f32[1,128]{1,0:T(1,128)S(1)} %get-tuple-element.16.k_gain_ref, bf16[128,512]{1,0:T(8,128)(2,1)S(1)} %get-tuple-element.17.qt_ref, f32[4,512]{1,0:T(4,128)S(1)} %get-tuple-element.18.bias_ref, bf16[1,2,200,128]{3,2,1,0:T(8,128)(2,1)S(1)} %collective-permute-done.3.refs_0_, ...), custom_call_target="tpu_custom_call" | custom-call | flops 52428800 | tf_op jit(solution)/shard_map/attend/pallas_call | solution.py:321
  (1 shorter events, 0.0 us)
Async XLA Ops:
  0.0 3.0 %collective-permute-start = (bf16[2,2048,128]{2,1,0:T(8,128)(2,1)}, bf16[2,2048,128]{2,1,0:T(8,128)(2,1)S(1)}, u32[]{:S(2)}, u32[]{:S(2)}) collective-permute-start(bf16[2,2048,128]{2,1,0:T(8,128)(2,1)} %w_hbm.1), channel_id=1, source_target_pairs={{0,4},{4,0},{1,5},{5,1},{2,6},{6,2},{3,7},{7,3},{8,12},{12,8},{9,1... | collective-permute-start | bytes 3145736 | tf_op jit(solution)/shard_map/ppermute | solution.py:191
  2.4 7.4 %collective-permute-start.1 = (bf16[1,2,200,128]{3,2,1,0:T(8,128)(2,1)S(1)}, bf16[1,2,200,128]{3,2,1,0:T(8,128)(2,1)S(1)}, u32[]{:S(2)}, u32[]{:S(2)}) collective-permute-start(bf16[1,2,200,128]{3,2,1,0:T(8,128)(2,1)S(1)} %get-tuple-element.19.own_ref), channel_id=1, source_target_pairs={{0,4},{1,5},{2,1},{3,0},{4,7},{5,6},{6,2},{7,3},{8,12},{9,13},{10,... | collective-permute-start | bytes 307208 | tf_op jit(solution)/shard_map/ppermute | solution.py:202
  3.4 7.3 %collective-permute-start.2 = (bf16[1,2,200,128]{3,2,1,0:T(8,128)(2,1)S(1)}, bf16[1,2,200,128]{3,2,1,0:T(8,128)(2,1)S(1)}, u32[]{:S(2)}, u32[]{:S(2)}) collective-permute-start(bf16[1,2,200,128]{3,2,1,0:T(8,128)(2,1)S(1)} %other_heads.1.other_ref), channel_id=1, source_target_pairs={{0,3},{1,2},{2,6},{3,7},{4,0},{5,1},{6,5},{7,4},{8,11},{9,10},{10,... | collective-permute-start | bytes 307208 | tf_op jit(solution)/shard_map/ppermute | solution.py:202
  10.7 5.0 %collective-permute-start.5 = (bf16[1,2,200,128]{3,2,1,0:T(8,128)(2,1)S(1)}, bf16[1,2,200,128]{3,2,1,0:T(8,128)(2,1)S(1)}, u32[]{:S(2)}, u32[]{:S(2)}) collective-permute-start(bf16[1,2,200,128]{3,2,1,0:T(8,128)(2,1)S(1)} %pair_sum.1.keep_ref), channel_id=1, source_target_pairs={{0,1},{1,0},{2,3},{3,2},{4,5},{5,4},{6,7},{7,6},{8,9},{9,8},{10,11... | collective-permute-start | bytes 307208 | tf_op jit(solution)/shard_map/ppermute | solution.py:191
  12.4 6.5 %collective-permute-start.3 = (bf16[1,2,200,128]{3,2,1,0:T(8,128)(2,1)S(1)}, bf16[1,2,200,128]{3,2,1,0:T(8,128)(2,1)S(1)}, u32[]{:S(2)}, u32[]{:S(2)}) collective-permute-start(bf16[1,2,200,128]{3,2,1,0:T(8,128)(2,1)S(1)} %pair_sum.1.keep_ref), channel_id=1, source_target_pairs={{0,24},{8,16},{16,8},{24,0},{1,25},{9,17},{17,9},{25,1},{2,26},{10... | collective-permute-start | bytes 307208 | tf_op jit(solution)/shard_map/ppermute | solution.py:191
  15.8 6.0 %collective-permute-start.6 = (bf16[2,200,128]{2,1,0:T(8,128)(2,1)S(1)}, bf16[2,200,128]{2,1,0:T(8,128)(2,1)S(1)}, u32[]{:S(2)}, u32[]{:S(2)}) collective-permute-start(bf16[2,200,128]{2,1,0:T(8,128)(2,1)S(1)} %sum_norm.1.refs_0_), channel_id=1, source_target_pairs={{0,8},{8,0},{16,24},{24,16},{1,9},{9,1},{17,25},{25,17},{2,10},{10... | collective-permute-start | bytes 307208 | tf_op jit(solution)/shard_map/ppermute | solution.py:191
  17.4 5.5 %collective-permute-start.7 = (bf16[2,200,128]{2,1,0:T(8,128)(2,1)S(1)}, bf16[2,200,128]{2,1,0:T(8,128)(2,1)S(1)}, u32[]{:S(2)}, u32[]{:S(2)}) collective-permute-start(bf16[2,200,128]{2,1,0:T(8,128)(2,1)S(1)} %sum_norm.1.refs_0_), channel_id=1, source_target_pairs={{0,16},{8,24},{16,0},{24,8},{1,17},{9,25},{17,1},{25,9},{2,18},{10... | collective-permute-start | bytes 307208 | tf_op jit(solution)/shard_map/ppermute | solution.py:191
  18.9 5.2 %collective-permute-start.4 = (bf16[1,2,200,128]{3,2,1,0:T(8,128)(2,1)S(1)}, bf16[1,2,200,128]{3,2,1,0:T(8,128)(2,1)S(1)}, u32[]{:S(2)}, u32[]{:S(2)}) collective-permute-start(bf16[1,2,200,128]{3,2,1,0:T(8,128)(2,1)S(1)} %collective-permute-done.3.refs_0_), channel_id=1, source_target_pairs={{0,1},{1,0},{2,3},{3,2},{4,5},{5,4},{6,7},{7,6},{8,9},{9,8},{10,11... | collective-permute-start | bytes 307208 | tf_op jit(solution)/shard_map/ppermute | solution.py:191

commit v3 on v1

--- a/solution.py
+++ b/solution.py
@@ -111,11 +111,17 @@
     prepare_queries(refs[:3], refs[5:8], refs[8], *refs[3:5])
 
 
-def pair_kernel(own_ref, other_ref, first_ref, second_ref, bias_ref, out_ref):
-    mine = lax.axis_index("tensor") // 2 == lax.axis_index("dp")
-    keep = jnp.where(mine, own_ref[...], other_ref[...]).astype(F32)
-    arrived = jnp.where(mine, first_ref[...], second_ref[...]).astype(F32)
-    out_ref[...] = (keep + arrived).astype(BF16)
+def first_sum_kernel(own_ref, first_ref, bias_ref, out_ref):
+    out_ref[...] = (own_ref[...].astype(F32) + first_ref[...].astype(F32)).astype(BF16)
+
+
+def has_own_head():
+    return lax.axis_index("tensor") // 2 == lax.axis_index("dp")
+
+
+def second_sum_kernel(first_sum_ref, other_ref, second_ref, out_ref):
+    total = (other_ref[...].astype(F32) + second_ref[...].astype(F32)).astype(BF16)
+    out_ref[...] = jnp.where(has_own_head(), first_sum_ref[...], total)
 
 
 def add_kernel(bit, keep_ref, arrived_ref, send_ref, next_ref, held):
@@ -135,8 +141,11 @@
     return normalize(keys, k_gain).astype(BF16), values.astype(BF16)
 
 
-def norm_kernel(k_gain_ref, keep_ref, arrived_ref, kv_ref):
-    kv_ref[0], kv_ref[1] = finish_rows(k_gain_ref[...], keep_ref.at[0], arrived_ref.at[0])
+def norm_kernel(k_gain_ref, keep_ref, *refs):
+    arrived = refs[0][0]
+    if len(refs) > 2:
+        arrived = jnp.where(has_own_head(), arrived, refs[1][0])
+    refs[-1][0], refs[-1][1] = finish_rows(k_gain_ref[...], keep_ref[0], arrived)
 
 
 def attend_kernel(near, far, tile_len, first, last, head_dim, k_gain_ref, qt_ref, bias_ref, *refs):
@@ -201,10 +210,19 @@
         ]
         return lax.ppermute(value, ("dp", "tensor"), hops)
 
+    def pair_swap(value, takers):
+        hops = [
+            (4 * d + t, 4 * d + (t ^ 1 if (t // 2 == d) == takers else t)) for d, t in devices
+        ]
+        return lax.ppermute(value, ("dp", "tensor"), hops)
+
     first = exchange(own, False)
     rest = other(1)
     second = exchange(rest, True)
-    return call(pair_kernel, shape_of(own.shape), 5, "pair_sum")(own, rest, first, second, bias)
+    first_sum = call(first_sum_kernel, shape_of(own.shape), 3, "first_sum")(own, first, bias)
+    early = pair_swap(first_sum, True)
+    total = call(second_sum_kernel, shape_of(own.shape), 3, "second_sum")(first_sum, rest, second)
+    return total, [early, pair_swap(total, False)]
 
 
 def sum_many_heads(own, others):
@@ -233,8 +251,8 @@
                 scratch=[pltpu.VMEM(now, BF16)],
             )(keep, arrived)
         else:
-            send = keep = call(add_last_kernel, shape_of(now), 2, "add_pair")(keep, arrived)
-    return send, keep
+            keep = call(add_last_kernel, shape_of(now), 2, "add_pair")(keep, arrived)
+    return keep
 
 
 def on_device(queries, images, kv_weight, q_gain, k_gain, tile_mask):
@@ -293,14 +311,16 @@
         )(x, others[k - 1])
 
     if n_dp == 2 and own_heads == 1:
-        send = keep = sum_two_heads(own, other, bias)
+        total, arrived = sum_two_heads(own, other, bias)
     else:
-        send, keep = sum_many_heads(own, [other(k) for k in range(1, n_dp)])
+        total = sum_many_heads(own, [other(k) for k in range(1, n_dp)])
+        arrived = [swap(total, "tensor", 1)]
     far = [step for step in range(1, n_section) if step & (step - 1)]
     near = [step for step in range(1, n_section) if not step & (step - 1)]
-    arrived = swap(send, "tensor", 1)
-    halves = [swap(send, "section", step) for step in far]
-    kv = call(norm_kernel, shape_of((2, rows, head_dim)), 3, "sum_norm")(gain, keep, arrived)
+    halves = [swap(total, "section", step) for step in far]
+    kv = call(norm_kernel, shape_of((2, rows, head_dim)), 2 + len(arrived), "sum_norm")(
+        gain, total, *arrived
+    )
     finished = [swap(kv, "section", step) for step in near]
     both = []
     for value in halves:

time: 25.3 us -> 26.5 us (1.047)
  the two profiles are of different devices: /device:TPU:0 before, /device:TPU:20 now
where the time goes in v3:
time: 26.5 us; the launch traced here: 26.3 us
  waiting for transfers between devices  10.3 us (39%)
  starting transfers between devices  9.85 us (37%)
  Pallas kernels  6.06 us (23%)
    ppermute x5, waiting for transfers between devices, swap(): lax.ppermute(value, axis, [(i, i ^ k) for i in range(lax.axis_size(axis))])  5.67 us
    ppermute x2, starting transfers between devices, pair_swap(): return lax.ppermute(value, ('dp', 'tensor'), hops)  5.42 us
    ppermute x5, starting transfers between devices, swap(): lax.ppermute(value, axis, [(i, i ^ k) for i in range(lax.axis_size(axis))])  3.83 us
    ppermute x2, waiting for transfers between devices, exchange(): return lax.ppermute(value, ('dp', 'tensor'), hops)  3.53 us
    pallas_call x3, Pallas kernels, on_device(): call(functools.partial(attend_kernel, here, there, tile_len, first, last,...  2.26 us
    pallas_call x1, Pallas kernels, on_device(): call(functools.partial(own_kernel, head_dim), [shape_of((own_heads, 2, ro...  1.92 us
    pallas_call x1, Pallas kernels, on_device(): call(query_kernel, [shape_of((head_dim, pairs)), shape_of((tiles, pairs),...  1.27 us
    ppermute x2, waiting for transfers between devices, pair_swap(): return lax.ppermute(value, ('dp', 'tensor'), hops)  1.12 us
  transfers between devices with their start and end apart: 9, of which 7 were waited for; matrix products, arithmetic and copies ran while one was open for 0% of the time, Pallas kernels for 18%

profile of v3, /device:TPU:20, one launch (start us, length us, event | category | flops | bytes accessed | tf_op | source)
XLA Modules:
  0.0 26.3 jit_solution(5349102143457276287)
XLA Ops:
  0.0 0.0 collective-permute-start.1
  0.0 1.9 %own_head.1 = (bf16[1,2,200,128]{3,2,1,0:T(8,128)(2,1)S(1)}, bf16[1,200,2048]{2,1,0:T(8,128)(2,1)S(1)}, f32[1,128]{1,0:T(1,128)S(1)}) custom-call(bf16[1,200,2048]{2,1,0:T(8,128)(2,1)} %x_hbm.1, bf16[2,2048,128]{2,1,0:T(8,128)(2,1)} %w_hbm.1, f32[1,128]{1,0:T(1,128)} %bitcast.5), custom_call_target="tpu_custom_call" | custom-call | flops 209715200 | bytes 1867776 | tf_op jit(solution)/shard_map/own_head/pallas_call | solution.py:280
  1.9 0.4 %collective-permute-start = (bf16[1,2,200,128]{3,2,1,0:T(8,128)(2,1)S(1)}, bf16[1,2,200,128]{3,2,1,0:T(8,128)(2,1)S(1)}, u32[]{:S(2)}, u32[]{:S(2)}) collective-permute-start(bf16[1,2,200,128]{3,2,1,0:T(8,128)(2,1)S(1)} %get-tuple-element.19.own_ref), channel_id=1, source_target_pairs={{0,4},{1,5},{2,0},{3,1},{4,6},{5,7},{6,2},{7,3},{8,12},{9,13},{10,... | collective-permute-start | bytes 307208 | tf_op jit(solution)/shard_map/ppermute | solution.py:211
  2.3 0.5 %collective-permute-done.1.w_ref = bf16[2,2048,128]{2,1,0:T(8,128)(2,1)S(1)} collective-permute-done((bf16[2,2048,128]{2,1,0:T(8,128)(2,1)}, bf16[2,2048,128]{2,1,0:T(8,128)(2,1)S(1)}, u32[]{:S(2)}, u32[]{:S(2)}) %collective-permute-start.1) | collective-permute-done | bytes 1048608 | tf_op jit(solution)/shard_map/ppermute | solution.py:200
  2.9 0.4 %other_heads.1.other_ref = bf16[1,2,200,128]{3,2,1,0:T(8,128)(2,1)S(1)} custom-call(bf16[1,200,2048]{2,1,0:T(8,128)(2,1)S(1)} %get-tuple-element.20.x_ref, bf16[2,2048,128]{2,1,0:T(8,128)(2,1)S(1)} %collective-permute-done.1.w_ref), custom_call_target="tpu_custom_call" | custom-call | flops 209715200 | tf_op jit(solution)/shard_map/other_heads/pallas_call | solution.py:309
  3.3 0.2 collective-permute-start.2
  3.5 1.3 %queries.1 = (bf16[128,512]{1,0:T(8,128)(2,1)S(1)}, f32[4,512]{1,0:T(4,128)S(1)}) custom-call(bf16[128,512]{1,0:T(8,128)(2,1)} %refs_0_.1, f32[1,128]{1,0:T(1,128)} %bitcast.4, s32[4,128]{1,0:T(4,128)} %bitcast.3), custom_call_target="tpu_custom_call" | custom-call | tf_op jit(solution)/shard_map/queries/pallas_call | solution.py:294
  4.8 0.0 collective-permute-done.first_ref
  4.8 0.7 %collective-permute-start.5 = (bf16[1,2,200,128]{3,2,1,0:T(8,128)(2,1)S(1)}, bf16[1,2,200,128]{3,2,1,0:T(8,128)(2,1)S(1)}, u32[]{:S(2)}, u32[]{:S(2)}) collective-permute-start(bf16[1,2,200,128]{3,2,1,0:T(8,128)(2,1)S(1)} %first_sum.1.first_sum_ref), channel_id=1, source_target_pairs={{0,1},{1,0},{2,2},{3,3},{4,4},{5,5},{6,7},{7,6},{8,9},{9,8},{10,10... | collective-permute-start | bytes 307208 | tf_op jit(solution)/shard_map/ppermute | solution.py:217
  5.5 3.5 %collective-permute-done.2.second_ref = bf16[1,2,200,128]{3,2,1,0:T(8,128)(2,1)S(1)} collective-permute-done((bf16[1,2,200,128]{3,2,1,0:T(8,128)(2,1)S(1)}, bf16[1,2,200,128]{3,2,1,0:T(8,128)(2,1)S(1)}, u32[]{:S(2)}, u32[]{:S(2)}) %collective-permute-start.2) | collective-permute-done | bytes 102432 | tf_op jit(solution)/shard_map/ppermute | solution.py:211
  9.0 4.8 %collective-permute-start.6 = (bf16[1,2,200,128]{3,2,1,0:T(8,128)(2,1)S(1)}, bf16[1,2,200,128]{3,2,1,0:T(8,128)(2,1)S(1)}, u32[]{:S(2)}, u32[]{:S(2)}) collective-permute-start(bf16[1,2,200,128]{3,2,1,0:T(8,128)(2,1)S(1)} %second_sum.1.keep_ref), channel_id=1, source_target_pairs={{0,0},{1,1},{2,3},{3,2},{4,5},{5,4},{6,6},{7,7},{8,8},{9,9},{10,11... | collective-permute-start | bytes 307208 | tf_op jit(solution)/shard_map/ppermute | solution.py:217
  13.8 1.5 %collective-permute-start.3 = (bf16[1,2,200,128]{3,2,1,0:T(8,128)(2,1)S(1)}, bf16[1,2,200,128]{3,2,1,0:T(8,128)(2,1)S(1)}, u32[]{:S(2)}, u32[]{:S(2)}) collective-permute-start(bf16[1,2,200,128]{3,2,1,0:T(8,128)(2,1)S(1)} %second_sum.1.keep_ref), channel_id=1, source_target_pairs={{0,24},{8,16},{16,8},{24,0},{1,25},{9,17},{17,9},{25,1},{2,26},{10... | collective-permute-start | bytes 307208 | tf_op jit(solution)/shard_map/ppermute | solution.py:200
  15.3 0.0 collective-permute-done.5.refs_0_
  15.3 1.1 %collective-permute-done.6.refs_1_ = bf16[1,2,200,128]{3,2,1,0:T(8,128)(2,1)S(1)} collective-permute-done((bf16[1,2,200,128]{3,2,1,0:T(8,128)(2,1)S(1)}, bf16[1,2,200,128]{3,2,1,0:T(8,128)(2,1)S(1)}, u32[]{:S(2)}, u32[]{:S(2)}) %collective-permute-start.6) | collective-permute-done | bytes 102432 | tf_op jit(solution)/shard_map/ppermute | solution.py:217
  16.4 0.1 sum_norm.1.refs_0_
  16.6 1.6 %collective-permute-start.7 = (bf16[2,200,128]{2,1,0:T(8,128)(2,1)S(1)}, bf16[2,200,128]{2,1,0:T(8,128)(2,1)S(1)}, u32[]{:S(2)}, u32[]{:S(2)}) collective-permute-start(bf16[2,200,128]{2,1,0:T(8,128)(2,1)S(1)} %sum_norm.1.refs_0_), channel_id=1, source_target_pairs={{0,8},{8,0},{16,24},{24,16},{1,9},{9,1},{17,25},{25,17},{2,10},{10... | collective-permute-start | bytes 307208 | tf_op jit(solution)/shard_map/ppermute | solution.py:200
  18.1 0.5 %collective-permute-start.8 = (bf16[2,200,128]{2,1,0:T(8,128)(2,1)S(1)}, bf16[2,200,128]{2,1,0:T(8,128)(2,1)S(1)}, u32[]{:S(2)}, u32[]{:S(2)}) collective-permute-start(bf16[2,200,128]{2,1,0:T(8,128)(2,1)S(1)} %sum_norm.1.refs_0_), channel_id=1, source_target_pairs={{0,16},{8,24},{16,0},{24,8},{1,17},{9,25},{17,1},{25,9},{2,18},{10... | collective-permute-start | bytes 307208 | tf_op jit(solution)/shard_map/ppermute | solution.py:200
  18.6 1.8 %collective-permute-done.3.refs_0_ = bf16[1,2,200,128]{3,2,1,0:T(8,128)(2,1)S(1)} collective-permute-done((bf16[1,2,200,128]{3,2,1,0:T(8,128)(2,1)S(1)}, bf16[1,2,200,128]{3,2,1,0:T(8,128)(2,1)S(1)}, u32[]{:S(2)}, u32[]{:S(2)}) %collective-permute-start.3) | collective-permute-done | bytes 102432 | tf_op jit(solution)/shard_map/ppermute | solution.py:200
  20.4 0.3 collective-permute-start.4
  20.7 0.4 %attend.3 = (f32[1,512]{1,0:T(1,128)S(1)}, f32[1,512]{1,0:T(1,128)S(1)}, f32[128,512]{1,0:T(8,128)S(1)}) custom-call(f32[1,128]{1,0:T(1,128)S(1)} %get-tuple-element.16.k_gain_ref, bf16[128,512]{1,0:T(8,128)(2,1)S(1)} %get-tuple-element.17.qt_ref, f32[4,512]{1,0:T(4,128)S(1)} %get-tuple-element.18.bias_ref, bf16[2,200,128]{2,1,0:T(8,128)(2,1)S(1)} %sum_norm.1.refs_0_), custom_call_target="tpu_custom_call" | custom-call | flops 52428800 | tf_op jit(solution)/shard_map/attend/pallas_call | solution.py:341
  21.1 0.2 collective-permute-done.7.refs_0_
  21.3 1.5 %collective-permute-done.8.refs_1_ = bf16[2,200,128]{2,1,0:T(8,128)(2,1)S(1)} collective-permute-done((bf16[2,200,128]{2,1,0:T(8,128)(2,1)S(1)}, bf16[2,200,128]{2,1,0:T(8,128)(2,1)S(1)}, u32[]{:S(2)}, u32[]{:S(2)}) %collective-permute-start.8) | collective-permute-done | bytes 102432 | tf_op jit(solution)/shard_map/ppermute | solution.py:200
  22.8 0.6 %attend.4 = (f32[1,512]{1,0:T(1,128)S(1)}, f32[1,512]{1,0:T(1,128)S(1)}, f32[128,512]{1,0:T(8,128)S(1)}) custom-call(f32[1,128]{1,0:T(1,128)S(1)} %get-tuple-element.16.k_gain_ref, bf16[128,512]{1,0:T(8,128)(2,1)S(1)} %get-tuple-element.17.qt_ref, f32[4,512]{1,0:T(4,128)S(1)} %get-tuple-element.18.bias_ref, ...), custom_call_target="tpu_custom_call" | custom-call | flops 104857600 | tf_op jit(solution)/shard_map/attend/pallas_call | solution.py:341
  23.4 1.7 %collective-permute-done.4.refs_1_ = bf16[1,2,200,128]{3,2,1,0:T(8,128)(2,1)S(1)} collective-permute-done((bf16[1,2,200,128]{3,2,1,0:T(8,128)(2,1)S(1)}, bf16[1,2,200,128]{3,2,1,0:T(8,128)(2,1)S(1)}, u32[]{:S(2)}, u32[]{:S(2)}) %collective-permute-start.4) | collective-permute-done | bytes 102432 | tf_op jit(solution)/shard_map/ppermute | solution.py:200
  25.1 1.3 %attend.5 = bf16[128,512]{1,0:T(8,128)(2,1)} custom-call(f32[1,128]{1,0:T(1,128)S(1)} %get-tuple-element.16.k_gain_ref, bf16[128,512]{1,0:T(8,128)(2,1)S(1)} %get-tuple-element.17.qt_ref, f32[4,512]{1,0:T(4,128)S(1)} %get-tuple-element.18.bias_ref, bf16[1,2,200,128]{3,2,1,0:T(8,128)(2,1)S(1)} %collective-permute-done.3.refs_0_, ...), custom_call_target="tpu_custom_call" | custom-call | flops 52428800 | tf_op jit(solution)/shard_map/attend/pallas_call | solution.py:341
  (2 shorter events, 0.1 us)
Async XLA Ops:
  0.0 2.9 %collective-permute-start.1 = (bf16[2,2048,128]{2,1,0:T(8,128)(2,1)}, bf16[2,2048,128]{2,1,0:T(8,128)(2,1)S(1)}, u32[]{:S(2)}, u32[]{:S(2)}) collective-permute-start(bf16[2,2048,128]{2,1,0:T(8,128)(2,1)} %w_hbm.1), channel_id=1, source_target_pairs={{0,4},{4,0},{1,5},{5,1},{2,6},{6,2},{3,7},{7,3},{8,12},{12,8},{9,1... | collective-permute-start | bytes 3145736 | tf_op jit(solution)/shard_map/ppermute | solution.py:200
  1.9 2.8 %collective-permute-start = (bf16[1,2,200,128]{3,2,1,0:T(8,128)(2,1)S(1)}, bf16[1,2,200,128]{3,2,1,0:T(8,128)(2,1)S(1)}, u32[]{:S(2)}, u32[]{:S(2)}) collective-permute-start(bf16[1,2,200,128]{3,2,1,0:T(8,128)(2,1)S(1)} %get-tuple-element.19.own_ref), channel_id=1, source_target_pairs={{0,4},{1,5},{2,0},{3,1},{4,6},{5,7},{6,2},{7,3},{8,12},{9,13},{10,... | collective-permute-start | bytes 307208 | tf_op jit(solution)/shard_map/ppermute | solution.py:211
  3.3 5.7 %collective-permute-start.2 = (bf16[1,2,200,128]{3,2,1,0:T(8,128)(2,1)S(1)}, bf16[1,2,200,128]{3,2,1,0:T(8,128)(2,1)S(1)}, u32[]{:S(2)}, u32[]{:S(2)}) collective-permute-start(bf16[1,2,200,128]{3,2,1,0:T(8,128)(2,1)S(1)} %other_heads.1.other_ref), channel_id=1, source_target_pairs={{0,2},{1,3},{2,6},{3,7},{4,0},{5,1},{6,4},{7,5},{8,10},{9,11},{10,... | collective-permute-start | bytes 307208 | tf_op jit(solution)/shard_map/ppermute | solution.py:211
  4.8 10.5 %collective-permute-start.5 = (bf16[1,2,200,128]{3,2,1,0:T(8,128)(2,1)S(1)}, bf16[1,2,200,128]{3,2,1,0:T(8,128)(2,1)S(1)}, u32[]{:S(2)}, u32[]{:S(2)}) collective-permute-start(bf16[1,2,200,128]{3,2,1,0:T(8,128)(2,1)S(1)} %first_sum.1.first_sum_ref), channel_id=1, source_target_pairs={{0,1},{1,0},{2,2},{3,3},{4,4},{5,5},{6,7},{7,6},{8,9},{9,8},{10,10... | collective-permute-start | bytes 307208 | tf_op jit(solution)/shard_map/ppermute | solution.py:217
  9.0 7.4 %collective-permute-start.6 = (bf16[1,2,200,128]{3,2,1,0:T(8,128)(2,1)S(1)}, bf16[1,2,200,128]{3,2,1,0:T(8,128)(2,1)S(1)}, u32[]{:S(2)}, u32[]{:S(2)}) collective-permute-start(bf16[1,2,200,128]{3,2,1,0:T(8,128)(2,1)S(1)} %second_sum.1.keep_ref), channel_id=1, source_target_pairs={{0,0},{1,1},{2,3},{3,2},{4,5},{5,4},{6,6},{7,7},{8,8},{9,9},{10,11... | collective-permute-start | bytes 307208 | tf_op jit(solution)/shard_map/ppermute | solution.py:217
  13.8 6.6 %collective-permute-start.3 = (bf16[1,2,200,128]{3,2,1,0:T(8,128)(2,1)S(1)}, bf16[1,2,200,128]{3,2,1,0:T(8,128)(2,1)S(1)}, u32[]{:S(2)}, u32[]{:S(2)}) collective-permute-start(bf16[1,2,200,128]{3,2,1,0:T(8,128)(2,1)S(1)} %second_sum.1.keep_ref), channel_id=1, source_target_pairs={{0,24},{8,16},{16,8},{24,0},{1,25},{9,17},{17,9},{25,1},{2,26},{10... | collective-permute-start | bytes 307208 | tf_op jit(solution)/shard_map/ppermute | solution.py:200
  16.6 4.7 %collective-permute-start.7 = (bf16[2,200,128]{2,1,0:T(8,128)(2,1)S(1)}, bf16[2,200,128]{2,1,0:T(8,128)(2,1)S(1)}, u32[]{:S(2)}, u32[]{:S(2)}) collective-permute-start(bf16[2,200,128]{2,1,0:T(8,128)(2,1)S(1)} %sum_norm.1.refs_0_), channel_id=1, source_target_pairs={{0,8},{8,0},{16,24},{24,16},{1,9},{9,1},{17,25},{25,17},{2,10},{10... | collective-permute-start | bytes 307208 | tf_op jit(solution)/shard_map/ppermute | solution.py:200
  18.1 4.7 %collective-permute-start.8 = (bf16[2,200,128]{2,1,0:T(8,128)(2,1)S(1)}, bf16[2,200,128]{2,1,0:T(8,128)(2,1)S(1)}, u32[]{:S(2)}, u32[]{:S(2)}) collective-permute-start(bf16[2,200,128]{2,1,0:T(8,128)(2,1)S(1)} %sum_norm.1.refs_0_), channel_id=1, source_target_pairs={{0,16},{8,24},{16,0},{24,8},{1,17},{9,25},{17,1},{25,9},{2,18},{10... | collective-permute-start | bytes 307208 | tf_op jit(solution)/shard_map/ppermute | solution.py:200
  20.4 4.7 %collective-permute-start.4 = (bf16[1,2,200,128]{3,2,1,0:T(8,128)(2,1)S(1)}, bf16[1,2,200,128]{3,2,1,0:T(8,128)(2,1)S(1)}, u32[]{:S(2)}, u32[]{:S(2)}) collective-permute-start(bf16[1,2,200,128]{3,2,1,0:T(8,128)(2,1)S(1)} %collective-permute-done.3.refs_0_), channel_id=1, source_target_pairs={{0,1},{1,0},{2,3},{3,2},{4,5},{5,4},{6,7},{7,6},{8,9},{9,8},{10,11... | collective-permute-start | bytes 307208 | tf_op jit(solution)/shard_map/ppermute | solution.py:200

commit v4 on v2

--- a/solution.py
+++ b/solution.py
@@ -194,16 +194,16 @@
 def sum_two_heads(own, other, bias):
     devices = [(d, t) for d in range(2) for t in range(4)]
 
-    def exchange(value, senders):
+    def exchange(value, senders, apart):
         hops = [
-            (4 * d + t, 4 * d + (t ^ 3) if (t // 2 == d) == senders else 4 * (1 - d) + t)
+            (4 * d + t, 4 * d + (t ^ apart) if (t // 2 == d) == senders else 4 * (1 - d) + t)
             for d, t in devices
         ]
         return lax.ppermute(value, ("dp", "tensor"), hops)
 
-    first = exchange(own, False)
+    first = exchange(own, False, 2)
     rest = other(1)
-    second = exchange(rest, True)
+    second = exchange(rest, True, 3)
     return call(pair_kernel, shape_of(own.shape), 5, "pair_sum")(own, rest, first, second, bias)
 
 

time: 25.5 us -> 25.3 us (level)
  starting transfers between devices: 15.4 us -> 14.9 us
  waiting for transfers between devices: 3.93 us -> 4.21 us
    ppermute x6, starting transfers between devices: 10.2 us -> 9.73 us  [swap(): lax.ppermute(value, axis, [(i, i ^ k) for i in range(lax.axis_size(axis))])]
    ppermute x6, waiting for transfers between devices: 2.96 us -> 3.24 us  [swap(): lax.ppermute(value, axis, [(i, i ^ k) for i in range(lax.axis_size(axis))])]
  transfers between devices with their start and end apart: 8 -> 8, of which waited for: 6 -> 5; matrix products, arithmetic and copies ran while one was open for 0% -> 0% of each run, Pallas kernels for 19% -> 19%
where the time goes in v4:
time: 25.3 us; the launch traced here: 25.2 us
  starting transfers between devices  14.9 us (59%)
  Pallas kernels  6.02 us (24%)
  waiting for transfers between devices  4.21 us (17%)
    ppermute x6, starting transfers between devices, swap(): lax.ppermute(value, axis, [(i, i ^ k) for i in range(lax.axis_size(axis))])  9.73 us
    ppermute x2, starting transfers between devices, exchange(): return lax.ppermute(value, ('dp', 'tensor'), hops)  5.15 us
    ppermute x6, waiting for transfers between devices, swap(): lax.ppermute(value, axis, [(i, i ^ k) for i in range(lax.axis_size(axis))])  3.24 us
    pallas_call x3, Pallas kernels, on_device(): call(functools.partial(attend_kernel, here, there, tile_len, first, last,...  2.27 us
    pallas_call x1, Pallas kernels, on_device(): call(functools.partial(own_kernel, head_dim), [shape_of((own_heads, 2, ro...  1.92 us
    pallas_call x1, Pallas kernels, on_device(): call(query_kernel, [shape_of((head_dim, pairs)), shape_of((tiles, pairs),...  1.27 us
    ppermute x2, waiting for transfers between devices, exchange(): return lax.ppermute(value, ('dp', 'tensor'), hops)  0.97 us
  transfers between devices with their start and end apart: 8, of which 5 were waited for; matrix products, arithmetic and copies ran while one was open for 0% of the time, Pallas kernels for 19%

profile of v4, /device:TPU:0, one launch (start us, length us, event | category | flops | bytes accessed | tf_op | source)
XLA Modules:
  0.0 25.2 jit_solution(17777560793985404535)
XLA Ops:
  0.0 0.5 %collective-permute-start = (bf16[2,2048,128]{2,1,0:T(8,128)(2,1)}, bf16[2,2048,128]{2,1,0:T(8,128)(2,1)S(1)}, u32[]{:S(2)}, u32[]{:S(2)}) collective-permute-start(bf16[2,2048,128]{2,1,0:T(8,128)(2,1)} %w_hbm.1), channel_id=1, source_target_pairs={{0,4},{4,0},{1,5},{5,1},{2,6},{6,2},{3,7},{7,3},{8,12},{12,8},{9,1... | collective-permute-start | bytes 3145736 | tf_op jit(solution)/shard_map/ppermute | solution.py:191
  0.5 1.9 %own_head.1 = (bf16[1,2,200,128]{3,2,1,0:T(8,128)(2,1)S(1)}, bf16[1,200,2048]{2,1,0:T(8,128)(2,1)S(1)}, f32[1,128]{1,0:T(1,128)S(1)}) custom-call(bf16[1,200,2048]{2,1,0:T(8,128)(2,1)} %x_hbm.1, bf16[2,2048,128]{2,1,0:T(8,128)(2,1)} %w_hbm.1, f32[1,128]{1,0:T(1,128)} %bitcast.5), custom_call_target="tpu_custom_call" | custom-call | flops 209715200 | bytes 1867776 | tf_op jit(solution)/shard_map/own_head/pallas_call | solution.py:262
  2.4 0.1 collective-permute-start.1
  2.5 0.5 %collective-permute-done.w_ref = bf16[2,2048,128]{2,1,0:T(8,128)(2,1)S(1)} collective-permute-done((bf16[2,2048,128]{2,1,0:T(8,128)(2,1)}, bf16[2,2048,128]{2,1,0:T(8,128)(2,1)S(1)}, u32[]{:S(2)}, u32[]{:S(2)}) %collective-permute-start) | collective-permute-done | bytes 1048608 | tf_op jit(solution)/shard_map/ppermute | solution.py:191
  3.0 0.4 %other_heads.1.other_ref = bf16[1,2,200,128]{3,2,1,0:T(8,128)(2,1)S(1)} custom-call(bf16[1,200,2048]{2,1,0:T(8,128)(2,1)S(1)} %get-tuple-element.20.x_ref, bf16[2,2048,128]{2,1,0:T(8,128)(2,1)S(1)} %collective-permute-done.w_ref), custom_call_target="tpu_custom_call" | custom-call | flops 209715200 | tf_op jit(solution)/shard_map/other_heads/pallas_call | solution.py:291
  3.4 5.0 %collective-permute-start.2 = (bf16[1,2,200,128]{3,2,1,0:T(8,128)(2,1)S(1)}, bf16[1,2,200,128]{3,2,1,0:T(8,128)(2,1)S(1)}, u32[]{:S(2)}, u32[]{:S(2)}) collective-permute-start(bf16[1,2,200,128]{3,2,1,0:T(8,128)(2,1)S(1)} %other_heads.1.other_ref), channel_id=1, source_target_pairs={{0,3},{1,2},{2,6},{3,7},{4,0},{5,1},{6,5},{7,4},{8,11},{9,10},{10,... | collective-permute-start | bytes 307208 | tf_op jit(solution)/shard_map/ppermute | solution.py:202
  8.4 1.3 %queries.1 = (bf16[128,512]{1,0:T(8,128)(2,1)S(1)}, f32[4,512]{1,0:T(4,128)S(1)}) custom-call(bf16[128,512]{1,0:T(8,128)(2,1)} %refs_0_.1, f32[1,128]{1,0:T(1,128)} %bitcast.4, s32[4,128]{1,0:T(4,128)} %bitcast.3), custom_call_target="tpu_custom_call" | custom-call | tf_op jit(solution)/shard_map/queries/pallas_call | solution.py:276
  9.7 0.0 collective-permute-done.1.first_ref
  9.7 1.0 %collective-permute-done.2.second_ref = bf16[1,2,200,128]{3,2,1,0:T(8,128)(2,1)S(1)} collective-permute-done((bf16[1,2,200,128]{3,2,1,0:T(8,128)(2,1)S(1)}, bf16[1,2,200,128]{3,2,1,0:T(8,128)(2,1)S(1)}, u32[]{:S(2)}, u32[]{:S(2)}) %collective-permute-start.2) | collective-permute-done | bytes 102432 | tf_op jit(solution)/shard_map/ppermute | solution.py:202
  10.7 2.0 %collective-permute-start.5 = (bf16[1,2,200,128]{3,2,1,0:T(8,128)(2,1)S(1)}, bf16[1,2,200,128]{3,2,1,0:T(8,128)(2,1)S(1)}, u32[]{:S(2)}, u32[]{:S(2)}) collective-permute-start(bf16[1,2,200,128]{3,2,1,0:T(8,128)(2,1)S(1)} %pair_sum.1.keep_ref), channel_id=1, source_target_pairs={{0,1},{1,0},{2,3},{3,2},{4,5},{5,4},{6,7},{7,6},{8,9},{9,8},{10,11... | collective-permute-start | bytes 307208 | tf_op jit(solution)/shard_map/ppermute | solution.py:191
  12.7 2.4 %collective-permute-start.3 = (bf16[1,2,200,128]{3,2,1,0:T(8,128)(2,1)S(1)}, bf16[1,2,200,128]{3,2,1,0:T(8,128)(2,1)S(1)}, u32[]{:S(2)}, u32[]{:S(2)}) collective-permute-start(bf16[1,2,200,128]{3,2,1,0:T(8,128)(2,1)S(1)} %pair_sum.1.keep_ref), channel_id=1, source_target_pairs={{0,24},{8,16},{16,8},{24,0},{1,25},{9,17},{17,9},{25,1},{2,26},{10... | collective-permute-start | bytes 307208 | tf_op jit(solution)/shard_map/ppermute | solution.py:191
  15.1 0.9 %collective-permute-done.5.arrived_ref = bf16[1,2,200,128]{3,2,1,0:T(8,128)(2,1)S(1)} collective-permute-done((bf16[1,2,200,128]{3,2,1,0:T(8,128)(2,1)S(1)}, bf16[1,2,200,128]{3,2,1,0:T(8,128)(2,1)S(1)}, u32[]{:S(2)}, u32[]{:S(2)}) %collective-permute-start.5) | collective-permute-done | bytes 102432 | tf_op jit(solution)/shard_map/ppermute | solution.py:191
  16.0 0.1 sum_norm.1.refs_0_
  16.2 1.6 %collective-permute-start.6 = (bf16[2,200,128]{2,1,0:T(8,128)(2,1)S(1)}, bf16[2,200,128]{2,1,0:T(8,128)(2,1)S(1)}, u32[]{:S(2)}, u32[]{:S(2)}) collective-permute-start(bf16[2,200,128]{2,1,0:T(8,128)(2,1)S(1)} %sum_norm.1.refs_0_), channel_id=1, source_target_pairs={{0,8},{8,0},{16,24},{24,16},{1,9},{9,1},{17,25},{25,17},{2,10},{10... | collective-permute-start | bytes 307208 | tf_op jit(solution)/shard_map/ppermute | solution.py:191
  17.7 1.5 %collective-permute-start.7 = (bf16[2,200,128]{2,1,0:T(8,128)(2,1)S(1)}, bf16[2,200,128]{2,1,0:T(8,128)(2,1)S(1)}, u32[]{:S(2)}, u32[]{:S(2)}) collective-permute-start(bf16[2,200,128]{2,1,0:T(8,128)(2,1)S(1)} %sum_norm.1.refs_0_), channel_id=1, source_target_pairs={{0,16},{8,24},{16,0},{24,8},{1,17},{9,25},{17,1},{25,9},{2,18},{10... | collective-permute-start | bytes 307208 | tf_op jit(solution)/shard_map/ppermute | solution.py:191
  19.2 0.0 collective-permute-done.3.refs_0_
  19.2 1.8 %collective-permute-start.4 = (bf16[1,2,200,128]{3,2,1,0:T(8,128)(2,1)S(1)}, bf16[1,2,200,128]{3,2,1,0:T(8,128)(2,1)S(1)}, u32[]{:S(2)}, u32[]{:S(2)}) collective-permute-start(bf16[1,2,200,128]{3,2,1,0:T(8,128)(2,1)S(1)} %collective-permute-done.3.refs_0_), channel_id=1, source_target_pairs={{0,1},{1,0},{2,3},{3,2},{4,5},{5,4},{6,7},{7,6},{8,9},{9,8},{10,11... | collective-permute-start | bytes 307208 | tf_op jit(solution)/shard_map/ppermute | solution.py:191
  21.0 0.4 %attend.3 = (f32[1,512]{1,0:T(1,128)S(1)}, f32[1,512]{1,0:T(1,128)S(1)}, f32[128,512]{1,0:T(8,128)S(1)}) custom-call(f32[1,128]{1,0:T(1,128)S(1)} %get-tuple-element.16.k_gain_ref, bf16[128,512]{1,0:T(8,128)(2,1)S(1)} %get-tuple-element.17.qt_ref, f32[4,512]{1,0:T(4,128)S(1)} %get-tuple-element.18.bias_ref, bf16[2,200,128]{2,1,0:T(8,128)(2,1)S(1)} %sum_norm.1.refs_0_), custom_call_target="tpu_custom_call" | custom-call | flops 52428800 | tf_op jit(solution)/shard_map/attend/pallas_call | solution.py:321
  21.5 0.0 collective-permute-done.6.refs_0_
  21.5 1.1 %collective-permute-done.7.refs_1_ = bf16[2,200,128]{2,1,0:T(8,128)(2,1)S(1)} collective-permute-done((bf16[2,200,128]{2,1,0:T(8,128)(2,1)S(1)}, bf16[2,200,128]{2,1,0:T(8,128)(2,1)S(1)}, u32[]{:S(2)}, u32[]{:S(2)}) %collective-permute-start.7) | collective-permute-done | bytes 102432 | tf_op jit(solution)/shard_map/ppermute | solution.py:191
  22.5 0.6 %attend.4 = (f32[1,512]{1,0:T(1,128)S(1)}, f32[1,512]{1,0:T(1,128)S(1)}, f32[128,512]{1,0:T(8,128)S(1)}) custom-call(f32[1,128]{1,0:T(1,128)S(1)} %get-tuple-element.16.k_gain_ref, bf16[128,512]{1,0:T(8,128)(2,1)S(1)} %get-tuple-element.17.qt_ref, f32[4,512]{1,0:T(4,128)S(1)} %get-tuple-element.18.bias_ref, ...), custom_call_target="tpu_custom_call" | custom-call | flops 104857600 | tf_op jit(solution)/shard_map/attend/pallas_call | solution.py:321
  23.1 0.8 %collective-permute-done.4.refs_1_ = bf16[1,2,200,128]{3,2,1,0:T(8,128)(2,1)S(1)} collective-permute-done((bf16[1,2,200,128]{3,2,1,0:T(8,128)(2,1)S(1)}, bf16[1,2,200,128]{3,2,1,0:T(8,128)(2,1)S(1)}, u32[]{:S(2)}, u32[]{:S(2)}) %collective-permute-start.4) | collective-permute-done | bytes 102432 | tf_op jit(solution)/shard_map/ppermute | solution.py:191
  23.9 1.3 %attend.5 = bf16[128,512]{1,0:T(8,128)(2,1)} custom-call(f32[1,128]{1,0:T(1,128)S(1)} %get-tuple-element.16.k_gain_ref, bf16[128,512]{1,0:T(8,128)(2,1)S(1)} %get-tuple-element.17.qt_ref, f32[4,512]{1,0:T(4,128)S(1)} %get-tuple-element.18.bias_ref, bf16[1,2,200,128]{3,2,1,0:T(8,128)(2,1)S(1)} %collective-permute-done.3.refs_0_, ...), custom_call_target="tpu_custom_call" | custom-call | flops 52428800 | tf_op jit(solution)/shard_map/attend/pallas_call | solution.py:321
  (1 shorter events, 0.0 us)
Async XLA Ops:
  0.0 3.0 %collective-permute-start = (bf16[2,2048,128]{2,1,0:T(8,128)(2,1)}, bf16[2,2048,128]{2,1,0:T(8,128)(2,1)S(1)}, u32[]{:S(2)}, u32[]{:S(2)}) collective-permute-start(bf16[2,2048,128]{2,1,0:T(8,128)(2,1)} %w_hbm.1), channel_id=1, source_target_pairs={{0,4},{4,0},{1,5},{5,1},{2,6},{6,2},{3,7},{7,3},{8,12},{12,8},{9,1... | collective-permute-start | bytes 3145736 | tf_op jit(solution)/shard_map/ppermute | solution.py:191
  2.4 7.3 %collective-permute-start.1 = (bf16[1,2,200,128]{3,2,1,0:T(8,128)(2,1)S(1)}, bf16[1,2,200,128]{3,2,1,0:T(8,128)(2,1)S(1)}, u32[]{:S(2)}, u32[]{:S(2)}) collective-permute-start(bf16[1,2,200,128]{3,2,1,0:T(8,128)(2,1)S(1)} %get-tuple-element.19.own_ref), channel_id=1, source_target_pairs={{0,4},{1,5},{2,0},{3,1},{4,6},{5,7},{6,2},{7,3},{8,12},{9,13},{10,... | collective-permute-start | bytes 307208 | tf_op jit(solution)/shard_map/ppermute | solution.py:202
  3.4 7.3 %collective-permute-start.2 = (bf16[1,2,200,128]{3,2,1,0:T(8,128)(2,1)S(1)}, bf16[1,2,200,128]{3,2,1,0:T(8,128)(2,1)S(1)}, u32[]{:S(2)}, u32[]{:S(2)}) collective-permute-start(bf16[1,2,200,128]{3,2,1,0:T(8,128)(2,1)S(1)} %other_heads.1.other_ref), channel_id=1, source_target_pairs={{0,3},{1,2},{2,6},{3,7},{4,0},{5,1},{6,5},{7,4},{8,11},{9,10},{10,... | collective-permute-start | bytes 307208 | tf_op jit(solution)/shard_map/ppermute | solution.py:202
  10.7 5.4 %collective-permute-start.5 = (bf16[1,2,200,128]{3,2,1,0:T(8,128)(2,1)S(1)}, bf16[1,2,200,128]{3,2,1,0:T(8,128)(2,1)S(1)}, u32[]{:S(2)}, u32[]{:S(2)}) collective-permute-start(bf16[1,2,200,128]{3,2,1,0:T(8,128)(2,1)S(1)} %pair_sum.1.keep_ref), channel_id=1, source_target_pairs={{0,1},{1,0},{2,3},{3,2},{4,5},{5,4},{6,7},{7,6},{8,9},{9,8},{10,11... | collective-permute-start | bytes 307208 | tf_op jit(solution)/shard_map/ppermute | solution.py:191
  12.7 6.6 %collective-permute-start.3 = (bf16[1,2,200,128]{3,2,1,0:T(8,128)(2,1)S(1)}, bf16[1,2,200,128]{3,2,1,0:T(8,128)(2,1)S(1)}, u32[]{:S(2)}, u32[]{:S(2)}) collective-permute-start(bf16[1,2,200,128]{3,2,1,0:T(8,128)(2,1)S(1)} %pair_sum.1.keep_ref), channel_id=1, source_target_pairs={{0,24},{8,16},{16,8},{24,0},{1,25},{9,17},{17,9},{25,1},{2,26},{10... | collective-permute-start | bytes 307208 | tf_op jit(solution)/shard_map/ppermute | solution.py:191
  16.2 5.3 %collective-permute-start.6 = (bf16[2,200,128]{2,1,0:T(8,128)(2,1)S(1)}, bf16[2,200,128]{2,1,0:T(8,128)(2,1)S(1)}, u32[]{:S(2)}, u32[]{:S(2)}) collective-permute-start(bf16[2,200,128]{2,1,0:T(8,128)(2,1)S(1)} %sum_norm.1.refs_0_), channel_id=1, source_target_pairs={{0,8},{8,0},{16,24},{24,16},{1,9},{9,1},{17,25},{25,17},{2,10},{10... | collective-permute-start | bytes 307208 | tf_op jit(solution)/shard_map/ppermute | solution.py:191
  17.7 4.8 %collective-permute-start.7 = (bf16[2,200,128]{2,1,0:T(8,128)(2,1)S(1)}, bf16[2,200,128]{2,1,0:T(8,128)(2,1)S(1)}, u32[]{:S(2)}, u32[]{:S(2)}) collective-permute-start(bf16[2,200,128]{2,1,0:T(8,128)(2,1)S(1)} %sum_norm.1.refs_0_), channel_id=1, source_target_pairs={{0,16},{8,24},{16,0},{24,8},{1,17},{9,25},{17,1},{25,9},{2,18},{10... | collective-permute-start | bytes 307208 | tf_op jit(solution)/shard_map/ppermute | solution.py:191
  19.2 4.7 %collective-permute-start.4 = (bf16[1,2,200,128]{3,2,1,0:T(8,128)(2,1)S(1)}, bf16[1,2,200,128]{3,2,1,0:T(8,128)(2,1)S(1)}, u32[]{:S(2)}, u32[]{:S(2)}) collective-permute-start(bf16[1,2,200,128]{3,2,1,0:T(8,128)(2,1)S(1)} %collective-permute-done.3.refs_0_), channel_id=1, source_target_pairs={{0,1},{1,0},{2,3},{3,2},{4,5},{5,4},{6,7},{7,6},{8,9},{9,8},{10,11... | collective-permute-start | bytes 307208 | tf_op jit(solution)/shard_map/ppermute | solution.py:191

commit v5 on v4

--- a/solution.py
+++ b/solution.py
@@ -75,7 +75,7 @@
 
 
 def own_kernel(
-    head_dim, x_hbm, w_hbm, k_gain_hbm, own_ref, x_ref, k_gain_ref, w_ref, sems
+    head_dim, x_hbm, w_hbm, k_gain_hbm, own_ref, x_ref, w_ref, k_gain_ref, sems
 ):
     moves = [(k_gain_hbm, k_gain_ref), (x_hbm, x_ref), (w_hbm, w_ref)]
     copies = [pltpu.make_async_copy(a, b, sems.at[i]) for i, (a, b) in enumerate(moves)]
@@ -111,11 +111,11 @@
     prepare_queries(refs[:3], refs[5:8], refs[8], *refs[3:5])
 
 
-def pair_kernel(own_ref, other_ref, first_ref, second_ref, bias_ref, out_ref):
+def pair_kernel(own_ref, first_ref, stayed_ref, crossed_ref, bias_ref, out_ref):
     mine = lax.axis_index("tensor") // 2 == lax.axis_index("dp")
-    keep = jnp.where(mine, own_ref[...], other_ref[...]).astype(F32)
-    arrived = jnp.where(mine, first_ref[...], second_ref[...]).astype(F32)
-    out_ref[...] = (keep + arrived).astype(BF16)
+    one = jnp.where(mine, own_ref[...], stayed_ref[...]).astype(F32)
+    two = jnp.where(mine, first_ref[...], crossed_ref[...]).astype(F32)
+    out_ref[...] = (one + two).astype(BF16)
 
 
 def add_kernel(bit, keep_ref, arrived_ref, send_ref, next_ref, held):
@@ -191,20 +191,24 @@
     return lax.ppermute(value, axis, [(i, i ^ k) for i in range(lax.axis_size(axis))])
 
 
-def sum_two_heads(own, other, bias):
+def sum_two_heads(own, images, w, bias, other):
     devices = [(d, t) for d in range(2) for t in range(4)]
 
-    def exchange(value, senders, apart):
-        hops = [
-            (4 * d + t, 4 * d + (t ^ apart) if (t // 2 == d) == senders else 4 * (1 - d) + t)
-            for d, t in devices
-        ]
+    def permute(value, away, home):
+        hops = []
+        for d, t in devices:
+            to_d, to_t = away(d, t) if t // 2 != d else home(d, t)
+            hops.append((4 * d + t, 4 * to_d + to_t))
         return lax.ppermute(value, ("dp", "tensor"), hops)
 
-    first = exchange(own, False, 2)
-    rest = other(1)
-    second = exchange(rest, True, 3)
-    return call(pair_kernel, shape_of(own.shape), 5, "pair_sum")(own, rest, first, second, bias)
+    other_image = swap(images, "dp", 1)
+    first = permute(own, lambda d, t: (d, t ^ 2), lambda d, t: (1 - d, t))
+    rest = other(other_image, w)
+    stayed = permute(rest, lambda d, t: (1 - d, t), lambda d, t: (1 - d, t))
+    crossed = permute(rest, lambda d, t: (1 - d, t ^ 2), lambda d, t: (d, t))
+    return call(pair_kernel, shape_of(own.shape), 5, "pair_sum")(
+        own, first, stayed, crossed, bias
+    )
 
 
 def sum_many_heads(own, others):
@@ -233,8 +237,8 @@
                 scratch=[pltpu.VMEM(now, BF16)],
             )(keep, arrived)
         else:
-            send = keep = call(add_last_kernel, shape_of(now), 2, "add_pair")(keep, arrived)
-    return send, keep
+            keep = call(add_last_kernel, shape_of(now), 2, "add_pair")(keep, arrived)
+    return keep
 
 
 def on_device(queries, images, kv_weight, q_gain, k_gain, tile_mask):
@@ -252,18 +256,18 @@
     pairs = tokens * (q_width // head_dim)
     work = 4 * rows * features * kv_weight.shape[2]
 
-    others = [swap(kv_weight, "dp", k) for k in range(1, n_dp)]
     in_hbm = [
         pltpu.with_memory_space_constraint(value, pltpu.HBM)
         for value in (
             images, kv_weight, k_gain.reshape(1, -1), queries, q_gain.reshape(1, -1), tile_mask.T,
         )
     ]
-    own, x, gain = call(
+    own, x, w, gain = call(
         functools.partial(own_kernel, head_dim),
         [
             shape_of((own_heads, 2, rows, head_dim)),
             shape_of(images.shape),
+            shape_of(kv_weight.shape),
             shape_of((1, head_dim), F32),
         ],
         3,
@@ -271,7 +275,7 @@
         flops=work,
         size=2 * (images.size + kv_weight.size),
         in_specs=[HBM] * 3,
-        scratch=[pltpu.VMEM(kv_weight.shape, BF16), pltpu.SemaphoreType.DMA((3,))],
+        scratch=[pltpu.SemaphoreType.DMA((3,))],
     )(*in_hbm[:3])
     qt, bias = call(
         query_kernel,
@@ -287,20 +291,21 @@
         ],
     )(*in_hbm[3:])
 
-    def other(k):
+    def other(rows_of, columns):
         return call(
             functools.partial(other_kernel, head_dim), shape_of(own.shape), 2, "other_heads", flops=work
-        )(x, others[k - 1])
+        )(rows_of, columns)
 
     if n_dp == 2 and own_heads == 1:
-        send = keep = sum_two_heads(own, other, bias)
+        total = sum_two_heads(own, images, w, bias, other)
     else:
-        send, keep = sum_many_heads(own, [other(k) for k in range(1, n_dp)])
+        rest = [other(x, swap(kv_weight, "dp", k)) for k in range(1, n_dp)]
+        total = sum_many_heads(own, rest)
     far = [step for step in range(1, n_section) if step & (step - 1)]
     near = [step for step in range(1, n_section) if not step & (step - 1)]
-    arrived = swap(send, "tensor", 1)
-    halves = [swap(send, "section", step) for step in far]
-    kv = call(norm_kernel, shape_of((2, rows, head_dim)), 3, "sum_norm")(gain, keep, arrived)
+    arrived = swap(total, "tensor", 1)
+    halves = [swap(total, "section", step) for step in far]
+    kv = call(norm_kernel, shape_of((2, rows, head_dim)), 3, "sum_norm")(gain, total, arrived)
     finished = [swap(kv, "section", step) for step in near]
     both = []
     for value in halves:

time: 25.3 us -> 26.9 us (1.063)
  the two profiles are of different devices: /device:TPU:0 before, /device:TPU:1 now
where the time goes in v5:
time: 26.9 us; the launch traced here: 26.8 us
  starting transfers between devices  13.7 us (51%)
  Pallas kernels  6.75 us (25%)
  waiting for transfers between devices  6.21 us (23%)
    ppermute x6, starting transfers between devices, swap(): lax.ppermute(value, axis, [(i, i ^ k) for i in range(lax.axis_size(axis))])  7.51 us
    ppermute x3, starting transfers between devices, permute(): return lax.ppermute(value, ('dp', 'tensor'), hops)  6.19 us
    ppermute x3, waiting for transfers between devices, permute(): return lax.ppermute(value, ('dp', 'tensor'), hops)  3.65 us
    pallas_call x1, Pallas kernels, on_device(): call(functools.partial(own_kernel, head_dim), [shape_of((own_heads, 2, ro...  2.63 us
    ppermute x6, waiting for transfers between devices, swap(): lax.ppermute(value, axis, [(i, i ^ k) for i in range(lax.axis_size(axis))])  2.56 us
    pallas_call x3, Pallas kernels, on_device(): call(functools.partial(attend_kernel, here, there, tile_len, first, last,...  2.27 us
    pallas_call x1, Pallas kernels, on_device(): call(query_kernel, [shape_of((head_dim, pairs)), shape_of((tiles, pairs),...  1.28 us
  transfers between devices with their start and end apart: 9, of which 5 were waited for; matrix products, arithmetic and copies ran while one was open for 0% of the time, Pallas kernels for 20%

profile of v5, /device:TPU:1, one launch (start us, length us, event | category | flops | bytes accessed | tf_op | source)
XLA Modules:
  0.0 26.8 jit_solution(17664214440990777763)
XLA Ops:
  0.0 0.1 collective-permute-start.1
  0.1 2.6 %own_head.1 = (bf16[1,2,200,128]{3,2,1,0:T(8,128)(2,1)S(1)}, bf16[1,200,2048]{2,1,0:T(8,128)(2,1)}, bf16[2,2048,128]{2,1,0:T(8,128)(2,1)S(1)}, f32[1,128]{1,0:T(1,128)S(1)}) custom-call(bf16[1,200,2048]{2,1,0:T(8,128)(2,1)} %x_hbm.1, bf16[2,2048,128]{2,1,0:T(8,128)(2,1)} %w_hbm.1, f32[1,128]{1,0:T(1,128)} %bitcast.5), custom_call_target="tpu_custom_call" | custom-call | flops 209715200 | bytes 1867776 | tf_op jit(solution)/shard_map/own_head/pallas_call | solution.py:265
  2.7 3.8 %collective-permute-start = (bf16[1,2,200,128]{3,2,1,0:T(8,128)(2,1)S(1)}, bf16[1,2,200,128]{3,2,1,0:T(8,128)(2,1)S(1)}, u32[]{:S(2)}, u32[]{:S(2)}) collective-permute-start(bf16[1,2,200,128]{3,2,1,0:T(8,128)(2,1)S(1)} %get-tuple-element.19.own_ref), channel_id=1, source_target_pairs={{0,4},{1,5},{2,0},{3,1},{4,6},{5,7},{6,2},{7,3},{8,12},{9,13},{10,... | collective-permute-start | bytes 307208 | tf_op jit(solution)/shard_map/ppermute | solution.py:202
  6.5 0.0 collective-permute-done.1.x_ref
  6.5 0.4 %other_heads.1 = bf16[1,2,200,128]{3,2,1,0:T(8,128)(2,1)S(1)} custom-call(bf16[1,200,2048]{2,1,0:T(8,128)(2,1)S(1)} %collective-permute-done.1.x_ref, bf16[2,2048,128]{2,1,0:T(8,128)(2,1)S(1)} %get-tuple-element.20.w_ref), custom_call_target="tpu_custom_call" | custom-call | flops 209715200 | tf_op jit(solution)/shard_map/other_heads/pallas_call | solution.py:295
  6.9 0.1 collective-permute-start.2
  7.0 2.3 %collective-permute-start.3 = (bf16[1,2,200,128]{3,2,1,0:T(8,128)(2,1)S(1)}, bf16[1,2,200,128]{3,2,1,0:T(8,128)(2,1)S(1)}, u32[]{:S(2)}, u32[]{:S(2)}) collective-permute-start(bf16[1,2,200,128]{3,2,1,0:T(8,128)(2,1)S(1)} %other_heads.1), channel_id=1, source_target_pairs={{0,0},{1,1},{2,4},{3,5},{4,2},{5,3},{6,6},{7,7},{8,8},{9,9},{10,12... | collective-permute-start | bytes 307208 | tf_op jit(solution)/shard_map/ppermute | solution.py:202
  9.3 1.3 %queries.1 = (bf16[128,512]{1,0:T(8,128)(2,1)S(1)}, f32[4,512]{1,0:T(4,128)S(1)}) custom-call(bf16[128,512]{1,0:T(8,128)(2,1)} %refs_0_.1, f32[1,128]{1,0:T(1,128)} %bitcast.4, s32[4,128]{1,0:T(4,128)} %bitcast.3), custom_call_target="tpu_custom_call" | custom-call | tf_op jit(solution)/shard_map/queries/pallas_call | solution.py:280
  10.6 0.0 collective-permute-done.first_ref
  10.6 0.0 collective-permute-done.2.stayed_ref
  10.6 3.6 %collective-permute-done.3.crossed_ref = bf16[1,2,200,128]{3,2,1,0:T(8,128)(2,1)S(1)} collective-permute-done((bf16[1,2,200,128]{3,2,1,0:T(8,128)(2,1)S(1)}, bf16[1,2,200,128]{3,2,1,0:T(8,128)(2,1)S(1)}, u32[]{:S(2)}, u32[]{:S(2)}) %collective-permute-start.3) | collective-permute-done | bytes 102432 | tf_op jit(solution)/shard_map/ppermute | solution.py:202
  14.3 0.1 pair_sum.1.keep_ref
  14.3 2.2 %collective-permute-start.6 = (bf16[1,2,200,128]{3,2,1,0:T(8,128)(2,1)S(1)}, bf16[1,2,200,128]{3,2,1,0:T(8,128)(2,1)S(1)}, u32[]{:S(2)}, u32[]{:S(2)}) collective-permute-start(bf16[1,2,200,128]{3,2,1,0:T(8,128)(2,1)S(1)} %pair_sum.1.keep_ref), channel_id=1, source_target_pairs={{0,1},{1,0},{2,3},{3,2},{4,5},{5,4},{6,7},{7,6},{8,9},{9,8},{10,11... | collective-permute-start | bytes 307208 | tf_op jit(solution)/shard_map/ppermute | solution.py:191
  16.5 2.2 %collective-permute-start.4 = (bf16[1,2,200,128]{3,2,1,0:T(8,128)(2,1)S(1)}, bf16[1,2,200,128]{3,2,1,0:T(8,128)(2,1)S(1)}, u32[]{:S(2)}, u32[]{:S(2)}) collective-permute-start(bf16[1,2,200,128]{3,2,1,0:T(8,128)(2,1)S(1)} %pair_sum.1.keep_ref), channel_id=1, source_target_pairs={{0,24},{8,16},{16,8},{24,0},{1,25},{9,17},{17,9},{25,1},{2,26},{10... | collective-permute-start | bytes 307208 | tf_op jit(solution)/shard_map/ppermute | solution.py:191
  18.6 0.2 collective-permute-done.6.arrived_ref
  18.8 0.1 sum_norm.1.refs_0_
  18.9 1.0 %collective-permute-start.7 = (bf16[2,200,128]{2,1,0:T(8,128)(2,1)S(1)}, bf16[2,200,128]{2,1,0:T(8,128)(2,1)S(1)}, u32[]{:S(2)}, u32[]{:S(2)}) collective-permute-start(bf16[2,200,128]{2,1,0:T(8,128)(2,1)S(1)} %sum_norm.1.refs_0_), channel_id=1, source_target_pairs={{0,8},{8,0},{16,24},{24,16},{1,9},{9,1},{17,25},{25,17},{2,10},{10... | collective-permute-start | bytes 307208 | tf_op jit(solution)/shard_map/ppermute | solution.py:191
  19.9 1.2 %collective-permute-start.8 = (bf16[2,200,128]{2,1,0:T(8,128)(2,1)S(1)}, bf16[2,200,128]{2,1,0:T(8,128)(2,1)S(1)}, u32[]{:S(2)}, u32[]{:S(2)}) collective-permute-start(bf16[2,200,128]{2,1,0:T(8,128)(2,1)S(1)} %sum_norm.1.refs_0_), channel_id=1, source_target_pairs={{0,16},{8,24},{16,0},{24,8},{1,17},{9,25},{17,1},{25,9},{2,18},{10... | collective-permute-start | bytes 307208 | tf_op jit(solution)/shard_map/ppermute | solution.py:191
  21.2 0.8 %collective-permute-done.4.refs_0_ = bf16[1,2,200,128]{3,2,1,0:T(8,128)(2,1)S(1)} collective-permute-done((bf16[1,2,200,128]{3,2,1,0:T(8,128)(2,1)S(1)}, bf16[1,2,200,128]{3,2,1,0:T(8,128)(2,1)S(1)}, u32[]{:S(2)}, u32[]{:S(2)}) %collective-permute-start.4) | collective-permute-done | bytes 102432 | tf_op jit(solution)/shard_map/ppermute | solution.py:191
  22.0 0.9 %collective-permute-start.5 = (bf16[1,2,200,128]{3,2,1,0:T(8,128)(2,1)S(1)}, bf16[1,2,200,128]{3,2,1,0:T(8,128)(2,1)S(1)}, u32[]{:S(2)}, u32[]{:S(2)}) collective-permute-start(bf16[1,2,200,128]{3,2,1,0:T(8,128)(2,1)S(1)} %collective-permute-done.4.refs_0_), channel_id=1, source_target_pairs={{0,1},{1,0},{2,3},{3,2},{4,5},{5,4},{6,7},{7,6},{8,9},{9,8},{10,11... | collective-permute-start | bytes 307208 | tf_op jit(solution)/shard_map/ppermute | solution.py:191
  22.9 0.4 %attend.3 = (f32[1,512]{1,0:T(1,128)S(1)}, f32[1,512]{1,0:T(1,128)S(1)}, f32[128,512]{1,0:T(8,128)S(1)}) custom-call(f32[1,128]{1,0:T(1,128)S(1)} %get-tuple-element.16.k_gain_ref, bf16[128,512]{1,0:T(8,128)(2,1)S(1)} %get-tuple-element.17.qt_ref, f32[4,512]{1,0:T(4,128)S(1)} %get-tuple-element.18.bias_ref, bf16[2,200,128]{2,1,0:T(8,128)(2,1)S(1)} %sum_norm.1.refs_0_), custom_call_target="tpu_custom_call" | custom-call | flops 52428800 | tf_op jit(solution)/shard_map/attend/pallas_call | solution.py:326
  23.4 0.0 collective-permute-done.7.refs_0_
  23.4 0.1 collective-permute-done.8.refs_1_
  23.4 0.6 %attend.4 = (f32[1,512]{1,0:T(1,128)S(1)}, f32[1,512]{1,0:T(1,128)S(1)}, f32[128,512]{1,0:T(8,128)S(1)}) custom-call(f32[1,128]{1,0:T(1,128)S(1)} %get-tuple-element.16.k_gain_ref, bf16[128,512]{1,0:T(8,128)(2,1)S(1)} %get-tuple-element.17.qt_ref, f32[4,512]{1,0:T(4,128)S(1)} %get-tuple-element.18.bias_ref, ...), custom_call_target="tpu_custom_call" | custom-call | flops 104857600 | tf_op jit(solution)/shard_map/attend/pallas_call | solution.py:326
  24.0 1.5 %collective-permute-done.5.refs_1_ = bf16[1,2,200,128]{3,2,1,0:T(8,128)(2,1)S(1)} collective-permute-done((bf16[1,2,200,128]{3,2,1,0:T(8,128)(2,1)S(1)}, bf16[1,2,200,128]{3,2,1,0:T(8,128)(2,1)S(1)}, u32[]{:S(2)}, u32[]{:S(2)}) %collective-permute-start.5) | collective-permute-done | bytes 102432 | tf_op jit(solution)/shard_map/ppermute | solution.py:191
  25.5 1.3 %attend.5 = bf16[128,512]{1,0:T(8,128)(2,1)} custom-call(f32[1,128]{1,0:T(1,128)S(1)} %get-tuple-element.16.k_gain_ref, bf16[128,512]{1,0:T(8,128)(2,1)S(1)} %get-tuple-element.17.qt_ref, f32[4,512]{1,0:T(4,128)S(1)} %get-tuple-element.18.bias_ref, bf16[1,2,200,128]{3,2,1,0:T(8,128)(2,1)S(1)} %collective-permute-done.4.refs_0_, ...), custom_call_target="tpu_custom_call" | custom-call | flops 52428800 | tf_op jit(solution)/shard_map/attend/pallas_call | solution.py:326
Async XLA Ops:
  0.0 6.5 %collective-permute-start.1 = (bf16[1,200,2048]{2,1,0:T(8,128)(2,1)}, bf16[1,200,2048]{2,1,0:T(8,128)(2,1)S(1)}, u32[]{:S(2)}, u32[]{:S(2)}) collective-permute-start(bf16[1,200,2048]{2,1,0:T(8,128)(2,1)} %x_hbm.1), channel_id=1, source_target_pairs={{0,4},{4,0},{1,5},{5,1},{2,6},{6,2},{3,7},{7,3},{8,12},{12,8},{9,1... | collective-permute-start | bytes 2457608 | tf_op jit(solution)/shard_map/ppermute | solution.py:191
  2.7 7.9 %collective-permute-start = (bf16[1,2,200,128]{3,2,1,0:T(8,128)(2,1)S(1)}, bf16[1,2,200,128]{3,2,1,0:T(8,128)(2,1)S(1)}, u32[]{:S(2)}, u32[]{:S(2)}) collective-permute-start(bf16[1,2,200,128]{3,2,1,0:T(8,128)(2,1)S(1)} %get-tuple-element.19.own_ref), channel_id=1, source_target_pairs={{0,4},{1,5},{2,0},{3,1},{4,6},{5,7},{6,2},{7,3},{8,12},{9,13},{10,... | collective-permute-start | bytes 307208 | tf_op jit(solution)/shard_map/ppermute | solution.py:202
  6.9 3.7 %collective-permute-start.2 = (bf16[1,2,200,128]{3,2,1,0:T(8,128)(2,1)S(1)}, bf16[1,2,200,128]{3,2,1,0:T(8,128)(2,1)S(1)}, u32[]{:S(2)}, u32[]{:S(2)}) collective-permute-start(bf16[1,2,200,128]{3,2,1,0:T(8,128)(2,1)S(1)} %other_heads.1), channel_id=1, source_target_pairs={{0,4},{1,5},{2,6},{3,7},{4,0},{5,1},{6,2},{7,3},{8,12},{9,13},{10,... | collective-permute-start | bytes 307208 | tf_op jit(solution)/shard_map/ppermute | solution.py:202
  7.0 7.3 %collective-permute-start.3 = (bf16[1,2,200,128]{3,2,1,0:T(8,128)(2,1)S(1)}, bf16[1,2,200,128]{3,2,1,0:T(8,128)(2,1)S(1)}, u32[]{:S(2)}, u32[]{:S(2)}) collective-permute-start(bf16[1,2,200,128]{3,2,1,0:T(8,128)(2,1)S(1)} %other_heads.1), channel_id=1, source_target_pairs={{0,0},{1,1},{2,4},{3,5},{4,2},{5,3},{6,6},{7,7},{8,8},{9,9},{10,12... | collective-permute-start | bytes 307208 | tf_op jit(solution)/shard_map/ppermute | solution.py:202
  14.3 4.5 %collective-permute-start.6 = (bf16[1,2,200,128]{3,2,1,0:T(8,128)(2,1)S(1)}, bf16[1,2,200,128]{3,2,1,0:T(8,128)(2,1)S(1)}, u32[]{:S(2)}, u32[]{:S(2)}) collective-permute-start(bf16[1,2,200,128]{3,2,1,0:T(8,128)(2,1)S(1)} %pair_sum.1.keep_ref), channel_id=1, source_target_pairs={{0,1},{1,0},{2,3},{3,2},{4,5},{5,4},{6,7},{7,6},{8,9},{9,8},{10,11... | collective-permute-start | bytes 307208 | tf_op jit(solution)/shard_map/ppermute | solution.py:191
  16.5 5.5 %collective-permute-start.4 = (bf16[1,2,200,128]{3,2,1,0:T(8,128)(2,1)S(1)}, bf16[1,2,200,128]{3,2,1,0:T(8,128)(2,1)S(1)}, u32[]{:S(2)}, u32[]{:S(2)}) collective-permute-start(bf16[1,2,200,128]{3,2,1,0:T(8,128)(2,1)S(1)} %pair_sum.1.keep_ref), channel_id=1, source_target_pairs={{0,24},{8,16},{16,8},{24,0},{1,25},{9,17},{17,9},{25,1},{2,26},{10... | collective-permute-start | bytes 307208 | tf_op jit(solution)/shard_map/ppermute | solution.py:191
  18.9 4.4 %collective-permute-start.7 = (bf16[2,200,128]{2,1,0:T(8,128)(2,1)S(1)}, bf16[2,200,128]{2,1,0:T(8,128)(2,1)S(1)}, u32[]{:S(2)}, u32[]{:S(2)}) collective-permute-start(bf16[2,200,128]{2,1,0:T(8,128)(2,1)S(1)} %sum_norm.1.refs_0_), channel_id=1, source_target_pairs={{0,8},{8,0},{16,24},{24,16},{1,9},{9,1},{17,25},{25,17},{2,10},{10... | collective-permute-start | bytes 307208 | tf_op jit(solution)/shard_map/ppermute | solution.py:191
  19.9 3.5 %collective-permute-start.8 = (bf16[2,200,128]{2,1,0:T(8,128)(2,1)S(1)}, bf16[2,200,128]{2,1,0:T(8,128)(2,1)S(1)}, u32[]{:S(2)}, u32[]{:S(2)}) collective-permute-start(bf16[2,200,128]{2,1,0:T(8,128)(2,1)S(1)} %sum_norm.1.refs_0_), channel_id=1, source_target_pairs={{0,16},{8,24},{16,0},{24,8},{1,17},{9,25},{17,1},{25,9},{2,18},{10... | collective-permute-start | bytes 307208 | tf_op jit(solution)/shard_map/ppermute | solution.py:191
  22.0 3.5 %collective-permute-start.5 = (bf16[1,2,200,128]{3,2,1,0:T(8,128)(2,1)S(1)}, bf16[1,2,200,128]{3,2,1,0:T(8,128)(2,1)S(1)}, u32[]{:S(2)}, u32[]{:S(2)}) collective-permute-start(bf16[1,2,200,128]{3,2,1,0:T(8,128)(2,1)S(1)} %collective-permute-done.4.refs_0_), channel_id=1, source_target_pairs={{0,1},{1,0},{2,3},{3,2},{4,5},{5,4},{6,7},{7,6},{8,9},{9,8},{10,11... | collective-permute-start | bytes 307208 | tf_op jit(solution)/shard_map/ppermute | solution.py:191

commit v6 on v5

--- a/solution.py
+++ b/solution.py
@@ -57,13 +57,9 @@
         ref[base + head, 1] = both[:, width + lo : width + lo + head_dim]
 
 
-def prepare_queries(hbm, vmem, sems, qt_ref, bias_ref):
-    copies = [pltpu.make_async_copy(a, b, sems.at[i]) for i, (a, b) in enumerate(zip(hbm, vmem))]
-    for copy in copies:
-        copy.start()
+def prepare_queries(copies, q_ref, q_gain_ref, mask_ref, qt_ref, bias_ref):
     for copy in copies:
         copy.wait()
-    q_ref, q_gain_ref, mask_ref = vmem
     tokens = q_ref.shape[0]
     head_dim = q_gain_ref.shape[1]
     bias = jnp.where(mask_ref[...] > 0, 0.0, MASKED_SCORE).astype(F32)
@@ -74,26 +70,86 @@
         bias_ref[:, head * tokens : (head + 1) * tokens] = bias
 
 
-def own_kernel(
-    head_dim, x_hbm, w_hbm, k_gain_hbm, own_ref, x_ref, w_ref, k_gain_ref, sems
-):
-    moves = [(k_gain_hbm, k_gain_ref), (x_hbm, x_ref), (w_hbm, w_ref)]
-    copies = [pltpu.make_async_copy(a, b, sems.at[i]) for i, (a, b) in enumerate(moves)]
+def start_copies(sources, targets, sems, first=0):
+    copies = [
+        pltpu.make_async_copy(a, b, sems.at[first + i]) for i, (a, b) in enumerate(zip(sources, targets))
+    ]
     for copy in copies:
         copy.start()
-    for copy in copies:
+    return copies
+
+
+def own_kernel(head_dim, x_hbm, w_hbm, own_ref, x_ref, w_ref, sems):
+    for copy in start_copies((x_hbm, w_hbm), (x_ref, w_ref), sems):
         copy.wait()
     store_heads(own_ref, 0, project(x_ref[0], w_ref[...]), head_dim)
+
+
+def other_kernel(head_dim, x_ref, w_ref, other_ref):
+    store_heads(other_ref, 0, project(x_ref[0], w_ref[...]), head_dim)
+
+
+def query_kernel(
+    q_hbm, q_gain_hbm, mask_hbm, k_gain_hbm, qt_ref, bias_ref, k_gain_ref,
+    q_ref, q_gain_ref, mask_ref, sems,
+):
+    copies = start_copies(
+        (q_hbm, q_gain_hbm, mask_hbm, k_gain_hbm), (q_ref, q_gain_ref, mask_ref, k_gain_ref), sems
+    )
+    prepare_queries(copies, q_ref, q_gain_ref, mask_ref, qt_ref, bias_ref)
+
+
+def is_home():
+    return lax.axis_index("tensor") // 2 == lax.axis_index("dp")
+
+
+def away_kernel(head_dim, x_hbm, w_hbm, own_ref, x_ref, w_ref, sems):
+    @pl.when(is_home())
+    def _():
+        own_ref[...] = jnp.zeros_like(own_ref)
+
+    @pl.when(jnp.logical_not(is_home()))
+    def _():
+        own_kernel(head_dim, x_hbm, w_hbm, own_ref, x_ref, w_ref, sems)
+
+
+def home_kernel(head_dim, x_hbm, w_other_ref, other_ref, x_ref, sems):
+    @pl.when(is_home())
+    def _():
+        for copy in start_copies((x_hbm,), (x_ref,), sems):
+            copy.wait()
+        store_heads(other_ref, 0, project(x_ref[0], w_other_ref[...]), head_dim)
+
+    @pl.when(jnp.logical_not(is_home()))
+    def _():
+        other_ref[...] = jnp.zeros_like(other_ref)
+
+
+def keep_kernel(
+    head_dim, after_ref, w_other_ref, x_hbm, w_hbm, q_hbm, q_gain_hbm, mask_hbm, k_gain_hbm,
+    keep_ref, qt_ref, bias_ref, k_gain_ref, x_ref, w_ref, q_ref, q_gain_ref, mask_ref, sems,
+):
+    copies = start_copies(
+        (q_hbm, q_gain_hbm, mask_hbm, k_gain_hbm), (q_ref, q_gain_ref, mask_ref, k_gain_ref), sems
+    )
+    moves = start_copies((x_hbm, w_hbm), (x_ref, w_ref), sems, len(copies))
+    prepare_queries(copies, q_ref, q_gain_ref, mask_ref, qt_ref, bias_ref)
+    for copy in moves:
+        copy.wait()
+
+    @pl.when(is_home())
+    def _():
+        store_heads(keep_ref, 0, project(x_ref[0], w_ref[...]), head_dim)
+
+    @pl.when(jnp.logical_not(is_home()))
+    def _():
+        store_heads(keep_ref, 0, project(x_ref[0], w_other_ref[...]), head_dim)
 
 
 def split_half(held, send_ref, keep_ref, partner_heads, own_heads):
     for i in range(send_ref.shape[0]):
         send_ref[i] = held[partner_heads + i]
         keep_ref[i] = held[own_heads + i]
-
-
-def other_kernel(head_dim, x_ref, w_ref, other_ref):
-    store_heads(other_ref, 0, project(x_ref[0], w_ref[...]), head_dim)
 
 
 def spread_kernel(n_dp, n_tensor, own_ref, *refs):
@@ -107,15 +163,9 @@
     split_half(held, send_ref, keep_ref, (1 - upper) * half, upper * half)
 
 
-def query_kernel(*refs):
-    prepare_queries(refs[:3], refs[5:8], refs[8], *refs[3:5])
-
-
-def pair_kernel(own_ref, first_ref, stayed_ref, crossed_ref, bias_ref, out_ref):
-    mine = lax.axis_index("tensor") // 2 == lax.axis_index("dp")
-    one = jnp.where(mine, own_ref[...], stayed_ref[...]).astype(F32)
-    two = jnp.where(mine, first_ref[...], crossed_ref[...]).astype(F32)
-    out_ref[...] = (one + two).astype(BF16)
+def pair_kernel(keep_ref, first_ref, second_ref, out_ref):
+    arrived = jnp.where(is_home(), first_ref[...], second_ref[...]).astype(F32)
+    out_ref[...] = (keep_ref[...].astype(F32) + arrived).astype(BF16)
 
 
 def add_kernel(bit, keep_ref, arrived_ref, send_ref, next_ref, held):
@@ -191,24 +241,13 @@
     return lax.ppermute(value, axis, [(i, i ^ k) for i in range(lax.axis_size(axis))])
 
 
-def sum_two_heads(own, images, w, bias, other):
-    devices = [(d, t) for d in range(2) for t in range(4)]
-
-    def permute(value, away, home):
-        hops = []
-        for d, t in devices:
-            to_d, to_t = away(d, t) if t // 2 != d else home(d, t)
-            hops.append((4 * d + t, 4 * to_d + to_t))
-        return lax.ppermute(value, ("dp", "tensor"), hops)
-
-    other_image = swap(images, "dp", 1)
-    first = permute(own, lambda d, t: (d, t ^ 2), lambda d, t: (1 - d, t))
-    rest = other(other_image, w)
-    stayed = permute(rest, lambda d, t: (1 - d, t), lambda d, t: (1 - d, t))
-    crossed = permute(rest, lambda d, t: (1 - d, t ^ 2), lambda d, t: (d, t))
-    return call(pair_kernel, shape_of(own.shape), 5, "pair_sum")(
-        own, first, stayed, crossed, bias
-    )
+def exchange_two_heads(value, home_sends):
+    hops = []
+    for d in range(2):
+        for t in range(4):
+            sends = (t // 2 == d) == home_sends
+            hops.append((4 * d + t, 4 * d + (t ^ 2) if sends else 4 * (1 - d) + t))
+    return lax.ppermute(value, ("dp", "tensor"), hops)
 
 
 def sum_many_heads(own, others):
@@ -256,50 +295,80 @@
     pairs = tokens * (q_width // head_dim)
     work = 4 * rows * features * kv_weight.shape[2]
 
-    in_hbm = [
+    x, w, *small = [
         pltpu.with_memory_space_constraint(value, pltpu.HBM)
         for value in (
-            images, kv_weight, k_gain.reshape(1, -1), queries, q_gain.reshape(1, -1), tile_mask.T,
+            images, kv_weight, queries, q_gain.reshape(1, -1), tile_mask.T, k_gain.reshape(1, -1),
         )
     ]
-    own, x, w, gain = call(
-        functools.partial(own_kernel, head_dim),
-        [
-            shape_of((own_heads, 2, rows, head_dim)),
-            shape_of(images.shape),
-            shape_of(kv_weight.shape),
-            shape_of((1, head_dim), F32),
-        ],
-        3,
-        "own_head",
-        flops=work,
-        size=2 * (images.size + kv_weight.size),
-        in_specs=[HBM] * 3,
-        scratch=[pltpu.SemaphoreType.DMA((3,))],
-    )(*in_hbm[:3])
-    qt, bias = call(
-        query_kernel,
-        [shape_of((head_dim, pairs)), shape_of((tiles, pairs), F32)],
-        3,
-        "queries",
-        in_specs=[HBM] * 3,
-        scratch=[
-            pltpu.VMEM(queries.shape, BF16),
-            pltpu.VMEM((1, head_dim), F32),
-            pltpu.VMEM((tiles, tokens), jnp.int32),
-            pltpu.SemaphoreType.DMA((3,)),
-        ],
-    )(*in_hbm[3:])
-
-    def other(rows_of, columns):
-        return call(
-            functools.partial(other_kernel, head_dim), shape_of(own.shape), 2, "other_heads", flops=work
-        )(rows_of, columns)
-
+    product = shape_of((own_heads, 2, rows, head_dim))
+    x_scratch, w_scratch = pltpu.VMEM(images.shape, BF16), pltpu.VMEM(kv_weight.shape, BF16)
+    prepared = [
+        shape_of((head_dim, pairs)),
+        shape_of((tiles, pairs), F32),
+        shape_of((1, head_dim), F32),
+    ]
+    query_scratch = [
+        pltpu.VMEM(queries.shape, BF16),
+        pltpu.VMEM((1, head_dim), F32),
+        pltpu.VMEM((tiles, tokens), jnp.int32),
+    ]
+    others = [swap(kv_weight, "dp", k) for k in range(1, n_dp)]
     if n_dp == 2 and own_heads == 1:
-        total = sum_two_heads(own, images, w, bias, other)
+        away = call(
+            functools.partial(away_kernel, head_dim),
+            product,
+            2,
+            "away_own",
+            flops=work,
+            in_specs=[HBM] * 2,
+            scratch=[x_scratch, w_scratch, pltpu.SemaphoreType.DMA((2,))],
+        )(x, w)
+        first = exchange_two_heads(away, False)
+        home = call(
+            functools.partial(home_kernel, head_dim),
+            product,
+            2,
+            "home_other",
+            flops=work,
+            in_specs=[HBM, VMEM],
+            scratch=[x_scratch, pltpu.SemaphoreType.DMA((1,))],
+        )(x, others[0])
+        second = exchange_two_heads(home, True)
+        keep, qt, bias, gain = call(
+            functools.partial(keep_kernel, head_dim),
+            [product, *prepared],
+            8,
+            "keep_queries",
+            flops=work,
+            in_specs=[VMEM] * 2 + [HBM] * 6,
+            scratch=[x_scratch, w_scratch, *query_scratch, pltpu.SemaphoreType.DMA((6,))],
+        )(home, others[0], x, w, *small)
+        total = call(pair_kernel, product, 3, "pair_sum")(keep, first, second)
     else:
-        rest = [other(x, swap(kv_weight, "dp", k)) for k in range(1, n_dp)]
+        own, x_here = call(
+            functools.partial(own_kernel, head_dim),
+            [product, shape_of(images.shape)],
+            2,
+            "own_heads",
+            flops=work,
+            in_specs=[HBM] * 2,
+            scratch=[w_scratch, pltpu.SemaphoreType.DMA((2,))],
+        )(x, w)
+        qt, bias, gain = call(
+            query_kernel,
+            prepared,
+            4,
+            "queries",
+            in_specs=[HBM] * 4,
+            scratch=[*query_scratch, pltpu.SemaphoreType.DMA((4,))],
+        )(*small)
+        rest = [
+            call(functools.partial(other_kernel, head_dim), product, 2, "other_heads", flops=work)(
+                x_here, other
+            )
+            for other in others
+        ]
         total = sum_many_heads(own, rest)
     far = [step for step in range(1, n_section) if step & (step - 1)]
     near = [step for step in range(1, n_section) if not step & (step - 1)]

time: 26.9 us -> 24.3 us (0.903)
  the two profiles are of different devices: /device:TPU:1 before, /device:TPU:0 now
where the time goes in v6:
time: 24.3 us; the launch traced here: 24.1 us
  starting transfers between devices  15.5 us (64%)
  Pallas kernels  6.08 us (25%)
  waiting for transfers between devices  2.49 us (10%)
    ppermute x6, starting transfers between devices, swap(): lax.ppermute(value, axis, [(i, i ^ k) for i in range(lax.axis_size(axis))])  11 us
    ppermute x2, starting transfers between devices, exchange_two_heads(): return lax.ppermute(value, ('dp', 'tensor'), hops)  4.45 us
    ppermute x6, waiting for transfers between devices, swap(): lax.ppermute(value, axis, [(i, i ^ k) for i in range(lax.axis_size(axis))])  2.3 us
    pallas_call x3, Pallas kernels, on_device(): call(functools.partial(attend_kernel, here, there, tile_len, first, last,...  2.27 us
    pallas_call x1, Pallas kernels, on_device(): call(functools.partial(keep_kernel, head_dim), [product, *prepared], 8, '...  2.05 us
    pallas_call x1, Pallas kernels, on_device(): call(functools.partial(home_kernel, head_dim), product, 2, 'home_other',...  1.57 us
  transfers between devices with their start and end apart: 8, of which 5 were waited for; matrix products, arithmetic and copies ran while one was open for 0% of the time, Pallas kernels for 20%

profile of v6, /device:TPU:0, one launch (start us, length us, event | category | flops | bytes accessed | tf_op | source)
XLA Modules:
  0.0 24.1 jit_solution(4096260615745064978)
XLA Ops:
  0.0 0.5 %collective-permute-start = (bf16[2,2048,128]{2,1,0:T(8,128)(2,1)}, bf16[2,2048,128]{2,1,0:T(8,128)(2,1)S(1)}, u32[]{:S(2)}, u32[]{:S(2)}) collective-permute-start(bf16[2,2048,128]{2,1,0:T(8,128)(2,1)} %w_hbm.3), channel_id=1, source_target_pairs={{0,4},{4,0},{1,5},{5,1},{2,6},{6,2},{3,7},{7,3},{8,12},{12,8},{9,1... | collective-permute-start | bytes 3145736 | tf_op jit(solution)/shard_map/ppermute | solution.py:241
  0.5 2.0 %collective-permute-start.1 = (bf16[1,2,200,128]{3,2,1,0:T(8,128)(2,1)S(1)}, bf16[1,2,200,128]{3,2,1,0:T(8,128)(2,1)S(1)}, u32[]{:S(2)}, u32[]{:S(2)}) collective-permute-start(bf16[1,2,200,128]{3,2,1,0:T(8,128)(2,1)S(1)} %away_own.1), channel_id=1, source_target_pairs={{0,4},{1,5},{2,0},{3,1},{4,6},{5,7},{6,2},{7,3},{8,12},{9,13},{10,... | collective-permute-start | bytes 307208 | tf_op jit(solution)/shard_map/ppermute | solution.py:250
  2.5 0.5 %collective-permute-done.w_other_ref = bf16[2,2048,128]{2,1,0:T(8,128)(2,1)S(1)} collective-permute-done((bf16[2,2048,128]{2,1,0:T(8,128)(2,1)}, bf16[2,2048,128]{2,1,0:T(8,128)(2,1)S(1)}, u32[]{:S(2)}, u32[]{:S(2)}) %collective-permute-start) | collective-permute-done | bytes 1048608 | tf_op jit(solution)/shard_map/ppermute | solution.py:241
  3.0 1.6 %home_other.1.after_ref = bf16[1,2,200,128]{3,2,1,0:T(8,128)(2,1)S(1)} custom-call(bf16[1,200,2048]{2,1,0:T(8,128)(2,1)} %x_hbm.5, bf16[2,2048,128]{2,1,0:T(8,128)(2,1)S(1)} %collective-permute-done.w_other_ref), custom_call_target="tpu_custom_call" | custom-call | flops 209715200 | tf_op jit(solution)/shard_map/home_other/pallas_call | solution.py:328
  4.5 2.5 %collective-permute-start.2 = (bf16[1,2,200,128]{3,2,1,0:T(8,128)(2,1)S(1)}, bf16[1,2,200,128]{3,2,1,0:T(8,128)(2,1)S(1)}, u32[]{:S(2)}, u32[]{:S(2)}) collective-permute-start(bf16[1,2,200,128]{3,2,1,0:T(8,128)(2,1)S(1)} %home_other.1.after_ref), channel_id=1, source_target_pairs={{0,2},{1,3},{2,6},{3,7},{4,0},{5,1},{6,4},{7,5},{8,10},{9,11},{10,... | collective-permute-start | bytes 307208 | tf_op jit(solution)/shard_map/ppermute | solution.py:250
  7.0 2.0 %keep_queries.1 = (bf16[1,2,200,128]{3,2,1,0:T(8,128)(2,1)S(1)}, bf16[128,512]{1,0:T(8,128)(2,1)S(1)}, f32[4,512]{1,0:T(4,128)S(1)}, f32[1,128]{1,0:T(1,128)S(1)}) custom-call(bf16[1,2,200,128]{3,2,1,0:T(8,128)(2,1)S(1)} %home_other.1.after_ref, bf16[2,2048,128]{2,1,0:T(8,128)(2,1)S(1)} %collective-permute-done.w_other_ref, bf16[1,200,2048]{2,1,0:T(8,128)(2,1)} %x_hbm.5, ...), custom_call_target="tpu_custom_call" | custom-call | flops 209715200 | tf_op jit(solution)/shard_map/keep_queries/pallas_call | solution.py:338
  9.1 0.0 collective-permute-done.1.first_ref
  9.1 0.2 collective-permute-done.2.second_ref
  9.3 2.6 %collective-permute-start.5 = (bf16[1,2,200,128]{3,2,1,0:T(8,128)(2,1)S(1)}, bf16[1,2,200,128]{3,2,1,0:T(8,128)(2,1)S(1)}, u32[]{:S(2)}, u32[]{:S(2)}) collective-permute-start(bf16[1,2,200,128]{3,2,1,0:T(8,128)(2,1)S(1)} %pair_sum.1.keep_ref), channel_id=1, source_target_pairs={{0,1},{1,0},{2,3},{3,2},{4,5},{5,4},{6,7},{7,6},{8,9},{9,8},{10,11... | collective-permute-start | bytes 307208 | tf_op jit(solution)/shard_map/ppermute | solution.py:241
  11.9 2.5 %collective-permute-start.3 = (bf16[1,2,200,128]{3,2,1,0:T(8,128)(2,1)S(1)}, bf16[1,2,200,128]{3,2,1,0:T(8,128)(2,1)S(1)}, u32[]{:S(2)}, u32[]{:S(2)}) collective-permute-start(bf16[1,2,200,128]{3,2,1,0:T(8,128)(2,1)S(1)} %pair_sum.1.keep_ref), channel_id=1, source_target_pairs={{0,24},{8,16},{16,8},{24,0},{1,25},{9,17},{17,9},{25,1},{2,26},{10... | collective-permute-start | bytes 307208 | tf_op jit(solution)/shard_map/ppermute | solution.py:241
  14.3 0.2 collective-permute-done.5.arrived_ref
  14.5 0.1 sum_norm.1.refs_0_
  14.7 1.6 %collective-permute-start.6 = (bf16[2,200,128]{2,1,0:T(8,128)(2,1)S(1)}, bf16[2,200,128]{2,1,0:T(8,128)(2,1)S(1)}, u32[]{:S(2)}, u32[]{:S(2)}) collective-permute-start(bf16[2,200,128]{2,1,0:T(8,128)(2,1)S(1)} %sum_norm.1.refs_0_), channel_id=1, source_target_pairs={{0,8},{8,0},{16,24},{24,16},{1,9},{9,1},{17,25},{25,17},{2,10},{10... | collective-permute-start | bytes 307208 | tf_op jit(solution)/shard_map/ppermute | solution.py:241
  16.2 1.5 %collective-permute-start.7 = (bf16[2,200,128]{2,1,0:T(8,128)(2,1)S(1)}, bf16[2,200,128]{2,1,0:T(8,128)(2,1)S(1)}, u32[]{:S(2)}, u32[]{:S(2)}) collective-permute-start(bf16[2,200,128]{2,1,0:T(8,128)(2,1)S(1)} %sum_norm.1.refs_0_), channel_id=1, source_target_pairs={{0,16},{8,24},{16,0},{24,8},{1,17},{9,25},{17,1},{25,9},{2,18},{10... | collective-permute-start | bytes 307208 | tf_op jit(solution)/shard_map/ppermute | solution.py:241
  17.8 0.0 collective-permute-done.3.refs_0_
  17.8 2.5 %collective-permute-start.4 = (bf16[1,2,200,128]{3,2,1,0:T(8,128)(2,1)S(1)}, bf16[1,2,200,128]{3,2,1,0:T(8,128)(2,1)S(1)}, u32[]{:S(2)}, u32[]{:S(2)}) collective-permute-start(bf16[1,2,200,128]{3,2,1,0:T(8,128)(2,1)S(1)} %collective-permute-done.3.refs_0_), channel_id=1, source_target_pairs={{0,1},{1,0},{2,3},{3,2},{4,5},{5,4},{6,7},{7,6},{8,9},{9,8},{10,11... | collective-permute-start | bytes 307208 | tf_op jit(solution)/shard_map/ppermute | solution.py:241
  20.2 0.4 %attend.3 = (f32[1,512]{1,0:T(1,128)S(1)}, f32[1,512]{1,0:T(1,128)S(1)}, f32[128,512]{1,0:T(8,128)S(1)}) custom-call(f32[1,128]{1,0:T(1,128)S(1)} %get-tuple-element.15.k_gain_ref, bf16[128,512]{1,0:T(8,128)(2,1)S(1)} %get-tuple-element.16.qt_ref, f32[4,512]{1,0:T(4,128)S(1)} %get-tuple-element.17.bias_ref, bf16[2,200,128]{2,1,0:T(8,128)(2,1)S(1)} %sum_norm.1.refs_0_), custom_call_target="tpu_custom_call" | custom-call | flops 52428800 | tf_op jit(solution)/shard_map/attend/pallas_call | solution.py:395
  20.7 0.0 collective-permute-done.6.refs_0_
  20.7 0.9 %collective-permute-done.7.refs_1_ = bf16[2,200,128]{2,1,0:T(8,128)(2,1)S(1)} collective-permute-done((bf16[2,200,128]{2,1,0:T(8,128)(2,1)S(1)}, bf16[2,200,128]{2,1,0:T(8,128)(2,1)S(1)}, u32[]{:S(2)}, u32[]{:S(2)}) %collective-permute-start.7) | collective-permute-done | bytes 102432 | tf_op jit(solution)/shard_map/ppermute | solution.py:241
  21.6 0.6 %attend.4 = (f32[1,512]{1,0:T(1,128)S(1)}, f32[1,512]{1,0:T(1,128)S(1)}, f32[128,512]{1,0:T(8,128)S(1)}) custom-call(f32[1,128]{1,0:T(1,128)S(1)} %get-tuple-element.15.k_gain_ref, bf16[128,512]{1,0:T(8,128)(2,1)S(1)} %get-tuple-element.16.qt_ref, f32[4,512]{1,0:T(4,128)S(1)} %get-tuple-element.17.bias_ref, ...), custom_call_target="tpu_custom_call" | custom-call | flops 104857600 | tf_op jit(solution)/shard_map/attend/pallas_call | solution.py:395
  22.2 0.7 %collective-permute-done.4.refs_1_ = bf16[1,2,200,128]{3,2,1,0:T(8,128)(2,1)S(1)} collective-permute-done((bf16[1,2,200,128]{3,2,1,0:T(8,128)(2,1)S(1)}, bf16[1,2,200,128]{3,2,1,0:T(8,128)(2,1)S(1)}, u32[]{:S(2)}, u32[]{:S(2)}) %collective-permute-start.4) | collective-permute-done | bytes 102432 | tf_op jit(solution)/shard_map/ppermute | solution.py:241
  22.9 1.3 %attend.5 = bf16[128,512]{1,0:T(8,128)(2,1)} custom-call(f32[1,128]{1,0:T(1,128)S(1)} %get-tuple-element.15.k_gain_ref, bf16[128,512]{1,0:T(8,128)(2,1)S(1)} %get-tuple-element.16.qt_ref, f32[4,512]{1,0:T(4,128)S(1)} %get-tuple-element.17.bias_ref, bf16[1,2,200,128]{3,2,1,0:T(8,128)(2,1)S(1)} %collective-permute-done.3.refs_0_, ...), custom_call_target="tpu_custom_call" | custom-call | flops 52428800 | tf_op jit(solution)/shard_map/attend/pallas_call | solution.py:395
  (2 shorter events, 0.1 us)
Async XLA Ops:
  0.0 3.0 %collective-permute-start = (bf16[2,2048,128]{2,1,0:T(8,128)(2,1)}, bf16[2,2048,128]{2,1,0:T(8,128)(2,1)S(1)}, u32[]{:S(2)}, u32[]{:S(2)}) collective-permute-start(bf16[2,2048,128]{2,1,0:T(8,128)(2,1)} %w_hbm.3), channel_id=1, source_target_pairs={{0,4},{4,0},{1,5},{5,1},{2,6},{6,2},{3,7},{7,3},{8,12},{12,8},{9,1... | collective-permute-start | bytes 3145736 | tf_op jit(solution)/shard_map/ppermute | solution.py:241
  0.5 8.6 %collective-permute-start.1 = (bf16[1,2,200,128]{3,2,1,0:T(8,128)(2,1)S(1)}, bf16[1,2,200,128]{3,2,1,0:T(8,128)(2,1)S(1)}, u32[]{:S(2)}, u32[]{:S(2)}) collective-permute-start(bf16[1,2,200,128]{3,2,1,0:T(8,128)(2,1)S(1)} %away_own.1), channel_id=1, source_target_pairs={{0,4},{1,5},{2,0},{3,1},{4,6},{5,7},{6,2},{7,3},{8,12},{9,13},{10,... | collective-permute-start | bytes 307208 | tf_op jit(solution)/shard_map/ppermute | solution.py:250
  4.5 4.7 %collective-permute-start.2 = (bf16[1,2,200,128]{3,2,1,0:T(8,128)(2,1)S(1)}, bf16[1,2,200,128]{3,2,1,0:T(8,128)(2,1)S(1)}, u32[]{:S(2)}, u32[]{:S(2)}) collective-permute-start(bf16[1,2,200,128]{3,2,1,0:T(8,128)(2,1)S(1)} %home_other.1.after_ref), channel_id=1, source_target_pairs={{0,2},{1,3},{2,6},{3,7},{4,0},{5,1},{6,4},{7,5},{8,10},{9,11},{10,... | collective-permute-start | bytes 307208 | tf_op jit(solution)/shard_map/ppermute | solution.py:250
  9.3 5.2 %collective-permute-start.5 = (bf16[1,2,200,128]{3,2,1,0:T(8,128)(2,1)S(1)}, bf16[1,2,200,128]{3,2,1,0:T(8,128)(2,1)S(1)}, u32[]{:S(2)}, u32[]{:S(2)}) collective-permute-start(bf16[1,2,200,128]{3,2,1,0:T(8,128)(2,1)S(1)} %pair_sum.1.keep_ref), channel_id=1, source_target_pairs={{0,1},{1,0},{2,3},{3,2},{4,5},{5,4},{6,7},{7,6},{8,9},{9,8},{10,11... | collective-permute-start | bytes 307208 | tf_op jit(solution)/shard_map/ppermute | solution.py:241
  11.9 5.9 %collective-permute-start.3 = (bf16[1,2,200,128]{3,2,1,0:T(8,128)(2,1)S(1)}, bf16[1,2,200,128]{3,2,1,0:T(8,128)(2,1)S(1)}, u32[]{:S(2)}, u32[]{:S(2)}) collective-permute-start(bf16[1,2,200,128]{3,2,1,0:T(8,128)(2,1)S(1)} %pair_sum.1.keep_ref), channel_id=1, source_target_pairs={{0,24},{8,16},{16,8},{24,0},{1,25},{9,17},{17,9},{25,1},{2,26},{10... | collective-permute-start | bytes 307208 | tf_op jit(solution)/shard_map/ppermute | solution.py:241
  14.7 6.0 %collective-permute-start.6 = (bf16[2,200,128]{2,1,0:T(8,128)(2,1)S(1)}, bf16[2,200,128]{2,1,0:T(8,128)(2,1)S(1)}, u32[]{:S(2)}, u32[]{:S(2)}) collective-permute-start(bf16[2,200,128]{2,1,0:T(8,128)(2,1)S(1)} %sum_norm.1.refs_0_), channel_id=1, source_target_pairs={{0,8},{8,0},{16,24},{24,16},{1,9},{9,1},{17,25},{25,17},{2,10},{10... | collective-permute-start | bytes 307208 | tf_op jit(solution)/shard_map/ppermute | solution.py:241
  16.2 5.4 %collective-permute-start.7 = (bf16[2,200,128]{2,1,0:T(8,128)(2,1)S(1)}, bf16[2,200,128]{2,1,0:T(8,128)(2,1)S(1)}, u32[]{:S(2)}, u32[]{:S(2)}) collective-permute-start(bf16[2,200,128]{2,1,0:T(8,128)(2,1)S(1)} %sum_norm.1.refs_0_), channel_id=1, source_target_pairs={{0,16},{8,24},{16,0},{24,8},{1,17},{9,25},{17,1},{25,9},{2,18},{10... | collective-permute-start | bytes 307208 | tf_op jit(solution)/shard_map/ppermute | solution.py:241
  17.8 5.1 %collective-permute-start.4 = (bf16[1,2,200,128]{3,2,1,0:T(8,128)(2,1)S(1)}, bf16[1,2,200,128]{3,2,1,0:T(8,128)(2,1)S(1)}, u32[]{:S(2)}, u32[]{:S(2)}) collective-permute-start(bf16[1,2,200,128]{3,2,1,0:T(8,128)(2,1)S(1)} %collective-permute-done.3.refs_0_), channel_id=1, source_target_pairs={{0,1},{1,0},{2,3},{3,2},{4,5},{5,4},{6,7},{7,6},{8,9},{9,8},{10,11... | collective-permute-start | bytes 307208 | tf_op jit(solution)/shard_map/ppermute | solution.py:241

commit v7 on v6

--- a/solution.py
+++ b/solution.py
@@ -90,7 +90,7 @@
 
 
 def query_kernel(
-    q_hbm, q_gain_hbm, mask_hbm, k_gain_hbm, qt_ref, bias_ref, k_gain_ref,
+    after_ref, q_hbm, q_gain_hbm, mask_hbm, k_gain_hbm, qt_ref, bias_ref, k_gain_ref,
     q_ref, q_gain_ref, mask_ref, sems,
 ):
     copies = start_copies(
@@ -103,7 +103,7 @@
     return lax.axis_index("tensor") // 2 == lax.axis_index("dp")
 
 
-def away_kernel(head_dim, x_hbm, w_hbm, own_ref, x_ref, w_ref, sems):
+def away_kernel(head_dim, x_hbm, w_hbm, own_ref, w_ref, x_ref, sems):
     @pl.when(is_home())
     def _():
         own_ref[...] = jnp.zeros_like(own_ref)
@@ -113,37 +113,26 @@
         own_kernel(head_dim, x_hbm, w_hbm, own_ref, x_ref, w_ref, sems)
 
 
-def home_kernel(head_dim, x_hbm, w_other_ref, other_ref, x_ref, sems):
+def crossing_kernel(head_dim, x_other_ref, w_ref, other_ref):
     @pl.when(is_home())
     def _():
-        for copy in start_copies((x_hbm,), (x_ref,), sems):
-            copy.wait()
-        store_heads(other_ref, 0, project(x_ref[0], w_other_ref[...]), head_dim)
+        other_ref[...] = jnp.zeros_like(other_ref)
 
     @pl.when(jnp.logical_not(is_home()))
     def _():
-        other_ref[...] = jnp.zeros_like(other_ref)
-
-
-def keep_kernel(
-    head_dim, after_ref, w_other_ref, x_hbm, w_hbm, q_hbm, q_gain_hbm, mask_hbm, k_gain_hbm,
-    keep_ref, qt_ref, bias_ref, k_gain_ref, x_ref, w_ref, q_ref, q_gain_ref, mask_ref, sems,
-):
-    copies = start_copies(
-        (q_hbm, q_gain_hbm, mask_hbm, k_gain_hbm), (q_ref, q_gain_ref, mask_ref, k_gain_ref), sems
-    )
-    moves = start_copies((x_hbm, w_hbm), (x_ref, w_ref), sems, len(copies))
-    prepare_queries(copies, q_ref, q_gain_ref, mask_ref, qt_ref, bias_ref)
-    for copy in moves:
-        copy.wait()
-
+        store_heads(other_ref, 0, project(x_other_ref[0], w_ref[...]), head_dim)
+
+
+def home_kernel(head_dim, after_ref, x_other_ref, x_hbm, w_hbm, keep_ref, pass_ref, x_ref, w_ref, sems):
     @pl.when(is_home())
     def _():
-        store_heads(keep_ref, 0, project(x_ref[0], w_ref[...]), head_dim)
+        own_kernel(head_dim, x_hbm, w_hbm, keep_ref, x_ref, w_ref, sems)
+        store_heads(pass_ref, 0, project(x_other_ref[0], w_ref[...]), head_dim)
 
     @pl.when(jnp.logical_not(is_home()))
     def _():
-        store_heads(keep_ref, 0, project(x_ref[0], w_other_ref[...]), head_dim)
+        keep_ref[...] = jnp.zeros_like(keep_ref)
+        pass_ref[...] = jnp.zeros_like(pass_ref)
 
 
 def split_half(held, send_ref, keep_ref, partner_heads, own_heads):
@@ -163,9 +152,14 @@
     split_half(held, send_ref, keep_ref, (1 - upper) * half, upper * half)
 
 
-def pair_kernel(keep_ref, first_ref, second_ref, out_ref):
-    arrived = jnp.where(is_home(), first_ref[...], second_ref[...]).astype(F32)
-    out_ref[...] = (keep_ref[...].astype(F32) + arrived).astype(BF16)
+def arrival_kernel(keep_ref, first_ref, crossed_ref, out_ref):
+    complete = keep_ref[...].astype(F32) + first_ref[...].astype(F32)
+    out_ref[...] = jnp.where(is_home(), complete, crossed_ref[...].astype(F32))
+
+
+def pair_kernel(arrival_ref, passed_ref, bias_ref, out_ref):
+    passed = jnp.where(is_home(), 0.0, passed_ref[...].astype(F32))
+    out_ref[...] = (arrival_ref[...] + passed).astype(BF16)
 
 
 def add_kernel(bit, keep_ref, arrived_ref, send_ref, next_ref, held):
@@ -241,12 +235,12 @@
     return lax.ppermute(value, axis, [(i, i ^ k) for i in range(lax.axis_size(axis))])
 
 
-def exchange_two_heads(value, home_sends):
+def permute_two_heads(value, away, home):
     hops = []
     for d in range(2):
         for t in range(4):
-            sends = (t // 2 == d) == home_sends
-            hops.append((4 * d + t, 4 * d + (t ^ 2) if sends else 4 * (1 - d) + t))
+            to_d, to_t = home(d, t) if t // 2 == d else away(d, t)
+            hops.append((4 * d + t, 4 * to_d + to_t))
     return lax.ppermute(value, ("dp", "tensor"), hops)
 
 
@@ -313,38 +307,45 @@
         pltpu.VMEM((1, head_dim), F32),
         pltpu.VMEM((tiles, tokens), jnp.int32),
     ]
-    others = [swap(kv_weight, "dp", k) for k in range(1, n_dp)]
+    query_call = call(
+        query_kernel,
+        prepared,
+        5,
+        "queries",
+        in_specs=[VMEM] + [HBM] * 4,
+        scratch=[*query_scratch, pltpu.SemaphoreType.DMA((4,))],
+    )
     if n_dp == 2 and own_heads == 1:
-        away = call(
+        x_other = swap(images, "dp", 1)
+        own, w_here = call(
             functools.partial(away_kernel, head_dim),
-            product,
+            [product, shape_of(kv_weight.shape)],
             2,
             "away_own",
             flops=work,
             in_specs=[HBM] * 2,
+            scratch=[x_scratch, pltpu.SemaphoreType.DMA((2,))],
+        )(x, w)
+        first = permute_two_heads(own, lambda d, t: (d, t ^ 2), lambda d, t: (1 - d, t))
+        crossing = call(
+            functools.partial(crossing_kernel, head_dim), product, 2, "away_other", flops=work
+        )(x_other, w_here)
+        crossed = permute_two_heads(crossing, lambda d, t: (1 - d, t ^ 2), lambda d, t: (d, t))
+        keep, passing = call(
+            functools.partial(home_kernel, head_dim),
+            [product, product],
+            4,
+            "home_both",
+            flops=2 * work,
+            in_specs=[VMEM] * 2 + [HBM] * 2,
             scratch=[x_scratch, w_scratch, pltpu.SemaphoreType.DMA((2,))],
-        )(x, w)
-        first = exchange_two_heads(away, False)
-        home = call(
-            functools.partial(home_kernel, head_dim),
-            product,
-            2,
-            "home_other",
-            flops=work,
-            in_specs=[HBM, VMEM],
-            scratch=[x_scratch, pltpu.SemaphoreType.DMA((1,))],
-        )(x, others[0])
-        second = exchange_two_heads(home, True)
-        keep, qt, bias, gain = call(
-            functools.partial(keep_kernel, head_dim),
-            [product, *prepared],
-            8,
-            "keep_queries",
-            flops=work,
-            in_specs=[VMEM] * 2 + [HBM] * 6,
-            scratch=[x_scratch, w_scratch, *query_scratch, pltpu.SemaphoreType.DMA((6,))],
-        )(home, others[0], x, w, *small)
-        total = call(pair_kernel, product, 3, "pair_sum")(keep, first, second)
+        )(crossing, x_other, x, w)
+        passed = swap(passing, "dp", 1)
+        qt, bias, gain = query_call(keep, *small)
+        arrival = call(arrival_kernel, shape_of(product.shape, F32), 3, "arrival")(
+            keep, first, crossed
+        )
+        total = call(pair_kernel, product, 3, "pair_sum")(arrival, passed, bias)
     else:
         own, x_here = call(
             functools.partial(own_kernel, head_dim),
@@ -355,14 +356,8 @@
             in_specs=[HBM] * 2,
             scratch=[w_scratch, pltpu.SemaphoreType.DMA((2,))],
         )(x, w)
-        qt, bias, gain = call(
-            query_kernel,
-            prepared,
-            4,
-            "queries",
-            in_specs=[HBM] * 4,
-            scratch=[*query_scratch, pltpu.SemaphoreType.DMA((4,))],
-        )(*small)
+        qt, bias, gain = query_call(own, *small)
+        others = [swap(kv_weight, "dp", k) for k in range(1, n_dp)]
         rest = [
             call(functools.partial(other_kernel, head_dim), product, 2, "other_heads", flops=work)(
                 x_here, other

time: 24.3 us -> 25.9 us (1.066)
  the two profiles are of different devices: /device:TPU:0 before, /device:TPU:24 now
where the time goes in v7:
time: 25.9 us; the launch traced here: 25.7 us
  waiting for transfers between devices  10.3 us (40%)
  starting transfers between devices  9.14 us (35%)
  Pallas kernels  6.11 us (24%)
    ppermute x7, starting transfers between devices, swap(): lax.ppermute(value, axis, [(i, i ^ k) for i in range(lax.axis_size(axis))])  6.84 us
    ppermute x7, waiting for transfers between devices, swap(): lax.ppermute(value, axis, [(i, i ^ k) for i in range(lax.axis_size(axis))])  6.32 us
    ppermute x2, waiting for transfers between devices, permute_two_heads(): return lax.ppermute(value, ('dp', 'tensor'), hops)  4.02 us
    ppermute x2, starting transfers between devices, permute_two_heads(): return lax.ppermute(value, ('dp', 'tensor'), hops)  2.3 us
    pallas_call x3, Pallas kernels, on_device(): call(functools.partial(attend_kernel, here, there, tile_len, first, last,...  2.27 us
    pallas_call x1, Pallas kernels, on_device(): call(functools.partial(away_kernel, head_dim), [product, shape_of(kv_weig...  1.91 us
    pallas_call x1, Pallas kernels, on_device(): qt, bias, gain = query_call(keep, *small)  1.28 us
  transfers between devices with their start and end apart: 9, of which 6 were waited for; matrix products, arithmetic and copies ran while one was open for 0% of the time, Pallas kernels for 19%

profile of v7, /device:TPU:24, one launch (start us, length us, event | category | flops | bytes accessed | tf_op | source)
XLA Modules:
  0.0 25.7 jit_solution(5529950521406835296)
XLA Ops:
  0.0 0.0 collective-permute-start
  0.0 1.9 %away_own.1 = (bf16[1,2,200,128]{3,2,1,0:T(8,128)(2,1)S(1)}, bf16[2,2048,128]{2,1,0:T(8,128)(2,1)S(1)}) custom-call(bf16[1,200,2048]{2,1,0:T(8,128)(2,1)} %x_hbm.3, bf16[2,2048,128]{2,1,0:T(8,128)(2,1)} %w_hbm.3), custom_call_target="tpu_custom_call" | custom-call | flops 209715200 | tf_op jit(solution)/shard_map/away_own/pallas_call | solution.py:320
  1.9 0.1 collective-permute-start.1
  2.0 0.6 %collective-permute-done.x_other_ref = bf16[1,200,2048]{2,1,0:T(8,128)(2,1)S(1)} collective-permute-done((bf16[1,200,2048]{2,1,0:T(8,128)(2,1)}, bf16[1,200,2048]{2,1,0:T(8,128)(2,1)S(1)}, u32[]{:S(2)}, u32[]{:S(2)}) %collective-permute-start) | collective-permute-done | bytes 819232 | tf_op jit(solution)/shard_map/ppermute | solution.py:235
  2.5 0.4 %away_other.1.after_ref = bf16[1,2,200,128]{3,2,1,0:T(8,128)(2,1)S(1)} custom-call(bf16[1,200,2048]{2,1,0:T(8,128)(2,1)S(1)} %collective-permute-done.x_other_ref, bf16[2,2048,128]{2,1,0:T(8,128)(2,1)S(1)} %get-tuple-element.18.w_ref), custom_call_target="tpu_custom_call" | custom-call | flops 209715200 | tf_op jit(solution)/shard_map/away_other/pallas_call | solution.py:330
  2.9 2.2 %collective-permute-start.2 = (bf16[1,2,200,128]{3,2,1,0:T(8,128)(2,1)S(1)}, bf16[1,2,200,128]{3,2,1,0:T(8,128)(2,1)S(1)}, u32[]{:S(2)}, u32[]{:S(2)}) collective-permute-start(bf16[1,2,200,128]{3,2,1,0:T(8,128)(2,1)S(1)} %away_other.1.after_ref), channel_id=1, source_target_pairs={{0,0},{1,1},{2,4},{3,5},{4,2},{5,3},{6,6},{7,7},{8,8},{9,9},{10,12... | collective-permute-start | bytes 307208 | tf_op jit(solution)/shard_map/ppermute | solution.py:244
  5.2 0.1 home_both.1
  5.3 0.3 %collective-permute-start.3 = (bf16[1,2,200,128]{3,2,1,0:T(8,128)(2,1)S(1)}, bf16[1,2,200,128]{3,2,1,0:T(8,128)(2,1)S(1)}, u32[]{:S(2)}, u32[]{:S(2)}) collective-permute-start(bf16[1,2,200,128]{3,2,1,0:T(8,128)(2,1)S(1)} %get-tuple-element.24), channel_id=1, source_target_pairs={{0,4},{4,0},{1,5},{5,1},{2,6},{6,2},{3,7},{7,3},{8,12},{12,8},{9,1... | collective-permute-start | bytes 307208 | tf_op jit(solution)/shard_map/ppermute | solution.py:235
  5.6 1.3 %queries.1 = (bf16[128,512]{1,0:T(8,128)(2,1)S(1)}, f32[4,512]{1,0:T(4,128)S(1)}, f32[1,128]{1,0:T(1,128)S(1)}) custom-call(bf16[1,2,200,128]{3,2,1,0:T(8,128)(2,1)S(1)} %get-tuple-element.19.after_ref.keep_ref, bf16[128,512]{1,0:T(8,128)(2,1)} %q_hbm.1, f32[1,128]{1,0:T(1,128)} %bitcast.4, s32[4,128]{1,0:T(4,128)} %bitcast.3, f32[1,128]{1,0:T(1,128)} %bitcast.5), custom_call_target="tpu_custom_call" | custom-call | tf_op jit(solution)/shard_map/queries/pallas_call | solution.py:344
  6.9 0.0 collective-permute-done.1.first_ref
  6.9 4.0 %collective-permute-done.2.crossed_ref = bf16[1,2,200,128]{3,2,1,0:T(8,128)(2,1)S(1)} collective-permute-done((bf16[1,2,200,128]{3,2,1,0:T(8,128)(2,1)S(1)}, bf16[1,2,200,128]{3,2,1,0:T(8,128)(2,1)S(1)}, u32[]{:S(2)}, u32[]{:S(2)}) %collective-permute-start.2) | collective-permute-done | bytes 102432 | tf_op jit(solution)/shard_map/ppermute | solution.py:244
  10.9 0.0 collective-permute-done.3.passed_ref
  11.0 0.1 collective-permute-start.6
  11.1 2.5 %collective-permute-start.4 = (bf16[1,2,200,128]{3,2,1,0:T(8,128)(2,1)S(1)}, bf16[1,2,200,128]{3,2,1,0:T(8,128)(2,1)S(1)}, u32[]{:S(2)}, u32[]{:S(2)}) collective-permute-start(bf16[1,2,200,128]{3,2,1,0:T(8,128)(2,1)S(1)} %pair_sum.1.keep_ref), channel_id=1, source_target_pairs={{0,24},{8,16},{16,8},{24,0},{1,25},{9,17},{17,9},{25,1},{2,26},{10... | collective-permute-start | bytes 307208 | tf_op jit(solution)/shard_map/ppermute | solution.py:235
  13.6 2.1 %collective-permute-done.6.arrived_ref = bf16[1,2,200,128]{3,2,1,0:T(8,128)(2,1)S(1)} collective-permute-done((bf16[1,2,200,128]{3,2,1,0:T(8,128)(2,1)S(1)}, bf16[1,2,200,128]{3,2,1,0:T(8,128)(2,1)S(1)}, u32[]{:S(2)}, u32[]{:S(2)}) %collective-permute-start.6) | collective-permute-done | bytes 102432 | tf_op jit(solution)/shard_map/ppermute | solution.py:235
  15.7 0.1 sum_norm.1.refs_0_
  15.9 1.6 %collective-permute-start.8 = (bf16[2,200,128]{2,1,0:T(8,128)(2,1)S(1)}, bf16[2,200,128]{2,1,0:T(8,128)(2,1)S(1)}, u32[]{:S(2)}, u32[]{:S(2)}) collective-permute-start(bf16[2,200,128]{2,1,0:T(8,128)(2,1)S(1)} %sum_norm.1.refs_0_), channel_id=1, source_target_pairs={{0,16},{8,24},{16,0},{24,8},{1,17},{9,25},{17,1},{25,9},{2,18},{10... | collective-permute-start | bytes 307208 | tf_op jit(solution)/shard_map/ppermute | solution.py:235
  17.4 2.3 %collective-permute-start.7 = (bf16[2,200,128]{2,1,0:T(8,128)(2,1)S(1)}, bf16[2,200,128]{2,1,0:T(8,128)(2,1)S(1)}, u32[]{:S(2)}, u32[]{:S(2)}) collective-permute-start(bf16[2,200,128]{2,1,0:T(8,128)(2,1)S(1)} %sum_norm.1.refs_0_), channel_id=1, source_target_pairs={{0,8},{8,0},{16,24},{24,16},{1,9},{9,1},{17,25},{25,17},{2,10},{10... | collective-permute-start | bytes 307208 | tf_op jit(solution)/shard_map/ppermute | solution.py:235
  19.8 0.0 collective-permute-done.4.refs_0_
  19.8 0.0 collective-permute-start.5
  19.8 0.4 %attend.3 = (f32[1,512]{1,0:T(1,128)S(1)}, f32[1,512]{1,0:T(1,128)S(1)}, f32[128,512]{1,0:T(8,128)S(1)}) custom-call(f32[1,128]{1,0:T(1,128)S(1)} %get-tuple-element.20.k_gain_ref, bf16[128,512]{1,0:T(8,128)(2,1)S(1)} %get-tuple-element.21.qt_ref, f32[4,512]{1,0:T(4,128)S(1)} %get-tuple-element.22.bias_ref, bf16[2,200,128]{2,1,0:T(8,128)(2,1)S(1)} %sum_norm.1.refs_0_), custom_call_target="tpu_custom_call" | custom-call | flops 52428800 | tf_op jit(solution)/shard_map/attend/pallas_call | solution.py:390
  20.2 0.4 %collective-permute-done.8.refs_1_ = bf16[2,200,128]{2,1,0:T(8,128)(2,1)S(1)} collective-permute-done((bf16[2,200,128]{2,1,0:T(8,128)(2,1)S(1)}, bf16[2,200,128]{2,1,0:T(8,128)(2,1)S(1)}, u32[]{:S(2)}, u32[]{:S(2)}) %collective-permute-start.8) | collective-permute-done | bytes 102432 | tf_op jit(solution)/shard_map/ppermute | solution.py:235
  20.6 1.8 %collective-permute-done.7.refs_0_ = bf16[2,200,128]{2,1,0:T(8,128)(2,1)S(1)} collective-permute-done((bf16[2,200,128]{2,1,0:T(8,128)(2,1)S(1)}, bf16[2,200,128]{2,1,0:T(8,128)(2,1)S(1)}, u32[]{:S(2)}, u32[]{:S(2)}) %collective-permute-start.7) | collective-permute-done | bytes 102432 | tf_op jit(solution)/shard_map/ppermute | solution.py:235
  22.4 0.6 %attend.4 = (f32[1,512]{1,0:T(1,128)S(1)}, f32[1,512]{1,0:T(1,128)S(1)}, f32[128,512]{1,0:T(8,128)S(1)}) custom-call(f32[1,128]{1,0:T(1,128)S(1)} %get-tuple-element.20.k_gain_ref, bf16[128,512]{1,0:T(8,128)(2,1)S(1)} %get-tuple-element.21.qt_ref, f32[4,512]{1,0:T(4,128)S(1)} %get-tuple-element.22.bias_ref, ...), custom_call_target="tpu_custom_call" | custom-call | flops 104857600 | tf_op jit(solution)/shard_map/attend/pallas_call | solution.py:390
  23.0 1.4 %collective-permute-done.5.refs_1_ = bf16[1,2,200,128]{3,2,1,0:T(8,128)(2,1)S(1)} collective-permute-done((bf16[1,2,200,128]{3,2,1,0:T(8,128)(2,1)S(1)}, bf16[1,2,200,128]{3,2,1,0:T(8,128)(2,1)S(1)}, u32[]{:S(2)}, u32[]{:S(2)}) %collective-permute-start.5) | collective-permute-done | bytes 102432 | tf_op jit(solution)/shard_map/ppermute | solution.py:235
  24.4 1.3 %attend.5 = bf16[128,512]{1,0:T(8,128)(2,1)} custom-call(f32[1,128]{1,0:T(1,128)S(1)} %get-tuple-element.20.k_gain_ref, bf16[128,512]{1,0:T(8,128)(2,1)S(1)} %get-tuple-element.21.qt_ref, f32[4,512]{1,0:T(4,128)S(1)} %get-tuple-element.22.bias_ref, bf16[1,2,200,128]{3,2,1,0:T(8,128)(2,1)S(1)} %collective-permute-done.4.refs_0_, ...), custom_call_target="tpu_custom_call" | custom-call | flops 52428800 | tf_op jit(solution)/shard_map/attend/pallas_call | solution.py:390
  (2 shorter events, 0.1 us)
Async XLA Ops:
  0.0 2.5 %collective-permute-start = (bf16[1,200,2048]{2,1,0:T(8,128)(2,1)}, bf16[1,200,2048]{2,1,0:T(8,128)(2,1)S(1)}, u32[]{:S(2)}, u32[]{:S(2)}) collective-permute-start(bf16[1,200,2048]{2,1,0:T(8,128)(2,1)} %x_hbm.3), channel_id=1, source_target_pairs={{0,4},{4,0},{1,5},{5,1},{2,6},{6,2},{3,7},{7,3},{8,12},{12,8},{9,1... | collective-permute-start | bytes 2457608 | tf_op jit(solution)/shard_map/ppermute | solution.py:235
  1.9 5.0 %collective-permute-start.1 = (bf16[1,2,200,128]{3,2,1,0:T(8,128)(2,1)S(1)}, bf16[1,2,200,128]{3,2,1,0:T(8,128)(2,1)S(1)}, u32[]{:S(2)}, u32[]{:S(2)}) collective-permute-start(bf16[1,2,200,128]{3,2,1,0:T(8,128)(2,1)S(1)} %get-tuple-element.23), channel_id=1, source_target_pairs={{0,4},{1,5},{2,0},{3,1},{4,6},{5,7},{6,2},{7,3},{8,12},{9,13},{10,... | collective-permute-start | bytes 307208 | tf_op jit(solution)/shard_map/ppermute | solution.py:244
  2.9 8.0 %collective-permute-start.2 = (bf16[1,2,200,128]{3,2,1,0:T(8,128)(2,1)S(1)}, bf16[1,2,200,128]{3,2,1,0:T(8,128)(2,1)S(1)}, u32[]{:S(2)}, u32[]{:S(2)}) collective-permute-start(bf16[1,2,200,128]{3,2,1,0:T(8,128)(2,1)S(1)} %away_other.1.after_ref), channel_id=1, source_target_pairs={{0,0},{1,1},{2,4},{3,5},{4,2},{5,3},{6,6},{7,7},{8,8},{9,9},{10,12... | collective-permute-start | bytes 307208 | tf_op jit(solution)/shard_map/ppermute | solution.py:244
  5.3 5.7 %collective-permute-start.3 = (bf16[1,2,200,128]{3,2,1,0:T(8,128)(2,1)S(1)}, bf16[1,2,200,128]{3,2,1,0:T(8,128)(2,1)S(1)}, u32[]{:S(2)}, u32[]{:S(2)}) collective-permute-start(bf16[1,2,200,128]{3,2,1,0:T(8,128)(2,1)S(1)} %get-tuple-element.24), channel_id=1, source_target_pairs={{0,4},{4,0},{1,5},{5,1},{2,6},{6,2},{3,7},{7,3},{8,12},{12,8},{9,1... | collective-permute-start | bytes 307208 | tf_op jit(solution)/shard_map/ppermute | solution.py:235
  11.0 4.7 %collective-permute-start.6 = (bf16[1,2,200,128]{3,2,1,0:T(8,128)(2,1)S(1)}, bf16[1,2,200,128]{3,2,1,0:T(8,128)(2,1)S(1)}, u32[]{:S(2)}, u32[]{:S(2)}) collective-permute-start(bf16[1,2,200,128]{3,2,1,0:T(8,128)(2,1)S(1)} %pair_sum.1.keep_ref), channel_id=1, source_target_pairs={{0,1},{1,0},{2,3},{3,2},{4,5},{5,4},{6,7},{7,6},{8,9},{9,8},{10,11... | collective-permute-start | bytes 307208 | tf_op jit(solution)/shard_map/ppermute | solution.py:235
  11.1 8.7 %collective-permute-start.4 = (bf16[1,2,200,128]{3,2,1,0:T(8,128)(2,1)S(1)}, bf16[1,2,200,128]{3,2,1,0:T(8,128)(2,1)S(1)}, u32[]{:S(2)}, u32[]{:S(2)}) collective-permute-start(bf16[1,2,200,128]{3,2,1,0:T(8,128)(2,1)S(1)} %pair_sum.1.keep_ref), channel_id=1, source_target_pairs={{0,24},{8,16},{16,8},{24,0},{1,25},{9,17},{17,9},{25,1},{2,26},{10... | collective-permute-start | bytes 307208 | tf_op jit(solution)/shard_map/ppermute | solution.py:235
  15.9 4.7 %collective-permute-start.8 = (bf16[2,200,128]{2,1,0:T(8,128)(2,1)S(1)}, bf16[2,200,128]{2,1,0:T(8,128)(2,1)S(1)}, u32[]{:S(2)}, u32[]{:S(2)}) collective-permute-start(bf16[2,200,128]{2,1,0:T(8,128)(2,1)S(1)} %sum_norm.1.refs_0_), channel_id=1, source_target_pairs={{0,16},{8,24},{16,0},{24,8},{1,17},{9,25},{17,1},{25,9},{2,18},{10... | collective-permute-start | bytes 307208 | tf_op jit(solution)/shard_map/ppermute | solution.py:235
  17.4 5.0 %collective-permute-start.7 = (bf16[2,200,128]{2,1,0:T(8,128)(2,1)S(1)}, bf16[2,200,128]{2,1,0:T(8,128)(2,1)S(1)}, u32[]{:S(2)}, u32[]{:S(2)}) collective-permute-start(bf16[2,200,128]{2,1,0:T(8,128)(2,1)S(1)} %sum_norm.1.refs_0_), channel_id=1, source_target_pairs={{0,8},{8,0},{16,24},{24,16},{1,9},{9,1},{17,25},{25,17},{2,10},{10... | collective-permute-start | bytes 307208 | tf_op jit(solution)/shard_map/ppermute | solution.py:235
  19.8 4.7 %collective-permute-start.5 = (bf16[1,2,200,128]{3,2,1,0:T(8,128)(2,1)S(1)}, bf16[1,2,200,128]{3,2,1,0:T(8,128)(2,1)S(1)}, u32[]{:S(2)}, u32[]{:S(2)}) collective-permute-start(bf16[1,2,200,128]{3,2,1,0:T(8,128)(2,1)S(1)} %collective-permute-done.4.refs_0_), channel_id=1, source_target_pairs={{0,1},{1,0},{2,3},{3,2},{4,5},{5,4},{6,7},{7,6},{8,9},{9,8},{10,11... | collective-permute-start | bytes 307208 | tf_op jit(solution)/shard_map/ppermute | solution.py:235

commit v8 on v6

--- a/solution.py
+++ b/solution.py
@@ -15,6 +15,7 @@
 F32 = jnp.float32
 MIB = 1024 * 1024
 LIMIT = 24 * MIB
+PARTS = 4
 BF16 = jnp.bfloat16
 
 
@@ -23,14 +24,14 @@
 
 
 def call(
-    kernel, outs, n_in, name, flops=0, size=0, exps=0, in_specs=None, scratch=()
+    kernel, outs, n_in, name, flops=0, size=0, exps=0, in_specs=None, out_specs=None, scratch=()
 ):
     many = isinstance(outs, list)
     return pl.pallas_call(
         kernel,
         out_shape=outs,
         in_specs=in_specs or [VMEM] * n_in,
-        out_specs=[VMEM] * len(outs) if many else VMEM,
+        out_specs=out_specs or ([VMEM] * len(outs) if many else VMEM),
         scratch_shapes=scratch,
         compiler_params=pltpu.CompilerParams(vmem_limit_bytes=LIMIT),
         cost_estimate=pl.CostEstimate(flops=flops, bytes_accessed=size, transcendentals=exps),
@@ -80,9 +81,25 @@
 
 
 def own_kernel(head_dim, x_hbm, w_hbm, own_ref, x_ref, w_ref, sems):
-    for copy in start_copies((x_hbm, w_hbm), (x_ref, w_ref), sems):
-        copy.wait()
-    store_heads(own_ref, 0, project(x_ref[0], w_ref[...]), head_dim)
+    step = w_ref.shape[1] // PARTS
+    spans = [pl.ds(i * step, step) for i in range(PARTS)]
+    sources, targets = [x_hbm], [x_ref]
+    for span in spans:
+        sources += [w_hbm.at[0, span], w_hbm.at[1, span]]
+        targets += [w_ref.at[0, span], w_ref.at[1, span]]
+    copies = start_copies(sources, targets, sems)
+    copies[0].wait()
+    total = None
+    for i, span in enumerate(spans):
+        copies[2 * i + 1].wait()
+        copies[2 * i + 2].wait()
+        part = jnp.dot(
+            x_ref[0, :, span],
+            jnp.concatenate([w_ref[0, span], w_ref[1, span]], axis=1),
+            preferred_element_type=F32,
+        )
+        total = part if total is None else total + part
+    store_heads(own_ref, 0, total.astype(BF16), head_dim)
 
 
 def other_kernel(head_dim, x_ref, w_ref, other_ref):
@@ -209,32 +226,46 @@
         scores.append(score)
         biases.append(bias)
         top = jnp.maximum(top, jnp.max(score, axis=0, keepdims=True) + bias)
-    row_sum, mixed = 0.0, 0.0
+    all_weights = []
+    row_sum, scale = 0.0, None
     if not first:
         scale = jnp.exp(top_in[...] - top)
         row_sum = sum_in[...] * scale
-        mixed = mixed_in[...] * scale
-    for (_, values), score, bias in zip(parts, scores, biases):
+    for score, bias in zip(scores, biases):
         weights = jnp.exp(score + (bias - top))
         row_sum = row_sum + jnp.sum(weights, axis=0, keepdims=True)
-        mixed = mixed + lax.dot_general(
-            values, weights.astype(BF16), (((0,), (0,)), ((), ())), preferred_element_type=F32
-        )
+        all_weights.append(weights.astype(BF16))
+
+    def mix(columns):
+        mixed = 0.0 if first else mixed_in[:, columns] * scale[:, columns]
+        for (_, values), weights in zip(parts, all_weights):
+            mixed = mixed + lax.dot_general(
+                values, weights[:, columns], (((0,), (0,)), ((), ())), preferred_element_type=F32
+            )
+        return mixed
+
     if not last:
         top_out, sum_out, mixed_out = refs
         top_out[...] = top
         sum_out[...] = row_sum
-        mixed_out[...] = mixed
+        mixed_out[...] = mix(slice(None))
         return
-    (out,) = refs
+    out_hbm, held, sems = refs
     has_any = jnp.max(bias_ref[...], axis=0, keepdims=True) > -1.0
     inverse = jnp.where(has_any, 1.0 / jnp.where(has_any, row_sum, 1.0), 0.0)
-    context = (mixed * inverse).astype(BF16)
-    tokens = out.shape[0]
-    for head in range(out.shape[1] // head_dim):
-        out[:, head * head_dim : (head + 1) * head_dim] = context[
-            :, head * tokens : (head + 1) * tokens
-        ].T
+    tokens = held.shape[1]
+    copies = []
+    for head in range(held.shape[0]):
+        columns = slice(head * tokens, (head + 1) * tokens)
+        held[head] = (mix(columns) * inverse[:, columns]).astype(BF16).T
+        copies.append(
+            pltpu.make_async_copy(
+                held.at[head], out_hbm.at[:, pl.ds(head * head_dim, head_dim)], sems.at[head]
+            )
+        )
+        copies[-1].start()
+    for copy in copies:
+        copy.wait()
 
 
 def swap(value, axis, k):
@@ -322,7 +353,7 @@
             "away_own",
             flops=work,
             in_specs=[HBM] * 2,
-            scratch=[x_scratch, w_scratch, pltpu.SemaphoreType.DMA((2,))],
+            scratch=[x_scratch, w_scratch, pltpu.SemaphoreType.DMA((1 + 2 * PARTS,))],
         )(x, w)
         first = exchange_two_heads(away, False)
         home = call(
@@ -353,7 +384,7 @@
             "own_heads",
             flops=work,
             in_specs=[HBM] * 2,
-            scratch=[w_scratch, pltpu.SemaphoreType.DMA((2,))],
+            scratch=[w_scratch, pltpu.SemaphoreType.DMA((1 + 2 * PARTS,))],
         )(x, w)
         qt, bias, gain = call(
             query_kernel,
@@ -399,6 +430,13 @@
             "attend",
             flops=4 * pairs * rows * head_dim * parts,
             exps=pairs * rows * parts,
+            out_specs=HBM if last else None,
+            scratch=[
+                pltpu.VMEM((q_width // head_dim, tokens, head_dim), BF16),
+                pltpu.SemaphoreType.DMA((q_width // head_dim,)),
+            ]
+            if last
+            else (),
         )(gain, qt, bias, *operands, *state)
     return state
 

time: 24.3 us -> 24.5 us (level)
  no operation moved by 1% of the time
where the time goes in v8:
time: 24.5 us; the launch traced here: 24.3 us
  starting transfers between devices  15.7 us (64%)
  Pallas kernels  6.14 us (25%)
  waiting for transfers between devices  2.44 us (10%)
    ppermute x6, starting transfers between devices, swap(): lax.ppermute(value, axis, [(i, i ^ k) for i in range(lax.axis_size(axis))])  11 us
    ppermute x2, starting transfers between devices, exchange_two_heads(): return lax.ppermute(value, ('dp', 'tensor'), hops)  4.62 us
    pallas_call x3, Pallas kernels, on_device(): call(functools.partial(attend_kernel, here, there, tile_len, first, last,...  2.27 us
    ppermute x6, waiting for transfers between devices, swap(): lax.ppermute(value, axis, [(i, i ^ k) for i in range(lax.axis_size(axis))])  2.25 us
    pallas_call x1, Pallas kernels, on_device(): call(functools.partial(keep_kernel, head_dim), [product, *prepared], 8, '...  2.05 us
    pallas_call x1, Pallas kernels, on_device(): call(functools.partial(home_kernel, head_dim), product, 2, 'home_other',...  1.57 us
  transfers between devices with their start and end apart: 8, of which 5 were waited for; matrix products, arithmetic and copies ran while one was open for 0% of the time, Pallas kernels for 20%

profile of v8, /device:TPU:0, one launch (start us, length us, event | category | flops | bytes accessed | tf_op | source)
XLA Modules:
  0.0 24.3 jit_solution(8877364153302092711)
XLA Ops:
  0.0 0.5 %collective-permute-start = (bf16[2,2048,128]{2,1,0:T(8,128)(2,1)}, bf16[2,2048,128]{2,1,0:T(8,128)(2,1)S(1)}, u32[]{:S(2)}, u32[]{:S(2)}) collective-permute-start(bf16[2,2048,128]{2,1,0:T(8,128)(2,1)} %w_hbm.3), channel_id=1, source_target_pairs={{0,4},{4,0},{1,5},{5,1},{2,6},{6,2},{3,7},{7,3},{8,12},{12,8},{9,1... | collective-permute-start | bytes 3145736 | tf_op jit(solution)/shard_map/ppermute | solution.py:272
  0.5 0.1 away_own.1
  0.6 2.1 %collective-permute-start.1 = (bf16[1,2,200,128]{3,2,1,0:T(8,128)(2,1)S(1)}, bf16[1,2,200,128]{3,2,1,0:T(8,128)(2,1)S(1)}, u32[]{:S(2)}, u32[]{:S(2)}) collective-permute-start(bf16[1,2,200,128]{3,2,1,0:T(8,128)(2,1)S(1)} %away_own.1), channel_id=1, source_target_pairs={{0,4},{1,5},{2,0},{3,1},{4,6},{5,7},{6,2},{7,3},{8,12},{9,13},{10,... | collective-permute-start | bytes 307208 | tf_op jit(solution)/shard_map/ppermute | solution.py:281
  2.7 0.2 %collective-permute-done.w_other_ref = bf16[2,2048,128]{2,1,0:T(8,128)(2,1)S(1)} collective-permute-done((bf16[2,2048,128]{2,1,0:T(8,128)(2,1)}, bf16[2,2048,128]{2,1,0:T(8,128)(2,1)S(1)}, u32[]{:S(2)}, u32[]{:S(2)}) %collective-permute-start) | collective-permute-done | bytes 1048608 | tf_op jit(solution)/shard_map/ppermute | solution.py:272
  3.0 1.6 %home_other.1.after_ref = bf16[1,2,200,128]{3,2,1,0:T(8,128)(2,1)S(1)} custom-call(bf16[1,200,2048]{2,1,0:T(8,128)(2,1)} %x_hbm.5, bf16[2,2048,128]{2,1,0:T(8,128)(2,1)S(1)} %collective-permute-done.w_other_ref), custom_call_target="tpu_custom_call" | custom-call | flops 209715200 | tf_op jit(solution)/shard_map/home_other/pallas_call | solution.py:359
  4.5 2.5 %collective-permute-start.2 = (bf16[1,2,200,128]{3,2,1,0:T(8,128)(2,1)S(1)}, bf16[1,2,200,128]{3,2,1,0:T(8,128)(2,1)S(1)}, u32[]{:S(2)}, u32[]{:S(2)}) collective-permute-start(bf16[1,2,200,128]{3,2,1,0:T(8,128)(2,1)S(1)} %home_other.1.after_ref), channel_id=1, source_target_pairs={{0,2},{1,3},{2,6},{3,7},{4,0},{5,1},{6,4},{7,5},{8,10},{9,11},{10,... | collective-permute-start | bytes 307208 | tf_op jit(solution)/shard_map/ppermute | solution.py:281
  7.0 2.0 %keep_queries.1 = (bf16[1,2,200,128]{3,2,1,0:T(8,128)(2,1)S(1)}, bf16[128,512]{1,0:T(8,128)(2,1)S(1)}, f32[4,512]{1,0:T(4,128)S(1)}, f32[1,128]{1,0:T(1,128)S(1)}) custom-call(bf16[1,2,200,128]{3,2,1,0:T(8,128)(2,1)S(1)} %home_other.1.after_ref, bf16[2,2048,128]{2,1,0:T(8,128)(2,1)S(1)} %collective-permute-done.w_other_ref, bf16[1,200,2048]{2,1,0:T(8,128)(2,1)} %x_hbm.5, ...), custom_call_target="tpu_custom_call" | custom-call | flops 209715200 | tf_op jit(solution)/shard_map/keep_queries/pallas_call | solution.py:369
  9.1 0.0 collective-permute-done.1.first_ref
  9.1 0.2 collective-permute-done.2.second_ref
  9.3 2.6 %collective-permute-start.5 = (bf16[1,2,200,128]{3,2,1,0:T(8,128)(2,1)S(1)}, bf16[1,2,200,128]{3,2,1,0:T(8,128)(2,1)S(1)}, u32[]{:S(2)}, u32[]{:S(2)}) collective-permute-start(bf16[1,2,200,128]{3,2,1,0:T(8,128)(2,1)S(1)} %pair_sum.1.keep_ref), channel_id=1, source_target_pairs={{0,1},{1,0},{2,3},{3,2},{4,5},{5,4},{6,7},{7,6},{8,9},{9,8},{10,11... | collective-permute-start | bytes 307208 | tf_op jit(solution)/shard_map/ppermute | solution.py:272
  11.9 2.5 %collective-permute-start.3 = (bf16[1,2,200,128]{3,2,1,0:T(8,128)(2,1)S(1)}, bf16[1,2,200,128]{3,2,1,0:T(8,128)(2,1)S(1)}, u32[]{:S(2)}, u32[]{:S(2)}) collective-permute-start(bf16[1,2,200,128]{3,2,1,0:T(8,128)(2,1)S(1)} %pair_sum.1.keep_ref), channel_id=1, source_target_pairs={{0,24},{8,16},{16,8},{24,0},{1,25},{9,17},{17,9},{25,1},{2,26},{10... | collective-permute-start | bytes 307208 | tf_op jit(solution)/shard_map/ppermute | solution.py:272
  14.3 0.4 %collective-permute-done.5.arrived_ref = bf16[1,2,200,128]{3,2,1,0:T(8,128)(2,1)S(1)} collective-permute-done((bf16[1,2,200,128]{3,2,1,0:T(8,128)(2,1)S(1)}, bf16[1,2,200,128]{3,2,1,0:T(8,128)(2,1)S(1)}, u32[]{:S(2)}, u32[]{:S(2)}) %collective-permute-start.5) | collective-permute-done | bytes 102432 | tf_op jit(solution)/shard_map/ppermute | solution.py:272
  14.7 0.1 sum_norm.1.refs_0_
  14.8 1.6 %collective-permute-start.6 = (bf16[2,200,128]{2,1,0:T(8,128)(2,1)S(1)}, bf16[2,200,128]{2,1,0:T(8,128)(2,1)S(1)}, u32[]{:S(2)}, u32[]{:S(2)}) collective-permute-start(bf16[2,200,128]{2,1,0:T(8,128)(2,1)S(1)} %sum_norm.1.refs_0_), channel_id=1, source_target_pairs={{0,8},{8,0},{16,24},{24,16},{1,9},{9,1},{17,25},{25,17},{2,10},{10... | collective-permute-start | bytes 307208 | tf_op jit(solution)/shard_map/ppermute | solution.py:272
  16.4 1.5 %collective-permute-start.7 = (bf16[2,200,128]{2,1,0:T(8,128)(2,1)S(1)}, bf16[2,200,128]{2,1,0:T(8,128)(2,1)S(1)}, u32[]{:S(2)}, u32[]{:S(2)}) collective-permute-start(bf16[2,200,128]{2,1,0:T(8,128)(2,1)S(1)} %sum_norm.1.refs_0_), channel_id=1, source_target_pairs={{0,16},{8,24},{16,0},{24,8},{1,17},{9,25},{17,1},{25,9},{2,18},{10... | collective-permute-start | bytes 307208 | tf_op jit(solution)/shard_map/ppermute | solution.py:272
  17.9 0.0 collective-permute-done.3.refs_0_
  17.9 2.5 %collective-permute-start.4 = (bf16[1,2,200,128]{3,2,1,0:T(8,128)(2,1)S(1)}, bf16[1,2,200,128]{3,2,1,0:T(8,128)(2,1)S(1)}, u32[]{:S(2)}, u32[]{:S(2)}) collective-permute-start(bf16[1,2,200,128]{3,2,1,0:T(8,128)(2,1)S(1)} %collective-permute-done.3.refs_0_), channel_id=1, source_target_pairs={{0,1},{1,0},{2,3},{3,2},{4,5},{5,4},{6,7},{7,6},{8,9},{9,8},{10,11... | collective-permute-start | bytes 307208 | tf_op jit(solution)/shard_map/ppermute | solution.py:272
  20.4 0.4 %attend.3 = (f32[1,512]{1,0:T(1,128)S(1)}, f32[1,512]{1,0:T(1,128)S(1)}, f32[128,512]{1,0:T(8,128)S(1)}) custom-call(f32[1,128]{1,0:T(1,128)S(1)} %get-tuple-element.15.k_gain_ref, bf16[128,512]{1,0:T(8,128)(2,1)S(1)} %get-tuple-element.16.qt_ref, f32[4,512]{1,0:T(4,128)S(1)} %get-tuple-element.17.bias_ref, bf16[2,200,128]{2,1,0:T(8,128)(2,1)S(1)} %sum_norm.1.refs_0_), custom_call_target="tpu_custom_call" | custom-call | flops 52428800 | tf_op jit(solution)/shard_map/attend/pallas_call | solution.py:426
  20.8 0.0 collective-permute-done.6.refs_0_
  20.8 1.0 %collective-permute-done.7.refs_1_ = bf16[2,200,128]{2,1,0:T(8,128)(2,1)S(1)} collective-permute-done((bf16[2,200,128]{2,1,0:T(8,128)(2,1)S(1)}, bf16[2,200,128]{2,1,0:T(8,128)(2,1)S(1)}, u32[]{:S(2)}, u32[]{:S(2)}) %collective-permute-start.7) | collective-permute-done | bytes 102432 | tf_op jit(solution)/shard_map/ppermute | solution.py:272
  21.8 0.6 %attend.4 = (f32[1,512]{1,0:T(1,128)S(1)}, f32[1,512]{1,0:T(1,128)S(1)}, f32[128,512]{1,0:T(8,128)S(1)}) custom-call(f32[1,128]{1,0:T(1,128)S(1)} %get-tuple-element.15.k_gain_ref, bf16[128,512]{1,0:T(8,128)(2,1)S(1)} %get-tuple-element.16.qt_ref, f32[4,512]{1,0:T(4,128)S(1)} %get-tuple-element.17.bias_ref, ...), custom_call_target="tpu_custom_call" | custom-call | flops 104857600 | tf_op jit(solution)/shard_map/attend/pallas_call | solution.py:426
  22.4 0.7 %collective-permute-done.4.refs_1_ = bf16[1,2,200,128]{3,2,1,0:T(8,128)(2,1)S(1)} collective-permute-done((bf16[1,2,200,128]{3,2,1,0:T(8,128)(2,1)S(1)}, bf16[1,2,200,128]{3,2,1,0:T(8,128)(2,1)S(1)}, u32[]{:S(2)}, u32[]{:S(2)}) %collective-permute-start.4) | collective-permute-done | bytes 102432 | tf_op jit(solution)/shard_map/ppermute | solution.py:272
  23.0 1.3 %attend.5 = bf16[128,512]{1,0:T(8,128)(2,1)} custom-call(f32[1,128]{1,0:T(1,128)S(1)} %get-tuple-element.15.k_gain_ref, bf16[128,512]{1,0:T(8,128)(2,1)S(1)} %get-tuple-element.16.qt_ref, f32[4,512]{1,0:T(4,128)S(1)} %get-tuple-element.17.bias_ref, bf16[1,2,200,128]{3,2,1,0:T(8,128)(2,1)S(1)} %collective-permute-done.3.refs_0_, ...), custom_call_target="tpu_custom_call" | custom-call | flops 52428800 | tf_op jit(solution)/shard_map/attend/pallas_call | solution.py:426
  (1 shorter events, 0.0 us)
Async XLA Ops:
  0.0 3.0 %collective-permute-start = (bf16[2,2048,128]{2,1,0:T(8,128)(2,1)}, bf16[2,2048,128]{2,1,0:T(8,128)(2,1)S(1)}, u32[]{:S(2)}, u32[]{:S(2)}) collective-permute-start(bf16[2,2048,128]{2,1,0:T(8,128)(2,1)} %w_hbm.3), channel_id=1, source_target_pairs={{0,4},{4,0},{1,5},{5,1},{2,6},{6,2},{3,7},{7,3},{8,12},{12,8},{9,1... | collective-permute-start | bytes 3145736 | tf_op jit(solution)/shard_map/ppermute | solution.py:272
  0.6 8.5 %collective-permute-start.1 = (bf16[1,2,200,128]{3,2,1,0:T(8,128)(2,1)S(1)}, bf16[1,2,200,128]{3,2,1,0:T(8,128)(2,1)S(1)}, u32[]{:S(2)}, u32[]{:S(2)}) collective-permute-start(bf16[1,2,200,128]{3,2,1,0:T(8,128)(2,1)S(1)} %away_own.1), channel_id=1, source_target_pairs={{0,4},{1,5},{2,0},{3,1},{4,6},{5,7},{6,2},{7,3},{8,12},{9,13},{10,... | collective-permute-start | bytes 307208 | tf_op jit(solution)/shard_map/ppermute | solution.py:281
  4.5 4.7 %collective-permute-start.2 = (bf16[1,2,200,128]{3,2,1,0:T(8,128)(2,1)S(1)}, bf16[1,2,200,128]{3,2,1,0:T(8,128)(2,1)S(1)}, u32[]{:S(2)}, u32[]{:S(2)}) collective-permute-start(bf16[1,2,200,128]{3,2,1,0:T(8,128)(2,1)S(1)} %home_other.1.after_ref), channel_id=1, source_target_pairs={{0,2},{1,3},{2,6},{3,7},{4,0},{5,1},{6,4},{7,5},{8,10},{9,11},{10,... | collective-permute-start | bytes 307208 | tf_op jit(solution)/shard_map/ppermute | solution.py:281
  9.3 5.4 %collective-permute-start.5 = (bf16[1,2,200,128]{3,2,1,0:T(8,128)(2,1)S(1)}, bf16[1,2,200,128]{3,2,1,0:T(8,128)(2,1)S(1)}, u32[]{:S(2)}, u32[]{:S(2)}) collective-permute-start(bf16[1,2,200,128]{3,2,1,0:T(8,128)(2,1)S(1)} %pair_sum.1.keep_ref), channel_id=1, source_target_pairs={{0,1},{1,0},{2,3},{3,2},{4,5},{5,4},{6,7},{7,6},{8,9},{9,8},{10,11... | collective-permute-start | bytes 307208 | tf_op jit(solution)/shard_map/ppermute | solution.py:272
  11.9 6.0 %collective-permute-start.3 = (bf16[1,2,200,128]{3,2,1,0:T(8,128)(2,1)S(1)}, bf16[1,2,200,128]{3,2,1,0:T(8,128)(2,1)S(1)}, u32[]{:S(2)}, u32[]{:S(2)}) collective-permute-start(bf16[1,2,200,128]{3,2,1,0:T(8,128)(2,1)S(1)} %pair_sum.1.keep_ref), channel_id=1, source_target_pairs={{0,24},{8,16},{16,8},{24,0},{1,25},{9,17},{17,9},{25,1},{2,26},{10... | collective-permute-start | bytes 307208 | tf_op jit(solution)/shard_map/ppermute | solution.py:272
  14.8 6.0 %collective-permute-start.6 = (bf16[2,200,128]{2,1,0:T(8,128)(2,1)S(1)}, bf16[2,200,128]{2,1,0:T(8,128)(2,1)S(1)}, u32[]{:S(2)}, u32[]{:S(2)}) collective-permute-start(bf16[2,200,128]{2,1,0:T(8,128)(2,1)S(1)} %sum_norm.1.refs_0_), channel_id=1, source_target_pairs={{0,8},{8,0},{16,24},{24,16},{1,9},{9,1},{17,25},{25,17},{2,10},{10... | collective-permute-start | bytes 307208 | tf_op jit(solution)/shard_map/ppermute | solution.py:272
  16.4 5.4 %collective-permute-start.7 = (bf16[2,200,128]{2,1,0:T(8,128)(2,1)S(1)}, bf16[2,200,128]{2,1,0:T(8,128)(2,1)S(1)}, u32[]{:S(2)}, u32[]{:S(2)}) collective-permute-start(bf16[2,200,128]{2,1,0:T(8,128)(2,1)S(1)} %sum_norm.1.refs_0_), channel_id=1, source_target_pairs={{0,16},{8,24},{16,0},{24,8},{1,17},{9,25},{17,1},{25,9},{2,18},{10... | collective-permute-start | bytes 307208 | tf_op jit(solution)/shard_map/ppermute | solution.py:272
  17.9 5.1 %collective-permute-start.4 = (bf16[1,2,200,128]{3,2,1,0:T(8,128)(2,1)S(1)}, bf16[1,2,200,128]{3,2,1,0:T(8,128)(2,1)S(1)}, u32[]{:S(2)}, u32[]{:S(2)}) collective-permute-start(bf16[1,2,200,128]{3,2,1,0:T(8,128)(2,1)S(1)} %collective-permute-done.3.refs_0_), channel_id=1, source_target_pairs={{0,1},{1,0},{2,3},{3,2},{4,5},{5,4},{6,7},{7,6},{8,9},{9,8},{10,11... | collective-permute-start | bytes 307208 | tf_op jit(solution)/shard_map/ppermute | solution.py:272

commit v9 on v6

--- a/solution.py
+++ b/solution.py
@@ -23,7 +23,7 @@
 
 
 def call(
-    kernel, outs, n_in, name, flops=0, size=0, exps=0, in_specs=None, scratch=()
+    kernel, outs, n_in, name, flops=0, size=0, exps=0, in_specs=None, scratch=(), aliases=None
 ):
     many = isinstance(outs, list)
     return pl.pallas_call(
@@ -32,6 +32,7 @@
         in_specs=in_specs or [VMEM] * n_in,
         out_specs=[VMEM] * len(outs) if many else VMEM,
         scratch_shapes=scratch,
+        input_output_aliases=aliases or {},
         compiler_params=pltpu.CompilerParams(vmem_limit_bytes=LIMIT),
         cost_estimate=pl.CostEstimate(flops=flops, bytes_accessed=size, transcendentals=exps),
         name=name,
@@ -129,11 +130,15 @@
     head_dim, after_ref, w_other_ref, x_hbm, w_hbm, q_hbm, q_gain_hbm, mask_hbm, k_gain_hbm,
     keep_ref, qt_ref, bias_ref, k_gain_ref, x_ref, w_ref, q_ref, q_gain_ref, mask_ref, sems,
 ):
-    copies = start_copies(
-        (q_hbm, q_gain_hbm, mask_hbm, k_gain_hbm), (q_ref, q_gain_ref, mask_ref, k_gain_ref), sems
-    )
-    moves = start_copies((x_hbm, w_hbm), (x_ref, w_ref), sems, len(copies))
-    prepare_queries(copies, q_ref, q_gain_ref, mask_ref, qt_ref, bias_ref)
+    moves = start_copies((x_hbm, w_hbm), (x_ref, w_ref), sems, 4)
+
+    @pl.when(is_first_core())
+    def _():
+        query_kernel(
+            q_hbm, q_gain_hbm, mask_hbm, k_gain_hbm, qt_ref, bias_ref, k_gain_ref,
+            q_ref, q_gain_ref, mask_ref, sems,
+        )
+
     for copy in moves:
         copy.wait()
 
@@ -163,9 +168,23 @@
     split_half(held, send_ref, keep_ref, (1 - upper) * half, upper * half)
 
 
-def pair_kernel(keep_ref, first_ref, second_ref, out_ref):
+def is_first_core():
+    return lax.axis_index("dp") == 0
+
+
+def pair_kernel(
+    keep_ref, first_ref, second_ref, qt_in, bias_in, k_gain_in, q_hbm, q_gain_hbm, mask_hbm, k_gain_hbm,
+    out_ref, qt_ref, bias_ref, k_gain_ref, q_ref, q_gain_ref, mask_ref, sems,
+):
     arrived = jnp.where(is_home(), first_ref[...], second_ref[...]).astype(F32)
     out_ref[...] = (keep_ref[...].astype(F32) + arrived).astype(BF16)
+
+    @pl.when(jnp.logical_not(is_first_core()))
+    def _():
+        query_kernel(
+            q_hbm, q_gain_hbm, mask_hbm, k_gain_hbm, qt_ref, bias_ref, k_gain_ref,
+            q_ref, q_gain_ref, mask_ref, sems,
+        )
 
 
 def add_kernel(bit, keep_ref, arrived_ref, send_ref, next_ref, held):
@@ -344,7 +363,15 @@
             in_specs=[VMEM] * 2 + [HBM] * 6,
             scratch=[x_scratch, w_scratch, *query_scratch, pltpu.SemaphoreType.DMA((6,))],
         )(home, others[0], x, w, *small)
-        total = call(pair_kernel, product, 3, "pair_sum")(keep, first, second)
+        total, qt, bias, gain = call(
+            pair_kernel,
+            [product, *prepared],
+            10,
+            "pair_sum",
+            in_specs=[VMEM] * 6 + [HBM] * 4,
+            scratch=[*query_scratch, pltpu.SemaphoreType.DMA((4,))],
+            aliases={3: 1, 4: 2, 5: 3},
+        )(keep, first, second, qt, bias, gain, *small)
     else:
         own, x_here = call(
             functools.partial(own_kernel, head_dim),

time: 24.3 us -> 25.2 us (1.037)
  waiting for transfers between devices: 2.49 us -> 3.67 us
  starting transfers between devices: 15.5 us -> 14.9 us
    ppermute x6, waiting for transfers between devices: 2.3 us -> 3.66 us  [swap(): lax.ppermute(value, axis, [(i, i ^ k) for i in range(lax.axis_size(axis))])]
    ppermute x6, starting transfers between devices: 11 us -> 10.5 us  [swap(): lax.ppermute(value, axis, [(i, i ^ k) for i in range(lax.axis_size(axis))])]
where the time goes in v9:
time: 25.2 us; the launch traced here: 25 us
  starting transfers between devices  14.9 us (59%)
  Pallas kernels  6.33 us (25%)
  waiting for transfers between devices  3.67 us (15%)
    ppermute x6, starting transfers between devices, swap(): lax.ppermute(value, axis, [(i, i ^ k) for i in range(lax.axis_size(axis))])  10.5 us
    ppermute x2, starting transfers between devices, exchange_two_heads(): return lax.ppermute(value, ('dp', 'tensor'), hops)  4.45 us
    ppermute x6, waiting for transfers between devices, swap(): lax.ppermute(value, axis, [(i, i ^ k) for i in range(lax.axis_size(axis))])  3.66 us
    pallas_call x3, Pallas kernels, on_device(): call(functools.partial(attend_kernel, here, there, tile_len, first, last,...  2.26 us
    pallas_call x1, Pallas kernels, on_device(): call(functools.partial(keep_kernel, head_dim), [product, *prepared], 8, '...  2.26 us
    pallas_call x1, Pallas kernels, on_device(): call(functools.partial(home_kernel, head_dim), product, 2, 'home_other',...  1.57 us
  transfers between devices with their start and end apart: 8, of which 5 were waited for; matrix products, arithmetic and copies ran while one was open for 0% of the time, Pallas kernels for 20%

profile of v9, /device:TPU:0, one launch (start us, length us, event | category | flops | bytes accessed | tf_op | source)
XLA Modules:
  0.0 25.0 jit_solution(12903986338234302029)
XLA Ops:
  0.0 0.5 %collective-permute-start = (bf16[2,2048,128]{2,1,0:T(8,128)(2,1)}, bf16[2,2048,128]{2,1,0:T(8,128)(2,1)S(1)}, u32[]{:S(2)}, u32[]{:S(2)}) collective-permute-start(bf16[2,2048,128]{2,1,0:T(8,128)(2,1)} %w_hbm.3), channel_id=1, source_target_pairs={{0,4},{4,0},{1,5},{5,1},{2,6},{6,2},{3,7},{7,3},{8,12},{12,8},{9,1... | collective-permute-start | bytes 3145736 | tf_op jit(solution)/shard_map/ppermute | solution.py:260
  0.5 2.0 %collective-permute-start.1 = (bf16[1,2,200,128]{3,2,1,0:T(8,128)(2,1)S(1)}, bf16[1,2,200,128]{3,2,1,0:T(8,128)(2,1)S(1)}, u32[]{:S(2)}, u32[]{:S(2)}) collective-permute-start(bf16[1,2,200,128]{3,2,1,0:T(8,128)(2,1)S(1)} %away_own.1), channel_id=1, source_target_pairs={{0,4},{1,5},{2,0},{3,1},{4,6},{5,7},{6,2},{7,3},{8,12},{9,13},{10,... | collective-permute-start | bytes 307208 | tf_op jit(solution)/shard_map/ppermute | solution.py:269
  2.5 0.5 %collective-permute-done.w_other_ref = bf16[2,2048,128]{2,1,0:T(8,128)(2,1)S(1)} collective-permute-done((bf16[2,2048,128]{2,1,0:T(8,128)(2,1)}, bf16[2,2048,128]{2,1,0:T(8,128)(2,1)S(1)}, u32[]{:S(2)}, u32[]{:S(2)}) %collective-permute-start) | collective-permute-done | bytes 1048608 | tf_op jit(solution)/shard_map/ppermute | solution.py:260
  3.0 1.6 %home_other.1.after_ref = bf16[1,2,200,128]{3,2,1,0:T(8,128)(2,1)S(1)} custom-call(bf16[1,200,2048]{2,1,0:T(8,128)(2,1)} %x_hbm.5, bf16[2,2048,128]{2,1,0:T(8,128)(2,1)S(1)} %collective-permute-done.w_other_ref), custom_call_target="tpu_custom_call" | custom-call | flops 209715200 | tf_op jit(solution)/shard_map/home_other/pallas_call | solution.py:347
  4.5 2.5 %collective-permute-start.2 = (bf16[1,2,200,128]{3,2,1,0:T(8,128)(2,1)S(1)}, bf16[1,2,200,128]{3,2,1,0:T(8,128)(2,1)S(1)}, u32[]{:S(2)}, u32[]{:S(2)}) collective-permute-start(bf16[1,2,200,128]{3,2,1,0:T(8,128)(2,1)S(1)} %home_other.1.after_ref), channel_id=1, source_target_pairs={{0,2},{1,3},{2,6},{3,7},{4,0},{5,1},{6,4},{7,5},{8,10},{9,11},{10,... | collective-permute-start | bytes 307208 | tf_op jit(solution)/shard_map/ppermute | solution.py:269
  7.0 2.3 %keep_queries.1 = (bf16[1,2,200,128]{3,2,1,0:T(8,128)(2,1)S(1)}, bf16[128,512]{1,0:T(8,128)(2,1)S(1)}, f32[4,512]{1,0:T(4,128)S(1)}, f32[1,128]{1,0:T(1,128)S(1)}) custom-call(bf16[1,2,200,128]{3,2,1,0:T(8,128)(2,1)S(1)} %home_other.1.after_ref, bf16[2,2048,128]{2,1,0:T(8,128)(2,1)S(1)} %collective-permute-done.w_other_ref, bf16[1,200,2048]{2,1,0:T(8,128)(2,1)} %x_hbm.5, ...), custom_call_target="tpu_custom_call" | custom-call | flops 209715200 | tf_op jit(solution)/shard_map/keep_queries/pallas_call | solution.py:357
  9.3 0.0 collective-permute-done.1.first_ref
  9.3 0.0 collective-permute-done.2.second_ref
  9.3 0.1 pair_sum.1
  9.4 2.5 %collective-permute-start.5 = (bf16[1,2,200,128]{3,2,1,0:T(8,128)(2,1)S(1)}, bf16[1,2,200,128]{3,2,1,0:T(8,128)(2,1)S(1)}, u32[]{:S(2)}, u32[]{:S(2)}) collective-permute-start(bf16[1,2,200,128]{3,2,1,0:T(8,128)(2,1)S(1)} %get-tuple-element.26.keep_ref), channel_id=1, source_target_pairs={{0,1},{1,0},{2,3},{3,2},{4,5},{5,4},{6,7},{7,6},{8,9},{9,8},{10,11... | collective-permute-start | bytes 307208 | tf_op jit(solution)/shard_map/ppermute | solution.py:260
  11.9 2.4 %collective-permute-start.3 = (bf16[1,2,200,128]{3,2,1,0:T(8,128)(2,1)S(1)}, bf16[1,2,200,128]{3,2,1,0:T(8,128)(2,1)S(1)}, u32[]{:S(2)}, u32[]{:S(2)}) collective-permute-start(bf16[1,2,200,128]{3,2,1,0:T(8,128)(2,1)S(1)} %get-tuple-element.26.keep_ref), channel_id=1, source_target_pairs={{0,24},{8,16},{16,8},{24,0},{1,25},{9,17},{17,9},{25,1},{2,26},{10... | collective-permute-start | bytes 307208 | tf_op jit(solution)/shard_map/ppermute | solution.py:260
  14.3 0.2 collective-permute-done.5.arrived_ref
  14.6 0.1 sum_norm.1.refs_0_
  14.7 1.6 %collective-permute-start.6 = (bf16[2,200,128]{2,1,0:T(8,128)(2,1)S(1)}, bf16[2,200,128]{2,1,0:T(8,128)(2,1)S(1)}, u32[]{:S(2)}, u32[]{:S(2)}) collective-permute-start(bf16[2,200,128]{2,1,0:T(8,128)(2,1)S(1)} %sum_norm.1.refs_0_), channel_id=1, source_target_pairs={{0,8},{8,0},{16,24},{24,16},{1,9},{9,1},{17,25},{25,17},{2,10},{10... | collective-permute-start | bytes 307208 | tf_op jit(solution)/shard_map/ppermute | solution.py:260
  16.2 1.5 %collective-permute-start.7 = (bf16[2,200,128]{2,1,0:T(8,128)(2,1)S(1)}, bf16[2,200,128]{2,1,0:T(8,128)(2,1)S(1)}, u32[]{:S(2)}, u32[]{:S(2)}) collective-permute-start(bf16[2,200,128]{2,1,0:T(8,128)(2,1)S(1)} %sum_norm.1.refs_0_), channel_id=1, source_target_pairs={{0,16},{8,24},{16,0},{24,8},{1,17},{9,25},{17,1},{25,9},{2,18},{10... | collective-permute-start | bytes 307208 | tf_op jit(solution)/shard_map/ppermute | solution.py:260
  17.7 0.5 %collective-permute-done.3.refs_0_ = bf16[1,2,200,128]{3,2,1,0:T(8,128)(2,1)S(1)} collective-permute-done((bf16[1,2,200,128]{3,2,1,0:T(8,128)(2,1)S(1)}, bf16[1,2,200,128]{3,2,1,0:T(8,128)(2,1)S(1)}, u32[]{:S(2)}, u32[]{:S(2)}) %collective-permute-start.3) | collective-permute-done | bytes 102432 | tf_op jit(solution)/shard_map/ppermute | solution.py:260
  18.3 2.0 %collective-permute-start.4 = (bf16[1,2,200,128]{3,2,1,0:T(8,128)(2,1)S(1)}, bf16[1,2,200,128]{3,2,1,0:T(8,128)(2,1)S(1)}, u32[]{:S(2)}, u32[]{:S(2)}) collective-permute-start(bf16[1,2,200,128]{3,2,1,0:T(8,128)(2,1)S(1)} %collective-permute-done.3.refs_0_), channel_id=1, source_target_pairs={{0,1},{1,0},{2,3},{3,2},{4,5},{5,4},{6,7},{7,6},{8,9},{9,8},{10,11... | collective-permute-start | bytes 307208 | tf_op jit(solution)/shard_map/ppermute | solution.py:260
  20.2 0.4 %attend.3 = (f32[1,512]{1,0:T(1,128)S(1)}, f32[1,512]{1,0:T(1,128)S(1)}, f32[128,512]{1,0:T(8,128)S(1)}) custom-call(f32[1,128]{1,0:T(1,128)S(1)} %get-tuple-element.23.k_gain_ref, bf16[128,512]{1,0:T(8,128)(2,1)S(1)} %get-tuple-element.24.qt_ref, f32[4,512]{1,0:T(4,128)S(1)} %get-tuple-element.25.bias_ref, bf16[2,200,128]{2,1,0:T(8,128)(2,1)S(1)} %sum_norm.1.refs_0_), custom_call_target="tpu_custom_call" | custom-call | flops 52428800 | tf_op jit(solution)/shard_map/attend/pallas_call | solution.py:422
  20.7 0.0 collective-permute-done.6.refs_0_
  20.7 0.2 collective-permute-done.7.refs_1_
  20.9 0.6 %attend.4 = (f32[1,512]{1,0:T(1,128)S(1)}, f32[1,512]{1,0:T(1,128)S(1)}, f32[128,512]{1,0:T(8,128)S(1)}) custom-call(f32[1,128]{1,0:T(1,128)S(1)} %get-tuple-element.23.k_gain_ref, bf16[128,512]{1,0:T(8,128)(2,1)S(1)} %get-tuple-element.24.qt_ref, f32[4,512]{1,0:T(4,128)S(1)} %get-tuple-element.25.bias_ref, ...), custom_call_target="tpu_custom_call" | custom-call | flops 104857600 | tf_op jit(solution)/shard_map/attend/pallas_call | solution.py:422
  21.5 2.2 %collective-permute-done.4.refs_1_ = bf16[1,2,200,128]{3,2,1,0:T(8,128)(2,1)S(1)} collective-permute-done((bf16[1,2,200,128]{3,2,1,0:T(8,128)(2,1)S(1)}, bf16[1,2,200,128]{3,2,1,0:T(8,128)(2,1)S(1)}, u32[]{:S(2)}, u32[]{:S(2)}) %collective-permute-start.4) | collective-permute-done | bytes 102432 | tf_op jit(solution)/shard_map/ppermute | solution.py:260
  23.7 1.3 %attend.5 = bf16[128,512]{1,0:T(8,128)(2,1)} custom-call(f32[1,128]{1,0:T(1,128)S(1)} %get-tuple-element.23.k_gain_ref, bf16[128,512]{1,0:T(8,128)(2,1)S(1)} %get-tuple-element.24.qt_ref, f32[4,512]{1,0:T(4,128)S(1)} %get-tuple-element.25.bias_ref, bf16[1,2,200,128]{3,2,1,0:T(8,128)(2,1)S(1)} %collective-permute-done.3.refs_0_, ...), custom_call_target="tpu_custom_call" | custom-call | flops 52428800 | tf_op jit(solution)/shard_map/attend/pallas_call | solution.py:422
  (1 shorter events, 0.0 us)
Async XLA Ops:
  0.0 3.0 %collective-permute-start = (bf16[2,2048,128]{2,1,0:T(8,128)(2,1)}, bf16[2,2048,128]{2,1,0:T(8,128)(2,1)S(1)}, u32[]{:S(2)}, u32[]{:S(2)}) collective-permute-start(bf16[2,2048,128]{2,1,0:T(8,128)(2,1)} %w_hbm.3), channel_id=1, source_target_pairs={{0,4},{4,0},{1,5},{5,1},{2,6},{6,2},{3,7},{7,3},{8,12},{12,8},{9,1... | collective-permute-start | bytes 3145736 | tf_op jit(solution)/shard_map/ppermute | solution.py:260
  0.5 8.8 %collective-permute-start.1 = (bf16[1,2,200,128]{3,2,1,0:T(8,128)(2,1)S(1)}, bf16[1,2,200,128]{3,2,1,0:T(8,128)(2,1)S(1)}, u32[]{:S(2)}, u32[]{:S(2)}) collective-permute-start(bf16[1,2,200,128]{3,2,1,0:T(8,128)(2,1)S(1)} %away_own.1), channel_id=1, source_target_pairs={{0,4},{1,5},{2,0},{3,1},{4,6},{5,7},{6,2},{7,3},{8,12},{9,13},{10,... | collective-permute-start | bytes 307208 | tf_op jit(solution)/shard_map/ppermute | solution.py:269
  4.5 4.8 %collective-permute-start.2 = (bf16[1,2,200,128]{3,2,1,0:T(8,128)(2,1)S(1)}, bf16[1,2,200,128]{3,2,1,0:T(8,128)(2,1)S(1)}, u32[]{:S(2)}, u32[]{:S(2)}) collective-permute-start(bf16[1,2,200,128]{3,2,1,0:T(8,128)(2,1)S(1)} %home_other.1.after_ref), channel_id=1, source_target_pairs={{0,2},{1,3},{2,6},{3,7},{4,0},{5,1},{6,4},{7,5},{8,10},{9,11},{10,... | collective-permute-start | bytes 307208 | tf_op jit(solution)/shard_map/ppermute | solution.py:269
  9.4 5.2 %collective-permute-start.5 = (bf16[1,2,200,128]{3,2,1,0:T(8,128)(2,1)S(1)}, bf16[1,2,200,128]{3,2,1,0:T(8,128)(2,1)S(1)}, u32[]{:S(2)}, u32[]{:S(2)}) collective-permute-start(bf16[1,2,200,128]{3,2,1,0:T(8,128)(2,1)S(1)} %get-tuple-element.26.keep_ref), channel_id=1, source_target_pairs={{0,1},{1,0},{2,3},{3,2},{4,5},{5,4},{6,7},{7,6},{8,9},{9,8},{10,11... | collective-permute-start | bytes 307208 | tf_op jit(solution)/shard_map/ppermute | solution.py:260
  11.9 6.4 %collective-permute-start.3 = (bf16[1,2,200,128]{3,2,1,0:T(8,128)(2,1)S(1)}, bf16[1,2,200,128]{3,2,1,0:T(8,128)(2,1)S(1)}, u32[]{:S(2)}, u32[]{:S(2)}) collective-permute-start(bf16[1,2,200,128]{3,2,1,0:T(8,128)(2,1)S(1)} %get-tuple-element.26.keep_ref), channel_id=1, source_target_pairs={{0,24},{8,16},{16,8},{24,0},{1,25},{9,17},{17,9},{25,1},{2,26},{10... | collective-permute-start | bytes 307208 | tf_op jit(solution)/shard_map/ppermute | solution.py:260
  14.7 6.0 %collective-permute-start.6 = (bf16[2,200,128]{2,1,0:T(8,128)(2,1)S(1)}, bf16[2,200,128]{2,1,0:T(8,128)(2,1)S(1)}, u32[]{:S(2)}, u32[]{:S(2)}) collective-permute-start(bf16[2,200,128]{2,1,0:T(8,128)(2,1)S(1)} %sum_norm.1.refs_0_), channel_id=1, source_target_pairs={{0,8},{8,0},{16,24},{24,16},{1,9},{9,1},{17,25},{25,17},{2,10},{10... | collective-permute-start | bytes 307208 | tf_op jit(solution)/shard_map/ppermute | solution.py:260
  16.2 4.7 %collective-permute-start.7 = (bf16[2,200,128]{2,1,0:T(8,128)(2,1)S(1)}, bf16[2,200,128]{2,1,0:T(8,128)(2,1)S(1)}, u32[]{:S(2)}, u32[]{:S(2)}) collective-permute-start(bf16[2,200,128]{2,1,0:T(8,128)(2,1)S(1)} %sum_norm.1.refs_0_), channel_id=1, source_target_pairs={{0,16},{8,24},{16,0},{24,8},{1,17},{9,25},{17,1},{25,9},{2,18},{10... | collective-permute-start | bytes 307208 | tf_op jit(solution)/shard_map/ppermute | solution.py:260
  18.3 5.5 %collective-permute-start.4 = (bf16[1,2,200,128]{3,2,1,0:T(8,128)(2,1)S(1)}, bf16[1,2,200,128]{3,2,1,0:T(8,128)(2,1)S(1)}, u32[]{:S(2)}, u32[]{:S(2)}) collective-permute-start(bf16[1,2,200,128]{3,2,1,0:T(8,128)(2,1)S(1)} %collective-permute-done.3.refs_0_), channel_id=1, source_target_pairs={{0,1},{1,0},{2,3},{3,2},{4,5},{5,4},{6,7},{7,6},{8,9},{9,8},{10,11... | collective-permute-start | bytes 307208 | tf_op jit(solution)/shard_map/ppermute | solution.py:260

commit v10 on v6

--- a/solution.py
+++ b/solution.py
@@ -113,11 +113,16 @@
         own_kernel(head_dim, x_hbm, w_hbm, own_ref, x_ref, w_ref, sems)
 
 
-def home_kernel(head_dim, x_hbm, w_other_ref, other_ref, x_ref, sems):
+def load_kernel(after_ref, x_hbm, x_ref, sems):
     @pl.when(is_home())
     def _():
         for copy in start_copies((x_hbm,), (x_ref,), sems):
             copy.wait()
+
+
+def home_kernel(head_dim, x_ref, w_other_ref, other_ref):
+    @pl.when(is_home())
+    def _():
         store_heads(other_ref, 0, project(x_ref[0], w_other_ref[...]), head_dim)
 
     @pl.when(jnp.logical_not(is_home()))
@@ -325,15 +330,17 @@
             scratch=[x_scratch, w_scratch, pltpu.SemaphoreType.DMA((2,))],
         )(x, w)
         first = exchange_two_heads(away, False)
+        x_home = call(
+            load_kernel,
+            shape_of(images.shape),
+            2,
+            "home_rows",
+            in_specs=[VMEM, HBM],
+            scratch=[pltpu.SemaphoreType.DMA((1,))],
+        )(away, x)
         home = call(
-            functools.partial(home_kernel, head_dim),
-            product,
-            2,
-            "home_other",
-            flops=work,
-            in_specs=[HBM, VMEM],
-            scratch=[x_scratch, pltpu.SemaphoreType.DMA((1,))],
-        )(x, others[0])
+            functools.partial(home_kernel, head_dim), product, 2, "home_other", flops=work
+        )(x_home, others[0])
         second = exchange_two_heads(home, True)
         keep, qt, bias, gain = call(
             functools.partial(keep_kernel, head_dim),

time: 24.3 us -> 24.3 us (level)
  waiting for transfers between devices: 2.49 us -> 2.05 us
  starting transfers between devices: 15.5 us -> 15.9 us
    pallas_call x1, Pallas kernels: 1.57 us -> 0.41 us  [on_device(): call(functools.partial(home_kernel, head_dim), product, 2, 'home_other',...]
    pallas_call x0 -> x1, Pallas kernels: none -> 1.15 us  [on_device(): call(load_kernel, shape_of(images.shape), 2, 'home_rows', in_specs=[VMEM,...]
    ppermute x2, starting transfers between devices: 4.45 us -> 4.9 us  [exchange_two_heads(): return lax.ppermute(value, ('dp', 'tensor'), hops)]
    ppermute x6, waiting for transfers between devices: 2.3 us -> 1.86 us  [swap(): lax.ppermute(value, axis, [(i, i ^ k) for i in range(lax.axis_size(axis))])]
  transfers between devices with their start and end apart: 8 -> 8, of which waited for: 5 -> 4; matrix products, arithmetic and copies ran while one was open for 0% -> 0% of each run, Pallas kernels for 20% -> 20%
where the time goes in v10:
time: 24.3 us; the launch traced here: 24.1 us
  starting transfers between devices  15.9 us (65%)
  Pallas kernels  6.07 us (25%)
  waiting for transfers between devices  2.05 us (8%)
    ppermute x6, starting transfers between devices, swap(): lax.ppermute(value, axis, [(i, i ^ k) for i in range(lax.axis_size(axis))])  11 us
    ppermute x2, starting transfers between devices, exchange_two_heads(): return lax.ppermute(value, ('dp', 'tensor'), hops)  4.9 us
    pallas_call x3, Pallas kernels, on_device(): call(functools.partial(attend_kernel, here, there, tile_len, first, last,...  2.27 us
    pallas_call x1, Pallas kernels, on_device(): call(functools.partial(keep_kernel, head_dim), [product, *prepared], 8, '...  2.05 us
    ppermute x6, waiting for transfers between devices, swap(): lax.ppermute(value, axis, [(i, i ^ k) for i in range(lax.axis_size(axis))])  1.86 us
    pallas_call x1, Pallas kernels, on_device(): call(load_kernel, shape_of(images.shape), 2, 'home_rows', in_specs=[VMEM,...  1.15 us
  transfers between devices with their start and end apart: 8, of which 4 were waited for; matrix products, arithmetic and copies ran while one was open for 0% of the time, Pallas kernels for 20%

profile of v10, /device:TPU:0, one launch (start us, length us, event | category | flops | bytes accessed | tf_op | source)
XLA Modules:
  0.0 24.1 jit_solution(2362252284792116272)
XLA Ops:
  0.0 0.5 %collective-permute-start = (bf16[2,2048,128]{2,1,0:T(8,128)(2,1)}, bf16[2,2048,128]{2,1,0:T(8,128)(2,1)S(1)}, u32[]{:S(2)}, u32[]{:S(2)}) collective-permute-start(bf16[2,2048,128]{2,1,0:T(8,128)(2,1)} %w_hbm.3), channel_id=1, source_target_pairs={{0,4},{4,0},{1,5},{5,1},{2,6},{6,2},{3,7},{7,3},{8,12},{12,8},{9,1... | collective-permute-start | bytes 3145736 | tf_op jit(solution)/shard_map/ppermute | solution.py:246
  0.5 2.0 %collective-permute-start.1 = (bf16[1,2,200,128]{3,2,1,0:T(8,128)(2,1)S(1)}, bf16[1,2,200,128]{3,2,1,0:T(8,128)(2,1)S(1)}, u32[]{:S(2)}, u32[]{:S(2)}) collective-permute-start(bf16[1,2,200,128]{3,2,1,0:T(8,128)(2,1)S(1)} %away_own.1.after_ref), channel_id=1, source_target_pairs={{0,4},{1,5},{2,0},{3,1},{4,6},{5,7},{6,2},{7,3},{8,12},{9,13},{10,... | collective-permute-start | bytes 307208 | tf_op jit(solution)/shard_map/ppermute | solution.py:255
  2.5 1.2 %home_rows.1.x_ref = bf16[1,200,2048]{2,1,0:T(8,128)(2,1)S(1)} custom-call(bf16[1,2,200,128]{3,2,1,0:T(8,128)(2,1)S(1)} %away_own.1.after_ref, bf16[1,200,2048]{2,1,0:T(8,128)(2,1)} %x_hbm.5), custom_call_target="tpu_custom_call" | custom-call | tf_op jit(solution)/shard_map/home_rows/pallas_call | solution.py:333
  3.6 0.0 collective-permute-done.w_other_ref
  3.6 0.4 %home_other.1.after_ref = bf16[1,2,200,128]{3,2,1,0:T(8,128)(2,1)S(1)} custom-call(bf16[1,200,2048]{2,1,0:T(8,128)(2,1)S(1)} %home_rows.1.x_ref, bf16[2,2048,128]{2,1,0:T(8,128)(2,1)S(1)} %collective-permute-done.w_other_ref), custom_call_target="tpu_custom_call" | custom-call | flops 209715200 | tf_op jit(solution)/shard_map/home_other/pallas_call | solution.py:341
  4.1 2.9 %collective-permute-start.2 = (bf16[1,2,200,128]{3,2,1,0:T(8,128)(2,1)S(1)}, bf16[1,2,200,128]{3,2,1,0:T(8,128)(2,1)S(1)}, u32[]{:S(2)}, u32[]{:S(2)}) collective-permute-start(bf16[1,2,200,128]{3,2,1,0:T(8,128)(2,1)S(1)} %home_other.1.after_ref), channel_id=1, source_target_pairs={{0,2},{1,3},{2,6},{3,7},{4,0},{5,1},{6,4},{7,5},{8,10},{9,11},{10,... | collective-permute-start | bytes 307208 | tf_op jit(solution)/shard_map/ppermute | solution.py:255
  7.0 2.0 %keep_queries.1 = (bf16[1,2,200,128]{3,2,1,0:T(8,128)(2,1)S(1)}, bf16[128,512]{1,0:T(8,128)(2,1)S(1)}, f32[4,512]{1,0:T(4,128)S(1)}, f32[1,128]{1,0:T(1,128)S(1)}) custom-call(bf16[1,2,200,128]{3,2,1,0:T(8,128)(2,1)S(1)} %home_other.1.after_ref, bf16[2,2048,128]{2,1,0:T(8,128)(2,1)S(1)} %collective-permute-done.w_other_ref, bf16[1,200,2048]{2,1,0:T(8,128)(2,1)} %x_hbm.5, ...), custom_call_target="tpu_custom_call" | custom-call | flops 209715200 | tf_op jit(solution)/shard_map/keep_queries/pallas_call | solution.py:345
  9.0 0.0 collective-permute-done.1.first_ref
  9.1 0.2 collective-permute-done.2.second_ref
  9.3 2.6 %collective-permute-start.5 = (bf16[1,2,200,128]{3,2,1,0:T(8,128)(2,1)S(1)}, bf16[1,2,200,128]{3,2,1,0:T(8,128)(2,1)S(1)}, u32[]{:S(2)}, u32[]{:S(2)}) collective-permute-start(bf16[1,2,200,128]{3,2,1,0:T(8,128)(2,1)S(1)} %pair_sum.1.keep_ref), channel_id=1, source_target_pairs={{0,1},{1,0},{2,3},{3,2},{4,5},{5,4},{6,7},{7,6},{8,9},{9,8},{10,11... | collective-permute-start | bytes 307208 | tf_op jit(solution)/shard_map/ppermute | solution.py:246
  11.8 2.4 %collective-permute-start.3 = (bf16[1,2,200,128]{3,2,1,0:T(8,128)(2,1)S(1)}, bf16[1,2,200,128]{3,2,1,0:T(8,128)(2,1)S(1)}, u32[]{:S(2)}, u32[]{:S(2)}) collective-permute-start(bf16[1,2,200,128]{3,2,1,0:T(8,128)(2,1)S(1)} %pair_sum.1.keep_ref), channel_id=1, source_target_pairs={{0,24},{8,16},{16,8},{24,0},{1,25},{9,17},{17,9},{25,1},{2,26},{10... | collective-permute-start | bytes 307208 | tf_op jit(solution)/shard_map/ppermute | solution.py:246
  14.3 0.2 collective-permute-done.5.arrived_ref
  14.5 0.1 sum_norm.1.refs_0_
  14.6 1.6 %collective-permute-start.7 = (bf16[2,200,128]{2,1,0:T(8,128)(2,1)S(1)}, bf16[2,200,128]{2,1,0:T(8,128)(2,1)S(1)}, u32[]{:S(2)}, u32[]{:S(2)}) collective-permute-start(bf16[2,200,128]{2,1,0:T(8,128)(2,1)S(1)} %sum_norm.1.refs_0_), channel_id=1, source_target_pairs={{0,16},{8,24},{16,0},{24,8},{1,17},{9,25},{17,1},{25,9},{2,18},{10... | collective-permute-start | bytes 307208 | tf_op jit(solution)/shard_map/ppermute | solution.py:246
  16.2 1.5 %collective-permute-start.6 = (bf16[2,200,128]{2,1,0:T(8,128)(2,1)S(1)}, bf16[2,200,128]{2,1,0:T(8,128)(2,1)S(1)}, u32[]{:S(2)}, u32[]{:S(2)}) collective-permute-start(bf16[2,200,128]{2,1,0:T(8,128)(2,1)S(1)} %sum_norm.1.refs_0_), channel_id=1, source_target_pairs={{0,8},{8,0},{16,24},{24,16},{1,9},{9,1},{17,25},{25,17},{2,10},{10... | collective-permute-start | bytes 307208 | tf_op jit(solution)/shard_map/ppermute | solution.py:246
  17.7 0.0 collective-permute-done.3.refs_0_
  17.7 2.5 %collective-permute-start.4 = (bf16[1,2,200,128]{3,2,1,0:T(8,128)(2,1)S(1)}, bf16[1,2,200,128]{3,2,1,0:T(8,128)(2,1)S(1)}, u32[]{:S(2)}, u32[]{:S(2)}) collective-permute-start(bf16[1,2,200,128]{3,2,1,0:T(8,128)(2,1)S(1)} %collective-permute-done.3.refs_0_), channel_id=1, source_target_pairs={{0,1},{1,0},{2,3},{3,2},{4,5},{5,4},{6,7},{7,6},{8,9},{9,8},{10,11... | collective-permute-start | bytes 307208 | tf_op jit(solution)/shard_map/ppermute | solution.py:246
  20.1 0.4 %attend.3 = (f32[1,512]{1,0:T(1,128)S(1)}, f32[1,512]{1,0:T(1,128)S(1)}, f32[128,512]{1,0:T(8,128)S(1)}) custom-call(f32[1,128]{1,0:T(1,128)S(1)} %get-tuple-element.15.k_gain_ref, bf16[128,512]{1,0:T(8,128)(2,1)S(1)} %get-tuple-element.16.qt_ref, f32[4,512]{1,0:T(4,128)S(1)} %get-tuple-element.17.bias_ref, bf16[2,200,128]{2,1,0:T(8,128)(2,1)S(1)} %sum_norm.1.refs_0_), custom_call_target="tpu_custom_call" | custom-call | flops 52428800 | tf_op jit(solution)/shard_map/attend/pallas_call | solution.py:402
  20.6 0.0 collective-permute-done.7.refs_1_
  20.6 1.0 %collective-permute-done.6.refs_0_ = bf16[2,200,128]{2,1,0:T(8,128)(2,1)S(1)} collective-permute-done((bf16[2,200,128]{2,1,0:T(8,128)(2,1)S(1)}, bf16[2,200,128]{2,1,0:T(8,128)(2,1)S(1)}, u32[]{:S(2)}, u32[]{:S(2)}) %collective-permute-start.6) | collective-permute-done | bytes 102432 | tf_op jit(solution)/shard_map/ppermute | solution.py:246
  21.6 0.6 %attend.4 = (f32[1,512]{1,0:T(1,128)S(1)}, f32[1,512]{1,0:T(1,128)S(1)}, f32[128,512]{1,0:T(8,128)S(1)}) custom-call(f32[1,128]{1,0:T(1,128)S(1)} %get-tuple-element.15.k_gain_ref, bf16[128,512]{1,0:T(8,128)(2,1)S(1)} %get-tuple-element.16.qt_ref, f32[4,512]{1,0:T(4,128)S(1)} %get-tuple-element.17.bias_ref, ...), custom_call_target="tpu_custom_call" | custom-call | flops 104857600 | tf_op jit(solution)/shard_map/attend/pallas_call | solution.py:402
  22.2 0.6 %collective-permute-done.4.refs_1_ = bf16[1,2,200,128]{3,2,1,0:T(8,128)(2,1)S(1)} collective-permute-done((bf16[1,2,200,128]{3,2,1,0:T(8,128)(2,1)S(1)}, bf16[1,2,200,128]{3,2,1,0:T(8,128)(2,1)S(1)}, u32[]{:S(2)}, u32[]{:S(2)}) %collective-permute-start.4) | collective-permute-done | bytes 102432 | tf_op jit(solution)/shard_map/ppermute | solution.py:246
  22.8 1.3 %attend.5 = bf16[128,512]{1,0:T(8,128)(2,1)} custom-call(f32[1,128]{1,0:T(1,128)S(1)} %get-tuple-element.15.k_gain_ref, bf16[128,512]{1,0:T(8,128)(2,1)S(1)} %get-tuple-element.16.qt_ref, f32[4,512]{1,0:T(4,128)S(1)} %get-tuple-element.17.bias_ref, bf16[1,2,200,128]{3,2,1,0:T(8,128)(2,1)S(1)} %collective-permute-done.3.refs_0_, ...), custom_call_target="tpu_custom_call" | custom-call | flops 52428800 | tf_op jit(solution)/shard_map/attend/pallas_call | solution.py:402
  (2 shorter events, 0.1 us)
Async XLA Ops:
  0.0 3.6 %collective-permute-start = (bf16[2,2048,128]{2,1,0:T(8,128)(2,1)}, bf16[2,2048,128]{2,1,0:T(8,128)(2,1)S(1)}, u32[]{:S(2)}, u32[]{:S(2)}) collective-permute-start(bf16[2,2048,128]{2,1,0:T(8,128)(2,1)} %w_hbm.3), channel_id=1, source_target_pairs={{0,4},{4,0},{1,5},{5,1},{2,6},{6,2},{3,7},{7,3},{8,12},{12,8},{9,1... | collective-permute-start | bytes 3145736 | tf_op jit(solution)/shard_map/ppermute | solution.py:246
  0.5 8.6 %collective-permute-start.1 = (bf16[1,2,200,128]{3,2,1,0:T(8,128)(2,1)S(1)}, bf16[1,2,200,128]{3,2,1,0:T(8,128)(2,1)S(1)}, u32[]{:S(2)}, u32[]{:S(2)}) collective-permute-start(bf16[1,2,200,128]{3,2,1,0:T(8,128)(2,1)S(1)} %away_own.1.after_ref), channel_id=1, source_target_pairs={{0,4},{1,5},{2,0},{3,1},{4,6},{5,7},{6,2},{7,3},{8,12},{9,13},{10,... | collective-permute-start | bytes 307208 | tf_op jit(solution)/shard_map/ppermute | solution.py:255
  4.1 5.2 %collective-permute-start.2 = (bf16[1,2,200,128]{3,2,1,0:T(8,128)(2,1)S(1)}, bf16[1,2,200,128]{3,2,1,0:T(8,128)(2,1)S(1)}, u32[]{:S(2)}, u32[]{:S(2)}) collective-permute-start(bf16[1,2,200,128]{3,2,1,0:T(8,128)(2,1)S(1)} %home_other.1.after_ref), channel_id=1, source_target_pairs={{0,2},{1,3},{2,6},{3,7},{4,0},{5,1},{6,4},{7,5},{8,10},{9,11},{10,... | collective-permute-start | bytes 307208 | tf_op jit(solution)/shard_map/ppermute | solution.py:255
  9.3 5.2 %collective-permute-start.5 = (bf16[1,2,200,128]{3,2,1,0:T(8,128)(2,1)S(1)}, bf16[1,2,200,128]{3,2,1,0:T(8,128)(2,1)S(1)}, u32[]{:S(2)}, u32[]{:S(2)}) collective-permute-start(bf16[1,2,200,128]{3,2,1,0:T(8,128)(2,1)S(1)} %pair_sum.1.keep_ref), channel_id=1, source_target_pairs={{0,1},{1,0},{2,3},{3,2},{4,5},{5,4},{6,7},{7,6},{8,9},{9,8},{10,11... | collective-permute-start | bytes 307208 | tf_op jit(solution)/shard_map/ppermute | solution.py:246
  11.8 5.8 %collective-permute-start.3 = (bf16[1,2,200,128]{3,2,1,0:T(8,128)(2,1)S(1)}, bf16[1,2,200,128]{3,2,1,0:T(8,128)(2,1)S(1)}, u32[]{:S(2)}, u32[]{:S(2)}) collective-permute-start(bf16[1,2,200,128]{3,2,1,0:T(8,128)(2,1)S(1)} %pair_sum.1.keep_ref), channel_id=1, source_target_pairs={{0,24},{8,16},{16,8},{24,0},{1,25},{9,17},{17,9},{25,1},{2,26},{10... | collective-permute-start | bytes 307208 | tf_op jit(solution)/shard_map/ppermute | solution.py:246
  14.6 6.0 %collective-permute-start.7 = (bf16[2,200,128]{2,1,0:T(8,128)(2,1)S(1)}, bf16[2,200,128]{2,1,0:T(8,128)(2,1)S(1)}, u32[]{:S(2)}, u32[]{:S(2)}) collective-permute-start(bf16[2,200,128]{2,1,0:T(8,128)(2,1)S(1)} %sum_norm.1.refs_0_), channel_id=1, source_target_pairs={{0,16},{8,24},{16,0},{24,8},{1,17},{9,25},{17,1},{25,9},{2,18},{10... | collective-permute-start | bytes 307208 | tf_op jit(solution)/shard_map/ppermute | solution.py:246
  16.2 5.4 %collective-permute-start.6 = (bf16[2,200,128]{2,1,0:T(8,128)(2,1)S(1)}, bf16[2,200,128]{2,1,0:T(8,128)(2,1)S(1)}, u32[]{:S(2)}, u32[]{:S(2)}) collective-permute-start(bf16[2,200,128]{2,1,0:T(8,128)(2,1)S(1)} %sum_norm.1.refs_0_), channel_id=1, source_target_pairs={{0,8},{8,0},{16,24},{24,16},{1,9},{9,1},{17,25},{25,17},{2,10},{10... | collective-permute-start | bytes 307208 | tf_op jit(solution)/shard_map/ppermute | solution.py:246
  17.7 5.1 %collective-permute-start.4 = (bf16[1,2,200,128]{3,2,1,0:T(8,128)(2,1)S(1)}, bf16[1,2,200,128]{3,2,1,0:T(8,128)(2,1)S(1)}, u32[]{:S(2)}, u32[]{:S(2)}) collective-permute-start(bf16[1,2,200,128]{3,2,1,0:T(8,128)(2,1)S(1)} %collective-permute-done.3.refs_0_), channel_id=1, source_target_pairs={{0,1},{1,0},{2,3},{3,2},{4,5},{5,4},{6,7},{7,6},{8,9},{9,8},{10,11... | collective-permute-start | bytes 307208 | tf_op jit(solution)/shard_map/ppermute | solution.py:246

commit v11 on v10

--- a/solution.py
+++ b/solution.py
@@ -246,12 +246,12 @@
     return lax.ppermute(value, axis, [(i, i ^ k) for i in range(lax.axis_size(axis))])
 
 
-def exchange_two_heads(value, home_sends):
+def exchange_two_heads(value, home_sends, apart):
     hops = []
     for d in range(2):
         for t in range(4):
             sends = (t // 2 == d) == home_sends
-            hops.append((4 * d + t, 4 * d + (t ^ 2) if sends else 4 * (1 - d) + t))
+            hops.append((4 * d + t, 4 * d + (t ^ apart) if sends else 4 * (1 - d) + t))
     return lax.ppermute(value, ("dp", "tensor"), hops)
 
 
@@ -329,7 +329,7 @@
             in_specs=[HBM] * 2,
             scratch=[x_scratch, w_scratch, pltpu.SemaphoreType.DMA((2,))],
         )(x, w)
-        first = exchange_two_heads(away, False)
+        first = exchange_two_heads(away, False, 2)
         x_home = call(
             load_kernel,
             shape_of(images.shape),
@@ -341,7 +341,7 @@
         home = call(
             functools.partial(home_kernel, head_dim), product, 2, "home_other", flops=work
         )(x_home, others[0])
-        second = exchange_two_heads(home, True)
+        second = exchange_two_heads(home, True, 3)
         keep, qt, bias, gain = call(
             functools.partial(keep_kernel, head_dim),
             [product, *prepared],

time: 24.3 us -> 25.2 us (1.037)
  waiting for transfers between devices: 2.05 us -> 6.84 us
  starting transfers between devices: 15.9 us -> 12 us
    ppermute x6, starting transfers between devices: 11 us -> 6.12 us  [swap(): lax.ppermute(value, axis, [(i, i ^ k) for i in range(lax.axis_size(axis))])]
    ppermute x6, waiting for transfers between devices: 1.86 us -> 6.65 us  [swap(): lax.ppermute(value, axis, [(i, i ^ k) for i in range(lax.axis_size(axis))])]
    ppermute x2, starting transfers between devices: 4.9 us -> 5.92 us  [exchange_two_heads(): return lax.ppermute(value, ('dp', 'tensor'), hops)]
  transfers between devices with their start and end apart: 8 -> 8, of which waited for: 4 -> 5; matrix products, arithmetic and copies ran while one was open for 0% -> 0% of each run, Pallas kernels for 20% -> 19%
where the time goes in v11:
time: 25.2 us; the launch traced here: 25 us
  starting transfers between devices  12 us (48%)
  waiting for transfers between devices  6.84 us (27%)
  Pallas kernels  6.07 us (24%)
    ppermute x6, waiting for transfers between devices, swap(): lax.ppermute(value, axis, [(i, i ^ k) for i in range(lax.axis_size(axis))])  6.65 us
    ppermute x6, starting transfers between devices, swap(): lax.ppermute(value, axis, [(i, i ^ k) for i in range(lax.axis_size(axis))])  6.12 us
    ppermute x2, starting transfers between devices, exchange_two_heads(): return lax.ppermute(value, ('dp', 'tensor'), hops)  5.92 us
    pallas_call x3, Pallas kernels, on_device(): call(functools.partial(attend_kernel, here, there, tile_len, first, last,...  2.27 us
    pallas_call x1, Pallas kernels, on_device(): call(functools.partial(keep_kernel, head_dim), [product, *prepared], 8, '...  2.04 us
    pallas_call x1, Pallas kernels, on_device(): call(load_kernel, shape_of(images.shape), 2, 'home_rows', in_specs=[VMEM,...  1.15 us
  transfers between devices with their start and end apart: 8, of which 5 were waited for; matrix products, arithmetic and copies ran while one was open for 0% of the time, Pallas kernels for 19%

profile of v11, /device:TPU:0, one launch (start us, length us, event | category | flops | bytes accessed | tf_op | source)
XLA Modules:
  0.0 25.0 jit_solution(15301877227181721846)
XLA Ops:
  0.0 0.5 %collective-permute-start = (bf16[2,2048,128]{2,1,0:T(8,128)(2,1)}, bf16[2,2048,128]{2,1,0:T(8,128)(2,1)S(1)}, u32[]{:S(2)}, u32[]{:S(2)}) collective-permute-start(bf16[2,2048,128]{2,1,0:T(8,128)(2,1)} %w_hbm.3), channel_id=1, source_target_pairs={{0,4},{4,0},{1,5},{5,1},{2,6},{6,2},{3,7},{7,3},{8,12},{12,8},{9,1... | collective-permute-start | bytes 3145736 | tf_op jit(solution)/shard_map/ppermute | solution.py:246
  0.5 2.0 %collective-permute-start.1 = (bf16[1,2,200,128]{3,2,1,0:T(8,128)(2,1)S(1)}, bf16[1,2,200,128]{3,2,1,0:T(8,128)(2,1)S(1)}, u32[]{:S(2)}, u32[]{:S(2)}) collective-permute-start(bf16[1,2,200,128]{3,2,1,0:T(8,128)(2,1)S(1)} %away_own.1.after_ref), channel_id=1, source_target_pairs={{0,4},{1,5},{2,0},{3,1},{4,6},{5,7},{6,2},{7,3},{8,12},{9,13},{10,... | collective-permute-start | bytes 307208 | tf_op jit(solution)/shard_map/ppermute | solution.py:255
  2.5 1.2 %home_rows.1.x_ref = bf16[1,200,2048]{2,1,0:T(8,128)(2,1)S(1)} custom-call(bf16[1,2,200,128]{3,2,1,0:T(8,128)(2,1)S(1)} %away_own.1.after_ref, bf16[1,200,2048]{2,1,0:T(8,128)(2,1)} %x_hbm.5), custom_call_target="tpu_custom_call" | custom-call | tf_op jit(solution)/shard_map/home_rows/pallas_call | solution.py:333
  3.6 0.0 collective-permute-done.w_other_ref
  3.6 0.4 %home_other.1.after_ref = bf16[1,2,200,128]{3,2,1,0:T(8,128)(2,1)S(1)} custom-call(bf16[1,200,2048]{2,1,0:T(8,128)(2,1)S(1)} %home_rows.1.x_ref, bf16[2,2048,128]{2,1,0:T(8,128)(2,1)S(1)} %collective-permute-done.w_other_ref), custom_call_target="tpu_custom_call" | custom-call | flops 209715200 | tf_op jit(solution)/shard_map/home_other/pallas_call | solution.py:341
  4.1 3.9 %collective-permute-start.2 = (bf16[1,2,200,128]{3,2,1,0:T(8,128)(2,1)S(1)}, bf16[1,2,200,128]{3,2,1,0:T(8,128)(2,1)S(1)}, u32[]{:S(2)}, u32[]{:S(2)}) collective-permute-start(bf16[1,2,200,128]{3,2,1,0:T(8,128)(2,1)S(1)} %home_other.1.after_ref), channel_id=1, source_target_pairs={{0,3},{1,2},{2,6},{3,7},{4,0},{5,1},{6,5},{7,4},{8,11},{9,10},{10,... | collective-permute-start | bytes 307208 | tf_op jit(solution)/shard_map/ppermute | solution.py:255
  8.0 2.0 %keep_queries.1 = (bf16[1,2,200,128]{3,2,1,0:T(8,128)(2,1)S(1)}, bf16[128,512]{1,0:T(8,128)(2,1)S(1)}, f32[4,512]{1,0:T(4,128)S(1)}, f32[1,128]{1,0:T(1,128)S(1)}) custom-call(bf16[1,2,200,128]{3,2,1,0:T(8,128)(2,1)S(1)} %home_other.1.after_ref, bf16[2,2048,128]{2,1,0:T(8,128)(2,1)S(1)} %collective-permute-done.w_other_ref, bf16[1,200,2048]{2,1,0:T(8,128)(2,1)} %x_hbm.5, ...), custom_call_target="tpu_custom_call" | custom-call | flops 209715200 | tf_op jit(solution)/shard_map/keep_queries/pallas_call | solution.py:345
  10.1 0.0 collective-permute-done.1.first_ref
  10.1 0.2 collective-permute-done.2.second_ref
  10.3 0.1 collective-permute-start.5
  10.4 2.5 %collective-permute-start.3 = (bf16[1,2,200,128]{3,2,1,0:T(8,128)(2,1)S(1)}, bf16[1,2,200,128]{3,2,1,0:T(8,128)(2,1)S(1)}, u32[]{:S(2)}, u32[]{:S(2)}) collective-permute-start(bf16[1,2,200,128]{3,2,1,0:T(8,128)(2,1)S(1)} %pair_sum.1.keep_ref), channel_id=1, source_target_pairs={{0,24},{8,16},{16,8},{24,0},{1,25},{9,17},{17,9},{25,1},{2,26},{10... | collective-permute-start | bytes 307208 | tf_op jit(solution)/shard_map/ppermute | solution.py:246
  12.9 3.0 %collective-permute-done.5.arrived_ref = bf16[1,2,200,128]{3,2,1,0:T(8,128)(2,1)S(1)} collective-permute-done((bf16[1,2,200,128]{3,2,1,0:T(8,128)(2,1)S(1)}, bf16[1,2,200,128]{3,2,1,0:T(8,128)(2,1)S(1)}, u32[]{:S(2)}, u32[]{:S(2)}) %collective-permute-start.5) | collective-permute-done | bytes 102432 | tf_op jit(solution)/shard_map/ppermute | solution.py:246
  15.9 0.1 sum_norm.1.refs_0_
  16.0 1.6 %collective-permute-start.7 = (bf16[2,200,128]{2,1,0:T(8,128)(2,1)S(1)}, bf16[2,200,128]{2,1,0:T(8,128)(2,1)S(1)}, u32[]{:S(2)}, u32[]{:S(2)}) collective-permute-start(bf16[2,200,128]{2,1,0:T(8,128)(2,1)S(1)} %sum_norm.1.refs_0_), channel_id=1, source_target_pairs={{0,16},{8,24},{16,0},{24,8},{1,17},{9,25},{17,1},{25,9},{2,18},{10... | collective-permute-start | bytes 307208 | tf_op jit(solution)/shard_map/ppermute | solution.py:246
  17.6 1.5 %collective-permute-start.6 = (bf16[2,200,128]{2,1,0:T(8,128)(2,1)S(1)}, bf16[2,200,128]{2,1,0:T(8,128)(2,1)S(1)}, u32[]{:S(2)}, u32[]{:S(2)}) collective-permute-start(bf16[2,200,128]{2,1,0:T(8,128)(2,1)S(1)} %sum_norm.1.refs_0_), channel_id=1, source_target_pairs={{0,8},{8,0},{16,24},{24,16},{1,9},{9,1},{17,25},{25,17},{2,10},{10... | collective-permute-start | bytes 307208 | tf_op jit(solution)/shard_map/ppermute | solution.py:246
  19.1 0.0 collective-permute-done.3.refs_0_
  19.1 0.0 collective-permute-start.4
  19.1 0.4 %attend.3 = (f32[1,512]{1,0:T(1,128)S(1)}, f32[1,512]{1,0:T(1,128)S(1)}, f32[128,512]{1,0:T(8,128)S(1)}) custom-call(f32[1,128]{1,0:T(1,128)S(1)} %get-tuple-element.15.k_gain_ref, bf16[128,512]{1,0:T(8,128)(2,1)S(1)} %get-tuple-element.16.qt_ref, f32[4,512]{1,0:T(4,128)S(1)} %get-tuple-element.17.bias_ref, bf16[2,200,128]{2,1,0:T(8,128)(2,1)S(1)} %sum_norm.1.refs_0_), custom_call_target="tpu_custom_call" | custom-call | flops 52428800 | tf_op jit(solution)/shard_map/attend/pallas_call | solution.py:402
  19.5 1.2 %collective-permute-done.7.refs_1_ = bf16[2,200,128]{2,1,0:T(8,128)(2,1)S(1)} collective-permute-done((bf16[2,200,128]{2,1,0:T(8,128)(2,1)S(1)}, bf16[2,200,128]{2,1,0:T(8,128)(2,1)S(1)}, u32[]{:S(2)}, u32[]{:S(2)}) %collective-permute-start.7) | collective-permute-done | bytes 102432 | tf_op jit(solution)/shard_map/ppermute | solution.py:246
  20.8 1.5 %collective-permute-done.6.refs_0_ = bf16[2,200,128]{2,1,0:T(8,128)(2,1)S(1)} collective-permute-done((bf16[2,200,128]{2,1,0:T(8,128)(2,1)S(1)}, bf16[2,200,128]{2,1,0:T(8,128)(2,1)S(1)}, u32[]{:S(2)}, u32[]{:S(2)}) %collective-permute-start.6) | collective-permute-done | bytes 102432 | tf_op jit(solution)/shard_map/ppermute | solution.py:246
  22.3 0.6 %attend.4 = (f32[1,512]{1,0:T(1,128)S(1)}, f32[1,512]{1,0:T(1,128)S(1)}, f32[128,512]{1,0:T(8,128)S(1)}) custom-call(f32[1,128]{1,0:T(1,128)S(1)} %get-tuple-element.15.k_gain_ref, bf16[128,512]{1,0:T(8,128)(2,1)S(1)} %get-tuple-element.16.qt_ref, f32[4,512]{1,0:T(4,128)S(1)} %get-tuple-element.17.bias_ref, ...), custom_call_target="tpu_custom_call" | custom-call | flops 104857600 | tf_op jit(solution)/shard_map/attend/pallas_call | solution.py:402
  22.9 0.9 %collective-permute-done.4.refs_1_ = bf16[1,2,200,128]{3,2,1,0:T(8,128)(2,1)S(1)} collective-permute-done((bf16[1,2,200,128]{3,2,1,0:T(8,128)(2,1)S(1)}, bf16[1,2,200,128]{3,2,1,0:T(8,128)(2,1)S(1)}, u32[]{:S(2)}, u32[]{:S(2)}) %collective-permute-start.4) | collective-permute-done | bytes 102432 | tf_op jit(solution)/shard_map/ppermute | solution.py:246
  23.8 1.3 %attend.5 = bf16[128,512]{1,0:T(8,128)(2,1)} custom-call(f32[1,128]{1,0:T(1,128)S(1)} %get-tuple-element.15.k_gain_ref, bf16[128,512]{1,0:T(8,128)(2,1)S(1)} %get-tuple-element.16.qt_ref, f32[4,512]{1,0:T(4,128)S(1)} %get-tuple-element.17.bias_ref, bf16[1,2,200,128]{3,2,1,0:T(8,128)(2,1)S(1)} %collective-permute-done.3.refs_0_, ...), custom_call_target="tpu_custom_call" | custom-call | flops 52428800 | tf_op jit(solution)/shard_map/attend/pallas_call | solution.py:402
  (2 shorter events, 0.1 us)
Async XLA Ops:
  0.0 3.6 %collective-permute-start = (bf16[2,2048,128]{2,1,0:T(8,128)(2,1)}, bf16[2,2048,128]{2,1,0:T(8,128)(2,1)S(1)}, u32[]{:S(2)}, u32[]{:S(2)}) collective-permute-start(bf16[2,2048,128]{2,1,0:T(8,128)(2,1)} %w_hbm.3), channel_id=1, source_target_pairs={{0,4},{4,0},{1,5},{5,1},{2,6},{6,2},{3,7},{7,3},{8,12},{12,8},{9,1... | collective-permute-start | bytes 3145736 | tf_op jit(solution)/shard_map/ppermute | solution.py:246
  0.5 9.6 %collective-permute-start.1 = (bf16[1,2,200,128]{3,2,1,0:T(8,128)(2,1)S(1)}, bf16[1,2,200,128]{3,2,1,0:T(8,128)(2,1)S(1)}, u32[]{:S(2)}, u32[]{:S(2)}) collective-permute-start(bf16[1,2,200,128]{3,2,1,0:T(8,128)(2,1)S(1)} %away_own.1.after_ref), channel_id=1, source_target_pairs={{0,4},{1,5},{2,0},{3,1},{4,6},{5,7},{6,2},{7,3},{8,12},{9,13},{10,... | collective-permute-start | bytes 307208 | tf_op jit(solution)/shard_map/ppermute | solution.py:255
  4.1 6.2 %collective-permute-start.2 = (bf16[1,2,200,128]{3,2,1,0:T(8,128)(2,1)S(1)}, bf16[1,2,200,128]{3,2,1,0:T(8,128)(2,1)S(1)}, u32[]{:S(2)}, u32[]{:S(2)}) collective-permute-start(bf16[1,2,200,128]{3,2,1,0:T(8,128)(2,1)S(1)} %home_other.1.after_ref), channel_id=1, source_target_pairs={{0,3},{1,2},{2,6},{3,7},{4,0},{5,1},{6,5},{7,4},{8,11},{9,10},{10,... | collective-permute-start | bytes 307208 | tf_op jit(solution)/shard_map/ppermute | solution.py:255
  10.3 5.6 %collective-permute-start.5 = (bf16[1,2,200,128]{3,2,1,0:T(8,128)(2,1)S(1)}, bf16[1,2,200,128]{3,2,1,0:T(8,128)(2,1)S(1)}, u32[]{:S(2)}, u32[]{:S(2)}) collective-permute-start(bf16[1,2,200,128]{3,2,1,0:T(8,128)(2,1)S(1)} %pair_sum.1.keep_ref), channel_id=1, source_target_pairs={{0,1},{1,0},{2,3},{3,2},{4,5},{5,4},{6,7},{7,6},{8,9},{9,8},{10,11... | collective-permute-start | bytes 307208 | tf_op jit(solution)/shard_map/ppermute | solution.py:246
  10.4 8.7 %collective-permute-start.3 = (bf16[1,2,200,128]{3,2,1,0:T(8,128)(2,1)S(1)}, bf16[1,2,200,128]{3,2,1,0:T(8,128)(2,1)S(1)}, u32[]{:S(2)}, u32[]{:S(2)}) collective-permute-start(bf16[1,2,200,128]{3,2,1,0:T(8,128)(2,1)S(1)} %pair_sum.1.keep_ref), channel_id=1, source_target_pairs={{0,24},{8,16},{16,8},{24,0},{1,25},{9,17},{17,9},{25,1},{2,26},{10... | collective-permute-start | bytes 307208 | tf_op jit(solution)/shard_map/ppermute | solution.py:246
  16.0 4.7 %collective-permute-start.7 = (bf16[2,200,128]{2,1,0:T(8,128)(2,1)S(1)}, bf16[2,200,128]{2,1,0:T(8,128)(2,1)S(1)}, u32[]{:S(2)}, u32[]{:S(2)}) collective-permute-start(bf16[2,200,128]{2,1,0:T(8,128)(2,1)S(1)} %sum_norm.1.refs_0_), channel_id=1, source_target_pairs={{0,16},{8,24},{16,0},{24,8},{1,17},{9,25},{17,1},{25,9},{2,18},{10... | collective-permute-start | bytes 307208 | tf_op jit(solution)/shard_map/ppermute | solution.py:246
  17.6 4.7 %collective-permute-start.6 = (bf16[2,200,128]{2,1,0:T(8,128)(2,1)S(1)}, bf16[2,200,128]{2,1,0:T(8,128)(2,1)S(1)}, u32[]{:S(2)}, u32[]{:S(2)}) collective-permute-start(bf16[2,200,128]{2,1,0:T(8,128)(2,1)S(1)} %sum_norm.1.refs_0_), channel_id=1, source_target_pairs={{0,8},{8,0},{16,24},{24,16},{1,9},{9,1},{17,25},{25,17},{2,10},{10... | collective-permute-start | bytes 307208 | tf_op jit(solution)/shard_map/ppermute | solution.py:246
  19.1 4.7 %collective-permute-start.4 = (bf16[1,2,200,128]{3,2,1,0:T(8,128)(2,1)S(1)}, bf16[1,2,200,128]{3,2,1,0:T(8,128)(2,1)S(1)}, u32[]{:S(2)}, u32[]{:S(2)}) collective-permute-start(bf16[1,2,200,128]{3,2,1,0:T(8,128)(2,1)S(1)} %collective-permute-done.3.refs_0_), channel_id=1, source_target_pairs={{0,1},{1,0},{2,3},{3,2},{4,5},{5,4},{6,7},{7,6},{8,9},{9,8},{10,11... | collective-permute-start | bytes 307208 | tf_op jit(solution)/shard_map/ppermute | solution.py:246

commit v12 on v11

--- a/solution.py
+++ b/solution.py
@@ -168,9 +168,13 @@
     split_half(held, send_ref, keep_ref, (1 - upper) * half, upper * half)
 
 
-def pair_kernel(keep_ref, first_ref, second_ref, out_ref):
-    arrived = jnp.where(is_home(), first_ref[...], second_ref[...]).astype(F32)
-    out_ref[...] = (keep_ref[...].astype(F32) + arrived).astype(BF16)
+def first_sum_kernel(keep_ref, first_ref, out_ref):
+    out_ref[...] = (keep_ref[...].astype(F32) + first_ref[...].astype(F32)).astype(BF16)
+
+
+def second_sum_kernel(first_sum_ref, keep_ref, second_ref, out_ref):
+    total = (keep_ref[...].astype(F32) + second_ref[...].astype(F32)).astype(BF16)
+    out_ref[...] = jnp.where(is_home(), first_sum_ref[...], total)
 
 
 def add_kernel(bit, keep_ref, arrived_ref, send_ref, next_ref, held):
@@ -190,8 +194,12 @@
     return normalize(keys, k_gain).astype(BF16), values.astype(BF16)
 
 
-def norm_kernel(k_gain_ref, keep_ref, arrived_ref, kv_ref):
-    kv_ref[0], kv_ref[1] = finish_rows(k_gain_ref[...], keep_ref.at[0], arrived_ref.at[0])
+def norm_kernel(k_gain_ref, keep_ref, *refs):
+    arrived_refs, kv_ref = refs[:-1], refs[-1]
+    arrived = arrived_refs[0][0]
+    if len(arrived_refs) > 1:
+        arrived = jnp.where(is_home(), arrived, arrived_refs[1][0])
+    kv_ref[0], kv_ref[1] = finish_rows(k_gain_ref[...], keep_ref[0], arrived)
 
 
 def attend_kernel(near, far, tile_len, first, last, head_dim, k_gain_ref, qt_ref, bias_ref, *refs):
@@ -246,13 +254,29 @@
     return lax.ppermute(value, axis, [(i, i ^ k) for i in range(lax.axis_size(axis))])
 
 
-def exchange_two_heads(value, home_sends, apart):
+def permute_two_heads(value, away, home):
     hops = []
     for d in range(2):
         for t in range(4):
-            sends = (t // 2 == d) == home_sends
-            hops.append((4 * d + t, 4 * d + (t ^ apart) if sends else 4 * (1 - d) + t))
+            to_d, to_t = home(d, t) if t // 2 == d else away(d, t)
+            hops.append((4 * d + t, 4 * to_d + to_t))
     return lax.ppermute(value, ("dp", "tensor"), hops)
+
+
+def across(d, t):
+    return d, t ^ 2
+
+
+def next_core(d, t):
+    return 1 - d, t
+
+
+def next_tensor(d, t):
+    return d, t ^ 1
+
+
+def itself(d, t):
+    return d, t
 
 
 def sum_many_heads(own, others):
@@ -329,7 +353,7 @@
             in_specs=[HBM] * 2,
             scratch=[x_scratch, w_scratch, pltpu.SemaphoreType.DMA((2,))],
         )(x, w)
-        first = exchange_two_heads(away, False, 2)
+        first = permute_two_heads(away, across, next_core)
         x_home = call(
             load_kernel,
             shape_of(images.shape),
@@ -341,7 +365,7 @@
         home = call(
             functools.partial(home_kernel, head_dim), product, 2, "home_other", flops=work
         )(x_home, others[0])
-        second = exchange_two_heads(home, True, 3)
+        second = permute_two_heads(home, next_core, across)
         keep, qt, bias, gain = call(
             functools.partial(keep_kernel, head_dim),
             [product, *prepared],
@@ -351,7 +375,10 @@
             in_specs=[VMEM] * 2 + [HBM] * 6,
             scratch=[x_scratch, w_scratch, *query_scratch, pltpu.SemaphoreType.DMA((6,))],
         )(home, others[0], x, w, *small)
-        total = call(pair_kernel, product, 3, "pair_sum")(keep, first, second)
+        first_sum = call(first_sum_kernel, product, 2, "first_sum")(keep, first)
+        arrived = [permute_two_heads(first_sum, itself, next_tensor)]
+        total = call(second_sum_kernel, product, 3, "second_sum")(first_sum, keep, second)
+        arrived.append(permute_two_heads(total, next_tensor, itself))
     else:
         own, x_here = call(
             functools.partial(own_kernel, head_dim),
@@ -377,11 +404,13 @@
             for other in others
         ]
         total = sum_many_heads(own, rest)
+        arrived = [swap(total, "tensor", 1)]
     far = [step for step in range(1, n_section) if step & (step - 1)]
     near = [step for step in range(1, n_section) if not step & (step - 1)]
-    arrived = swap(total, "tensor", 1)
     halves = [swap(total, "section", step) for step in far]
-    kv = call(norm_kernel, shape_of((2, rows, head_dim)), 3, "sum_norm")(gain, total, arrived)
+    kv = call(norm_kernel, shape_of((2, rows, head_dim)), 2 + len(arrived), "sum_norm")(
+        gain, total, *arrived
+    )
     finished = [swap(kv, "section", step) for step in near]
     both = []
     for value in halves:

time: 25.2 us -> 26.1 us (1.036)
  starting transfers between devices: 12 us -> 16.6 us
  waiting for transfers between devices: 6.84 us -> 3.1 us
    ppermute x6 -> x5, waiting for transfers between devices: 6.65 us -> 3.09 us  [swap(): lax.ppermute(value, axis, [(i, i ^ k) for i in range(lax.axis_size(axis))])]
    ppermute x2 -> x4, starting transfers between devices: 5.92 us -> 9.05 us  [permute_two_heads(): return lax.ppermute(value, ('dp', 'tensor'), hops)]
    ppermute x6 -> x5, starting transfers between devices: 6.12 us -> 7.52 us  [swap(): lax.ppermute(value, axis, [(i, i ^ k) for i in range(lax.axis_size(axis))])]
  transfers between devices with their start and end apart: 8 -> 9, of which waited for: 5 -> 3; matrix products, arithmetic and copies ran while one was open for 0% -> 0% of each run, Pallas kernels for 19% -> 19%
where the time goes in v12:
time: 26.1 us; the launch traced here: 25.9 us
  starting transfers between devices  16.6 us (64%)
  Pallas kernels  6.13 us (23%)
  waiting for transfers between devices  3.1 us (12%)
    ppermute x4, starting transfers between devices, permute_two_heads(): return lax.ppermute(value, ('dp', 'tensor'), hops)  9.05 us
    ppermute x5, starting transfers between devices, swap(): lax.ppermute(value, axis, [(i, i ^ k) for i in range(lax.axis_size(axis))])  7.52 us
    ppermute x5, waiting for transfers between devices, swap(): lax.ppermute(value, axis, [(i, i ^ k) for i in range(lax.axis_size(axis))])  3.09 us
    pallas_call x3, Pallas kernels, on_device(): call(functools.partial(attend_kernel, here, there, tile_len, first, last,...  2.27 us
    pallas_call x1, Pallas kernels, on_device(): call(functools.partial(keep_kernel, head_dim), [product, *prepared], 8, '...  2.05 us
    pallas_call x1, Pallas kernels, on_device(): call(load_kernel, shape_of(images.shape), 2, 'home_rows', in_specs=[VMEM,...  1.15 us
  transfers between devices with their start and end apart: 9, of which 3 were waited for; matrix products, arithmetic and copies ran while one was open for 0% of the time, Pallas kernels for 19%

profile of v12, /device:TPU:0, one launch (start us, length us, event | category | flops | bytes accessed | tf_op | source)
XLA Modules:
  0.0 25.9 jit_solution(17594719162535446798)
XLA Ops:
  0.0 0.5 %collective-permute-start = (bf16[2,2048,128]{2,1,0:T(8,128)(2,1)}, bf16[2,2048,128]{2,1,0:T(8,128)(2,1)S(1)}, u32[]{:S(2)}, u32[]{:S(2)}) collective-permute-start(bf16[2,2048,128]{2,1,0:T(8,128)(2,1)} %w_hbm.3), channel_id=1, source_target_pairs={{0,4},{4,0},{1,5},{5,1},{2,6},{6,2},{3,7},{7,3},{8,12},{12,8},{9,1... | collective-permute-start | bytes 3145736 | tf_op jit(solution)/shard_map/ppermute | solution.py:254
  0.5 2.0 %collective-permute-start.1 = (bf16[1,2,200,128]{3,2,1,0:T(8,128)(2,1)S(1)}, bf16[1,2,200,128]{3,2,1,0:T(8,128)(2,1)S(1)}, u32[]{:S(2)}, u32[]{:S(2)}) collective-permute-start(bf16[1,2,200,128]{3,2,1,0:T(8,128)(2,1)S(1)} %away_own.1.after_ref), channel_id=1, source_target_pairs={{0,4},{1,5},{2,0},{3,1},{4,6},{5,7},{6,2},{7,3},{8,12},{9,13},{10,... | collective-permute-start | bytes 307208 | tf_op jit(solution)/shard_map/ppermute | solution.py:263
  2.5 1.2 %home_rows.1.x_ref = bf16[1,200,2048]{2,1,0:T(8,128)(2,1)S(1)} custom-call(bf16[1,2,200,128]{3,2,1,0:T(8,128)(2,1)S(1)} %away_own.1.after_ref, bf16[1,200,2048]{2,1,0:T(8,128)(2,1)} %x_hbm.5), custom_call_target="tpu_custom_call" | custom-call | tf_op jit(solution)/shard_map/home_rows/pallas_call | solution.py:357
  3.6 0.0 collective-permute-done.w_other_ref
  3.6 0.4 %home_other.1.after_ref = bf16[1,2,200,128]{3,2,1,0:T(8,128)(2,1)S(1)} custom-call(bf16[1,200,2048]{2,1,0:T(8,128)(2,1)S(1)} %home_rows.1.x_ref, bf16[2,2048,128]{2,1,0:T(8,128)(2,1)S(1)} %collective-permute-done.w_other_ref), custom_call_target="tpu_custom_call" | custom-call | flops 209715200 | tf_op jit(solution)/shard_map/home_other/pallas_call | solution.py:365
  4.1 2.9 %collective-permute-start.2 = (bf16[1,2,200,128]{3,2,1,0:T(8,128)(2,1)S(1)}, bf16[1,2,200,128]{3,2,1,0:T(8,128)(2,1)S(1)}, u32[]{:S(2)}, u32[]{:S(2)}) collective-permute-start(bf16[1,2,200,128]{3,2,1,0:T(8,128)(2,1)S(1)} %home_other.1.after_ref), channel_id=1, source_target_pairs={{0,2},{1,3},{2,6},{3,7},{4,0},{5,1},{6,4},{7,5},{8,10},{9,11},{10,... | collective-permute-start | bytes 307208 | tf_op jit(solution)/shard_map/ppermute | solution.py:263
  7.0 2.0 %keep_queries.1 = (bf16[1,2,200,128]{3,2,1,0:T(8,128)(2,1)S(1)}, bf16[128,512]{1,0:T(8,128)(2,1)S(1)}, f32[4,512]{1,0:T(4,128)S(1)}, f32[1,128]{1,0:T(1,128)S(1)}) custom-call(bf16[1,2,200,128]{3,2,1,0:T(8,128)(2,1)S(1)} %home_other.1.after_ref, bf16[2,2048,128]{2,1,0:T(8,128)(2,1)S(1)} %collective-permute-done.w_other_ref, bf16[1,200,2048]{2,1,0:T(8,128)(2,1)} %x_hbm.5, ...), custom_call_target="tpu_custom_call" | custom-call | flops 209715200 | tf_op jit(solution)/shard_map/keep_queries/pallas_call | solution.py:369
  9.0 0.0 collective-permute-done.1.first_ref
  9.1 3.5 %collective-permute-start.5 = (bf16[1,2,200,128]{3,2,1,0:T(8,128)(2,1)S(1)}, bf16[1,2,200,128]{3,2,1,0:T(8,128)(2,1)S(1)}, u32[]{:S(2)}, u32[]{:S(2)}) collective-permute-start(bf16[1,2,200,128]{3,2,1,0:T(8,128)(2,1)S(1)} %first_sum.1.first_sum_ref), channel_id=1, source_target_pairs={{0,1},{1,0},{2,2},{3,3},{4,4},{5,5},{6,7},{7,6},{8,9},{9,8},{10,10... | collective-permute-start | bytes 307208 | tf_op jit(solution)/shard_map/ppermute | solution.py:263
  12.6 0.0 collective-permute-done.2.second_ref
  12.6 0.7 %collective-permute-start.6 = (bf16[1,2,200,128]{3,2,1,0:T(8,128)(2,1)S(1)}, bf16[1,2,200,128]{3,2,1,0:T(8,128)(2,1)S(1)}, u32[]{:S(2)}, u32[]{:S(2)}) collective-permute-start(bf16[1,2,200,128]{3,2,1,0:T(8,128)(2,1)S(1)} %second_sum.1.keep_ref), channel_id=1, source_target_pairs={{0,0},{1,1},{2,3},{3,2},{4,5},{5,4},{6,6},{7,7},{8,8},{9,9},{10,11... | collective-permute-start | bytes 307208 | tf_op jit(solution)/shard_map/ppermute | solution.py:263
  13.3 2.5 %collective-permute-start.3 = (bf16[1,2,200,128]{3,2,1,0:T(8,128)(2,1)S(1)}, bf16[1,2,200,128]{3,2,1,0:T(8,128)(2,1)S(1)}, u32[]{:S(2)}, u32[]{:S(2)}) collective-permute-start(bf16[1,2,200,128]{3,2,1,0:T(8,128)(2,1)S(1)} %second_sum.1.keep_ref), channel_id=1, source_target_pairs={{0,24},{8,16},{16,8},{24,0},{1,25},{9,17},{17,9},{25,1},{2,26},{10... | collective-permute-start | bytes 307208 | tf_op jit(solution)/shard_map/ppermute | solution.py:254
  15.8 0.0 collective-permute-done.5.refs_0_
  15.8 0.0 collective-permute-done.6.refs_1_
  15.8 0.1 sum_norm.1.refs_0_
  16.0 1.4 %collective-permute-start.8 = (bf16[2,200,128]{2,1,0:T(8,128)(2,1)S(1)}, bf16[2,200,128]{2,1,0:T(8,128)(2,1)S(1)}, u32[]{:S(2)}, u32[]{:S(2)}) collective-permute-start(bf16[2,200,128]{2,1,0:T(8,128)(2,1)S(1)} %sum_norm.1.refs_0_), channel_id=1, source_target_pairs={{0,16},{8,24},{16,0},{24,8},{1,17},{9,25},{17,1},{25,9},{2,18},{10... | collective-permute-start | bytes 307208 | tf_op jit(solution)/shard_map/ppermute | solution.py:254
  17.4 1.5 %collective-permute-start.7 = (bf16[2,200,128]{2,1,0:T(8,128)(2,1)S(1)}, bf16[2,200,128]{2,1,0:T(8,128)(2,1)S(1)}, u32[]{:S(2)}, u32[]{:S(2)}) collective-permute-start(bf16[2,200,128]{2,1,0:T(8,128)(2,1)S(1)} %sum_norm.1.refs_0_), channel_id=1, source_target_pairs={{0,8},{8,0},{16,24},{24,16},{1,9},{9,1},{17,25},{25,17},{2,10},{10... | collective-permute-start | bytes 307208 | tf_op jit(solution)/shard_map/ppermute | solution.py:254
  18.9 0.6 %collective-permute-done.3.refs_0_ = bf16[1,2,200,128]{3,2,1,0:T(8,128)(2,1)S(1)} collective-permute-done((bf16[1,2,200,128]{3,2,1,0:T(8,128)(2,1)S(1)}, bf16[1,2,200,128]{3,2,1,0:T(8,128)(2,1)S(1)}, u32[]{:S(2)}, u32[]{:S(2)}) %collective-permute-start.3) | collective-permute-done | bytes 102432 | tf_op jit(solution)/shard_map/ppermute | solution.py:254
  19.5 1.7 %collective-permute-start.4 = (bf16[1,2,200,128]{3,2,1,0:T(8,128)(2,1)S(1)}, bf16[1,2,200,128]{3,2,1,0:T(8,128)(2,1)S(1)}, u32[]{:S(2)}, u32[]{:S(2)}) collective-permute-start(bf16[1,2,200,128]{3,2,1,0:T(8,128)(2,1)S(1)} %collective-permute-done.3.refs_0_), channel_id=1, source_target_pairs={{0,1},{1,0},{2,3},{3,2},{4,5},{5,4},{6,7},{7,6},{8,9},{9,8},{10,11... | collective-permute-start | bytes 307208 | tf_op jit(solution)/shard_map/ppermute | solution.py:254
  21.2 0.4 %attend.3 = (f32[1,512]{1,0:T(1,128)S(1)}, f32[1,512]{1,0:T(1,128)S(1)}, f32[128,512]{1,0:T(8,128)S(1)}) custom-call(f32[1,128]{1,0:T(1,128)S(1)} %get-tuple-element.15.k_gain_ref, bf16[128,512]{1,0:T(8,128)(2,1)S(1)} %get-tuple-element.16.qt_ref, f32[4,512]{1,0:T(4,128)S(1)} %get-tuple-element.17.bias_ref, bf16[2,200,128]{2,1,0:T(8,128)(2,1)S(1)} %sum_norm.1.refs_0_), custom_call_target="tpu_custom_call" | custom-call | flops 52428800 | tf_op jit(solution)/shard_map/attend/pallas_call | solution.py:431
  21.6 0.0 collective-permute-done.8.refs_1_
  21.6 1.2 %collective-permute-done.7.refs_0_ = bf16[2,200,128]{2,1,0:T(8,128)(2,1)S(1)} collective-permute-done((bf16[2,200,128]{2,1,0:T(8,128)(2,1)S(1)}, bf16[2,200,128]{2,1,0:T(8,128)(2,1)S(1)}, u32[]{:S(2)}, u32[]{:S(2)}) %collective-permute-start.7) | collective-permute-done | bytes 102432 | tf_op jit(solution)/shard_map/ppermute | solution.py:254
  22.8 0.6 %attend.4 = (f32[1,512]{1,0:T(1,128)S(1)}, f32[1,512]{1,0:T(1,128)S(1)}, f32[128,512]{1,0:T(8,128)S(1)}) custom-call(f32[1,128]{1,0:T(1,128)S(1)} %get-tuple-element.15.k_gain_ref, bf16[128,512]{1,0:T(8,128)(2,1)S(1)} %get-tuple-element.16.qt_ref, f32[4,512]{1,0:T(4,128)S(1)} %get-tuple-element.17.bias_ref, ...), custom_call_target="tpu_custom_call" | custom-call | flops 104857600 | tf_op jit(solution)/shard_map/attend/pallas_call | solution.py:431
  23.4 1.2 %collective-permute-done.4.refs_1_ = bf16[1,2,200,128]{3,2,1,0:T(8,128)(2,1)S(1)} collective-permute-done((bf16[1,2,200,128]{3,2,1,0:T(8,128)(2,1)S(1)}, bf16[1,2,200,128]{3,2,1,0:T(8,128)(2,1)S(1)}, u32[]{:S(2)}, u32[]{:S(2)}) %collective-permute-start.4) | collective-permute-done | bytes 102432 | tf_op jit(solution)/shard_map/ppermute | solution.py:254
  24.7 1.3 %attend.5 = bf16[128,512]{1,0:T(8,128)(2,1)} custom-call(f32[1,128]{1,0:T(1,128)S(1)} %get-tuple-element.15.k_gain_ref, bf16[128,512]{1,0:T(8,128)(2,1)S(1)} %get-tuple-element.16.qt_ref, f32[4,512]{1,0:T(4,128)S(1)} %get-tuple-element.17.bias_ref, bf16[1,2,200,128]{3,2,1,0:T(8,128)(2,1)S(1)} %collective-permute-done.3.refs_0_, ...), custom_call_target="tpu_custom_call" | custom-call | flops 52428800 | tf_op jit(solution)/shard_map/attend/pallas_call | solution.py:431
  (3 shorter events, 0.1 us)
Async XLA Ops:
  0.0 3.6 %collective-permute-start = (bf16[2,2048,128]{2,1,0:T(8,128)(2,1)}, bf16[2,2048,128]{2,1,0:T(8,128)(2,1)S(1)}, u32[]{:S(2)}, u32[]{:S(2)}) collective-permute-start(bf16[2,2048,128]{2,1,0:T(8,128)(2,1)} %w_hbm.3), channel_id=1, source_target_pairs={{0,4},{4,0},{1,5},{5,1},{2,6},{6,2},{3,7},{7,3},{8,12},{12,8},{9,1... | collective-permute-start | bytes 3145736 | tf_op jit(solution)/shard_map/ppermute | solution.py:254
  0.5 8.6 %collective-permute-start.1 = (bf16[1,2,200,128]{3,2,1,0:T(8,128)(2,1)S(1)}, bf16[1,2,200,128]{3,2,1,0:T(8,128)(2,1)S(1)}, u32[]{:S(2)}, u32[]{:S(2)}) collective-permute-start(bf16[1,2,200,128]{3,2,1,0:T(8,128)(2,1)S(1)} %away_own.1.after_ref), channel_id=1, source_target_pairs={{0,4},{1,5},{2,0},{3,1},{4,6},{5,7},{6,2},{7,3},{8,12},{9,13},{10,... | collective-permute-start | bytes 307208 | tf_op jit(solution)/shard_map/ppermute | solution.py:263
  4.1 8.5 %collective-permute-start.2 = (bf16[1,2,200,128]{3,2,1,0:T(8,128)(2,1)S(1)}, bf16[1,2,200,128]{3,2,1,0:T(8,128)(2,1)S(1)}, u32[]{:S(2)}, u32[]{:S(2)}) collective-permute-start(bf16[1,2,200,128]{3,2,1,0:T(8,128)(2,1)S(1)} %home_other.1.after_ref), channel_id=1, source_target_pairs={{0,2},{1,3},{2,6},{3,7},{4,0},{5,1},{6,4},{7,5},{8,10},{9,11},{10,... | collective-permute-start | bytes 307208 | tf_op jit(solution)/shard_map/ppermute | solution.py:263
  9.1 6.7 %collective-permute-start.5 = (bf16[1,2,200,128]{3,2,1,0:T(8,128)(2,1)S(1)}, bf16[1,2,200,128]{3,2,1,0:T(8,128)(2,1)S(1)}, u32[]{:S(2)}, u32[]{:S(2)}) collective-permute-start(bf16[1,2,200,128]{3,2,1,0:T(8,128)(2,1)S(1)} %first_sum.1.first_sum_ref), channel_id=1, source_target_pairs={{0,1},{1,0},{2,2},{3,3},{4,4},{5,5},{6,7},{7,6},{8,9},{9,8},{10,10... | collective-permute-start | bytes 307208 | tf_op jit(solution)/shard_map/ppermute | solution.py:263
  12.6 3.2 %collective-permute-start.6 = (bf16[1,2,200,128]{3,2,1,0:T(8,128)(2,1)S(1)}, bf16[1,2,200,128]{3,2,1,0:T(8,128)(2,1)S(1)}, u32[]{:S(2)}, u32[]{:S(2)}) collective-permute-start(bf16[1,2,200,128]{3,2,1,0:T(8,128)(2,1)S(1)} %second_sum.1.keep_ref), channel_id=1, source_target_pairs={{0,0},{1,1},{2,3},{3,2},{4,5},{5,4},{6,6},{7,7},{8,8},{9,9},{10,11... | collective-permute-start | bytes 307208 | tf_op jit(solution)/shard_map/ppermute | solution.py:263
  13.3 6.2 %collective-permute-start.3 = (bf16[1,2,200,128]{3,2,1,0:T(8,128)(2,1)S(1)}, bf16[1,2,200,128]{3,2,1,0:T(8,128)(2,1)S(1)}, u32[]{:S(2)}, u32[]{:S(2)}) collective-permute-start(bf16[1,2,200,128]{3,2,1,0:T(8,128)(2,1)S(1)} %second_sum.1.keep_ref), channel_id=1, source_target_pairs={{0,24},{8,16},{16,8},{24,0},{1,25},{9,17},{17,9},{25,1},{2,26},{10... | collective-permute-start | bytes 307208 | tf_op jit(solution)/shard_map/ppermute | solution.py:254
  16.0 5.6 %collective-permute-start.8 = (bf16[2,200,128]{2,1,0:T(8,128)(2,1)S(1)}, bf16[2,200,128]{2,1,0:T(8,128)(2,1)S(1)}, u32[]{:S(2)}, u32[]{:S(2)}) collective-permute-start(bf16[2,200,128]{2,1,0:T(8,128)(2,1)S(1)} %sum_norm.1.refs_0_), channel_id=1, source_target_pairs={{0,16},{8,24},{16,0},{24,8},{1,17},{9,25},{17,1},{25,9},{2,18},{10... | collective-permute-start | bytes 307208 | tf_op jit(solution)/shard_map/ppermute | solution.py:254
  17.4 5.5 %collective-permute-start.7 = (bf16[2,200,128]{2,1,0:T(8,128)(2,1)S(1)}, bf16[2,200,128]{2,1,0:T(8,128)(2,1)S(1)}, u32[]{:S(2)}, u32[]{:S(2)}) collective-permute-start(bf16[2,200,128]{2,1,0:T(8,128)(2,1)S(1)} %sum_norm.1.refs_0_), channel_id=1, source_target_pairs={{0,8},{8,0},{16,24},{24,16},{1,9},{9,1},{17,25},{25,17},{2,10},{10... | collective-permute-start | bytes 307208 | tf_op jit(solution)/shard_map/ppermute | solution.py:254
  19.5 5.2 %collective-permute-start.4 = (bf16[1,2,200,128]{3,2,1,0:T(8,128)(2,1)S(1)}, bf16[1,2,200,128]{3,2,1,0:T(8,128)(2,1)S(1)}, u32[]{:S(2)}, u32[]{:S(2)}) collective-permute-start(bf16[1,2,200,128]{3,2,1,0:T(8,128)(2,1)S(1)} %collective-permute-done.3.refs_0_), channel_id=1, source_target_pairs={{0,1},{1,0},{2,3},{3,2},{4,5},{5,4},{6,7},{7,6},{8,9},{9,8},{10,11... | collective-permute-start | bytes 307208 | tf_op jit(solution)/shard_map/ppermute | solution.py:254

commit v13 on v10

--- a/solution.py
+++ b/solution.py
@@ -23,7 +23,7 @@
 
 
 def call(
-    kernel, outs, n_in, name, flops=0, size=0, exps=0, in_specs=None, scratch=()
+    kernel, outs, n_in, name, flops=0, size=0, exps=0, in_specs=None, scratch=(), aliases=None
 ):
     many = isinstance(outs, list)
     return pl.pallas_call(
@@ -32,6 +32,7 @@
         in_specs=in_specs or [VMEM] * n_in,
         out_specs=[VMEM] * len(outs) if many else VMEM,
         scratch_shapes=scratch,
+        input_output_aliases=aliases or {},
         compiler_params=pltpu.CompilerParams(vmem_limit_bytes=LIMIT),
         cost_estimate=pl.CostEstimate(flops=flops, bytes_accessed=size, transcendentals=exps),
         name=name,
@@ -70,9 +71,9 @@
         bias_ref[:, head * tokens : (head + 1) * tokens] = bias
 
 
-def start_copies(sources, targets, sems, first=0):
+def start_copies(sources, targets, sems):
     copies = [
-        pltpu.make_async_copy(a, b, sems.at[first + i]) for i, (a, b) in enumerate(zip(sources, targets))
+        pltpu.make_async_copy(a, b, sems.at[i]) for i, (a, b) in enumerate(zip(sources, targets))
     ]
     for copy in copies:
         copy.start()
@@ -113,10 +114,10 @@
         own_kernel(head_dim, x_hbm, w_hbm, own_ref, x_ref, w_ref, sems)
 
 
-def load_kernel(after_ref, x_hbm, x_ref, sems):
+def load_kernel(x_in, x_hbm, w_hbm, x_ref, w_ref, sems):
     @pl.when(is_home())
     def _():
-        for copy in start_copies((x_hbm,), (x_ref,), sems):
+        for copy in start_copies((x_hbm, w_hbm), (x_ref, w_ref), sems):
             copy.wait()
 
 
@@ -131,24 +132,22 @@
 
 
 def keep_kernel(
-    head_dim, after_ref, w_other_ref, x_hbm, w_hbm, q_hbm, q_gain_hbm, mask_hbm, k_gain_hbm,
-    keep_ref, qt_ref, bias_ref, k_gain_ref, x_ref, w_ref, q_ref, q_gain_ref, mask_ref, sems,
+    head_dim, after_ref, w_other_ref, x_ref, w_ref, q_hbm, q_gain_hbm, mask_hbm, k_gain_hbm,
+    keep_ref, qt_ref, bias_ref, k_gain_ref, q_ref, q_gain_ref, mask_ref, sems,
 ):
     copies = start_copies(
         (q_hbm, q_gain_hbm, mask_hbm, k_gain_hbm), (q_ref, q_gain_ref, mask_ref, k_gain_ref), sems
     )
-    moves = start_copies((x_hbm, w_hbm), (x_ref, w_ref), sems, len(copies))
+
+    @pl.when(is_home())
+    def _():
+        store_heads(keep_ref, 0, project(x_ref[0], w_ref[...]), head_dim)
+
+    @pl.when(jnp.logical_not(is_home()))
+    def _():
+        store_heads(keep_ref, 0, project(x_ref[0], w_other_ref[...]), head_dim)
+
     prepare_queries(copies, q_ref, q_gain_ref, mask_ref, qt_ref, bias_ref)
-    for copy in moves:
-        copy.wait()
-
-    @pl.when(is_home())
-    def _():
-        store_heads(keep_ref, 0, project(x_ref[0], w_ref[...]), head_dim)
-
-    @pl.when(jnp.logical_not(is_home()))
-    def _():
-        store_heads(keep_ref, 0, project(x_ref[0], w_other_ref[...]), head_dim)
 
 
 def split_half(held, send_ref, keep_ref, partner_heads, own_heads):
@@ -307,7 +306,7 @@
         )
     ]
     product = shape_of((own_heads, 2, rows, head_dim))
-    x_scratch, w_scratch = pltpu.VMEM(images.shape, BF16), pltpu.VMEM(kv_weight.shape, BF16)
+    w_scratch = pltpu.VMEM(kv_weight.shape, BF16)
     prepared = [
         shape_of((head_dim, pairs)),
         shape_of((tiles, pairs), F32),
@@ -320,27 +319,28 @@
     ]
     others = [swap(kv_weight, "dp", k) for k in range(1, n_dp)]
     if n_dp == 2 and own_heads == 1:
-        away = call(
+        away, x_away = call(
             functools.partial(away_kernel, head_dim),
-            product,
+            [product, shape_of(images.shape)],
             2,
             "away_own",
             flops=work,
             in_specs=[HBM] * 2,
-            scratch=[x_scratch, w_scratch, pltpu.SemaphoreType.DMA((2,))],
+            scratch=[w_scratch, pltpu.SemaphoreType.DMA((2,))],
         )(x, w)
         first = exchange_two_heads(away, False)
-        x_home = call(
+        x_here, w_home = call(
             load_kernel,
-            shape_of(images.shape),
-            2,
-            "home_rows",
-            in_specs=[VMEM, HBM],
-            scratch=[pltpu.SemaphoreType.DMA((1,))],
-        )(away, x)
+            [shape_of(images.shape), shape_of(kv_weight.shape)],
+            3,
+            "home_load",
+            in_specs=[VMEM] + [HBM] * 2,
+            scratch=[pltpu.SemaphoreType.DMA((2,))],
+            aliases={0: 0},
+        )(x_away, x, w)
         home = call(
             functools.partial(home_kernel, head_dim), product, 2, "home_other", flops=work
-        )(x_home, others[0])
+        )(x_here, others[0])
         second = exchange_two_heads(home, True)
         keep, qt, bias, gain = call(
             functools.partial(keep_kernel, head_dim),
@@ -348,9 +348,9 @@
             8,
             "keep_queries",
             flops=work,
-            in_specs=[VMEM] * 2 + [HBM] * 6,
-            scratch=[x_scratch, w_scratch, *query_scratch, pltpu.SemaphoreType.DMA((6,))],
-        )(home, others[0], x, w, *small)
+            in_specs=[VMEM] * 4 + [HBM] * 4,
+            scratch=[*query_scratch, pltpu.SemaphoreType.DMA((4,))],
+        )(home, others[0], x_here, w_home, *small)
         total = call(pair_kernel, product, 3, "pair_sum")(keep, first, second)
     else:
         own, x_here = call(

time: 24.3 us -> 24.2 us (level)
  waiting for transfers between devices: 2.05 us -> 2.81 us
  Pallas kernels: 6.07 us -> 5.64 us
  starting transfers between devices: 15.9 us -> 15.6 us
    ppermute x2, waiting for transfers between devices: 0.19 us -> 0.96 us  [exchange_two_heads(): return lax.ppermute(value, ('dp', 'tensor'), hops)]
    pallas_call x1, Pallas kernels: 2.05 us -> 1.28 us  [on_device(): call(functools.partial(keep_kernel, head_dim), [product, *prepared], 8, '...]
    ppermute x2, starting transfers between devices: 4.9 us -> 4.56 us  [exchange_two_heads(): return lax.ppermute(value, ('dp', 'tensor'), hops)]
    pallas_call x2, Pallas kernels: 1.18 us -> 1.52 us  [the longest x1 1.49 us: on_device(): call(load_kernel, [shape_of(images.shape), shape_of(kv_weight.shape)], 3,...]
  transfers between devices with their start and end apart: 8 -> 8, of which waited for: 4 -> 5; matrix products, arithmetic and copies ran while one was open for 0% -> 0% of each run, Pallas kernels for 20% -> 18%
where the time goes in v13:
time: 24.2 us; the launch traced here: 24.1 us
  starting transfers between devices  15.6 us (64%)
  Pallas kernels  5.64 us (23%)
  waiting for transfers between devices  2.81 us (12%)
    ppermute x6, starting transfers between devices, swap(): lax.ppermute(value, axis, [(i, i ^ k) for i in range(lax.axis_size(axis))])  11 us
    ppermute x2, starting transfers between devices, exchange_two_heads(): return lax.ppermute(value, ('dp', 'tensor'), hops)  4.56 us
    pallas_call x3, Pallas kernels, on_device(): call(functools.partial(attend_kernel, here, there, tile_len, first, last,...  2.26 us
    ppermute x6, waiting for transfers between devices, swap(): lax.ppermute(value, axis, [(i, i ^ k) for i in range(lax.axis_size(axis))])  1.85 us
    pallas_call x1, Pallas kernels, on_device(): call(load_kernel, [shape_of(images.shape), shape_of(kv_weight.shape)], 3,...  1.49 us
    pallas_call x1, Pallas kernels, on_device(): call(functools.partial(keep_kernel, head_dim), [product, *prepared], 8, '...  1.28 us
    ppermute x2, waiting for transfers between devices, exchange_two_heads(): return lax.ppermute(value, ('dp', 'tensor'), hops)  0.96 us
  transfers between devices with their start and end apart: 8, of which 5 were waited for; matrix products, arithmetic and copies ran while one was open for 0% of the time, Pallas kernels for 18%

profile of v13, /device:TPU:0, one launch (start us, length us, event | category | flops | bytes accessed | tf_op | source)
XLA Modules:
  0.0 24.1 jit_solution(145787029486460827)
XLA Ops:
  0.0 0.5 %collective-permute-start = (bf16[2,2048,128]{2,1,0:T(8,128)(2,1)}, bf16[2,2048,128]{2,1,0:T(8,128)(2,1)S(1)}, u32[]{:S(2)}, u32[]{:S(2)}) collective-permute-start(bf16[2,2048,128]{2,1,0:T(8,128)(2,1)} %w_hbm.3), channel_id=1, source_target_pairs={{0,4},{4,0},{1,5},{5,1},{2,6},{6,2},{3,7},{7,3},{8,12},{12,8},{9,1... | collective-permute-start | bytes 3145736 | tf_op jit(solution)/shard_map/ppermute | solution.py:245
  0.5 2.0 %collective-permute-start.1 = (bf16[1,2,200,128]{3,2,1,0:T(8,128)(2,1)S(1)}, bf16[1,2,200,128]{3,2,1,0:T(8,128)(2,1)S(1)}, u32[]{:S(2)}, u32[]{:S(2)}) collective-permute-start(bf16[1,2,200,128]{3,2,1,0:T(8,128)(2,1)S(1)} %get-tuple-element.26), channel_id=1, source_target_pairs={{0,4},{1,5},{2,0},{3,1},{4,6},{5,7},{6,2},{7,3},{8,12},{9,13},{10,... | collective-permute-start | bytes 307208 | tf_op jit(solution)/shard_map/ppermute | solution.py:254
  2.5 1.5 %home_load.1 = (bf16[1,200,2048]{2,1,0:T(8,128)(2,1)S(1)}, bf16[2,2048,128]{2,1,0:T(8,128)(2,1)S(1)}) custom-call(bf16[1,200,2048]{2,1,0:T(8,128)(2,1)S(1)} %get-tuple-element.19.x_in, bf16[1,200,2048]{2,1,0:T(8,128)(2,1)} %x_hbm.3, bf16[2,2048,128]{2,1,0:T(8,128)(2,1)} %w_hbm.3), custom_call_target="tpu_custom_call", output_to_operand_aliasing={{0}: (0, {})} | custom-call | tf_op jit(solution)/shard_map/home_load/pallas_call | solution.py:332
  4.0 0.0 collective-permute-done.w_other_ref
  4.0 0.4 %home_other.1.after_ref = bf16[1,2,200,128]{3,2,1,0:T(8,128)(2,1)S(1)} custom-call(bf16[1,200,2048]{2,1,0:T(8,128)(2,1)S(1)} %get-tuple-element.20.x_ref, bf16[2,2048,128]{2,1,0:T(8,128)(2,1)S(1)} %collective-permute-done.w_other_ref), custom_call_target="tpu_custom_call" | custom-call | flops 209715200 | tf_op jit(solution)/shard_map/home_other/pallas_call | solution.py:341
  4.4 2.6 %collective-permute-start.2 = (bf16[1,2,200,128]{3,2,1,0:T(8,128)(2,1)S(1)}, bf16[1,2,200,128]{3,2,1,0:T(8,128)(2,1)S(1)}, u32[]{:S(2)}, u32[]{:S(2)}) collective-permute-start(bf16[1,2,200,128]{3,2,1,0:T(8,128)(2,1)S(1)} %home_other.1.after_ref), channel_id=1, source_target_pairs={{0,2},{1,3},{2,6},{3,7},{4,0},{5,1},{6,4},{7,5},{8,10},{9,11},{10,... | collective-permute-start | bytes 307208 | tf_op jit(solution)/shard_map/ppermute | solution.py:254
  7.0 1.3 %keep_queries.1 = (bf16[1,2,200,128]{3,2,1,0:T(8,128)(2,1)S(1)}, bf16[128,512]{1,0:T(8,128)(2,1)S(1)}, f32[4,512]{1,0:T(4,128)S(1)}, f32[1,128]{1,0:T(1,128)S(1)}) custom-call(bf16[1,2,200,128]{3,2,1,0:T(8,128)(2,1)S(1)} %home_other.1.after_ref, bf16[2,2048,128]{2,1,0:T(8,128)(2,1)S(1)} %collective-permute-done.w_other_ref, ...), custom_call_target="tpu_custom_call" | custom-call | flops 209715200 | tf_op jit(solution)/shard_map/keep_queries/pallas_call | solution.py:345
  8.3 0.4 %collective-permute-done.1.first_ref = bf16[1,2,200,128]{3,2,1,0:T(8,128)(2,1)S(1)} collective-permute-done((bf16[1,2,200,128]{3,2,1,0:T(8,128)(2,1)S(1)}, bf16[1,2,200,128]{3,2,1,0:T(8,128)(2,1)S(1)}, u32[]{:S(2)}, u32[]{:S(2)}) %collective-permute-start.1) | collective-permute-done | bytes 102432 | tf_op jit(solution)/shard_map/ppermute | solution.py:254
  8.7 0.6 %collective-permute-done.2.second_ref = bf16[1,2,200,128]{3,2,1,0:T(8,128)(2,1)S(1)} collective-permute-done((bf16[1,2,200,128]{3,2,1,0:T(8,128)(2,1)S(1)}, bf16[1,2,200,128]{3,2,1,0:T(8,128)(2,1)S(1)}, u32[]{:S(2)}, u32[]{:S(2)}) %collective-permute-start.2) | collective-permute-done | bytes 102432 | tf_op jit(solution)/shard_map/ppermute | solution.py:254
  9.3 2.6 %collective-permute-start.5 = (bf16[1,2,200,128]{3,2,1,0:T(8,128)(2,1)S(1)}, bf16[1,2,200,128]{3,2,1,0:T(8,128)(2,1)S(1)}, u32[]{:S(2)}, u32[]{:S(2)}) collective-permute-start(bf16[1,2,200,128]{3,2,1,0:T(8,128)(2,1)S(1)} %pair_sum.1.keep_ref), channel_id=1, source_target_pairs={{0,1},{1,0},{2,3},{3,2},{4,5},{5,4},{6,7},{7,6},{8,9},{9,8},{10,11... | collective-permute-start | bytes 307208 | tf_op jit(solution)/shard_map/ppermute | solution.py:245
  11.8 2.4 %collective-permute-start.3 = (bf16[1,2,200,128]{3,2,1,0:T(8,128)(2,1)S(1)}, bf16[1,2,200,128]{3,2,1,0:T(8,128)(2,1)S(1)}, u32[]{:S(2)}, u32[]{:S(2)}) collective-permute-start(bf16[1,2,200,128]{3,2,1,0:T(8,128)(2,1)S(1)} %pair_sum.1.keep_ref), channel_id=1, source_target_pairs={{0,24},{8,16},{16,8},{24,0},{1,25},{9,17},{17,9},{25,1},{2,26},{10... | collective-permute-start | bytes 307208 | tf_op jit(solution)/shard_map/ppermute | solution.py:245
  14.3 0.2 collective-permute-done.5.arrived_ref
  14.5 0.1 sum_norm.1.refs_0_
  14.6 1.6 %collective-permute-start.7 = (bf16[2,200,128]{2,1,0:T(8,128)(2,1)S(1)}, bf16[2,200,128]{2,1,0:T(8,128)(2,1)S(1)}, u32[]{:S(2)}, u32[]{:S(2)}) collective-permute-start(bf16[2,200,128]{2,1,0:T(8,128)(2,1)S(1)} %sum_norm.1.refs_0_), channel_id=1, source_target_pairs={{0,16},{8,24},{16,0},{24,8},{1,17},{9,25},{17,1},{25,9},{2,18},{10... | collective-permute-start | bytes 307208 | tf_op jit(solution)/shard_map/ppermute | solution.py:245
  16.2 1.5 %collective-permute-start.6 = (bf16[2,200,128]{2,1,0:T(8,128)(2,1)S(1)}, bf16[2,200,128]{2,1,0:T(8,128)(2,1)S(1)}, u32[]{:S(2)}, u32[]{:S(2)}) collective-permute-start(bf16[2,200,128]{2,1,0:T(8,128)(2,1)S(1)} %sum_norm.1.refs_0_), channel_id=1, source_target_pairs={{0,8},{8,0},{16,24},{24,16},{1,9},{9,1},{17,25},{25,17},{2,10},{10... | collective-permute-start | bytes 307208 | tf_op jit(solution)/shard_map/ppermute | solution.py:245
  17.7 0.0 collective-permute-done.3.refs_0_
  17.7 2.5 %collective-permute-start.4 = (bf16[1,2,200,128]{3,2,1,0:T(8,128)(2,1)S(1)}, bf16[1,2,200,128]{3,2,1,0:T(8,128)(2,1)S(1)}, u32[]{:S(2)}, u32[]{:S(2)}) collective-permute-start(bf16[1,2,200,128]{3,2,1,0:T(8,128)(2,1)S(1)} %collective-permute-done.3.refs_0_), channel_id=1, source_target_pairs={{0,1},{1,0},{2,3},{3,2},{4,5},{5,4},{6,7},{7,6},{8,9},{9,8},{10,11... | collective-permute-start | bytes 307208 | tf_op jit(solution)/shard_map/ppermute | solution.py:245
  20.2 0.4 %attend.3 = (f32[1,512]{1,0:T(1,128)S(1)}, f32[1,512]{1,0:T(1,128)S(1)}, f32[128,512]{1,0:T(8,128)S(1)}) custom-call(f32[1,128]{1,0:T(1,128)S(1)} %get-tuple-element.22.k_gain_ref, bf16[128,512]{1,0:T(8,128)(2,1)S(1)} %get-tuple-element.23.qt_ref, f32[4,512]{1,0:T(4,128)S(1)} %get-tuple-element.24.bias_ref, bf16[2,200,128]{2,1,0:T(8,128)(2,1)S(1)} %sum_norm.1.refs_0_), custom_call_target="tpu_custom_call" | custom-call | flops 52428800 | tf_op jit(solution)/shard_map/attend/pallas_call | solution.py:402
  20.6 0.0 collective-permute-done.7.refs_1_
  20.6 1.0 %collective-permute-done.6.refs_0_ = bf16[2,200,128]{2,1,0:T(8,128)(2,1)S(1)} collective-permute-done((bf16[2,200,128]{2,1,0:T(8,128)(2,1)S(1)}, bf16[2,200,128]{2,1,0:T(8,128)(2,1)S(1)}, u32[]{:S(2)}, u32[]{:S(2)}) %collective-permute-start.6) | collective-permute-done | bytes 102432 | tf_op jit(solution)/shard_map/ppermute | solution.py:245
  21.6 0.6 %attend.4 = (f32[1,512]{1,0:T(1,128)S(1)}, f32[1,512]{1,0:T(1,128)S(1)}, f32[128,512]{1,0:T(8,128)S(1)}) custom-call(f32[1,128]{1,0:T(1,128)S(1)} %get-tuple-element.22.k_gain_ref, bf16[128,512]{1,0:T(8,128)(2,1)S(1)} %get-tuple-element.23.qt_ref, f32[4,512]{1,0:T(4,128)S(1)} %get-tuple-element.24.bias_ref, ...), custom_call_target="tpu_custom_call" | custom-call | flops 104857600 | tf_op jit(solution)/shard_map/attend/pallas_call | solution.py:402
  22.2 0.6 %collective-permute-done.4.refs_1_ = bf16[1,2,200,128]{3,2,1,0:T(8,128)(2,1)S(1)} collective-permute-done((bf16[1,2,200,128]{3,2,1,0:T(8,128)(2,1)S(1)}, bf16[1,2,200,128]{3,2,1,0:T(8,128)(2,1)S(1)}, u32[]{:S(2)}, u32[]{:S(2)}) %collective-permute-start.4) | collective-permute-done | bytes 102432 | tf_op jit(solution)/shard_map/ppermute | solution.py:245
  22.8 1.3 %attend.5 = bf16[128,512]{1,0:T(8,128)(2,1)} custom-call(f32[1,128]{1,0:T(1,128)S(1)} %get-tuple-element.22.k_gain_ref, bf16[128,512]{1,0:T(8,128)(2,1)S(1)} %get-tuple-element.23.qt_ref, f32[4,512]{1,0:T(4,128)S(1)} %get-tuple-element.24.bias_ref, bf16[1,2,200,128]{3,2,1,0:T(8,128)(2,1)S(1)} %collective-permute-done.3.refs_0_, ...), custom_call_target="tpu_custom_call" | custom-call | flops 52428800 | tf_op jit(solution)/shard_map/attend/pallas_call | solution.py:402
  (2 shorter events, 0.1 us)
Async XLA Ops:
  0.0 4.0 %collective-permute-start = (bf16[2,2048,128]{2,1,0:T(8,128)(2,1)}, bf16[2,2048,128]{2,1,0:T(8,128)(2,1)S(1)}, u32[]{:S(2)}, u32[]{:S(2)}) collective-permute-start(bf16[2,2048,128]{2,1,0:T(8,128)(2,1)} %w_hbm.3), channel_id=1, source_target_pairs={{0,4},{4,0},{1,5},{5,1},{2,6},{6,2},{3,7},{7,3},{8,12},{12,8},{9,1... | collective-permute-start | bytes 3145736 | tf_op jit(solution)/shard_map/ppermute | solution.py:245
  0.5 8.2 %collective-permute-start.1 = (bf16[1,2,200,128]{3,2,1,0:T(8,128)(2,1)S(1)}, bf16[1,2,200,128]{3,2,1,0:T(8,128)(2,1)S(1)}, u32[]{:S(2)}, u32[]{:S(2)}) collective-permute-start(bf16[1,2,200,128]{3,2,1,0:T(8,128)(2,1)S(1)} %get-tuple-element.26), channel_id=1, source_target_pairs={{0,4},{1,5},{2,0},{3,1},{4,6},{5,7},{6,2},{7,3},{8,12},{9,13},{10,... | collective-permute-start | bytes 307208 | tf_op jit(solution)/shard_map/ppermute | solution.py:254
  4.4 4.8 %collective-permute-start.2 = (bf16[1,2,200,128]{3,2,1,0:T(8,128)(2,1)S(1)}, bf16[1,2,200,128]{3,2,1,0:T(8,128)(2,1)S(1)}, u32[]{:S(2)}, u32[]{:S(2)}) collective-permute-start(bf16[1,2,200,128]{3,2,1,0:T(8,128)(2,1)S(1)} %home_other.1.after_ref), channel_id=1, source_target_pairs={{0,2},{1,3},{2,6},{3,7},{4,0},{5,1},{6,4},{7,5},{8,10},{9,11},{10,... | collective-permute-start | bytes 307208 | tf_op jit(solution)/shard_map/ppermute | solution.py:254
  9.3 5.2 %collective-permute-start.5 = (bf16[1,2,200,128]{3,2,1,0:T(8,128)(2,1)S(1)}, bf16[1,2,200,128]{3,2,1,0:T(8,128)(2,1)S(1)}, u32[]{:S(2)}, u32[]{:S(2)}) collective-permute-start(bf16[1,2,200,128]{3,2,1,0:T(8,128)(2,1)S(1)} %pair_sum.1.keep_ref), channel_id=1, source_target_pairs={{0,1},{1,0},{2,3},{3,2},{4,5},{5,4},{6,7},{7,6},{8,9},{9,8},{10,11... | collective-permute-start | bytes 307208 | tf_op jit(solution)/shard_map/ppermute | solution.py:245
  11.8 5.8 %collective-permute-start.3 = (bf16[1,2,200,128]{3,2,1,0:T(8,128)(2,1)S(1)}, bf16[1,2,200,128]{3,2,1,0:T(8,128)(2,1)S(1)}, u32[]{:S(2)}, u32[]{:S(2)}) collective-permute-start(bf16[1,2,200,128]{3,2,1,0:T(8,128)(2,1)S(1)} %pair_sum.1.keep_ref), channel_id=1, source_target_pairs={{0,24},{8,16},{16,8},{24,0},{1,25},{9,17},{17,9},{25,1},{2,26},{10... | collective-permute-start | bytes 307208 | tf_op jit(solution)/shard_map/ppermute | solution.py:245
  14.6 6.0 %collective-permute-start.7 = (bf16[2,200,128]{2,1,0:T(8,128)(2,1)S(1)}, bf16[2,200,128]{2,1,0:T(8,128)(2,1)S(1)}, u32[]{:S(2)}, u32[]{:S(2)}) collective-permute-start(bf16[2,200,128]{2,1,0:T(8,128)(2,1)S(1)} %sum_norm.1.refs_0_), channel_id=1, source_target_pairs={{0,16},{8,24},{16,0},{24,8},{1,17},{9,25},{17,1},{25,9},{2,18},{10... | collective-permute-start | bytes 307208 | tf_op jit(solution)/shard_map/ppermute | solution.py:245
  16.2 5.4 %collective-permute-start.6 = (bf16[2,200,128]{2,1,0:T(8,128)(2,1)S(1)}, bf16[2,200,128]{2,1,0:T(8,128)(2,1)S(1)}, u32[]{:S(2)}, u32[]{:S(2)}) collective-permute-start(bf16[2,200,128]{2,1,0:T(8,128)(2,1)S(1)} %sum_norm.1.refs_0_), channel_id=1, source_target_pairs={{0,8},{8,0},{16,24},{24,16},{1,9},{9,1},{17,25},{25,17},{2,10},{10... | collective-permute-start | bytes 307208 | tf_op jit(solution)/shard_map/ppermute | solution.py:245
  17.7 5.1 %collective-permute-start.4 = (bf16[1,2,200,128]{3,2,1,0:T(8,128)(2,1)S(1)}, bf16[1,2,200,128]{3,2,1,0:T(8,128)(2,1)S(1)}, u32[]{:S(2)}, u32[]{:S(2)}) collective-permute-start(bf16[1,2,200,128]{3,2,1,0:T(8,128)(2,1)S(1)} %collective-permute-done.3.refs_0_), channel_id=1, source_target_pairs={{0,1},{1,0},{2,3},{3,2},{4,5},{5,4},{6,7},{7,6},{8,9},{9,8},{10,11... | collective-permute-start | bytes 307208 | tf_op jit(solution)/shard_map/ppermute | solution.py:245

commit v14 on v10

--- a/solution.py
+++ b/solution.py
@@ -194,48 +194,74 @@
     kv_ref[0], kv_ref[1] = finish_rows(k_gain_ref[...], keep_ref.at[0], arrived_ref.at[0])
 
 
-def attend_kernel(near, far, tile_len, first, last, head_dim, k_gain_ref, qt_ref, bias_ref, *refs):
-    near_refs, refs = refs[: len(near)], refs[len(near) :]
-    far_refs, refs = refs[: 2 * len(far)], refs[2 * len(far) :]
+def part_kernel(half_ref, keys_ref, values_ref):
+    keys_ref[...] = half_ref[0, 0]
+    values_ref[...] = half_ref[0, 1]
+
+
+def score_sections(steps, tile_len, keys_of, top, qt_ref, bias_ref):
+    s = lax.axis_index("section")
+    qt = qt_ref[...]
+    scores = []
+    for step, keys in zip(steps, keys_of):
+        score = jnp.dot(keys, qt, preferred_element_type=F32)
+        bias = bias_ref[pl.ds(((s ^ step) * keys.shape[0]) // tile_len, 1), :]
+        scores.append((score, bias))
+        top = jnp.maximum(top, jnp.max(score, axis=0, keepdims=True) + bias)
+    weights = [jnp.exp(score + (bias - top)) for score, bias in scores]
+    return top, weights
+
+
+def mix(values, weights):
+    return lax.dot_general(values, weights, (((0,), (0,)), ((), ())), preferred_element_type=F32)
+
+
+def attend_kernel(steps, tile_len, first, qt_ref, bias_ref, *refs):
+    parts, refs = refs[: len(steps)], refs[len(steps) :]
     if not first:
         top_in, sum_in, mixed_in = refs[:3]
         refs = refs[3:]
-    s = lax.axis_index("section")
-    qt = qt_ref[...]
-    parts = [(part[0], part[1]) for part in near_refs]
-    for one, two in zip(far_refs[::2], far_refs[1::2]):
-        parts.append(finish_rows(k_gain_ref[...], one.at[0], two.at[0]))
-    rows = parts[0][0].shape[0]
-    scores, biases = [], []
-    top = TOP_FLOOR if first else top_in[...]
-    for step, (keys, _) in zip((*near, *far), parts):
-        score = jnp.dot(keys, qt, preferred_element_type=F32)
-        bias = bias_ref[pl.ds(((s ^ step) * rows) // tile_len, 1), :]
-        scores.append(score)
-        biases.append(bias)
-        top = jnp.maximum(top, jnp.max(score, axis=0, keepdims=True) + bias)
+    top_out, sum_out, mixed_out = refs
+    start = TOP_FLOOR if first else top_in[...]
+    top, all_weights = score_sections(steps, tile_len, [part[0] for part in parts], start, qt_ref, bias_ref)
     row_sum, mixed = 0.0, 0.0
     if not first:
         scale = jnp.exp(top_in[...] - top)
         row_sum = sum_in[...] * scale
         mixed = mixed_in[...] * scale
-    for (_, values), score, bias in zip(parts, scores, biases):
-        weights = jnp.exp(score + (bias - top))
+    for part, weights in zip(parts, all_weights):
         row_sum = row_sum + jnp.sum(weights, axis=0, keepdims=True)
-        mixed = mixed + lax.dot_general(
-            values, weights.astype(BF16), (((0,), (0,)), ((), ())), preferred_element_type=F32
-        )
-    if not last:
-        top_out, sum_out, mixed_out = refs
-        top_out[...] = top
-        sum_out[...] = row_sum
-        mixed_out[...] = mixed
-        return
-    (out,) = refs
+        mixed = mixed + mix(part[1], weights.astype(BF16))
+    top_out[...] = top
+    sum_out[...] = row_sum
+    mixed_out[...] = mixed
+
+
+def weigh_kernel(steps, tile_len, k_gain_ref, qt_ref, bias_ref, top_in, sum_in, mixed_in, *refs):
+    halves, (weights_out, inverse_out, mixed_out) = refs[:-3], refs[-3:]
+    keys_of = [
+        normalize(one[...].astype(F32) + two[...].astype(F32), k_gain_ref[...]).astype(BF16)
+        for one, two in zip(halves[::2], halves[1::2])
+    ]
+    top, all_weights = score_sections(steps, tile_len, keys_of, top_in[...], qt_ref, bias_ref)
+    scale = jnp.exp(top_in[...] - top)
+    row_sum = sum_in[...] * scale
+    for i, weights in enumerate(all_weights):
+        row_sum = row_sum + jnp.sum(weights, axis=0, keepdims=True)
+        weights_out[i] = weights.astype(BF16)
     has_any = jnp.max(bias_ref[...], axis=0, keepdims=True) > -1.0
-    inverse = jnp.where(has_any, 1.0 / jnp.where(has_any, row_sum, 1.0), 0.0)
-    context = (mixed * inverse).astype(BF16)
-    tokens = out.shape[0]
+    inverse_out[...] = jnp.where(has_any, 1.0 / jnp.where(has_any, row_sum, 1.0), 0.0)
+    mixed_out[...] = mixed_in[...] * scale
+
+
+def finish_kernel(weights_ref, inverse_ref, mixed_ref, *refs):
+    halves, out = refs[:-1], refs[-1]
+    mixed = mixed_ref[...]
+    for i, (one, two) in enumerate(zip(halves[::2], halves[1::2])):
+        values = (one[...].astype(F32) + two[...].astype(F32)).astype(BF16)
+        mixed = mixed + mix(values, weights_ref[i])
+    context = (mixed * inverse_ref[...]).astype(BF16)
+    tokens, head_dim = out.shape[0], mixed.shape[0]
     for head in range(out.shape[1] // head_dim):
         out[:, head * head_dim : (head + 1) * head_dim] = context[
             :, head * tokens : (head + 1) * tokens
@@ -383,31 +409,38 @@
     halves = [swap(total, "section", step) for step in far]
     kv = call(norm_kernel, shape_of((2, rows, head_dim)), 3, "sum_norm")(gain, total, arrived)
     finished = [swap(kv, "section", step) for step in near]
-    both = []
+    row = shape_of((rows, head_dim))
+    key_halves, value_halves = [], []
     for value in halves:
-        both += [value, swap(value, "tensor", 1)]
+        keys, values = call(part_kernel, [row, row], 1, "part")(value)
+        key_halves += [keys, swap(keys, "tensor", 1)]
+        value_halves += [values, swap(values, "tensor", 1)]
+    line, block = shape_of((1, pairs), F32), shape_of((head_dim, pairs), F32)
     state = []
-    for here, there, operands in (
-        ([0], [], [kv]),
-        (near, [], finished),
-        ([], far, both),
-    ):
-        first, last = here == [0], len(there) > 0
-        outs = (
-            shape_of((tokens, q_width))
-            if last
-            else [shape_of((1, pairs), F32), shape_of((1, pairs), F32), shape_of((head_dim, pairs), F32)]
-        )
-        parts = len(here) + len(there)
+    for steps, operands in (([0], [kv]), (near, finished)):
         state = call(
-            functools.partial(attend_kernel, here, there, tile_len, first, last, head_dim),
-            outs,
-            3 + len(operands) + len(state),
+            functools.partial(attend_kernel, steps, tile_len, steps == [0]),
+            [line, line, block],
+            2 + len(operands) + len(state),
             "attend",
-            flops=4 * pairs * rows * head_dim * parts,
-            exps=pairs * rows * parts,
-        )(gain, qt, bias, *operands, *state)
-    return state
+            flops=4 * pairs * rows * head_dim * len(steps),
+            exps=pairs * rows * len(steps),
+        )(qt, bias, *operands, *state)
+    weighed = call(
+        functools.partial(weigh_kernel, far, tile_len),
+        [shape_of((len(far), rows, pairs)), line, block],
+        6 + len(key_halves),
+        "weigh",
+        flops=2 * pairs * rows * head_dim * len(far),
+        exps=pairs * rows * len(far),
+    )(gain, qt, bias, *state, *key_halves)
+    return call(
+        finish_kernel,
+        shape_of((tokens, q_width)),
+        3 + len(value_halves),
+        "finish",
+        flops=2 * pairs * rows * head_dim * len(far),
+    )(*weighed, *value_halves)
 
 
 def solution(mesh):

time: 24.3 us -> 25.5 us (1.049)
  waiting for transfers between devices: 2.05 us -> 2.98 us
    ppermute x6 -> x7, waiting for transfers between devices: 1.86 us -> 2.79 us  [swap(): lax.ppermute(value, axis, [(i, i ^ k) for i in range(lax.axis_size(axis))])]
    ppermute x6 -> x7, starting transfers between devices: 11 us -> 11.1 us  [swap(): lax.ppermute(value, axis, [(i, i ^ k) for i in range(lax.axis_size(axis))])]
    pallas_call x3 -> x5, Pallas kernels: 2.27 us -> 2.37 us  [the longest x2 1.02 us: on_device(): call(functools.partial(attend_kernel, steps, tile_len, steps == [0]), [li...]
  transfers between devices with their start and end apart: 8 -> 9, of which waited for: 4 -> 5; matrix products, arithmetic and copies ran while one was open for 0% -> 0% of each run, Pallas kernels for 20% -> 21%
where the time goes in v14:
time: 25.5 us; the launch traced here: 25.3 us
  starting transfers between devices  16 us (63%)
  Pallas kernels  6.18 us (24%)
  waiting for transfers between devices  2.98 us (12%)
    ppermute x7, starting transfers between devices, swap(): lax.ppermute(value, axis, [(i, i ^ k) for i in range(lax.axis_size(axis))])  11.1 us
    ppermute x2, starting transfers between devices, exchange_two_heads(): return lax.ppermute(value, ('dp', 'tensor'), hops)  4.9 us
    ppermute x7, waiting for transfers between devices, swap(): lax.ppermute(value, axis, [(i, i ^ k) for i in range(lax.axis_size(axis))])  2.79 us
    pallas_call x1, Pallas kernels, on_device(): call(functools.partial(keep_kernel, head_dim), [product, *prepared], 8, '...  2.05 us
    pallas_call x1, Pallas kernels, on_device(): call(load_kernel, shape_of(images.shape), 2, 'home_rows', in_specs=[VMEM,...  1.15 us
    pallas_call x2, Pallas kernels, on_device(): call(functools.partial(attend_kernel, steps, tile_len, steps == [0]), [li...  1.02 us
    pallas_call x1, Pallas kernels, on_device(): call(finish_kernel, shape_of((tokens, q_width)), 3 + len(value_halves), '...  0.95 us
  transfers between devices with their start and end apart: 9, of which 5 were waited for; matrix products, arithmetic and copies ran while one was open for 0% of the time, Pallas kernels for 21%

profile of v14, /device:TPU:0, one launch (start us, length us, event | category | flops | bytes accessed | tf_op | source)
XLA Modules:
  0.0 25.3 jit_solution(16763109500260854538)
XLA Ops:
  0.0 0.5 %collective-permute-start = (bf16[2,2048,128]{2,1,0:T(8,128)(2,1)}, bf16[2,2048,128]{2,1,0:T(8,128)(2,1)S(1)}, u32[]{:S(2)}, u32[]{:S(2)}) collective-permute-start(bf16[2,2048,128]{2,1,0:T(8,128)(2,1)} %w_hbm.3), channel_id=1, source_target_pairs={{0,4},{4,0},{1,5},{5,1},{2,6},{6,2},{3,7},{7,3},{8,12},{12,8},{9,1... | collective-permute-start | bytes 3145736 | tf_op jit(solution)/shard_map/ppermute | solution.py:272
  0.5 2.0 %collective-permute-start.1 = (bf16[1,2,200,128]{3,2,1,0:T(8,128)(2,1)S(1)}, bf16[1,2,200,128]{3,2,1,0:T(8,128)(2,1)S(1)}, u32[]{:S(2)}, u32[]{:S(2)}) collective-permute-start(bf16[1,2,200,128]{3,2,1,0:T(8,128)(2,1)S(1)} %away_own.1.after_ref), channel_id=1, source_target_pairs={{0,4},{1,5},{2,0},{3,1},{4,6},{5,7},{6,2},{7,3},{8,12},{9,13},{10,... | collective-permute-start | bytes 307208 | tf_op jit(solution)/shard_map/ppermute | solution.py:281
  2.5 1.2 %home_rows.1.x_ref = bf16[1,200,2048]{2,1,0:T(8,128)(2,1)S(1)} custom-call(bf16[1,2,200,128]{3,2,1,0:T(8,128)(2,1)S(1)} %away_own.1.after_ref, bf16[1,200,2048]{2,1,0:T(8,128)(2,1)} %x_hbm.5), custom_call_target="tpu_custom_call" | custom-call | tf_op jit(solution)/shard_map/home_rows/pallas_call | solution.py:359
  3.6 0.0 collective-permute-done.w_other_ref
  3.6 0.4 %home_other.1.after_ref = bf16[1,2,200,128]{3,2,1,0:T(8,128)(2,1)S(1)} custom-call(bf16[1,200,2048]{2,1,0:T(8,128)(2,1)S(1)} %home_rows.1.x_ref, bf16[2,2048,128]{2,1,0:T(8,128)(2,1)S(1)} %collective-permute-done.w_other_ref), custom_call_target="tpu_custom_call" | custom-call | flops 209715200 | tf_op jit(solution)/shard_map/home_other/pallas_call | solution.py:367
  4.1 2.9 %collective-permute-start.2 = (bf16[1,2,200,128]{3,2,1,0:T(8,128)(2,1)S(1)}, bf16[1,2,200,128]{3,2,1,0:T(8,128)(2,1)S(1)}, u32[]{:S(2)}, u32[]{:S(2)}) collective-permute-start(bf16[1,2,200,128]{3,2,1,0:T(8,128)(2,1)S(1)} %home_other.1.after_ref), channel_id=1, source_target_pairs={{0,2},{1,3},{2,6},{3,7},{4,0},{5,1},{6,4},{7,5},{8,10},{9,11},{10,... | collective-permute-start | bytes 307208 | tf_op jit(solution)/shard_map/ppermute | solution.py:281
  7.0 2.0 %keep_queries.1 = (bf16[1,2,200,128]{3,2,1,0:T(8,128)(2,1)S(1)}, bf16[128,512]{1,0:T(8,128)(2,1)S(1)}, f32[4,512]{1,0:T(4,128)S(1)}, f32[1,128]{1,0:T(1,128)S(1)}) custom-call(bf16[1,2,200,128]{3,2,1,0:T(8,128)(2,1)S(1)} %home_other.1.after_ref, bf16[2,2048,128]{2,1,0:T(8,128)(2,1)S(1)} %collective-permute-done.w_other_ref, bf16[1,200,2048]{2,1,0:T(8,128)(2,1)} %x_hbm.5, ...), custom_call_target="tpu_custom_call" | custom-call | flops 209715200 | tf_op jit(solution)/shard_map/keep_queries/pallas_call | solution.py:371
  9.0 0.0 collective-permute-done.1.first_ref
  9.1 0.2 collective-permute-done.2.second_ref
  9.3 2.6 %collective-permute-start.3 = (bf16[1,2,200,128]{3,2,1,0:T(8,128)(2,1)S(1)}, bf16[1,2,200,128]{3,2,1,0:T(8,128)(2,1)S(1)}, u32[]{:S(2)}, u32[]{:S(2)}) collective-permute-start(bf16[1,2,200,128]{3,2,1,0:T(8,128)(2,1)S(1)} %pair_sum.1.keep_ref), channel_id=1, source_target_pairs={{0,1},{1,0},{2,3},{3,2},{4,5},{5,4},{6,7},{7,6},{8,9},{9,8},{10,11... | collective-permute-start | bytes 307208 | tf_op jit(solution)/shard_map/ppermute | solution.py:272
  11.8 2.4 %collective-permute-start.6 = (bf16[1,2,200,128]{3,2,1,0:T(8,128)(2,1)S(1)}, bf16[1,2,200,128]{3,2,1,0:T(8,128)(2,1)S(1)}, u32[]{:S(2)}, u32[]{:S(2)}) collective-permute-start(bf16[1,2,200,128]{3,2,1,0:T(8,128)(2,1)S(1)} %pair_sum.1.keep_ref), channel_id=1, source_target_pairs={{0,24},{8,16},{16,8},{24,0},{1,25},{9,17},{17,9},{25,1},{2,26},{10... | collective-permute-start | bytes 307208 | tf_op jit(solution)/shard_map/ppermute | solution.py:272
  14.3 0.2 collective-permute-done.3.arrived_ref
  14.5 0.1 sum_norm.1.refs_0_
  14.6 1.6 %collective-permute-start.5 = (bf16[2,200,128]{2,1,0:T(8,128)(2,1)S(1)}, bf16[2,200,128]{2,1,0:T(8,128)(2,1)S(1)}, u32[]{:S(2)}, u32[]{:S(2)}) collective-permute-start(bf16[2,200,128]{2,1,0:T(8,128)(2,1)S(1)} %sum_norm.1.refs_0_), channel_id=1, source_target_pairs={{0,16},{8,24},{16,0},{24,8},{1,17},{9,25},{17,1},{25,9},{2,18},{10... | collective-permute-start | bytes 307208 | tf_op jit(solution)/shard_map/ppermute | solution.py:272
  16.2 1.5 %collective-permute-start.4 = (bf16[2,200,128]{2,1,0:T(8,128)(2,1)S(1)}, bf16[2,200,128]{2,1,0:T(8,128)(2,1)S(1)}, u32[]{:S(2)}, u32[]{:S(2)}) collective-permute-start(bf16[2,200,128]{2,1,0:T(8,128)(2,1)S(1)} %sum_norm.1.refs_0_), channel_id=1, source_target_pairs={{0,8},{8,0},{16,24},{24,16},{1,9},{9,1},{17,25},{25,17},{2,10},{10... | collective-permute-start | bytes 307208 | tf_op jit(solution)/shard_map/ppermute | solution.py:272
  17.7 0.0 collective-permute-done.6.half_ref
  17.7 2.5 %collective-permute-start.7 = (bf16[200,128]{1,0:T(8,128)(2,1)S(1)}, bf16[200,128]{1,0:T(8,128)(2,1)S(1)}, u32[]{:S(2)}, u32[]{:S(2)}) collective-permute-start(bf16[200,128]{1,0:T(8,128)(2,1)S(1)} %get-tuple-element.30.refs_0_), channel_id=1, source_target_pairs={{0,1},{1,0},{2,3},{3,2},{4,5},{5,4},{6,7},{7,6},{8,9},{9,8},{10,11... | collective-permute-start | bytes 153608 | tf_op jit(solution)/shard_map/ppermute | solution.py:272
  20.2 0.1 collective-permute-start.8
  20.3 0.4 %attend.2 = (f32[1,512]{1,0:T(1,128)S(1)}, f32[1,512]{1,0:T(1,128)S(1)}, f32[128,512]{1,0:T(8,128)S(1)}) custom-call(bf16[128,512]{1,0:T(8,128)(2,1)S(1)} %get-tuple-element.21.qt_ref, f32[4,512]{1,0:T(4,128)S(1)} %get-tuple-element.22.bias_ref, bf16[2,200,128]{2,1,0:T(8,128)(2,1)S(1)} %sum_norm.1.refs_0_), custom_call_target="tpu_custom_call" | custom-call | flops 52428800 | tf_op jit(solution)/shard_map/attend/pallas_call | solution.py:421
  20.7 0.0 collective-permute-done.5.refs_1_
  20.8 0.9 %collective-permute-done.4.refs_0_ = bf16[2,200,128]{2,1,0:T(8,128)(2,1)S(1)} collective-permute-done((bf16[2,200,128]{2,1,0:T(8,128)(2,1)S(1)}, bf16[2,200,128]{2,1,0:T(8,128)(2,1)S(1)}, u32[]{:S(2)}, u32[]{:S(2)}) %collective-permute-start.4) | collective-permute-done | bytes 102432 | tf_op jit(solution)/shard_map/ppermute | solution.py:272
  21.6 0.6 %attend.3 = (f32[1,512]{1,0:T(1,128)S(1)}, f32[1,512]{1,0:T(1,128)S(1)}, f32[128,512]{1,0:T(8,128)S(1)}) custom-call(bf16[128,512]{1,0:T(8,128)(2,1)S(1)} %get-tuple-element.21.qt_ref, f32[4,512]{1,0:T(4,128)S(1)} %get-tuple-element.22.bias_ref, bf16[2,200,128]{2,1,0:T(8,128)(2,1)S(1)} %collective-permute-done.4.refs_0_, ...), custom_call_target="tpu_custom_call" | custom-call | flops 104857600 | tf_op jit(solution)/shard_map/attend/pallas_call | solution.py:421
  22.2 0.4 %collective-permute-done.7.refs_1_ = bf16[200,128]{1,0:T(8,128)(2,1)S(1)} collective-permute-done((bf16[200,128]{1,0:T(8,128)(2,1)S(1)}, bf16[200,128]{1,0:T(8,128)(2,1)S(1)}, u32[]{:S(2)}, u32[]{:S(2)}) %collective-permute-start.7) | collective-permute-done | bytes 51232 | tf_op jit(solution)/shard_map/ppermute | solution.py:272
  22.6 0.4 %weigh.1 = (bf16[1,200,512]{2,1,0:T(8,128)(2,1)S(1)}, f32[1,512]{1,0:T(1,128)S(1)}, f32[128,512]{1,0:T(8,128)S(1)}) custom-call(f32[1,128]{1,0:T(1,128)S(1)} %get-tuple-element.20.k_gain_ref, bf16[128,512]{1,0:T(8,128)(2,1)S(1)} %get-tuple-element.21.qt_ref, f32[4,512]{1,0:T(4,128)S(1)} %get-tuple-element.22.bias_ref, ...), custom_call_target="tpu_custom_call" | custom-call | flops 26214400 | tf_op jit(solution)/shard_map/weigh/pallas_call | solution.py:429
  23.0 1.4 %collective-permute-done.8.refs_1_ = bf16[200,128]{1,0:T(8,128)(2,1)S(1)} collective-permute-done((bf16[200,128]{1,0:T(8,128)(2,1)S(1)}, bf16[200,128]{1,0:T(8,128)(2,1)S(1)}, u32[]{:S(2)}, u32[]{:S(2)}) %collective-permute-start.8) | collective-permute-done | bytes 51232 | tf_op jit(solution)/shard_map/ppermute | solution.py:272
  24.3 0.9 %finish.1 = bf16[128,512]{1,0:T(8,128)(2,1)} custom-call(bf16[1,200,512]{2,1,0:T(8,128)(2,1)S(1)} %get-tuple-element.31.weights_ref, f32[1,512]{1,0:T(1,128)S(1)} %get-tuple-element.32.inverse_ref, f32[128,512]{1,0:T(8,128)S(1)} %get-tuple-element.33.mixed_ref, bf16[200,128]{1,0:T(8,128)(2,1)S(1)} %get-tuple-element.34.refs_0_, ...), custom_call_target="tpu_custom_call" | custom-call | flops 26214400 | tf_op jit(solution)/shard_map/finish/pallas_call | solution.py:437
  (3 shorter events, 0.1 us)
Async XLA Ops:
  0.0 3.6 %collective-permute-start = (bf16[2,2048,128]{2,1,0:T(8,128)(2,1)}, bf16[2,2048,128]{2,1,0:T(8,128)(2,1)S(1)}, u32[]{:S(2)}, u32[]{:S(2)}) collective-permute-start(bf16[2,2048,128]{2,1,0:T(8,128)(2,1)} %w_hbm.3), channel_id=1, source_target_pairs={{0,4},{4,0},{1,5},{5,1},{2,6},{6,2},{3,7},{7,3},{8,12},{12,8},{9,1... | collective-permute-start | bytes 3145736 | tf_op jit(solution)/shard_map/ppermute | solution.py:272
  0.5 8.6 %collective-permute-start.1 = (bf16[1,2,200,128]{3,2,1,0:T(8,128)(2,1)S(1)}, bf16[1,2,200,128]{3,2,1,0:T(8,128)(2,1)S(1)}, u32[]{:S(2)}, u32[]{:S(2)}) collective-permute-start(bf16[1,2,200,128]{3,2,1,0:T(8,128)(2,1)S(1)} %away_own.1.after_ref), channel_id=1, source_target_pairs={{0,4},{1,5},{2,0},{3,1},{4,6},{5,7},{6,2},{7,3},{8,12},{9,13},{10,... | collective-permute-start | bytes 307208 | tf_op jit(solution)/shard_map/ppermute | solution.py:281
  4.1 5.2 %collective-permute-start.2 = (bf16[1,2,200,128]{3,2,1,0:T(8,128)(2,1)S(1)}, bf16[1,2,200,128]{3,2,1,0:T(8,128)(2,1)S(1)}, u32[]{:S(2)}, u32[]{:S(2)}) collective-permute-start(bf16[1,2,200,128]{3,2,1,0:T(8,128)(2,1)S(1)} %home_other.1.after_ref), channel_id=1, source_target_pairs={{0,2},{1,3},{2,6},{3,7},{4,0},{5,1},{6,4},{7,5},{8,10},{9,11},{10,... | collective-permute-start | bytes 307208 | tf_op jit(solution)/shard_map/ppermute | solution.py:281
  9.3 5.2 %collective-permute-start.3 = (bf16[1,2,200,128]{3,2,1,0:T(8,128)(2,1)S(1)}, bf16[1,2,200,128]{3,2,1,0:T(8,128)(2,1)S(1)}, u32[]{:S(2)}, u32[]{:S(2)}) collective-permute-start(bf16[1,2,200,128]{3,2,1,0:T(8,128)(2,1)S(1)} %pair_sum.1.keep_ref), channel_id=1, source_target_pairs={{0,1},{1,0},{2,3},{3,2},{4,5},{5,4},{6,7},{7,6},{8,9},{9,8},{10,11... | collective-permute-start | bytes 307208 | tf_op jit(solution)/shard_map/ppermute | solution.py:272
  11.8 5.8 %collective-permute-start.6 = (bf16[1,2,200,128]{3,2,1,0:T(8,128)(2,1)S(1)}, bf16[1,2,200,128]{3,2,1,0:T(8,128)(2,1)S(1)}, u32[]{:S(2)}, u32[]{:S(2)}) collective-permute-start(bf16[1,2,200,128]{3,2,1,0:T(8,128)(2,1)S(1)} %pair_sum.1.keep_ref), channel_id=1, source_target_pairs={{0,24},{8,16},{16,8},{24,0},{1,25},{9,17},{17,9},{25,1},{2,26},{10... | collective-permute-start | bytes 307208 | tf_op jit(solution)/shard_map/ppermute | solution.py:272
  14.6 6.1 %collective-permute-start.5 = (bf16[2,200,128]{2,1,0:T(8,128)(2,1)S(1)}, bf16[2,200,128]{2,1,0:T(8,128)(2,1)S(1)}, u32[]{:S(2)}, u32[]{:S(2)}) collective-permute-start(bf16[2,200,128]{2,1,0:T(8,128)(2,1)S(1)} %sum_norm.1.refs_0_), channel_id=1, source_target_pairs={{0,16},{8,24},{16,0},{24,8},{1,17},{9,25},{17,1},{25,9},{2,18},{10... | collective-permute-start | bytes 307208 | tf_op jit(solution)/shard_map/ppermute | solution.py:272
  16.2 5.4 %collective-permute-start.4 = (bf16[2,200,128]{2,1,0:T(8,128)(2,1)S(1)}, bf16[2,200,128]{2,1,0:T(8,128)(2,1)S(1)}, u32[]{:S(2)}, u32[]{:S(2)}) collective-permute-start(bf16[2,200,128]{2,1,0:T(8,128)(2,1)S(1)} %sum_norm.1.refs_0_), channel_id=1, source_target_pairs={{0,8},{8,0},{16,24},{24,16},{1,9},{9,1},{17,25},{25,17},{2,10},{10... | collective-permute-start | bytes 307208 | tf_op jit(solution)/shard_map/ppermute | solution.py:272
  17.7 4.9 %collective-permute-start.7 = (bf16[200,128]{1,0:T(8,128)(2,1)S(1)}, bf16[200,128]{1,0:T(8,128)(2,1)S(1)}, u32[]{:S(2)}, u32[]{:S(2)}) collective-permute-start(bf16[200,128]{1,0:T(8,128)(2,1)S(1)} %get-tuple-element.30.refs_0_), channel_id=1, source_target_pairs={{0,1},{1,0},{2,3},{3,2},{4,5},{5,4},{6,7},{7,6},{8,9},{9,8},{10,11... | collective-permute-start | bytes 153608 | tf_op jit(solution)/shard_map/ppermute | solution.py:272
  20.2 4.1 %collective-permute-start.8 = (bf16[200,128]{1,0:T(8,128)(2,1)S(1)}, bf16[200,128]{1,0:T(8,128)(2,1)S(1)}, u32[]{:S(2)}, u32[]{:S(2)}) collective-permute-start(bf16[200,128]{1,0:T(8,128)(2,1)S(1)} %get-tuple-element.34.refs_0_), channel_id=1, source_target_pairs={{0,1},{1,0},{2,3},{3,2},{4,5},{5,4},{6,7},{7,6},{8,9},{9,8},{10,11... | collective-permute-start | bytes 153608 | tf_op jit(solution)/shard_map/ppermute | solution.py:272

commit v15 on v10

--- a/solution.py
+++ b/solution.py
@@ -53,8 +53,8 @@
     width = both.shape[1] // 2
     for head in range(width // head_dim):
         lo = head * head_dim
-        ref[base + head, 0] = both[:, lo : lo + head_dim]
-        ref[base + head, 1] = both[:, width + lo : width + lo + head_dim]
+        ref[base + head, :, :head_dim] = both[:, lo : lo + head_dim]
+        ref[base + head, :, head_dim:] = both[:, width + lo : width + lo + head_dim]
 
 
 def prepare_queries(copies, q_ref, q_gain_ref, mask_ref, qt_ref, bias_ref):
@@ -185,13 +185,16 @@
 
 
 def finish_rows(k_gain, one, two):
-    keys = one[0].astype(F32) + two[0].astype(F32)
-    values = one[1].astype(F32) + two[1].astype(F32)
-    return normalize(keys, k_gain).astype(BF16), values.astype(BF16)
+    total = one[...].astype(F32) + two[...].astype(F32)
+    head_dim = total.shape[1] // 2
+    keys = normalize(total[:, :head_dim], k_gain).astype(BF16)
+    return keys, total[:, head_dim:].astype(BF16)
 
 
 def norm_kernel(k_gain_ref, keep_ref, arrived_ref, kv_ref):
-    kv_ref[0], kv_ref[1] = finish_rows(k_gain_ref[...], keep_ref.at[0], arrived_ref.at[0])
+    keys, values = finish_rows(k_gain_ref[...], keep_ref.at[0], arrived_ref.at[0])
+    kv_ref[:, : keys.shape[1]] = keys
+    kv_ref[:, keys.shape[1] :] = values
 
 
 def attend_kernel(near, far, tile_len, first, last, head_dim, k_gain_ref, qt_ref, bias_ref, *refs):
@@ -202,7 +205,7 @@
         refs = refs[3:]
     s = lax.axis_index("section")
     qt = qt_ref[...]
-    parts = [(part[0], part[1]) for part in near_refs]
+    parts = [(part[:, :head_dim], part[:, head_dim:]) for part in near_refs]
     for one, two in zip(far_refs[::2], far_refs[1::2]):
         parts.append(finish_rows(k_gain_ref[...], one.at[0], two.at[0]))
     rows = parts[0][0].shape[0]
@@ -306,7 +309,7 @@
             images, kv_weight, queries, q_gain.reshape(1, -1), tile_mask.T, k_gain.reshape(1, -1),
         )
     ]
-    product = shape_of((own_heads, 2, rows, head_dim))
+    product = shape_of((own_heads, rows, 2 * head_dim))
     x_scratch, w_scratch = pltpu.VMEM(images.shape, BF16), pltpu.VMEM(kv_weight.shape, BF16)
     prepared = [
         shape_of((head_dim, pairs)),
@@ -381,7 +384,7 @@
     near = [step for step in range(1, n_section) if not step & (step - 1)]
     arrived = swap(total, "tensor", 1)
     halves = [swap(total, "section", step) for step in far]
-    kv = call(norm_kernel, shape_of((2, rows, head_dim)), 3, "sum_norm")(gain, total, arrived)
+    kv = call(norm_kernel, shape_of((rows, 2 * head_dim)), 3, "sum_norm")(gain, total, arrived)
     finished = [swap(kv, "section", step) for step in near]
     both = []
     for value in halves:

time: 24.3 us -> 24.3 us (level)
  no operation moved by 1% of the time
where the time goes in v15:
time: 24.3 us; the launch traced here: 24.1 us
  starting transfers between devices  15.9 us (65%)
  Pallas kernels  6.06 us (25%)
  waiting for transfers between devices  2.05 us (8%)
    ppermute x6, starting transfers between devices, swap(): lax.ppermute(value, axis, [(i, i ^ k) for i in range(lax.axis_size(axis))])  11 us
    ppermute x2, starting transfers between devices, exchange_two_heads(): return lax.ppermute(value, ('dp', 'tensor'), hops)  4.9 us
    pallas_call x3, Pallas kernels, on_device(): call(functools.partial(attend_kernel, here, there, tile_len, first, last,...  2.27 us
    pallas_call x1, Pallas kernels, on_device(): call(functools.partial(keep_kernel, head_dim), [product, *prepared], 8, '...  2.04 us
    ppermute x6, waiting for transfers between devices, swap(): lax.ppermute(value, axis, [(i, i ^ k) for i in range(lax.axis_size(axis))])  1.86 us
    pallas_call x1, Pallas kernels, on_device(): call(load_kernel, shape_of(images.shape), 2, 'home_rows', in_specs=[VMEM,...  1.15 us
  transfers between devices with their start and end apart: 8, of which 4 were waited for; matrix products, arithmetic and copies ran while one was open for 0% of the time, Pallas kernels for 20%

profile of v15, /device:TPU:0, one launch (start us, length us, event | category | flops | bytes accessed | tf_op | source)
XLA Modules:
  0.0 24.1 jit_solution(12407515552326636072)
XLA Ops:
  0.0 0.5 %collective-permute-start = (bf16[2,2048,128]{2,1,0:T(8,128)(2,1)}, bf16[2,2048,128]{2,1,0:T(8,128)(2,1)S(1)}, u32[]{:S(2)}, u32[]{:S(2)}) collective-permute-start(bf16[2,2048,128]{2,1,0:T(8,128)(2,1)} %w_hbm.3), channel_id=1, source_target_pairs={{0,4},{4,0},{1,5},{5,1},{2,6},{6,2},{3,7},{7,3},{8,12},{12,8},{9,1... | collective-permute-start | bytes 3145736 | tf_op jit(solution)/shard_map/ppermute | solution.py:249
  0.5 2.0 %collective-permute-start.1 = (bf16[1,200,256]{2,1,0:T(8,128)(2,1)S(1)}, bf16[1,200,256]{2,1,0:T(8,128)(2,1)S(1)}, u32[]{:S(2)}, u32[]{:S(2)}) collective-permute-start(bf16[1,200,256]{2,1,0:T(8,128)(2,1)S(1)} %away_own.1.after_ref), channel_id=1, source_target_pairs={{0,4},{1,5},{2,0},{3,1},{4,6},{5,7},{6,2},{7,3},{8,12},{9,13},{10,... | collective-permute-start | bytes 307208 | tf_op jit(solution)/shard_map/ppermute | solution.py:258
  2.5 1.2 %home_rows.1.x_ref = bf16[1,200,2048]{2,1,0:T(8,128)(2,1)S(1)} custom-call(bf16[1,200,256]{2,1,0:T(8,128)(2,1)S(1)} %away_own.1.after_ref, bf16[1,200,2048]{2,1,0:T(8,128)(2,1)} %x_hbm.5), custom_call_target="tpu_custom_call" | custom-call | tf_op jit(solution)/shard_map/home_rows/pallas_call | solution.py:336
  3.6 0.0 collective-permute-done.w_other_ref
  3.6 0.4 %home_other.1.after_ref = bf16[1,200,256]{2,1,0:T(8,128)(2,1)S(1)} custom-call(bf16[1,200,2048]{2,1,0:T(8,128)(2,1)S(1)} %home_rows.1.x_ref, bf16[2,2048,128]{2,1,0:T(8,128)(2,1)S(1)} %collective-permute-done.w_other_ref), custom_call_target="tpu_custom_call" | custom-call | flops 209715200 | tf_op jit(solution)/shard_map/home_other/pallas_call | solution.py:344
  4.1 2.9 %collective-permute-start.2 = (bf16[1,200,256]{2,1,0:T(8,128)(2,1)S(1)}, bf16[1,200,256]{2,1,0:T(8,128)(2,1)S(1)}, u32[]{:S(2)}, u32[]{:S(2)}) collective-permute-start(bf16[1,200,256]{2,1,0:T(8,128)(2,1)S(1)} %home_other.1.after_ref), channel_id=1, source_target_pairs={{0,2},{1,3},{2,6},{3,7},{4,0},{5,1},{6,4},{7,5},{8,10},{9,11},{10,... | collective-permute-start | bytes 307208 | tf_op jit(solution)/shard_map/ppermute | solution.py:258
  7.0 2.0 %keep_queries.1 = (bf16[1,200,256]{2,1,0:T(8,128)(2,1)S(1)}, bf16[128,512]{1,0:T(8,128)(2,1)S(1)}, f32[4,512]{1,0:T(4,128)S(1)}, f32[1,128]{1,0:T(1,128)S(1)}) custom-call(bf16[1,200,256]{2,1,0:T(8,128)(2,1)S(1)} %home_other.1.after_ref, bf16[2,2048,128]{2,1,0:T(8,128)(2,1)S(1)} %collective-permute-done.w_other_ref, bf16[1,200,2048]{2,1,0:T(8,128)(2,1)} %x_hbm.5, ...), custom_call_target="tpu_custom_call" | custom-call | flops 209715200 | tf_op jit(solution)/shard_map/keep_queries/pallas_call | solution.py:348
  9.0 0.0 collective-permute-done.1.first_ref
  9.0 0.2 collective-permute-done.2.second_ref
  9.3 2.6 %collective-permute-start.5 = (bf16[1,200,256]{2,1,0:T(8,128)(2,1)S(1)}, bf16[1,200,256]{2,1,0:T(8,128)(2,1)S(1)}, u32[]{:S(2)}, u32[]{:S(2)}) collective-permute-start(bf16[1,200,256]{2,1,0:T(8,128)(2,1)S(1)} %pair_sum.1.keep_ref), channel_id=1, source_target_pairs={{0,1},{1,0},{2,3},{3,2},{4,5},{5,4},{6,7},{7,6},{8,9},{9,8},{10,11... | collective-permute-start | bytes 307208 | tf_op jit(solution)/shard_map/ppermute | solution.py:249
  11.8 2.4 %collective-permute-start.3 = (bf16[1,200,256]{2,1,0:T(8,128)(2,1)S(1)}, bf16[1,200,256]{2,1,0:T(8,128)(2,1)S(1)}, u32[]{:S(2)}, u32[]{:S(2)}) collective-permute-start(bf16[1,200,256]{2,1,0:T(8,128)(2,1)S(1)} %pair_sum.1.keep_ref), channel_id=1, source_target_pairs={{0,24},{8,16},{16,8},{24,0},{1,25},{9,17},{17,9},{25,1},{2,26},{10... | collective-permute-start | bytes 307208 | tf_op jit(solution)/shard_map/ppermute | solution.py:249
  14.3 0.2 collective-permute-done.5.arrived_ref
  14.5 0.1 sum_norm.1.refs_0_
  14.6 1.6 %collective-permute-start.7 = (bf16[200,256]{1,0:T(8,128)(2,1)S(1)}, bf16[200,256]{1,0:T(8,128)(2,1)S(1)}, u32[]{:S(2)}, u32[]{:S(2)}) collective-permute-start(bf16[200,256]{1,0:T(8,128)(2,1)S(1)} %sum_norm.1.refs_0_), channel_id=1, source_target_pairs={{0,16},{8,24},{16,0},{24,8},{1,17},{9,25},{17,1},{25,9},{2,18},{10... | collective-permute-start | bytes 307208 | tf_op jit(solution)/shard_map/ppermute | solution.py:249
  16.2 1.5 %collective-permute-start.6 = (bf16[200,256]{1,0:T(8,128)(2,1)S(1)}, bf16[200,256]{1,0:T(8,128)(2,1)S(1)}, u32[]{:S(2)}, u32[]{:S(2)}) collective-permute-start(bf16[200,256]{1,0:T(8,128)(2,1)S(1)} %sum_norm.1.refs_0_), channel_id=1, source_target_pairs={{0,8},{8,0},{16,24},{24,16},{1,9},{9,1},{17,25},{25,17},{2,10},{10... | collective-permute-start | bytes 307208 | tf_op jit(solution)/shard_map/ppermute | solution.py:249
  17.7 0.0 collective-permute-done.3.refs_0_
  17.7 2.5 %collective-permute-start.4 = (bf16[1,200,256]{2,1,0:T(8,128)(2,1)S(1)}, bf16[1,200,256]{2,1,0:T(8,128)(2,1)S(1)}, u32[]{:S(2)}, u32[]{:S(2)}) collective-permute-start(bf16[1,200,256]{2,1,0:T(8,128)(2,1)S(1)} %collective-permute-done.3.refs_0_), channel_id=1, source_target_pairs={{0,1},{1,0},{2,3},{3,2},{4,5},{5,4},{6,7},{7,6},{8,9},{9,8},{10,11... | collective-permute-start | bytes 307208 | tf_op jit(solution)/shard_map/ppermute | solution.py:249
  20.1 0.4 %attend.3 = (f32[1,512]{1,0:T(1,128)S(1)}, f32[1,512]{1,0:T(1,128)S(1)}, f32[128,512]{1,0:T(8,128)S(1)}) custom-call(f32[1,128]{1,0:T(1,128)S(1)} %get-tuple-element.15.k_gain_ref, bf16[128,512]{1,0:T(8,128)(2,1)S(1)} %get-tuple-element.16.qt_ref, f32[4,512]{1,0:T(4,128)S(1)} %get-tuple-element.17.bias_ref, bf16[200,256]{1,0:T(8,128)(2,1)S(1)} %sum_norm.1.refs_0_), custom_call_target="tpu_custom_call" | custom-call | flops 52428800 | tf_op jit(solution)/shard_map/attend/pallas_call | solution.py:405
  20.6 0.0 collective-permute-done.7.refs_1_
  20.6 1.0 %collective-permute-done.6.refs_0_ = bf16[200,256]{1,0:T(8,128)(2,1)S(1)} collective-permute-done((bf16[200,256]{1,0:T(8,128)(2,1)S(1)}, bf16[200,256]{1,0:T(8,128)(2,1)S(1)}, u32[]{:S(2)}, u32[]{:S(2)}) %collective-permute-start.6) | collective-permute-done | bytes 102432 | tf_op jit(solution)/shard_map/ppermute | solution.py:249
  21.6 0.6 %attend.4 = (f32[1,512]{1,0:T(1,128)S(1)}, f32[1,512]{1,0:T(1,128)S(1)}, f32[128,512]{1,0:T(8,128)S(1)}) custom-call(f32[1,128]{1,0:T(1,128)S(1)} %get-tuple-element.15.k_gain_ref, bf16[128,512]{1,0:T(8,128)(2,1)S(1)} %get-tuple-element.16.qt_ref, f32[4,512]{1,0:T(4,128)S(1)} %get-tuple-element.17.bias_ref, ...), custom_call_target="tpu_custom_call" | custom-call | flops 104857600 | tf_op jit(solution)/shard_map/attend/pallas_call | solution.py:405
  22.2 0.6 %collective-permute-done.4.refs_1_ = bf16[1,200,256]{2,1,0:T(8,128)(2,1)S(1)} collective-permute-done((bf16[1,200,256]{2,1,0:T(8,128)(2,1)S(1)}, bf16[1,200,256]{2,1,0:T(8,128)(2,1)S(1)}, u32[]{:S(2)}, u32[]{:S(2)}) %collective-permute-start.4) | collective-permute-done | bytes 102432 | tf_op jit(solution)/shard_map/ppermute | solution.py:249
  22.8 1.3 %attend.5 = bf16[128,512]{1,0:T(8,128)(2,1)} custom-call(f32[1,128]{1,0:T(1,128)S(1)} %get-tuple-element.15.k_gain_ref, bf16[128,512]{1,0:T(8,128)(2,1)S(1)} %get-tuple-element.16.qt_ref, f32[4,512]{1,0:T(4,128)S(1)} %get-tuple-element.17.bias_ref, bf16[1,200,256]{2,1,0:T(8,128)(2,1)S(1)} %collective-permute-done.3.refs_0_, ...), custom_call_target="tpu_custom_call" | custom-call | flops 52428800 | tf_op jit(solution)/shard_map/attend/pallas_call | solution.py:405
  (2 shorter events, 0.1 us)
Async XLA Ops:
  0.0 3.6 %collective-permute-start = (bf16[2,2048,128]{2,1,0:T(8,128)(2,1)}, bf16[2,2048,128]{2,1,0:T(8,128)(2,1)S(1)}, u32[]{:S(2)}, u32[]{:S(2)}) collective-permute-start(bf16[2,2048,128]{2,1,0:T(8,128)(2,1)} %w_hbm.3), channel_id=1, source_target_pairs={{0,4},{4,0},{1,5},{5,1},{2,6},{6,2},{3,7},{7,3},{8,12},{12,8},{9,1... | collective-permute-start | bytes 3145736 | tf_op jit(solution)/shard_map/ppermute | solution.py:249
  0.5 8.6 %collective-permute-start.1 = (bf16[1,200,256]{2,1,0:T(8,128)(2,1)S(1)}, bf16[1,200,256]{2,1,0:T(8,128)(2,1)S(1)}, u32[]{:S(2)}, u32[]{:S(2)}) collective-permute-start(bf16[1,200,256]{2,1,0:T(8,128)(2,1)S(1)} %away_own.1.after_ref), channel_id=1, source_target_pairs={{0,4},{1,5},{2,0},{3,1},{4,6},{5,7},{6,2},{7,3},{8,12},{9,13},{10,... | collective-permute-start | bytes 307208 | tf_op jit(solution)/shard_map/ppermute | solution.py:258
  4.1 5.2 %collective-permute-start.2 = (bf16[1,200,256]{2,1,0:T(8,128)(2,1)S(1)}, bf16[1,200,256]{2,1,0:T(8,128)(2,1)S(1)}, u32[]{:S(2)}, u32[]{:S(2)}) collective-permute-start(bf16[1,200,256]{2,1,0:T(8,128)(2,1)S(1)} %home_other.1.after_ref), channel_id=1, source_target_pairs={{0,2},{1,3},{2,6},{3,7},{4,0},{5,1},{6,4},{7,5},{8,10},{9,11},{10,... | collective-permute-start | bytes 307208 | tf_op jit(solution)/shard_map/ppermute | solution.py:258
  9.3 5.2 %collective-permute-start.5 = (bf16[1,200,256]{2,1,0:T(8,128)(2,1)S(1)}, bf16[1,200,256]{2,1,0:T(8,128)(2,1)S(1)}, u32[]{:S(2)}, u32[]{:S(2)}) collective-permute-start(bf16[1,200,256]{2,1,0:T(8,128)(2,1)S(1)} %pair_sum.1.keep_ref), channel_id=1, source_target_pairs={{0,1},{1,0},{2,3},{3,2},{4,5},{5,4},{6,7},{7,6},{8,9},{9,8},{10,11... | collective-permute-start | bytes 307208 | tf_op jit(solution)/shard_map/ppermute | solution.py:249
  11.8 5.8 %collective-permute-start.3 = (bf16[1,200,256]{2,1,0:T(8,128)(2,1)S(1)}, bf16[1,200,256]{2,1,0:T(8,128)(2,1)S(1)}, u32[]{:S(2)}, u32[]{:S(2)}) collective-permute-start(bf16[1,200,256]{2,1,0:T(8,128)(2,1)S(1)} %pair_sum.1.keep_ref), channel_id=1, source_target_pairs={{0,24},{8,16},{16,8},{24,0},{1,25},{9,17},{17,9},{25,1},{2,26},{10... | collective-permute-start | bytes 307208 | tf_op jit(solution)/shard_map/ppermute | solution.py:249
  14.6 6.0 %collective-permute-start.7 = (bf16[200,256]{1,0:T(8,128)(2,1)S(1)}, bf16[200,256]{1,0:T(8,128)(2,1)S(1)}, u32[]{:S(2)}, u32[]{:S(2)}) collective-permute-start(bf16[200,256]{1,0:T(8,128)(2,1)S(1)} %sum_norm.1.refs_0_), channel_id=1, source_target_pairs={{0,16},{8,24},{16,0},{24,8},{1,17},{9,25},{17,1},{25,9},{2,18},{10... | collective-permute-start | bytes 307208 | tf_op jit(solution)/shard_map/ppermute | solution.py:249
  16.2 5.4 %collective-permute-start.6 = (bf16[200,256]{1,0:T(8,128)(2,1)S(1)}, bf16[200,256]{1,0:T(8,128)(2,1)S(1)}, u32[]{:S(2)}, u32[]{:S(2)}) collective-permute-start(bf16[200,256]{1,0:T(8,128)(2,1)S(1)} %sum_norm.1.refs_0_), channel_id=1, source_target_pairs={{0,8},{8,0},{16,24},{24,16},{1,9},{9,1},{17,25},{25,17},{2,10},{10... | collective-permute-start | bytes 307208 | tf_op jit(solution)/shard_map/ppermute | solution.py:249
  17.7 5.1 %collective-permute-start.4 = (bf16[1,200,256]{2,1,0:T(8,128)(2,1)S(1)}, bf16[1,200,256]{2,1,0:T(8,128)(2,1)S(1)}, u32[]{:S(2)}, u32[]{:S(2)}) collective-permute-start(bf16[1,200,256]{2,1,0:T(8,128)(2,1)S(1)} %collective-permute-done.3.refs_0_), channel_id=1, source_target_pairs={{0,1},{1,0},{2,3},{3,2},{4,5},{5,4},{6,7},{7,6},{8,9},{9,8},{10,11... | collective-permute-start | bytes 307208 | tf_op jit(solution)/shard_map/ppermute | solution.py:249

commit v16 on v15

--- a/solution.py
+++ b/solution.py
@@ -80,9 +80,16 @@
 
 
 def own_kernel(head_dim, x_hbm, w_hbm, own_ref, x_ref, w_ref, sems):
-    for copy in start_copies((x_hbm, w_hbm), (x_ref, w_ref), sems):
+    sources = (x_hbm, w_hbm.at[0], w_hbm.at[1])
+    rows, keys, values = start_copies(sources, (x_ref, w_ref.at[0], w_ref.at[1]), sems)
+    rows.wait()
+    for part, copy in enumerate((keys, values)):
         copy.wait()
-    store_heads(own_ref, 0, project(x_ref[0], w_ref[...]), head_dim)
+        product = jnp.dot(x_ref[0], w_ref[part], preferred_element_type=F32).astype(BF16)
+        for head in range(own_ref.shape[0]):
+            own_ref[head, :, part * head_dim : (part + 1) * head_dim] = product[
+                :, head * head_dim : (head + 1) * head_dim
+            ]
 
 
 def other_kernel(head_dim, x_ref, w_ref, other_ref):
@@ -330,7 +337,7 @@
             "away_own",
             flops=work,
             in_specs=[HBM] * 2,
-            scratch=[x_scratch, w_scratch, pltpu.SemaphoreType.DMA((2,))],
+            scratch=[x_scratch, w_scratch, pltpu.SemaphoreType.DMA((3,))],
         )(x, w)
         first = exchange_two_heads(away, False)
         x_home = call(
@@ -363,7 +370,7 @@
             "own_heads",
             flops=work,
             in_specs=[HBM] * 2,
-            scratch=[w_scratch, pltpu.SemaphoreType.DMA((2,))],
+            scratch=[w_scratch, pltpu.SemaphoreType.DMA((3,))],
         )(x, w)
         qt, bias, gain = call(
             query_kernel,

time: 24.3 us -> 24.4 us (level)
  no operation moved by 1% of the time
where the time goes in v16:
time: 24.4 us; the launch traced here: 24.2 us
  starting transfers between devices  15.9 us (65%)
  Pallas kernels  6.08 us (25%)
  waiting for transfers between devices  2.18 us (9%)
    ppermute x6, starting transfers between devices, swap(): lax.ppermute(value, axis, [(i, i ^ k) for i in range(lax.axis_size(axis))])  11 us
    ppermute x2, starting transfers between devices, exchange_two_heads(): return lax.ppermute(value, ('dp', 'tensor'), hops)  4.9 us
    pallas_call x3, Pallas kernels, on_device(): call(functools.partial(attend_kernel, here, there, tile_len, first, last,...  2.28 us
    pallas_call x1, Pallas kernels, on_device(): call(functools.partial(keep_kernel, head_dim), [product, *prepared], 8, '...  2.04 us
    ppermute x6, waiting for transfers between devices, swap(): lax.ppermute(value, axis, [(i, i ^ k) for i in range(lax.axis_size(axis))])  1.99 us
    pallas_call x1, Pallas kernels, on_device(): call(load_kernel, shape_of(images.shape), 2, 'home_rows', in_specs=[VMEM,...  1.15 us
  transfers between devices with their start and end apart: 8, of which 4 were waited for; matrix products, arithmetic and copies ran while one was open for 0% of the time, Pallas kernels for 20%

profile of v16, /device:TPU:0, one launch (start us, length us, event | category | flops | bytes accessed | tf_op | source)
XLA Modules:
  0.0 24.2 jit_solution(11589935618327690788)
XLA Ops:
  0.0 0.5 %collective-permute-start = (bf16[2,2048,128]{2,1,0:T(8,128)(2,1)}, bf16[2,2048,128]{2,1,0:T(8,128)(2,1)S(1)}, u32[]{:S(2)}, u32[]{:S(2)}) collective-permute-start(bf16[2,2048,128]{2,1,0:T(8,128)(2,1)} %w_hbm.3), channel_id=1, source_target_pairs={{0,4},{4,0},{1,5},{5,1},{2,6},{6,2},{3,7},{7,3},{8,12},{12,8},{9,1... | collective-permute-start | bytes 3145736 | tf_op jit(solution)/shard_map/ppermute | solution.py:256
  0.5 2.2 %collective-permute-start.1 = (bf16[1,200,256]{2,1,0:T(8,128)(2,1)S(1)}, bf16[1,200,256]{2,1,0:T(8,128)(2,1)S(1)}, u32[]{:S(2)}, u32[]{:S(2)}) collective-permute-start(bf16[1,200,256]{2,1,0:T(8,128)(2,1)S(1)} %away_own.1.after_ref), channel_id=1, source_target_pairs={{0,4},{1,5},{2,0},{3,1},{4,6},{5,7},{6,2},{7,3},{8,12},{9,13},{10,... | collective-permute-start | bytes 307208 | tf_op jit(solution)/shard_map/ppermute | solution.py:265
  2.7 1.2 %home_rows.1.x_ref = bf16[1,200,2048]{2,1,0:T(8,128)(2,1)S(1)} custom-call(bf16[1,200,256]{2,1,0:T(8,128)(2,1)S(1)} %away_own.1.after_ref, bf16[1,200,2048]{2,1,0:T(8,128)(2,1)} %x_hbm.5), custom_call_target="tpu_custom_call" | custom-call | tf_op jit(solution)/shard_map/home_rows/pallas_call | solution.py:343
  3.8 0.0 collective-permute-done.w_other_ref
  3.8 0.4 %home_other.1.after_ref = bf16[1,200,256]{2,1,0:T(8,128)(2,1)S(1)} custom-call(bf16[1,200,2048]{2,1,0:T(8,128)(2,1)S(1)} %home_rows.1.x_ref, bf16[2,2048,128]{2,1,0:T(8,128)(2,1)S(1)} %collective-permute-done.w_other_ref), custom_call_target="tpu_custom_call" | custom-call | flops 209715200 | tf_op jit(solution)/shard_map/home_other/pallas_call | solution.py:351
  4.2 2.7 %collective-permute-start.2 = (bf16[1,200,256]{2,1,0:T(8,128)(2,1)S(1)}, bf16[1,200,256]{2,1,0:T(8,128)(2,1)S(1)}, u32[]{:S(2)}, u32[]{:S(2)}) collective-permute-start(bf16[1,200,256]{2,1,0:T(8,128)(2,1)S(1)} %home_other.1.after_ref), channel_id=1, source_target_pairs={{0,2},{1,3},{2,6},{3,7},{4,0},{5,1},{6,4},{7,5},{8,10},{9,11},{10,... | collective-permute-start | bytes 307208 | tf_op jit(solution)/shard_map/ppermute | solution.py:265
  7.0 2.0 %keep_queries.1 = (bf16[1,200,256]{2,1,0:T(8,128)(2,1)S(1)}, bf16[128,512]{1,0:T(8,128)(2,1)S(1)}, f32[4,512]{1,0:T(4,128)S(1)}, f32[1,128]{1,0:T(1,128)S(1)}) custom-call(bf16[1,200,256]{2,1,0:T(8,128)(2,1)S(1)} %home_other.1.after_ref, bf16[2,2048,128]{2,1,0:T(8,128)(2,1)S(1)} %collective-permute-done.w_other_ref, bf16[1,200,2048]{2,1,0:T(8,128)(2,1)} %x_hbm.5, ...), custom_call_target="tpu_custom_call" | custom-call | flops 209715200 | tf_op jit(solution)/shard_map/keep_queries/pallas_call | solution.py:355
  9.0 0.0 collective-permute-done.1.first_ref
  9.0 0.2 collective-permute-done.2.second_ref
  9.3 2.6 %collective-permute-start.5 = (bf16[1,200,256]{2,1,0:T(8,128)(2,1)S(1)}, bf16[1,200,256]{2,1,0:T(8,128)(2,1)S(1)}, u32[]{:S(2)}, u32[]{:S(2)}) collective-permute-start(bf16[1,200,256]{2,1,0:T(8,128)(2,1)S(1)} %pair_sum.1.keep_ref), channel_id=1, source_target_pairs={{0,1},{1,0},{2,3},{3,2},{4,5},{5,4},{6,7},{7,6},{8,9},{9,8},{10,11... | collective-permute-start | bytes 307208 | tf_op jit(solution)/shard_map/ppermute | solution.py:256
  11.8 2.4 %collective-permute-start.3 = (bf16[1,200,256]{2,1,0:T(8,128)(2,1)S(1)}, bf16[1,200,256]{2,1,0:T(8,128)(2,1)S(1)}, u32[]{:S(2)}, u32[]{:S(2)}) collective-permute-start(bf16[1,200,256]{2,1,0:T(8,128)(2,1)S(1)} %pair_sum.1.keep_ref), channel_id=1, source_target_pairs={{0,24},{8,16},{16,8},{24,0},{1,25},{9,17},{17,9},{25,1},{2,26},{10... | collective-permute-start | bytes 307208 | tf_op jit(solution)/shard_map/ppermute | solution.py:256
  14.3 0.4 %collective-permute-done.5.arrived_ref = bf16[1,200,256]{2,1,0:T(8,128)(2,1)S(1)} collective-permute-done((bf16[1,200,256]{2,1,0:T(8,128)(2,1)S(1)}, bf16[1,200,256]{2,1,0:T(8,128)(2,1)S(1)}, u32[]{:S(2)}, u32[]{:S(2)}) %collective-permute-start.5) | collective-permute-done | bytes 102432 | tf_op jit(solution)/shard_map/ppermute | solution.py:256
  14.6 0.1 sum_norm.1.refs_0_
  14.8 1.6 %collective-permute-start.7 = (bf16[200,256]{1,0:T(8,128)(2,1)S(1)}, bf16[200,256]{1,0:T(8,128)(2,1)S(1)}, u32[]{:S(2)}, u32[]{:S(2)}) collective-permute-start(bf16[200,256]{1,0:T(8,128)(2,1)S(1)} %sum_norm.1.refs_0_), channel_id=1, source_target_pairs={{0,16},{8,24},{16,0},{24,8},{1,17},{9,25},{17,1},{25,9},{2,18},{10... | collective-permute-start | bytes 307208 | tf_op jit(solution)/shard_map/ppermute | solution.py:256
  16.3 1.5 %collective-permute-start.6 = (bf16[200,256]{1,0:T(8,128)(2,1)S(1)}, bf16[200,256]{1,0:T(8,128)(2,1)S(1)}, u32[]{:S(2)}, u32[]{:S(2)}) collective-permute-start(bf16[200,256]{1,0:T(8,128)(2,1)S(1)} %sum_norm.1.refs_0_), channel_id=1, source_target_pairs={{0,8},{8,0},{16,24},{24,16},{1,9},{9,1},{17,25},{25,17},{2,10},{10... | collective-permute-start | bytes 307208 | tf_op jit(solution)/shard_map/ppermute | solution.py:256
  17.8 0.0 collective-permute-done.3.refs_0_
  17.8 2.5 %collective-permute-start.4 = (bf16[1,200,256]{2,1,0:T(8,128)(2,1)S(1)}, bf16[1,200,256]{2,1,0:T(8,128)(2,1)S(1)}, u32[]{:S(2)}, u32[]{:S(2)}) collective-permute-start(bf16[1,200,256]{2,1,0:T(8,128)(2,1)S(1)} %collective-permute-done.3.refs_0_), channel_id=1, source_target_pairs={{0,1},{1,0},{2,3},{3,2},{4,5},{5,4},{6,7},{7,6},{8,9},{9,8},{10,11... | collective-permute-start | bytes 307208 | tf_op jit(solution)/shard_map/ppermute | solution.py:256
  20.3 0.4 %attend.3 = (f32[1,512]{1,0:T(1,128)S(1)}, f32[1,512]{1,0:T(1,128)S(1)}, f32[128,512]{1,0:T(8,128)S(1)}) custom-call(f32[1,128]{1,0:T(1,128)S(1)} %get-tuple-element.15.k_gain_ref, bf16[128,512]{1,0:T(8,128)(2,1)S(1)} %get-tuple-element.16.qt_ref, f32[4,512]{1,0:T(4,128)S(1)} %get-tuple-element.17.bias_ref, bf16[200,256]{1,0:T(8,128)(2,1)S(1)} %sum_norm.1.refs_0_), custom_call_target="tpu_custom_call" | custom-call | flops 52428800 | tf_op jit(solution)/shard_map/attend/pallas_call | solution.py:412
  20.7 0.0 collective-permute-done.7.refs_1_
  20.8 1.0 %collective-permute-done.6.refs_0_ = bf16[200,256]{1,0:T(8,128)(2,1)S(1)} collective-permute-done((bf16[200,256]{1,0:T(8,128)(2,1)S(1)}, bf16[200,256]{1,0:T(8,128)(2,1)S(1)}, u32[]{:S(2)}, u32[]{:S(2)}) %collective-permute-start.6) | collective-permute-done | bytes 102432 | tf_op jit(solution)/shard_map/ppermute | solution.py:256
  21.8 0.6 %attend.4 = (f32[1,512]{1,0:T(1,128)S(1)}, f32[1,512]{1,0:T(1,128)S(1)}, f32[128,512]{1,0:T(8,128)S(1)}) custom-call(f32[1,128]{1,0:T(1,128)S(1)} %get-tuple-element.15.k_gain_ref, bf16[128,512]{1,0:T(8,128)(2,1)S(1)} %get-tuple-element.16.qt_ref, f32[4,512]{1,0:T(4,128)S(1)} %get-tuple-element.17.bias_ref, ...), custom_call_target="tpu_custom_call" | custom-call | flops 104857600 | tf_op jit(solution)/shard_map/attend/pallas_call | solution.py:412
  22.3 0.6 %collective-permute-done.4.refs_1_ = bf16[1,200,256]{2,1,0:T(8,128)(2,1)S(1)} collective-permute-done((bf16[1,200,256]{2,1,0:T(8,128)(2,1)S(1)}, bf16[1,200,256]{2,1,0:T(8,128)(2,1)S(1)}, u32[]{:S(2)}, u32[]{:S(2)}) %collective-permute-start.4) | collective-permute-done | bytes 102432 | tf_op jit(solution)/shard_map/ppermute | solution.py:256
  23.0 1.3 %attend.5 = bf16[128,512]{1,0:T(8,128)(2,1)} custom-call(f32[1,128]{1,0:T(1,128)S(1)} %get-tuple-element.15.k_gain_ref, bf16[128,512]{1,0:T(8,128)(2,1)S(1)} %get-tuple-element.16.qt_ref, f32[4,512]{1,0:T(4,128)S(1)} %get-tuple-element.17.bias_ref, bf16[1,200,256]{2,1,0:T(8,128)(2,1)S(1)} %collective-permute-done.3.refs_0_, ...), custom_call_target="tpu_custom_call" | custom-call | flops 52428800 | tf_op jit(solution)/shard_map/attend/pallas_call | solution.py:412
  (2 shorter events, 0.1 us)
Async XLA Ops:
  0.0 3.8 %collective-permute-start = (bf16[2,2048,128]{2,1,0:T(8,128)(2,1)}, bf16[2,2048,128]{2,1,0:T(8,128)(2,1)S(1)}, u32[]{:S(2)}, u32[]{:S(2)}) collective-permute-start(bf16[2,2048,128]{2,1,0:T(8,128)(2,1)} %w_hbm.3), channel_id=1, source_target_pairs={{0,4},{4,0},{1,5},{5,1},{2,6},{6,2},{3,7},{7,3},{8,12},{12,8},{9,1... | collective-permute-start | bytes 3145736 | tf_op jit(solution)/shard_map/ppermute | solution.py:256
  0.5 8.5 %collective-permute-start.1 = (bf16[1,200,256]{2,1,0:T(8,128)(2,1)S(1)}, bf16[1,200,256]{2,1,0:T(8,128)(2,1)S(1)}, u32[]{:S(2)}, u32[]{:S(2)}) collective-permute-start(bf16[1,200,256]{2,1,0:T(8,128)(2,1)S(1)} %away_own.1.after_ref), channel_id=1, source_target_pairs={{0,4},{1,5},{2,0},{3,1},{4,6},{5,7},{6,2},{7,3},{8,12},{9,13},{10,... | collective-permute-start | bytes 307208 | tf_op jit(solution)/shard_map/ppermute | solution.py:265
  4.2 5.0 %collective-permute-start.2 = (bf16[1,200,256]{2,1,0:T(8,128)(2,1)S(1)}, bf16[1,200,256]{2,1,0:T(8,128)(2,1)S(1)}, u32[]{:S(2)}, u32[]{:S(2)}) collective-permute-start(bf16[1,200,256]{2,1,0:T(8,128)(2,1)S(1)} %home_other.1.after_ref), channel_id=1, source_target_pairs={{0,2},{1,3},{2,6},{3,7},{4,0},{5,1},{6,4},{7,5},{8,10},{9,11},{10,... | collective-permute-start | bytes 307208 | tf_op jit(solution)/shard_map/ppermute | solution.py:265
  9.3 5.4 %collective-permute-start.5 = (bf16[1,200,256]{2,1,0:T(8,128)(2,1)S(1)}, bf16[1,200,256]{2,1,0:T(8,128)(2,1)S(1)}, u32[]{:S(2)}, u32[]{:S(2)}) collective-permute-start(bf16[1,200,256]{2,1,0:T(8,128)(2,1)S(1)} %pair_sum.1.keep_ref), channel_id=1, source_target_pairs={{0,1},{1,0},{2,3},{3,2},{4,5},{5,4},{6,7},{7,6},{8,9},{9,8},{10,11... | collective-permute-start | bytes 307208 | tf_op jit(solution)/shard_map/ppermute | solution.py:256
  11.8 6.0 %collective-permute-start.3 = (bf16[1,200,256]{2,1,0:T(8,128)(2,1)S(1)}, bf16[1,200,256]{2,1,0:T(8,128)(2,1)S(1)}, u32[]{:S(2)}, u32[]{:S(2)}) collective-permute-start(bf16[1,200,256]{2,1,0:T(8,128)(2,1)S(1)} %pair_sum.1.keep_ref), channel_id=1, source_target_pairs={{0,24},{8,16},{16,8},{24,0},{1,25},{9,17},{17,9},{25,1},{2,26},{10... | collective-permute-start | bytes 307208 | tf_op jit(solution)/shard_map/ppermute | solution.py:256
  14.8 6.0 %collective-permute-start.7 = (bf16[200,256]{1,0:T(8,128)(2,1)S(1)}, bf16[200,256]{1,0:T(8,128)(2,1)S(1)}, u32[]{:S(2)}, u32[]{:S(2)}) collective-permute-start(bf16[200,256]{1,0:T(8,128)(2,1)S(1)} %sum_norm.1.refs_0_), channel_id=1, source_target_pairs={{0,16},{8,24},{16,0},{24,8},{1,17},{9,25},{17,1},{25,9},{2,18},{10... | collective-permute-start | bytes 307208 | tf_op jit(solution)/shard_map/ppermute | solution.py:256
  16.3 5.4 %collective-permute-start.6 = (bf16[200,256]{1,0:T(8,128)(2,1)S(1)}, bf16[200,256]{1,0:T(8,128)(2,1)S(1)}, u32[]{:S(2)}, u32[]{:S(2)}) collective-permute-start(bf16[200,256]{1,0:T(8,128)(2,1)S(1)} %sum_norm.1.refs_0_), channel_id=1, source_target_pairs={{0,8},{8,0},{16,24},{24,16},{1,9},{9,1},{17,25},{25,17},{2,10},{10... | collective-permute-start | bytes 307208 | tf_op jit(solution)/shard_map/ppermute | solution.py:256
  17.8 5.1 %collective-permute-start.4 = (bf16[1,200,256]{2,1,0:T(8,128)(2,1)S(1)}, bf16[1,200,256]{2,1,0:T(8,128)(2,1)S(1)}, u32[]{:S(2)}, u32[]{:S(2)}) collective-permute-start(bf16[1,200,256]{2,1,0:T(8,128)(2,1)S(1)} %collective-permute-done.3.refs_0_), channel_id=1, source_target_pairs={{0,1},{1,0},{2,3},{3,2},{4,5},{5,4},{6,7},{7,6},{8,9},{9,8},{10,11... | collective-permute-start | bytes 307208 | tf_op jit(solution)/shard_map/ppermute | solution.py:256

commit v17 on v13

--- a/solution.py
+++ b/solution.py
@@ -54,8 +54,8 @@
     width = both.shape[1] // 2
     for head in range(width // head_dim):
         lo = head * head_dim
-        ref[base + head, 0] = both[:, lo : lo + head_dim]
-        ref[base + head, 1] = both[:, width + lo : width + lo + head_dim]
+        ref[base + head, :, :head_dim] = both[:, lo : lo + head_dim]
+        ref[base + head, :, head_dim:] = both[:, width + lo : width + lo + head_dim]
 
 
 def prepare_queries(copies, q_ref, q_gain_ref, mask_ref, qt_ref, bias_ref):
@@ -184,13 +184,16 @@
 
 
 def finish_rows(k_gain, one, two):
-    keys = one[0].astype(F32) + two[0].astype(F32)
-    values = one[1].astype(F32) + two[1].astype(F32)
-    return normalize(keys, k_gain).astype(BF16), values.astype(BF16)
+    total = one[...].astype(F32) + two[...].astype(F32)
+    head_dim = total.shape[1] // 2
+    keys = normalize(total[:, :head_dim], k_gain).astype(BF16)
+    return keys, total[:, head_dim:].astype(BF16)
 
 
 def norm_kernel(k_gain_ref, keep_ref, arrived_ref, kv_ref):
-    kv_ref[0], kv_ref[1] = finish_rows(k_gain_ref[...], keep_ref.at[0], arrived_ref.at[0])
+    keys, values = finish_rows(k_gain_ref[...], keep_ref.at[0], arrived_ref.at[0])
+    kv_ref[:, : keys.shape[1]] = keys
+    kv_ref[:, keys.shape[1] :] = values
 
 
 def attend_kernel(near, far, tile_len, first, last, head_dim, k_gain_ref, qt_ref, bias_ref, *refs):
@@ -201,7 +204,7 @@
         refs = refs[3:]
     s = lax.axis_index("section")
     qt = qt_ref[...]
-    parts = [(part[0], part[1]) for part in near_refs]
+    parts = [(part[:, :head_dim], part[:, head_dim:]) for part in near_refs]
     for one, two in zip(far_refs[::2], far_refs[1::2]):
         parts.append(finish_rows(k_gain_ref[...], one.at[0], two.at[0]))
     rows = parts[0][0].shape[0]
@@ -305,7 +308,7 @@
             images, kv_weight, queries, q_gain.reshape(1, -1), tile_mask.T, k_gain.reshape(1, -1),
         )
     ]
-    product = shape_of((own_heads, 2, rows, head_dim))
+    product = shape_of((own_heads, rows, 2 * head_dim))
     w_scratch = pltpu.VMEM(kv_weight.shape, BF16)
     prepared = [
         shape_of((head_dim, pairs)),
@@ -381,7 +384,7 @@
     near = [step for step in range(1, n_section) if not step & (step - 1)]
     arrived = swap(total, "tensor", 1)
     halves = [swap(total, "section", step) for step in far]
-    kv = call(norm_kernel, shape_of((2, rows, head_dim)), 3, "sum_norm")(gain, total, arrived)
+    kv = call(norm_kernel, shape_of((rows, 2 * head_dim)), 3, "sum_norm")(gain, total, arrived)
     finished = [swap(kv, "section", step) for step in near]
     both = []
     for value in halves:

time: 24.2 us -> 24.2 us (level)
  no operation moved by 1% of the time
where the time goes in v17:
time: 24.2 us; the launch traced here: 24.1 us
  starting transfers between devices  15.6 us (64%)
  Pallas kernels  5.64 us (23%)
  waiting for transfers between devices  2.8 us (12%)
    ppermute x6, starting transfers between devices, swap(): lax.ppermute(value, axis, [(i, i ^ k) for i in range(lax.axis_size(axis))])  11 us
    ppermute x2, starting transfers between devices, exchange_two_heads(): return lax.ppermute(value, ('dp', 'tensor'), hops)  4.57 us
    pallas_call x3, Pallas kernels, on_device(): call(functools.partial(attend_kernel, here, there, tile_len, first, last,...  2.27 us
    ppermute x6, waiting for transfers between devices, swap(): lax.ppermute(value, axis, [(i, i ^ k) for i in range(lax.axis_size(axis))])  1.84 us
    pallas_call x1, Pallas kernels, on_device(): call(load_kernel, [shape_of(images.shape), shape_of(kv_weight.shape)], 3,...  1.49 us
    pallas_call x1, Pallas kernels, on_device(): call(functools.partial(keep_kernel, head_dim), [product, *prepared], 8, '...  1.28 us
    ppermute x2, waiting for transfers between devices, exchange_two_heads(): return lax.ppermute(value, ('dp', 'tensor'), hops)  0.96 us
  transfers between devices with their start and end apart: 8, of which 5 were waited for; matrix products, arithmetic and copies ran while one was open for 0% of the time, Pallas kernels for 18%

profile of v17, /device:TPU:0, one launch (start us, length us, event | category | flops | bytes accessed | tf_op | source)
XLA Modules:
  0.0 24.1 jit_solution(9969265307843953167)
XLA Ops:
  0.0 0.5 %collective-permute-start = (bf16[2,2048,128]{2,1,0:T(8,128)(2,1)}, bf16[2,2048,128]{2,1,0:T(8,128)(2,1)S(1)}, u32[]{:S(2)}, u32[]{:S(2)}) collective-permute-start(bf16[2,2048,128]{2,1,0:T(8,128)(2,1)} %w_hbm.3), channel_id=1, source_target_pairs={{0,4},{4,0},{1,5},{5,1},{2,6},{6,2},{3,7},{7,3},{8,12},{12,8},{9,1... | collective-permute-start | bytes 3145736 | tf_op jit(solution)/shard_map/ppermute | solution.py:248
  0.5 2.0 %collective-permute-start.1 = (bf16[1,200,256]{2,1,0:T(8,128)(2,1)S(1)}, bf16[1,200,256]{2,1,0:T(8,128)(2,1)S(1)}, u32[]{:S(2)}, u32[]{:S(2)}) collective-permute-start(bf16[1,200,256]{2,1,0:T(8,128)(2,1)S(1)} %get-tuple-element.26), channel_id=1, source_target_pairs={{0,4},{1,5},{2,0},{3,1},{4,6},{5,7},{6,2},{7,3},{8,12},{9,13},{10,... | collective-permute-start | bytes 307208 | tf_op jit(solution)/shard_map/ppermute | solution.py:257
  2.5 1.5 %home_load.1 = (bf16[1,200,2048]{2,1,0:T(8,128)(2,1)S(1)}, bf16[2,2048,128]{2,1,0:T(8,128)(2,1)S(1)}) custom-call(bf16[1,200,2048]{2,1,0:T(8,128)(2,1)S(1)} %get-tuple-element.19.x_in, bf16[1,200,2048]{2,1,0:T(8,128)(2,1)} %x_hbm.3, bf16[2,2048,128]{2,1,0:T(8,128)(2,1)} %w_hbm.3), custom_call_target="tpu_custom_call", output_to_operand_aliasing={{0}: (0, {})} | custom-call | tf_op jit(solution)/shard_map/home_load/pallas_call | solution.py:335
  4.0 0.0 collective-permute-done.w_other_ref
  4.0 0.4 %home_other.1.after_ref = bf16[1,200,256]{2,1,0:T(8,128)(2,1)S(1)} custom-call(bf16[1,200,2048]{2,1,0:T(8,128)(2,1)S(1)} %get-tuple-element.20.x_ref, bf16[2,2048,128]{2,1,0:T(8,128)(2,1)S(1)} %collective-permute-done.w_other_ref), custom_call_target="tpu_custom_call" | custom-call | flops 209715200 | tf_op jit(solution)/shard_map/home_other/pallas_call | solution.py:344
  4.4 2.6 %collective-permute-start.2 = (bf16[1,200,256]{2,1,0:T(8,128)(2,1)S(1)}, bf16[1,200,256]{2,1,0:T(8,128)(2,1)S(1)}, u32[]{:S(2)}, u32[]{:S(2)}) collective-permute-start(bf16[1,200,256]{2,1,0:T(8,128)(2,1)S(1)} %home_other.1.after_ref), channel_id=1, source_target_pairs={{0,2},{1,3},{2,6},{3,7},{4,0},{5,1},{6,4},{7,5},{8,10},{9,11},{10,... | collective-permute-start | bytes 307208 | tf_op jit(solution)/shard_map/ppermute | solution.py:257
  7.0 1.3 %keep_queries.1 = (bf16[1,200,256]{2,1,0:T(8,128)(2,1)S(1)}, bf16[128,512]{1,0:T(8,128)(2,1)S(1)}, f32[4,512]{1,0:T(4,128)S(1)}, f32[1,128]{1,0:T(1,128)S(1)}) custom-call(bf16[1,200,256]{2,1,0:T(8,128)(2,1)S(1)} %home_other.1.after_ref, bf16[2,2048,128]{2,1,0:T(8,128)(2,1)S(1)} %collective-permute-done.w_other_ref, ...), custom_call_target="tpu_custom_call" | custom-call | flops 209715200 | tf_op jit(solution)/shard_map/keep_queries/pallas_call | solution.py:348
  8.3 0.4 %collective-permute-done.1.first_ref = bf16[1,200,256]{2,1,0:T(8,128)(2,1)S(1)} collective-permute-done((bf16[1,200,256]{2,1,0:T(8,128)(2,1)S(1)}, bf16[1,200,256]{2,1,0:T(8,128)(2,1)S(1)}, u32[]{:S(2)}, u32[]{:S(2)}) %collective-permute-start.1) | collective-permute-done | bytes 102432 | tf_op jit(solution)/shard_map/ppermute | solution.py:257
  8.7 0.6 %collective-permute-done.2.second_ref = bf16[1,200,256]{2,1,0:T(8,128)(2,1)S(1)} collective-permute-done((bf16[1,200,256]{2,1,0:T(8,128)(2,1)S(1)}, bf16[1,200,256]{2,1,0:T(8,128)(2,1)S(1)}, u32[]{:S(2)}, u32[]{:S(2)}) %collective-permute-start.2) | collective-permute-done | bytes 102432 | tf_op jit(solution)/shard_map/ppermute | solution.py:257
  9.3 2.6 %collective-permute-start.5 = (bf16[1,200,256]{2,1,0:T(8,128)(2,1)S(1)}, bf16[1,200,256]{2,1,0:T(8,128)(2,1)S(1)}, u32[]{:S(2)}, u32[]{:S(2)}) collective-permute-start(bf16[1,200,256]{2,1,0:T(8,128)(2,1)S(1)} %pair_sum.1.keep_ref), channel_id=1, source_target_pairs={{0,1},{1,0},{2,3},{3,2},{4,5},{5,4},{6,7},{7,6},{8,9},{9,8},{10,11... | collective-permute-start | bytes 307208 | tf_op jit(solution)/shard_map/ppermute | solution.py:248
  11.8 2.4 %collective-permute-start.3 = (bf16[1,200,256]{2,1,0:T(8,128)(2,1)S(1)}, bf16[1,200,256]{2,1,0:T(8,128)(2,1)S(1)}, u32[]{:S(2)}, u32[]{:S(2)}) collective-permute-start(bf16[1,200,256]{2,1,0:T(8,128)(2,1)S(1)} %pair_sum.1.keep_ref), channel_id=1, source_target_pairs={{0,24},{8,16},{16,8},{24,0},{1,25},{9,17},{17,9},{25,1},{2,26},{10... | collective-permute-start | bytes 307208 | tf_op jit(solution)/shard_map/ppermute | solution.py:248
  14.3 0.2 collective-permute-done.5.arrived_ref
  14.5 0.1 sum_norm.1.refs_0_
  14.6 1.6 %collective-permute-start.7 = (bf16[200,256]{1,0:T(8,128)(2,1)S(1)}, bf16[200,256]{1,0:T(8,128)(2,1)S(1)}, u32[]{:S(2)}, u32[]{:S(2)}) collective-permute-start(bf16[200,256]{1,0:T(8,128)(2,1)S(1)} %sum_norm.1.refs_0_), channel_id=1, source_target_pairs={{0,16},{8,24},{16,0},{24,8},{1,17},{9,25},{17,1},{25,9},{2,18},{10... | collective-permute-start | bytes 307208 | tf_op jit(solution)/shard_map/ppermute | solution.py:248
  16.2 1.5 %collective-permute-start.6 = (bf16[200,256]{1,0:T(8,128)(2,1)S(1)}, bf16[200,256]{1,0:T(8,128)(2,1)S(1)}, u32[]{:S(2)}, u32[]{:S(2)}) collective-permute-start(bf16[200,256]{1,0:T(8,128)(2,1)S(1)} %sum_norm.1.refs_0_), channel_id=1, source_target_pairs={{0,8},{8,0},{16,24},{24,16},{1,9},{9,1},{17,25},{25,17},{2,10},{10... | collective-permute-start | bytes 307208 | tf_op jit(solution)/shard_map/ppermute | solution.py:248
  17.7 0.0 collective-permute-done.3.refs_0_
  17.7 2.5 %collective-permute-start.4 = (bf16[1,200,256]{2,1,0:T(8,128)(2,1)S(1)}, bf16[1,200,256]{2,1,0:T(8,128)(2,1)S(1)}, u32[]{:S(2)}, u32[]{:S(2)}) collective-permute-start(bf16[1,200,256]{2,1,0:T(8,128)(2,1)S(1)} %collective-permute-done.3.refs_0_), channel_id=1, source_target_pairs={{0,1},{1,0},{2,3},{3,2},{4,5},{5,4},{6,7},{7,6},{8,9},{9,8},{10,11... | collective-permute-start | bytes 307208 | tf_op jit(solution)/shard_map/ppermute | solution.py:248
  20.1 0.4 %attend.3 = (f32[1,512]{1,0:T(1,128)S(1)}, f32[1,512]{1,0:T(1,128)S(1)}, f32[128,512]{1,0:T(8,128)S(1)}) custom-call(f32[1,128]{1,0:T(1,128)S(1)} %get-tuple-element.22.k_gain_ref, bf16[128,512]{1,0:T(8,128)(2,1)S(1)} %get-tuple-element.23.qt_ref, f32[4,512]{1,0:T(4,128)S(1)} %get-tuple-element.24.bias_ref, bf16[200,256]{1,0:T(8,128)(2,1)S(1)} %sum_norm.1.refs_0_), custom_call_target="tpu_custom_call" | custom-call | flops 52428800 | tf_op jit(solution)/shard_map/attend/pallas_call | solution.py:405
  20.6 0.0 collective-permute-done.7.refs_1_
  20.6 1.0 %collective-permute-done.6.refs_0_ = bf16[200,256]{1,0:T(8,128)(2,1)S(1)} collective-permute-done((bf16[200,256]{1,0:T(8,128)(2,1)S(1)}, bf16[200,256]{1,0:T(8,128)(2,1)S(1)}, u32[]{:S(2)}, u32[]{:S(2)}) %collective-permute-start.6) | collective-permute-done | bytes 102432 | tf_op jit(solution)/shard_map/ppermute | solution.py:248
  21.6 0.6 %attend.4 = (f32[1,512]{1,0:T(1,128)S(1)}, f32[1,512]{1,0:T(1,128)S(1)}, f32[128,512]{1,0:T(8,128)S(1)}) custom-call(f32[1,128]{1,0:T(1,128)S(1)} %get-tuple-element.22.k_gain_ref, bf16[128,512]{1,0:T(8,128)(2,1)S(1)} %get-tuple-element.23.qt_ref, f32[4,512]{1,0:T(4,128)S(1)} %get-tuple-element.24.bias_ref, ...), custom_call_target="tpu_custom_call" | custom-call | flops 104857600 | tf_op jit(solution)/shard_map/attend/pallas_call | solution.py:405
  22.2 0.6 %collective-permute-done.4.refs_1_ = bf16[1,200,256]{2,1,0:T(8,128)(2,1)S(1)} collective-permute-done((bf16[1,200,256]{2,1,0:T(8,128)(2,1)S(1)}, bf16[1,200,256]{2,1,0:T(8,128)(2,1)S(1)}, u32[]{:S(2)}, u32[]{:S(2)}) %collective-permute-start.4) | collective-permute-done | bytes 102432 | tf_op jit(solution)/shard_map/ppermute | solution.py:248
  22.8 1.3 %attend.5 = bf16[128,512]{1,0:T(8,128)(2,1)} custom-call(f32[1,128]{1,0:T(1,128)S(1)} %get-tuple-element.22.k_gain_ref, bf16[128,512]{1,0:T(8,128)(2,1)S(1)} %get-tuple-element.23.qt_ref, f32[4,512]{1,0:T(4,128)S(1)} %get-tuple-element.24.bias_ref, bf16[1,200,256]{2,1,0:T(8,128)(2,1)S(1)} %collective-permute-done.3.refs_0_, ...), custom_call_target="tpu_custom_call" | custom-call | flops 52428800 | tf_op jit(solution)/shard_map/attend/pallas_call | solution.py:405
  (2 shorter events, 0.1 us)
Async XLA Ops:
  0.0 4.0 %collective-permute-start = (bf16[2,2048,128]{2,1,0:T(8,128)(2,1)}, bf16[2,2048,128]{2,1,0:T(8,128)(2,1)S(1)}, u32[]{:S(2)}, u32[]{:S(2)}) collective-permute-start(bf16[2,2048,128]{2,1,0:T(8,128)(2,1)} %w_hbm.3), channel_id=1, source_target_pairs={{0,4},{4,0},{1,5},{5,1},{2,6},{6,2},{3,7},{7,3},{8,12},{12,8},{9,1... | collective-permute-start | bytes 3145736 | tf_op jit(solution)/shard_map/ppermute | solution.py:248
  0.5 8.2 %collective-permute-start.1 = (bf16[1,200,256]{2,1,0:T(8,128)(2,1)S(1)}, bf16[1,200,256]{2,1,0:T(8,128)(2,1)S(1)}, u32[]{:S(2)}, u32[]{:S(2)}) collective-permute-start(bf16[1,200,256]{2,1,0:T(8,128)(2,1)S(1)} %get-tuple-element.26), channel_id=1, source_target_pairs={{0,4},{1,5},{2,0},{3,1},{4,6},{5,7},{6,2},{7,3},{8,12},{9,13},{10,... | collective-permute-start | bytes 307208 | tf_op jit(solution)/shard_map/ppermute | solution.py:257
  4.4 4.8 %collective-permute-start.2 = (bf16[1,200,256]{2,1,0:T(8,128)(2,1)S(1)}, bf16[1,200,256]{2,1,0:T(8,128)(2,1)S(1)}, u32[]{:S(2)}, u32[]{:S(2)}) collective-permute-start(bf16[1,200,256]{2,1,0:T(8,128)(2,1)S(1)} %home_other.1.after_ref), channel_id=1, source_target_pairs={{0,2},{1,3},{2,6},{3,7},{4,0},{5,1},{6,4},{7,5},{8,10},{9,11},{10,... | collective-permute-start | bytes 307208 | tf_op jit(solution)/shard_map/ppermute | solution.py:257
  9.3 5.2 %collective-permute-start.5 = (bf16[1,200,256]{2,1,0:T(8,128)(2,1)S(1)}, bf16[1,200,256]{2,1,0:T(8,128)(2,1)S(1)}, u32[]{:S(2)}, u32[]{:S(2)}) collective-permute-start(bf16[1,200,256]{2,1,0:T(8,128)(2,1)S(1)} %pair_sum.1.keep_ref), channel_id=1, source_target_pairs={{0,1},{1,0},{2,3},{3,2},{4,5},{5,4},{6,7},{7,6},{8,9},{9,8},{10,11... | collective-permute-start | bytes 307208 | tf_op jit(solution)/shard_map/ppermute | solution.py:248
  11.8 5.8 %collective-permute-start.3 = (bf16[1,200,256]{2,1,0:T(8,128)(2,1)S(1)}, bf16[1,200,256]{2,1,0:T(8,128)(2,1)S(1)}, u32[]{:S(2)}, u32[]{:S(2)}) collective-permute-start(bf16[1,200,256]{2,1,0:T(8,128)(2,1)S(1)} %pair_sum.1.keep_ref), channel_id=1, source_target_pairs={{0,24},{8,16},{16,8},{24,0},{1,25},{9,17},{17,9},{25,1},{2,26},{10... | collective-permute-start | bytes 307208 | tf_op jit(solution)/shard_map/ppermute | solution.py:248
  14.6 6.0 %collective-permute-start.7 = (bf16[200,256]{1,0:T(8,128)(2,1)S(1)}, bf16[200,256]{1,0:T(8,128)(2,1)S(1)}, u32[]{:S(2)}, u32[]{:S(2)}) collective-permute-start(bf16[200,256]{1,0:T(8,128)(2,1)S(1)} %sum_norm.1.refs_0_), channel_id=1, source_target_pairs={{0,16},{8,24},{16,0},{24,8},{1,17},{9,25},{17,1},{25,9},{2,18},{10... | collective-permute-start | bytes 307208 | tf_op jit(solution)/shard_map/ppermute | solution.py:248
  16.2 5.4 %collective-permute-start.6 = (bf16[200,256]{1,0:T(8,128)(2,1)S(1)}, bf16[200,256]{1,0:T(8,128)(2,1)S(1)}, u32[]{:S(2)}, u32[]{:S(2)}) collective-permute-start(bf16[200,256]{1,0:T(8,128)(2,1)S(1)} %sum_norm.1.refs_0_), channel_id=1, source_target_pairs={{0,8},{8,0},{16,24},{24,16},{1,9},{9,1},{17,25},{25,17},{2,10},{10... | collective-permute-start | bytes 307208 | tf_op jit(solution)/shard_map/ppermute | solution.py:248
  17.7 5.1 %collective-permute-start.4 = (bf16[1,200,256]{2,1,0:T(8,128)(2,1)S(1)}, bf16[1,200,256]{2,1,0:T(8,128)(2,1)S(1)}, u32[]{:S(2)}, u32[]{:S(2)}) collective-permute-start(bf16[1,200,256]{2,1,0:T(8,128)(2,1)S(1)} %collective-permute-done.3.refs_0_), channel_id=1, source_target_pairs={{0,1},{1,0},{2,3},{3,2},{4,5},{5,4},{6,7},{7,6},{8,9},{9,8},{10,11... | collective-permute-start | bytes 307208 | tf_op jit(solution)/shard_map/ppermute | solution.py:248

commit v18 on v17

--- a/solution.py
+++ b/solution.py
@@ -212,6 +212,8 @@
     top = TOP_FLOOR if first else top_in[...]
     for step, (keys, _) in zip((*near, *far), parts):
         score = jnp.dot(keys, qt, preferred_element_type=F32)
+        first_step, second_step = step
+        step = first_step + lax.axis_index("dp") % 2 * (second_step - first_step)
         bias = bias_ref[pl.ds(((s ^ step) * rows) // tile_len, 1), :]
         scores.append(score)
         biases.append(bias)
@@ -385,17 +387,26 @@
     arrived = swap(total, "tensor", 1)
     halves = [swap(total, "section", step) for step in far]
     kv = call(norm_kernel, shape_of((rows, 2 * head_dim)), 3, "sum_norm")(gain, total, arrived)
-    finished = [swap(kv, "section", step) for step in near]
+    near = list(zip(near, reversed(near)))
+    far = [(step, step) for step in far]
+    finished = []
+    for even, odd in near:
+        hops = [
+            (s * n_dp + d, (s ^ (odd if d % 2 else even)) * n_dp + d)
+            for s in range(n_section)
+            for d in range(n_dp)
+        ]
+        finished.append(lax.ppermute(kv, ("section", "dp"), hops))
     both = []
     for value in halves:
         both += [value, swap(value, "tensor", 1)]
     state = []
     for here, there, operands in (
-        ([0], [], [kv]),
+        ([(0, 0)], [], [kv]),
         (near, [], finished),
         ([], far, both),
     ):
-        first, last = here == [0], len(there) > 0
+        first, last = here == [(0, 0)], len(there) > 0
         outs = (
             shape_of((tokens, q_width))
             if last

time: 24.2 us -> 24.3 us (level)
    ppermute x0 -> x2, starting transfers between devices: none -> 3.08 us  [on_device(): finished.append(lax.ppermute(kv, ('section', 'dp'), hops))]
    ppermute x6 -> x4, starting transfers between devices: 11 us -> 7.92 us  [swap(): lax.ppermute(value, axis, [(i, i ^ k) for i in range(lax.axis_size(axis))])]
    ppermute x0 -> x2, waiting for transfers between devices: none -> 0.25 us  [on_device(): finished.append(lax.ppermute(kv, ('section', 'dp'), hops))]
    ppermute x6 -> x4, waiting for transfers between devices: 1.84 us -> 1.61 us  [swap(): lax.ppermute(value, axis, [(i, i ^ k) for i in range(lax.axis_size(axis))])]
where the time goes in v18:
time: 24.3 us; the launch traced here: 24.1 us
  starting transfers between devices  15.6 us (64%)
  Pallas kernels  5.64 us (23%)
  waiting for transfers between devices  2.82 us (12%)
    ppermute x4, starting transfers between devices, swap(): lax.ppermute(value, axis, [(i, i ^ k) for i in range(lax.axis_size(axis))])  7.92 us
    ppermute x2, starting transfers between devices, exchange_two_heads(): return lax.ppermute(value, ('dp', 'tensor'), hops)  4.57 us
    ppermute x2, starting transfers between devices, on_device(): finished.append(lax.ppermute(kv, ('section', 'dp'), hops))  3.08 us
    pallas_call x3, Pallas kernels, on_device(): call(functools.partial(attend_kernel, here, there, tile_len, first, last,...  2.27 us
    ppermute x4, waiting for transfers between devices, swap(): lax.ppermute(value, axis, [(i, i ^ k) for i in range(lax.axis_size(axis))])  1.61 us
    pallas_call x1, Pallas kernels, on_device(): call(load_kernel, [shape_of(images.shape), shape_of(kv_weight.shape)], 3,...  1.49 us
    pallas_call x1, Pallas kernels, on_device(): call(functools.partial(keep_kernel, head_dim), [product, *prepared], 8, '...  1.28 us
    ppermute x2, waiting for transfers between devices, exchange_two_heads(): return lax.ppermute(value, ('dp', 'tensor'), hops)  0.96 us
  transfers between devices with their start and end apart: 8, of which 5 were waited for; matrix products, arithmetic and copies ran while one was open for 0% of the time, Pallas kernels for 18%

profile of v18, /device:TPU:0, one launch (start us, length us, event | category | flops | bytes accessed | tf_op | source)
XLA Modules:
  0.0 24.1 jit_solution(14773180119365568653)
XLA Ops:
  0.0 0.5 %collective-permute-start = (bf16[2,2048,128]{2,1,0:T(8,128)(2,1)}, bf16[2,2048,128]{2,1,0:T(8,128)(2,1)S(1)}, u32[]{:S(2)}, u32[]{:S(2)}) collective-permute-start(bf16[2,2048,128]{2,1,0:T(8,128)(2,1)} %w_hbm.3), channel_id=1, source_target_pairs={{0,4},{4,0},{1,5},{5,1},{2,6},{6,2},{3,7},{7,3},{8,12},{12,8},{9,1... | collective-permute-start | bytes 3145736 | tf_op jit(solution)/shard_map/ppermute | solution.py:250
  0.5 2.0 %collective-permute-start.1 = (bf16[1,200,256]{2,1,0:T(8,128)(2,1)S(1)}, bf16[1,200,256]{2,1,0:T(8,128)(2,1)S(1)}, u32[]{:S(2)}, u32[]{:S(2)}) collective-permute-start(bf16[1,200,256]{2,1,0:T(8,128)(2,1)S(1)} %get-tuple-element.26), channel_id=1, source_target_pairs={{0,4},{1,5},{2,0},{3,1},{4,6},{5,7},{6,2},{7,3},{8,12},{9,13},{10,... | collective-permute-start | bytes 307208 | tf_op jit(solution)/shard_map/ppermute | solution.py:259
  2.5 1.5 %home_load.1 = (bf16[1,200,2048]{2,1,0:T(8,128)(2,1)S(1)}, bf16[2,2048,128]{2,1,0:T(8,128)(2,1)S(1)}) custom-call(bf16[1,200,2048]{2,1,0:T(8,128)(2,1)S(1)} %get-tuple-element.19.x_in, bf16[1,200,2048]{2,1,0:T(8,128)(2,1)} %x_hbm.3, bf16[2,2048,128]{2,1,0:T(8,128)(2,1)} %w_hbm.3), custom_call_target="tpu_custom_call", output_to_operand_aliasing={{0}: (0, {})} | custom-call | tf_op jit(solution)/shard_map/home_load/pallas_call | solution.py:337
  4.0 0.0 collective-permute-done.w_other_ref
  4.0 0.4 %home_other.1.after_ref = bf16[1,200,256]{2,1,0:T(8,128)(2,1)S(1)} custom-call(bf16[1,200,2048]{2,1,0:T(8,128)(2,1)S(1)} %get-tuple-element.20.x_ref, bf16[2,2048,128]{2,1,0:T(8,128)(2,1)S(1)} %collective-permute-done.w_other_ref), custom_call_target="tpu_custom_call" | custom-call | flops 209715200 | tf_op jit(solution)/shard_map/home_other/pallas_call | solution.py:346
  4.4 2.6 %collective-permute-start.2 = (bf16[1,200,256]{2,1,0:T(8,128)(2,1)S(1)}, bf16[1,200,256]{2,1,0:T(8,128)(2,1)S(1)}, u32[]{:S(2)}, u32[]{:S(2)}) collective-permute-start(bf16[1,200,256]{2,1,0:T(8,128)(2,1)S(1)} %home_other.1.after_ref), channel_id=1, source_target_pairs={{0,2},{1,3},{2,6},{3,7},{4,0},{5,1},{6,4},{7,5},{8,10},{9,11},{10,... | collective-permute-start | bytes 307208 | tf_op jit(solution)/shard_map/ppermute | solution.py:259
  7.0 1.3 %keep_queries.1 = (bf16[1,200,256]{2,1,0:T(8,128)(2,1)S(1)}, bf16[128,512]{1,0:T(8,128)(2,1)S(1)}, f32[4,512]{1,0:T(4,128)S(1)}, f32[1,128]{1,0:T(1,128)S(1)}) custom-call(bf16[1,200,256]{2,1,0:T(8,128)(2,1)S(1)} %home_other.1.after_ref, bf16[2,2048,128]{2,1,0:T(8,128)(2,1)S(1)} %collective-permute-done.w_other_ref, ...), custom_call_target="tpu_custom_call" | custom-call | flops 209715200 | tf_op jit(solution)/shard_map/keep_queries/pallas_call | solution.py:350
  8.3 0.4 %collective-permute-done.1.first_ref = bf16[1,200,256]{2,1,0:T(8,128)(2,1)S(1)} collective-permute-done((bf16[1,200,256]{2,1,0:T(8,128)(2,1)S(1)}, bf16[1,200,256]{2,1,0:T(8,128)(2,1)S(1)}, u32[]{:S(2)}, u32[]{:S(2)}) %collective-permute-start.1) | collective-permute-done | bytes 102432 | tf_op jit(solution)/shard_map/ppermute | solution.py:259
  8.7 0.6 %collective-permute-done.2.second_ref = bf16[1,200,256]{2,1,0:T(8,128)(2,1)S(1)} collective-permute-done((bf16[1,200,256]{2,1,0:T(8,128)(2,1)S(1)}, bf16[1,200,256]{2,1,0:T(8,128)(2,1)S(1)}, u32[]{:S(2)}, u32[]{:S(2)}) %collective-permute-start.2) | collective-permute-done | bytes 102432 | tf_op jit(solution)/shard_map/ppermute | solution.py:259
  9.3 2.6 %collective-permute-start.5 = (bf16[1,200,256]{2,1,0:T(8,128)(2,1)S(1)}, bf16[1,200,256]{2,1,0:T(8,128)(2,1)S(1)}, u32[]{:S(2)}, u32[]{:S(2)}) collective-permute-start(bf16[1,200,256]{2,1,0:T(8,128)(2,1)S(1)} %pair_sum.1.keep_ref), channel_id=1, source_target_pairs={{0,1},{1,0},{2,3},{3,2},{4,5},{5,4},{6,7},{7,6},{8,9},{9,8},{10,11... | collective-permute-start | bytes 307208 | tf_op jit(solution)/shard_map/ppermute | solution.py:250
  11.8 2.4 %collective-permute-start.3 = (bf16[1,200,256]{2,1,0:T(8,128)(2,1)S(1)}, bf16[1,200,256]{2,1,0:T(8,128)(2,1)S(1)}, u32[]{:S(2)}, u32[]{:S(2)}) collective-permute-start(bf16[1,200,256]{2,1,0:T(8,128)(2,1)S(1)} %pair_sum.1.keep_ref), channel_id=1, source_target_pairs={{0,24},{8,16},{16,8},{24,0},{1,25},{9,17},{17,9},{25,1},{2,26},{10... | collective-permute-start | bytes 307208 | tf_op jit(solution)/shard_map/ppermute | solution.py:250
  14.3 0.2 collective-permute-done.5.arrived_ref
  14.5 0.1 sum_norm.1.refs_0_
  14.6 1.6 %collective-permute-start.7 = (bf16[200,256]{1,0:T(8,128)(2,1)S(1)}, bf16[200,256]{1,0:T(8,128)(2,1)S(1)}, u32[]{:S(2)}, u32[]{:S(2)}) collective-permute-start(bf16[200,256]{1,0:T(8,128)(2,1)S(1)} %sum_norm.1.refs_0_), channel_id=1, source_target_pairs={{0,16},{4,12},{8,24},{12,4},{16,0},{20,28},{24,8},{28,20},{1,17},{... | collective-permute-start | bytes 307208 | tf_op jit(solution)/shard_map/ppermute | solution.py:399
  16.2 1.5 %collective-permute-start.6 = (bf16[200,256]{1,0:T(8,128)(2,1)S(1)}, bf16[200,256]{1,0:T(8,128)(2,1)S(1)}, u32[]{:S(2)}, u32[]{:S(2)}) collective-permute-start(bf16[200,256]{1,0:T(8,128)(2,1)S(1)} %sum_norm.1.refs_0_), channel_id=1, source_target_pairs={{0,8},{4,20},{8,0},{12,28},{16,24},{20,4},{24,16},{28,12},{1,9},{5... | collective-permute-start | bytes 307208 | tf_op jit(solution)/shard_map/ppermute | solution.py:399
  17.7 0.0 collective-permute-done.3.refs_0_
  17.7 2.5 %collective-permute-start.4 = (bf16[1,200,256]{2,1,0:T(8,128)(2,1)S(1)}, bf16[1,200,256]{2,1,0:T(8,128)(2,1)S(1)}, u32[]{:S(2)}, u32[]{:S(2)}) collective-permute-start(bf16[1,200,256]{2,1,0:T(8,128)(2,1)S(1)} %collective-permute-done.3.refs_0_), channel_id=1, source_target_pairs={{0,1},{1,0},{2,3},{3,2},{4,5},{5,4},{6,7},{7,6},{8,9},{9,8},{10,11... | collective-permute-start | bytes 307208 | tf_op jit(solution)/shard_map/ppermute | solution.py:250
  20.1 0.4 %attend.3 = (f32[1,512]{1,0:T(1,128)S(1)}, f32[1,512]{1,0:T(1,128)S(1)}, f32[128,512]{1,0:T(8,128)S(1)}) custom-call(f32[1,128]{1,0:T(1,128)S(1)} %get-tuple-element.22.k_gain_ref, bf16[128,512]{1,0:T(8,128)(2,1)S(1)} %get-tuple-element.23.qt_ref, f32[4,512]{1,0:T(4,128)S(1)} %get-tuple-element.24.bias_ref, bf16[200,256]{1,0:T(8,128)(2,1)S(1)} %sum_norm.1.refs_0_), custom_call_target="tpu_custom_call" | custom-call | flops 52428800 | tf_op jit(solution)/shard_map/attend/pallas_call | solution.py:416
  20.6 0.0 collective-permute-done.7.refs_1_
  20.6 0.2 %collective-permute-done.6.refs_0_ = bf16[200,256]{1,0:T(8,128)(2,1)S(1)} collective-permute-done((bf16[200,256]{1,0:T(8,128)(2,1)S(1)}, bf16[200,256]{1,0:T(8,128)(2,1)S(1)}, u32[]{:S(2)}, u32[]{:S(2)}) %collective-permute-start.6) | collective-permute-done | bytes 102432 | tf_op jit(solution)/shard_map/ppermute | solution.py:399
  20.8 0.6 %attend.4 = (f32[1,512]{1,0:T(1,128)S(1)}, f32[1,512]{1,0:T(1,128)S(1)}, f32[128,512]{1,0:T(8,128)S(1)}) custom-call(f32[1,128]{1,0:T(1,128)S(1)} %get-tuple-element.22.k_gain_ref, bf16[128,512]{1,0:T(8,128)(2,1)S(1)} %get-tuple-element.23.qt_ref, f32[4,512]{1,0:T(4,128)S(1)} %get-tuple-element.24.bias_ref, ...), custom_call_target="tpu_custom_call" | custom-call | flops 104857600 | tf_op jit(solution)/shard_map/attend/pallas_call | solution.py:416
  21.4 1.4 %collective-permute-done.4.refs_1_ = bf16[1,200,256]{2,1,0:T(8,128)(2,1)S(1)} collective-permute-done((bf16[1,200,256]{2,1,0:T(8,128)(2,1)S(1)}, bf16[1,200,256]{2,1,0:T(8,128)(2,1)S(1)}, u32[]{:S(2)}, u32[]{:S(2)}) %collective-permute-start.4) | collective-permute-done | bytes 102432 | tf_op jit(solution)/shard_map/ppermute | solution.py:250
  22.8 1.3 %attend.5 = bf16[128,512]{1,0:T(8,128)(2,1)} custom-call(f32[1,128]{1,0:T(1,128)S(1)} %get-tuple-element.22.k_gain_ref, bf16[128,512]{1,0:T(8,128)(2,1)S(1)} %get-tuple-element.23.qt_ref, f32[4,512]{1,0:T(4,128)S(1)} %get-tuple-element.24.bias_ref, bf16[1,200,256]{2,1,0:T(8,128)(2,1)S(1)} %collective-permute-done.3.refs_0_, ...), custom_call_target="tpu_custom_call" | custom-call | flops 52428800 | tf_op jit(solution)/shard_map/attend/pallas_call | solution.py:416
  (2 shorter events, 0.1 us)
Async XLA Ops:
  0.0 4.0 %collective-permute-start = (bf16[2,2048,128]{2,1,0:T(8,128)(2,1)}, bf16[2,2048,128]{2,1,0:T(8,128)(2,1)S(1)}, u32[]{:S(2)}, u32[]{:S(2)}) collective-permute-start(bf16[2,2048,128]{2,1,0:T(8,128)(2,1)} %w_hbm.3), channel_id=1, source_target_pairs={{0,4},{4,0},{1,5},{5,1},{2,6},{6,2},{3,7},{7,3},{8,12},{12,8},{9,1... | collective-permute-start | bytes 3145736 | tf_op jit(solution)/shard_map/ppermute | solution.py:250
  0.5 8.2 %collective-permute-start.1 = (bf16[1,200,256]{2,1,0:T(8,128)(2,1)S(1)}, bf16[1,200,256]{2,1,0:T(8,128)(2,1)S(1)}, u32[]{:S(2)}, u32[]{:S(2)}) collective-permute-start(bf16[1,200,256]{2,1,0:T(8,128)(2,1)S(1)} %get-tuple-element.26), channel_id=1, source_target_pairs={{0,4},{1,5},{2,0},{3,1},{4,6},{5,7},{6,2},{7,3},{8,12},{9,13},{10,... | collective-permute-start | bytes 307208 | tf_op jit(solution)/shard_map/ppermute | solution.py:259
  4.4 4.8 %collective-permute-start.2 = (bf16[1,200,256]{2,1,0:T(8,128)(2,1)S(1)}, bf16[1,200,256]{2,1,0:T(8,128)(2,1)S(1)}, u32[]{:S(2)}, u32[]{:S(2)}) collective-permute-start(bf16[1,200,256]{2,1,0:T(8,128)(2,1)S(1)} %home_other.1.after_ref), channel_id=1, source_target_pairs={{0,2},{1,3},{2,6},{3,7},{4,0},{5,1},{6,4},{7,5},{8,10},{9,11},{10,... | collective-permute-start | bytes 307208 | tf_op jit(solution)/shard_map/ppermute | solution.py:259
  9.3 5.2 %collective-permute-start.5 = (bf16[1,200,256]{2,1,0:T(8,128)(2,1)S(1)}, bf16[1,200,256]{2,1,0:T(8,128)(2,1)S(1)}, u32[]{:S(2)}, u32[]{:S(2)}) collective-permute-start(bf16[1,200,256]{2,1,0:T(8,128)(2,1)S(1)} %pair_sum.1.keep_ref), channel_id=1, source_target_pairs={{0,1},{1,0},{2,3},{3,2},{4,5},{5,4},{6,7},{7,6},{8,9},{9,8},{10,11... | collective-permute-start | bytes 307208 | tf_op jit(solution)/shard_map/ppermute | solution.py:250
  11.8 5.8 %collective-permute-start.3 = (bf16[1,200,256]{2,1,0:T(8,128)(2,1)S(1)}, bf16[1,200,256]{2,1,0:T(8,128)(2,1)S(1)}, u32[]{:S(2)}, u32[]{:S(2)}) collective-permute-start(bf16[1,200,256]{2,1,0:T(8,128)(2,1)S(1)} %pair_sum.1.keep_ref), channel_id=1, source_target_pairs={{0,24},{8,16},{16,8},{24,0},{1,25},{9,17},{17,9},{25,1},{2,26},{10... | collective-permute-start | bytes 307208 | tf_op jit(solution)/shard_map/ppermute | solution.py:250
  14.6 6.0 %collective-permute-start.7 = (bf16[200,256]{1,0:T(8,128)(2,1)S(1)}, bf16[200,256]{1,0:T(8,128)(2,1)S(1)}, u32[]{:S(2)}, u32[]{:S(2)}) collective-permute-start(bf16[200,256]{1,0:T(8,128)(2,1)S(1)} %sum_norm.1.refs_0_), channel_id=1, source_target_pairs={{0,16},{4,12},{8,24},{12,4},{16,0},{20,28},{24,8},{28,20},{1,17},{... | collective-permute-start | bytes 307208 | tf_op jit(solution)/shard_map/ppermute | solution.py:399
  16.2 4.7 %collective-permute-start.6 = (bf16[200,256]{1,0:T(8,128)(2,1)S(1)}, bf16[200,256]{1,0:T(8,128)(2,1)S(1)}, u32[]{:S(2)}, u32[]{:S(2)}) collective-permute-start(bf16[200,256]{1,0:T(8,128)(2,1)S(1)} %sum_norm.1.refs_0_), channel_id=1, source_target_pairs={{0,8},{4,20},{8,0},{12,28},{16,24},{20,4},{24,16},{28,12},{1,9},{5... | collective-permute-start | bytes 307208 | tf_op jit(solution)/shard_map/ppermute | solution.py:399
  17.7 5.2 %collective-permute-start.4 = (bf16[1,200,256]{2,1,0:T(8,128)(2,1)S(1)}, bf16[1,200,256]{2,1,0:T(8,128)(2,1)S(1)}, u32[]{:S(2)}, u32[]{:S(2)}) collective-permute-start(bf16[1,200,256]{2,1,0:T(8,128)(2,1)S(1)} %collective-permute-done.3.refs_0_), channel_id=1, source_target_pairs={{0,1},{1,0},{2,3},{3,2},{4,5},{5,4},{6,7},{7,6},{8,9},{9,8},{10,11... | collective-permute-start | bytes 307208 | tf_op jit(solution)/shard_map/ppermute | solution.py:250

commit v19 on v17

--- a/solution.py
+++ b/solution.py
@@ -236,12 +236,12 @@
     (out,) = refs
     has_any = jnp.max(bias_ref[...], axis=0, keepdims=True) > -1.0
     inverse = jnp.where(has_any, 1.0 / jnp.where(has_any, row_sum, 1.0), 0.0)
-    context = (mixed * inverse).astype(BF16)
+    context = mixed * inverse
     tokens = out.shape[0]
     for head in range(out.shape[1] // head_dim):
         out[:, head * head_dim : (head + 1) * head_dim] = context[
             :, head * tokens : (head + 1) * tokens
-        ].T
+        ].T.astype(BF16)
 
 
 def swap(value, axis, k):

time: 24.2 us -> 24.2 us (level)
  no operation moved by 1% of the time
where the time goes in v19:
time: 24.2 us; the launch traced here: 24.1 us
  starting transfers between devices  15.6 us (64%)
  Pallas kernels  5.63 us (23%)
  waiting for transfers between devices  2.8 us (12%)
    ppermute x6, starting transfers between devices, swap(): lax.ppermute(value, axis, [(i, i ^ k) for i in range(lax.axis_size(axis))])  11 us
    ppermute x2, starting transfers between devices, exchange_two_heads(): return lax.ppermute(value, ('dp', 'tensor'), hops)  4.57 us
    pallas_call x3, Pallas kernels, on_device(): call(functools.partial(attend_kernel, here, there, tile_len, first, last,...  2.26 us
    ppermute x6, waiting for transfers between devices, swap(): lax.ppermute(value, axis, [(i, i ^ k) for i in range(lax.axis_size(axis))])  1.84 us
    pallas_call x1, Pallas kernels, on_device(): call(load_kernel, [shape_of(images.shape), shape_of(kv_weight.shape)], 3,...  1.49 us
    pallas_call x1, Pallas kernels, on_device(): call(functools.partial(keep_kernel, head_dim), [product, *prepared], 8, '...  1.28 us
    ppermute x2, waiting for transfers between devices, exchange_two_heads(): return lax.ppermute(value, ('dp', 'tensor'), hops)  0.96 us
  transfers between devices with their start and end apart: 8, of which 5 were waited for; matrix products, arithmetic and copies ran while one was open for 0% of the time, Pallas kernels for 18%

profile of v19, /device:TPU:0, one launch (start us, length us, event | category | flops | bytes accessed | tf_op | source)
XLA Modules:
  0.0 24.1 jit_solution(7381031836346566346)
XLA Ops:
  0.0 0.5 %collective-permute-start = (bf16[2,2048,128]{2,1,0:T(8,128)(2,1)}, bf16[2,2048,128]{2,1,0:T(8,128)(2,1)S(1)}, u32[]{:S(2)}, u32[]{:S(2)}) collective-permute-start(bf16[2,2048,128]{2,1,0:T(8,128)(2,1)} %w_hbm.3), channel_id=1, source_target_pairs={{0,4},{4,0},{1,5},{5,1},{2,6},{6,2},{3,7},{7,3},{8,12},{12,8},{9,1... | collective-permute-start | bytes 3145736 | tf_op jit(solution)/shard_map/ppermute | solution.py:248
  0.5 2.0 %collective-permute-start.1 = (bf16[1,200,256]{2,1,0:T(8,128)(2,1)S(1)}, bf16[1,200,256]{2,1,0:T(8,128)(2,1)S(1)}, u32[]{:S(2)}, u32[]{:S(2)}) collective-permute-start(bf16[1,200,256]{2,1,0:T(8,128)(2,1)S(1)} %get-tuple-element.26), channel_id=1, source_target_pairs={{0,4},{1,5},{2,0},{3,1},{4,6},{5,7},{6,2},{7,3},{8,12},{9,13},{10,... | collective-permute-start | bytes 307208 | tf_op jit(solution)/shard_map/ppermute | solution.py:257
  2.5 1.5 %home_load.1 = (bf16[1,200,2048]{2,1,0:T(8,128)(2,1)S(1)}, bf16[2,2048,128]{2,1,0:T(8,128)(2,1)S(1)}) custom-call(bf16[1,200,2048]{2,1,0:T(8,128)(2,1)S(1)} %get-tuple-element.19.x_in, bf16[1,200,2048]{2,1,0:T(8,128)(2,1)} %x_hbm.3, bf16[2,2048,128]{2,1,0:T(8,128)(2,1)} %w_hbm.3), custom_call_target="tpu_custom_call", output_to_operand_aliasing={{0}: (0, {})} | custom-call | tf_op jit(solution)/shard_map/home_load/pallas_call | solution.py:335
  4.0 0.0 collective-permute-done.w_other_ref
  4.0 0.4 %home_other.1.after_ref = bf16[1,200,256]{2,1,0:T(8,128)(2,1)S(1)} custom-call(bf16[1,200,2048]{2,1,0:T(8,128)(2,1)S(1)} %get-tuple-element.20.x_ref, bf16[2,2048,128]{2,1,0:T(8,128)(2,1)S(1)} %collective-permute-done.w_other_ref), custom_call_target="tpu_custom_call" | custom-call | flops 209715200 | tf_op jit(solution)/shard_map/home_other/pallas_call | solution.py:344
  4.4 2.6 %collective-permute-start.2 = (bf16[1,200,256]{2,1,0:T(8,128)(2,1)S(1)}, bf16[1,200,256]{2,1,0:T(8,128)(2,1)S(1)}, u32[]{:S(2)}, u32[]{:S(2)}) collective-permute-start(bf16[1,200,256]{2,1,0:T(8,128)(2,1)S(1)} %home_other.1.after_ref), channel_id=1, source_target_pairs={{0,2},{1,3},{2,6},{3,7},{4,0},{5,1},{6,4},{7,5},{8,10},{9,11},{10,... | collective-permute-start | bytes 307208 | tf_op jit(solution)/shard_map/ppermute | solution.py:257
  7.0 1.3 %keep_queries.1 = (bf16[1,200,256]{2,1,0:T(8,128)(2,1)S(1)}, bf16[128,512]{1,0:T(8,128)(2,1)S(1)}, f32[4,512]{1,0:T(4,128)S(1)}, f32[1,128]{1,0:T(1,128)S(1)}) custom-call(bf16[1,200,256]{2,1,0:T(8,128)(2,1)S(1)} %home_other.1.after_ref, bf16[2,2048,128]{2,1,0:T(8,128)(2,1)S(1)} %collective-permute-done.w_other_ref, ...), custom_call_target="tpu_custom_call" | custom-call | flops 209715200 | tf_op jit(solution)/shard_map/keep_queries/pallas_call | solution.py:348
  8.3 0.4 %collective-permute-done.1.first_ref = bf16[1,200,256]{2,1,0:T(8,128)(2,1)S(1)} collective-permute-done((bf16[1,200,256]{2,1,0:T(8,128)(2,1)S(1)}, bf16[1,200,256]{2,1,0:T(8,128)(2,1)S(1)}, u32[]{:S(2)}, u32[]{:S(2)}) %collective-permute-start.1) | collective-permute-done | bytes 102432 | tf_op jit(solution)/shard_map/ppermute | solution.py:257
  8.7 0.6 %collective-permute-done.2.second_ref = bf16[1,200,256]{2,1,0:T(8,128)(2,1)S(1)} collective-permute-done((bf16[1,200,256]{2,1,0:T(8,128)(2,1)S(1)}, bf16[1,200,256]{2,1,0:T(8,128)(2,1)S(1)}, u32[]{:S(2)}, u32[]{:S(2)}) %collective-permute-start.2) | collective-permute-done | bytes 102432 | tf_op jit(solution)/shard_map/ppermute | solution.py:257
  9.3 2.6 %collective-permute-start.5 = (bf16[1,200,256]{2,1,0:T(8,128)(2,1)S(1)}, bf16[1,200,256]{2,1,0:T(8,128)(2,1)S(1)}, u32[]{:S(2)}, u32[]{:S(2)}) collective-permute-start(bf16[1,200,256]{2,1,0:T(8,128)(2,1)S(1)} %pair_sum.1.keep_ref), channel_id=1, source_target_pairs={{0,1},{1,0},{2,3},{3,2},{4,5},{5,4},{6,7},{7,6},{8,9},{9,8},{10,11... | collective-permute-start | bytes 307208 | tf_op jit(solution)/shard_map/ppermute | solution.py:248
  11.8 2.4 %collective-permute-start.3 = (bf16[1,200,256]{2,1,0:T(8,128)(2,1)S(1)}, bf16[1,200,256]{2,1,0:T(8,128)(2,1)S(1)}, u32[]{:S(2)}, u32[]{:S(2)}) collective-permute-start(bf16[1,200,256]{2,1,0:T(8,128)(2,1)S(1)} %pair_sum.1.keep_ref), channel_id=1, source_target_pairs={{0,24},{8,16},{16,8},{24,0},{1,25},{9,17},{17,9},{25,1},{2,26},{10... | collective-permute-start | bytes 307208 | tf_op jit(solution)/shard_map/ppermute | solution.py:248
  14.3 0.2 collective-permute-done.5.arrived_ref
  14.5 0.1 sum_norm.1.refs_0_
  14.6 1.6 %collective-permute-start.7 = (bf16[200,256]{1,0:T(8,128)(2,1)S(1)}, bf16[200,256]{1,0:T(8,128)(2,1)S(1)}, u32[]{:S(2)}, u32[]{:S(2)}) collective-permute-start(bf16[200,256]{1,0:T(8,128)(2,1)S(1)} %sum_norm.1.refs_0_), channel_id=1, source_target_pairs={{0,16},{8,24},{16,0},{24,8},{1,17},{9,25},{17,1},{25,9},{2,18},{10... | collective-permute-start | bytes 307208 | tf_op jit(solution)/shard_map/ppermute | solution.py:248
  16.2 1.5 %collective-permute-start.6 = (bf16[200,256]{1,0:T(8,128)(2,1)S(1)}, bf16[200,256]{1,0:T(8,128)(2,1)S(1)}, u32[]{:S(2)}, u32[]{:S(2)}) collective-permute-start(bf16[200,256]{1,0:T(8,128)(2,1)S(1)} %sum_norm.1.refs_0_), channel_id=1, source_target_pairs={{0,8},{8,0},{16,24},{24,16},{1,9},{9,1},{17,25},{25,17},{2,10},{10... | collective-permute-start | bytes 307208 | tf_op jit(solution)/shard_map/ppermute | solution.py:248
  17.7 0.0 collective-permute-done.3.refs_0_
  17.7 2.5 %collective-permute-start.4 = (bf16[1,200,256]{2,1,0:T(8,128)(2,1)S(1)}, bf16[1,200,256]{2,1,0:T(8,128)(2,1)S(1)}, u32[]{:S(2)}, u32[]{:S(2)}) collective-permute-start(bf16[1,200,256]{2,1,0:T(8,128)(2,1)S(1)} %collective-permute-done.3.refs_0_), channel_id=1, source_target_pairs={{0,1},{1,0},{2,3},{3,2},{4,5},{5,4},{6,7},{7,6},{8,9},{9,8},{10,11... | collective-permute-start | bytes 307208 | tf_op jit(solution)/shard_map/ppermute | solution.py:248
  20.1 0.4 %attend.3 = (f32[1,512]{1,0:T(1,128)S(1)}, f32[1,512]{1,0:T(1,128)S(1)}, f32[128,512]{1,0:T(8,128)S(1)}) custom-call(f32[1,128]{1,0:T(1,128)S(1)} %get-tuple-element.22.k_gain_ref, bf16[128,512]{1,0:T(8,128)(2,1)S(1)} %get-tuple-element.23.qt_ref, f32[4,512]{1,0:T(4,128)S(1)} %get-tuple-element.24.bias_ref, bf16[200,256]{1,0:T(8,128)(2,1)S(1)} %sum_norm.1.refs_0_), custom_call_target="tpu_custom_call" | custom-call | flops 52428800 | tf_op jit(solution)/shard_map/attend/pallas_call | solution.py:405
  20.6 0.0 collective-permute-done.7.refs_1_
  20.6 1.0 %collective-permute-done.6.refs_0_ = bf16[200,256]{1,0:T(8,128)(2,1)S(1)} collective-permute-done((bf16[200,256]{1,0:T(8,128)(2,1)S(1)}, bf16[200,256]{1,0:T(8,128)(2,1)S(1)}, u32[]{:S(2)}, u32[]{:S(2)}) %collective-permute-start.6) | collective-permute-done | bytes 102432 | tf_op jit(solution)/shard_map/ppermute | solution.py:248
  21.6 0.6 %attend.4 = (f32[1,512]{1,0:T(1,128)S(1)}, f32[1,512]{1,0:T(1,128)S(1)}, f32[128,512]{1,0:T(8,128)S(1)}) custom-call(f32[1,128]{1,0:T(1,128)S(1)} %get-tuple-element.22.k_gain_ref, bf16[128,512]{1,0:T(8,128)(2,1)S(1)} %get-tuple-element.23.qt_ref, f32[4,512]{1,0:T(4,128)S(1)} %get-tuple-element.24.bias_ref, ...), custom_call_target="tpu_custom_call" | custom-call | flops 104857600 | tf_op jit(solution)/shard_map/attend/pallas_call | solution.py:405
  22.2 0.6 %collective-permute-done.4.refs_1_ = bf16[1,200,256]{2,1,0:T(8,128)(2,1)S(1)} collective-permute-done((bf16[1,200,256]{2,1,0:T(8,128)(2,1)S(1)}, bf16[1,200,256]{2,1,0:T(8,128)(2,1)S(1)}, u32[]{:S(2)}, u32[]{:S(2)}) %collective-permute-start.4) | collective-permute-done | bytes 102432 | tf_op jit(solution)/shard_map/ppermute | solution.py:248
  22.8 1.3 %attend.5 = bf16[128,512]{1,0:T(8,128)(2,1)} custom-call(f32[1,128]{1,0:T(1,128)S(1)} %get-tuple-element.22.k_gain_ref, bf16[128,512]{1,0:T(8,128)(2,1)S(1)} %get-tuple-element.23.qt_ref, f32[4,512]{1,0:T(4,128)S(1)} %get-tuple-element.24.bias_ref, bf16[1,200,256]{2,1,0:T(8,128)(2,1)S(1)} %collective-permute-done.3.refs_0_, ...), custom_call_target="tpu_custom_call" | custom-call | flops 52428800 | tf_op jit(solution)/shard_map/attend/pallas_call | solution.py:405
  (2 shorter events, 0.1 us)
Async XLA Ops:
  0.0 4.0 %collective-permute-start = (bf16[2,2048,128]{2,1,0:T(8,128)(2,1)}, bf16[2,2048,128]{2,1,0:T(8,128)(2,1)S(1)}, u32[]{:S(2)}, u32[]{:S(2)}) collective-permute-start(bf16[2,2048,128]{2,1,0:T(8,128)(2,1)} %w_hbm.3), channel_id=1, source_target_pairs={{0,4},{4,0},{1,5},{5,1},{2,6},{6,2},{3,7},{7,3},{8,12},{12,8},{9,1... | collective-permute-start | bytes 3145736 | tf_op jit(solution)/shard_map/ppermute | solution.py:248
  0.5 8.2 %collective-permute-start.1 = (bf16[1,200,256]{2,1,0:T(8,128)(2,1)S(1)}, bf16[1,200,256]{2,1,0:T(8,128)(2,1)S(1)}, u32[]{:S(2)}, u32[]{:S(2)}) collective-permute-start(bf16[1,200,256]{2,1,0:T(8,128)(2,1)S(1)} %get-tuple-element.26), channel_id=1, source_target_pairs={{0,4},{1,5},{2,0},{3,1},{4,6},{5,7},{6,2},{7,3},{8,12},{9,13},{10,... | collective-permute-start | bytes 307208 | tf_op jit(solution)/shard_map/ppermute | solution.py:257
  4.4 4.8 %collective-permute-start.2 = (bf16[1,200,256]{2,1,0:T(8,128)(2,1)S(1)}, bf16[1,200,256]{2,1,0:T(8,128)(2,1)S(1)}, u32[]{:S(2)}, u32[]{:S(2)}) collective-permute-start(bf16[1,200,256]{2,1,0:T(8,128)(2,1)S(1)} %home_other.1.after_ref), channel_id=1, source_target_pairs={{0,2},{1,3},{2,6},{3,7},{4,0},{5,1},{6,4},{7,5},{8,10},{9,11},{10,... | collective-permute-start | bytes 307208 | tf_op jit(solution)/shard_map/ppermute | solution.py:257
  9.3 5.2 %collective-permute-start.5 = (bf16[1,200,256]{2,1,0:T(8,128)(2,1)S(1)}, bf16[1,200,256]{2,1,0:T(8,128)(2,1)S(1)}, u32[]{:S(2)}, u32[]{:S(2)}) collective-permute-start(bf16[1,200,256]{2,1,0:T(8,128)(2,1)S(1)} %pair_sum.1.keep_ref), channel_id=1, source_target_pairs={{0,1},{1,0},{2,3},{3,2},{4,5},{5,4},{6,7},{7,6},{8,9},{9,8},{10,11... | collective-permute-start | bytes 307208 | tf_op jit(solution)/shard_map/ppermute | solution.py:248
  11.8 5.8 %collective-permute-start.3 = (bf16[1,200,256]{2,1,0:T(8,128)(2,1)S(1)}, bf16[1,200,256]{2,1,0:T(8,128)(2,1)S(1)}, u32[]{:S(2)}, u32[]{:S(2)}) collective-permute-start(bf16[1,200,256]{2,1,0:T(8,128)(2,1)S(1)} %pair_sum.1.keep_ref), channel_id=1, source_target_pairs={{0,24},{8,16},{16,8},{24,0},{1,25},{9,17},{17,9},{25,1},{2,26},{10... | collective-permute-start | bytes 307208 | tf_op jit(solution)/shard_map/ppermute | solution.py:248
  14.6 6.0 %collective-permute-start.7 = (bf16[200,256]{1,0:T(8,128)(2,1)S(1)}, bf16[200,256]{1,0:T(8,128)(2,1)S(1)}, u32[]{:S(2)}, u32[]{:S(2)}) collective-permute-start(bf16[200,256]{1,0:T(8,128)(2,1)S(1)} %sum_norm.1.refs_0_), channel_id=1, source_target_pairs={{0,16},{8,24},{16,0},{24,8},{1,17},{9,25},{17,1},{25,9},{2,18},{10... | collective-permute-start | bytes 307208 | tf_op jit(solution)/shard_map/ppermute | solution.py:248
  16.2 5.4 %collective-permute-start.6 = (bf16[200,256]{1,0:T(8,128)(2,1)S(1)}, bf16[200,256]{1,0:T(8,128)(2,1)S(1)}, u32[]{:S(2)}, u32[]{:S(2)}) collective-permute-start(bf16[200,256]{1,0:T(8,128)(2,1)S(1)} %sum_norm.1.refs_0_), channel_id=1, source_target_pairs={{0,8},{8,0},{16,24},{24,16},{1,9},{9,1},{17,25},{25,17},{2,10},{10... | collective-permute-start | bytes 307208 | tf_op jit(solution)/shard_map/ppermute | solution.py:248
  17.7 5.1 %collective-permute-start.4 = (bf16[1,200,256]{2,1,0:T(8,128)(2,1)S(1)}, bf16[1,200,256]{2,1,0:T(8,128)(2,1)S(1)}, u32[]{:S(2)}, u32[]{:S(2)}) collective-permute-start(bf16[1,200,256]{2,1,0:T(8,128)(2,1)S(1)} %collective-permute-done.3.refs_0_), channel_id=1, source_target_pairs={{0,1},{1,0},{2,3},{3,2},{4,5},{5,4},{6,7},{7,6},{8,9},{9,8},{10,11... | collective-permute-start | bytes 307208 | tf_op jit(solution)/shard_map/ppermute | solution.py:248

commit v20 on v17

--- a/solution.py
+++ b/solution.py
@@ -392,7 +392,7 @@
     state = []
     for here, there, operands in (
         ([0], [], [kv]),
-        (near, [], finished),
+        *(([step], [], [part]) for step, part in zip(near, finished)),
         ([], far, both),
     ):
         first, last = here == [0], len(there) > 0

time: 24.2 us -> 24.2 us (level)
  Pallas kernels: 5.64 us -> 5.94 us
  waiting for transfers between devices: 2.8 us -> 2.5 us
    ppermute x6, waiting for transfers between devices: 1.84 us -> 1.53 us  [swap(): lax.ppermute(value, axis, [(i, i ^ k) for i in range(lax.axis_size(axis))])]
    pallas_call x3 -> x4, Pallas kernels: 2.27 us -> 2.57 us  [on_device(): call(functools.partial(attend_kernel, here, there, tile_len, first, last,...]
  transfers between devices with their start and end apart: 8 -> 8, of which waited for: 5 -> 5; matrix products, arithmetic and copies ran while one was open for 0% -> 0% of each run, Pallas kernels for 18% -> 19%
where the time goes in v20:
time: 24.2 us; the launch traced here: 24.1 us
  starting transfers between devices  15.6 us (64%)
  Pallas kernels  5.94 us (25%)
  waiting for transfers between devices  2.5 us (10%)
    ppermute x6, starting transfers between devices, swap(): lax.ppermute(value, axis, [(i, i ^ k) for i in range(lax.axis_size(axis))])  11 us
    ppermute x2, starting transfers between devices, exchange_two_heads(): return lax.ppermute(value, ('dp', 'tensor'), hops)  4.57 us
    pallas_call x4, Pallas kernels, on_device(): call(functools.partial(attend_kernel, here, there, tile_len, first, last,...  2.57 us
    ppermute x6, waiting for transfers between devices, swap(): lax.ppermute(value, axis, [(i, i ^ k) for i in range(lax.axis_size(axis))])  1.53 us
    pallas_call x1, Pallas kernels, on_device(): call(load_kernel, [shape_of(images.shape), shape_of(kv_weight.shape)], 3,...  1.49 us
    pallas_call x1, Pallas kernels, on_device(): call(functools.partial(keep_kernel, head_dim), [product, *prepared], 8, '...  1.28 us
    ppermute x2, waiting for transfers between devices, exchange_two_heads(): return lax.ppermute(value, ('dp', 'tensor'), hops)  0.96 us
  transfers between devices with their start and end apart: 8, of which 5 were waited for; matrix products, arithmetic and copies ran while one was open for 0% of the time, Pallas kernels for 19%

profile of v20, /device:TPU:0, one launch (start us, length us, event | category | flops | bytes accessed | tf_op | source)
XLA Modules:
  0.0 24.1 jit_solution(8803419161080449112)
XLA Ops:
  0.0 0.5 %collective-permute-start = (bf16[2,2048,128]{2,1,0:T(8,128)(2,1)}, bf16[2,2048,128]{2,1,0:T(8,128)(2,1)S(1)}, u32[]{:S(2)}, u32[]{:S(2)}) collective-permute-start(bf16[2,2048,128]{2,1,0:T(8,128)(2,1)} %w_hbm.3), channel_id=1, source_target_pairs={{0,4},{4,0},{1,5},{5,1},{2,6},{6,2},{3,7},{7,3},{8,12},{12,8},{9,1... | collective-permute-start | bytes 3145736 | tf_op jit(solution)/shard_map/ppermute | solution.py:248
  0.5 2.0 %collective-permute-start.1 = (bf16[1,200,256]{2,1,0:T(8,128)(2,1)S(1)}, bf16[1,200,256]{2,1,0:T(8,128)(2,1)S(1)}, u32[]{:S(2)}, u32[]{:S(2)}) collective-permute-start(bf16[1,200,256]{2,1,0:T(8,128)(2,1)S(1)} %get-tuple-element.29), channel_id=1, source_target_pairs={{0,4},{1,5},{2,0},{3,1},{4,6},{5,7},{6,2},{7,3},{8,12},{9,13},{10,... | collective-permute-start | bytes 307208 | tf_op jit(solution)/shard_map/ppermute | solution.py:257
  2.5 1.5 %home_load.1 = (bf16[1,200,2048]{2,1,0:T(8,128)(2,1)S(1)}, bf16[2,2048,128]{2,1,0:T(8,128)(2,1)S(1)}) custom-call(bf16[1,200,2048]{2,1,0:T(8,128)(2,1)S(1)} %get-tuple-element.22.x_in, bf16[1,200,2048]{2,1,0:T(8,128)(2,1)} %x_hbm.3, bf16[2,2048,128]{2,1,0:T(8,128)(2,1)} %w_hbm.3), custom_call_target="tpu_custom_call", output_to_operand_aliasing={{0}: (0, {})} | custom-call | tf_op jit(solution)/shard_map/home_load/pallas_call | solution.py:335
  4.0 0.0 collective-permute-done.w_other_ref
  4.0 0.4 %home_other.1.after_ref = bf16[1,200,256]{2,1,0:T(8,128)(2,1)S(1)} custom-call(bf16[1,200,2048]{2,1,0:T(8,128)(2,1)S(1)} %get-tuple-element.23.x_ref, bf16[2,2048,128]{2,1,0:T(8,128)(2,1)S(1)} %collective-permute-done.w_other_ref), custom_call_target="tpu_custom_call" | custom-call | flops 209715200 | tf_op jit(solution)/shard_map/home_other/pallas_call | solution.py:344
  4.4 2.6 %collective-permute-start.2 = (bf16[1,200,256]{2,1,0:T(8,128)(2,1)S(1)}, bf16[1,200,256]{2,1,0:T(8,128)(2,1)S(1)}, u32[]{:S(2)}, u32[]{:S(2)}) collective-permute-start(bf16[1,200,256]{2,1,0:T(8,128)(2,1)S(1)} %home_other.1.after_ref), channel_id=1, source_target_pairs={{0,2},{1,3},{2,6},{3,7},{4,0},{5,1},{6,4},{7,5},{8,10},{9,11},{10,... | collective-permute-start | bytes 307208 | tf_op jit(solution)/shard_map/ppermute | solution.py:257
  7.0 1.3 %keep_queries.1 = (bf16[1,200,256]{2,1,0:T(8,128)(2,1)S(1)}, bf16[128,512]{1,0:T(8,128)(2,1)S(1)}, f32[4,512]{1,0:T(4,128)S(1)}, f32[1,128]{1,0:T(1,128)S(1)}) custom-call(bf16[1,200,256]{2,1,0:T(8,128)(2,1)S(1)} %home_other.1.after_ref, bf16[2,2048,128]{2,1,0:T(8,128)(2,1)S(1)} %collective-permute-done.w_other_ref, ...), custom_call_target="tpu_custom_call" | custom-call | flops 209715200 | tf_op jit(solution)/shard_map/keep_queries/pallas_call | solution.py:348
  8.3 0.4 %collective-permute-done.1.first_ref = bf16[1,200,256]{2,1,0:T(8,128)(2,1)S(1)} collective-permute-done((bf16[1,200,256]{2,1,0:T(8,128)(2,1)S(1)}, bf16[1,200,256]{2,1,0:T(8,128)(2,1)S(1)}, u32[]{:S(2)}, u32[]{:S(2)}) %collective-permute-start.1) | collective-permute-done | bytes 102432 | tf_op jit(solution)/shard_map/ppermute | solution.py:257
  8.7 0.6 %collective-permute-done.2.second_ref = bf16[1,200,256]{2,1,0:T(8,128)(2,1)S(1)} collective-permute-done((bf16[1,200,256]{2,1,0:T(8,128)(2,1)S(1)}, bf16[1,200,256]{2,1,0:T(8,128)(2,1)S(1)}, u32[]{:S(2)}, u32[]{:S(2)}) %collective-permute-start.2) | collective-permute-done | bytes 102432 | tf_op jit(solution)/shard_map/ppermute | solution.py:257
  9.3 2.6 %collective-permute-start.5 = (bf16[1,200,256]{2,1,0:T(8,128)(2,1)S(1)}, bf16[1,200,256]{2,1,0:T(8,128)(2,1)S(1)}, u32[]{:S(2)}, u32[]{:S(2)}) collective-permute-start(bf16[1,200,256]{2,1,0:T(8,128)(2,1)S(1)} %pair_sum.1.keep_ref), channel_id=1, source_target_pairs={{0,1},{1,0},{2,3},{3,2},{4,5},{5,4},{6,7},{7,6},{8,9},{9,8},{10,11... | collective-permute-start | bytes 307208 | tf_op jit(solution)/shard_map/ppermute | solution.py:248
  11.8 2.4 %collective-permute-start.3 = (bf16[1,200,256]{2,1,0:T(8,128)(2,1)S(1)}, bf16[1,200,256]{2,1,0:T(8,128)(2,1)S(1)}, u32[]{:S(2)}, u32[]{:S(2)}) collective-permute-start(bf16[1,200,256]{2,1,0:T(8,128)(2,1)S(1)} %pair_sum.1.keep_ref), channel_id=1, source_target_pairs={{0,24},{8,16},{16,8},{24,0},{1,25},{9,17},{17,9},{25,1},{2,26},{10... | collective-permute-start | bytes 307208 | tf_op jit(solution)/shard_map/ppermute | solution.py:248
  14.3 0.2 collective-permute-done.5.arrived_ref
  14.5 0.1 sum_norm.1.refs_0_
  14.6 1.6 %collective-permute-start.7 = (bf16[200,256]{1,0:T(8,128)(2,1)S(1)}, bf16[200,256]{1,0:T(8,128)(2,1)S(1)}, u32[]{:S(2)}, u32[]{:S(2)}) collective-permute-start(bf16[200,256]{1,0:T(8,128)(2,1)S(1)} %sum_norm.1.refs_0_), channel_id=1, source_target_pairs={{0,8},{8,0},{16,24},{24,16},{1,9},{9,1},{17,25},{25,17},{2,10},{10... | collective-permute-start | bytes 307208 | tf_op jit(solution)/shard_map/ppermute | solution.py:248
  16.2 1.5 %collective-permute-start.6 = (bf16[200,256]{1,0:T(8,128)(2,1)S(1)}, bf16[200,256]{1,0:T(8,128)(2,1)S(1)}, u32[]{:S(2)}, u32[]{:S(2)}) collective-permute-start(bf16[200,256]{1,0:T(8,128)(2,1)S(1)} %sum_norm.1.refs_0_), channel_id=1, source_target_pairs={{0,16},{8,24},{16,0},{24,8},{1,17},{9,25},{17,1},{25,9},{2,18},{10... | collective-permute-start | bytes 307208 | tf_op jit(solution)/shard_map/ppermute | solution.py:248
  17.7 0.0 collective-permute-done.3.refs_0_
  17.7 2.5 %collective-permute-start.4 = (bf16[1,200,256]{2,1,0:T(8,128)(2,1)S(1)}, bf16[1,200,256]{2,1,0:T(8,128)(2,1)S(1)}, u32[]{:S(2)}, u32[]{:S(2)}) collective-permute-start(bf16[1,200,256]{2,1,0:T(8,128)(2,1)S(1)} %collective-permute-done.3.refs_0_), channel_id=1, source_target_pairs={{0,1},{1,0},{2,3},{3,2},{4,5},{5,4},{6,7},{7,6},{8,9},{9,8},{10,11... | collective-permute-start | bytes 307208 | tf_op jit(solution)/shard_map/ppermute | solution.py:248
  20.1 0.4 %attend.4 = (f32[1,512]{1,0:T(1,128)S(1)}, f32[1,512]{1,0:T(1,128)S(1)}, f32[128,512]{1,0:T(8,128)S(1)}) custom-call(f32[1,128]{1,0:T(1,128)S(1)} %get-tuple-element.25.k_gain_ref, bf16[128,512]{1,0:T(8,128)(2,1)S(1)} %get-tuple-element.26.qt_ref, f32[4,512]{1,0:T(4,128)S(1)} %get-tuple-element.27.bias_ref, bf16[200,256]{1,0:T(8,128)(2,1)S(1)} %sum_norm.1.refs_0_), custom_call_target="tpu_custom_call" | custom-call | flops 52428800 | tf_op jit(solution)/shard_map/attend/pallas_call | solution.py:405
  20.6 0.0 collective-permute-done.7.refs_0_
  20.6 0.4 %attend.5 = (f32[1,512]{1,0:T(1,128)S(1)}, f32[1,512]{1,0:T(1,128)S(1)}, f32[128,512]{1,0:T(8,128)S(1)}) custom-call(f32[1,128]{1,0:T(1,128)S(1)} %get-tuple-element.25.k_gain_ref, bf16[128,512]{1,0:T(8,128)(2,1)S(1)} %get-tuple-element.26.qt_ref, f32[4,512]{1,0:T(4,128)S(1)} %get-tuple-element.27.bias_ref, ...), custom_call_target="tpu_custom_call" | custom-call | flops 52428800 | tf_op jit(solution)/shard_map/attend/pallas_call | solution.py:405
  21.0 0.5 %collective-permute-done.6.refs_0_ = bf16[200,256]{1,0:T(8,128)(2,1)S(1)} collective-permute-done((bf16[200,256]{1,0:T(8,128)(2,1)S(1)}, bf16[200,256]{1,0:T(8,128)(2,1)S(1)}, u32[]{:S(2)}, u32[]{:S(2)}) %collective-permute-start.6) | collective-permute-done | bytes 102432 | tf_op jit(solution)/shard_map/ppermute | solution.py:248
  21.6 0.4 %attend.6 = (f32[1,512]{1,0:T(1,128)S(1)}, f32[1,512]{1,0:T(1,128)S(1)}, f32[128,512]{1,0:T(8,128)S(1)}) custom-call(f32[1,128]{1,0:T(1,128)S(1)} %get-tuple-element.25.k_gain_ref, bf16[128,512]{1,0:T(8,128)(2,1)S(1)} %get-tuple-element.26.qt_ref, f32[4,512]{1,0:T(4,128)S(1)} %get-tuple-element.27.bias_ref, ...), custom_call_target="tpu_custom_call" | custom-call | flops 52428800 | tf_op jit(solution)/shard_map/attend/pallas_call | solution.py:405
  22.0 0.8 %collective-permute-done.4.refs_1_ = bf16[1,200,256]{2,1,0:T(8,128)(2,1)S(1)} collective-permute-done((bf16[1,200,256]{2,1,0:T(8,128)(2,1)S(1)}, bf16[1,200,256]{2,1,0:T(8,128)(2,1)S(1)}, u32[]{:S(2)}, u32[]{:S(2)}) %collective-permute-start.4) | collective-permute-done | bytes 102432 | tf_op jit(solution)/shard_map/ppermute | solution.py:248
  22.8 1.3 %attend.7 = bf16[128,512]{1,0:T(8,128)(2,1)} custom-call(f32[1,128]{1,0:T(1,128)S(1)} %get-tuple-element.25.k_gain_ref, bf16[128,512]{1,0:T(8,128)(2,1)S(1)} %get-tuple-element.26.qt_ref, f32[4,512]{1,0:T(4,128)S(1)} %get-tuple-element.27.bias_ref, bf16[1,200,256]{2,1,0:T(8,128)(2,1)S(1)} %collective-permute-done.3.refs_0_, ...), custom_call_target="tpu_custom_call" | custom-call | flops 52428800 | tf_op jit(solution)/shard_map/attend/pallas_call | solution.py:405
  (2 shorter events, 0.1 us)
Async XLA Ops:
  0.0 4.0 %collective-permute-start = (bf16[2,2048,128]{2,1,0:T(8,128)(2,1)}, bf16[2,2048,128]{2,1,0:T(8,128)(2,1)S(1)}, u32[]{:S(2)}, u32[]{:S(2)}) collective-permute-start(bf16[2,2048,128]{2,1,0:T(8,128)(2,1)} %w_hbm.3), channel_id=1, source_target_pairs={{0,4},{4,0},{1,5},{5,1},{2,6},{6,2},{3,7},{7,3},{8,12},{12,8},{9,1... | collective-permute-start | bytes 3145736 | tf_op jit(solution)/shard_map/ppermute | solution.py:248
  0.5 8.2 %collective-permute-start.1 = (bf16[1,200,256]{2,1,0:T(8,128)(2,1)S(1)}, bf16[1,200,256]{2,1,0:T(8,128)(2,1)S(1)}, u32[]{:S(2)}, u32[]{:S(2)}) collective-permute-start(bf16[1,200,256]{2,1,0:T(8,128)(2,1)S(1)} %get-tuple-element.29), channel_id=1, source_target_pairs={{0,4},{1,5},{2,0},{3,1},{4,6},{5,7},{6,2},{7,3},{8,12},{9,13},{10,... | collective-permute-start | bytes 307208 | tf_op jit(solution)/shard_map/ppermute | solution.py:257
  4.4 4.8 %collective-permute-start.2 = (bf16[1,200,256]{2,1,0:T(8,128)(2,1)S(1)}, bf16[1,200,256]{2,1,0:T(8,128)(2,1)S(1)}, u32[]{:S(2)}, u32[]{:S(2)}) collective-permute-start(bf16[1,200,256]{2,1,0:T(8,128)(2,1)S(1)} %home_other.1.after_ref), channel_id=1, source_target_pairs={{0,2},{1,3},{2,6},{3,7},{4,0},{5,1},{6,4},{7,5},{8,10},{9,11},{10,... | collective-permute-start | bytes 307208 | tf_op jit(solution)/shard_map/ppermute | solution.py:257
  9.3 5.2 %collective-permute-start.5 = (bf16[1,200,256]{2,1,0:T(8,128)(2,1)S(1)}, bf16[1,200,256]{2,1,0:T(8,128)(2,1)S(1)}, u32[]{:S(2)}, u32[]{:S(2)}) collective-permute-start(bf16[1,200,256]{2,1,0:T(8,128)(2,1)S(1)} %pair_sum.1.keep_ref), channel_id=1, source_target_pairs={{0,1},{1,0},{2,3},{3,2},{4,5},{5,4},{6,7},{7,6},{8,9},{9,8},{10,11... | collective-permute-start | bytes 307208 | tf_op jit(solution)/shard_map/ppermute | solution.py:248
  11.8 5.8 %collective-permute-start.3 = (bf16[1,200,256]{2,1,0:T(8,128)(2,1)S(1)}, bf16[1,200,256]{2,1,0:T(8,128)(2,1)S(1)}, u32[]{:S(2)}, u32[]{:S(2)}) collective-permute-start(bf16[1,200,256]{2,1,0:T(8,128)(2,1)S(1)} %pair_sum.1.keep_ref), channel_id=1, source_target_pairs={{0,24},{8,16},{16,8},{24,0},{1,25},{9,17},{17,9},{25,1},{2,26},{10... | collective-permute-start | bytes 307208 | tf_op jit(solution)/shard_map/ppermute | solution.py:248
  14.6 6.0 %collective-permute-start.7 = (bf16[200,256]{1,0:T(8,128)(2,1)S(1)}, bf16[200,256]{1,0:T(8,128)(2,1)S(1)}, u32[]{:S(2)}, u32[]{:S(2)}) collective-permute-start(bf16[200,256]{1,0:T(8,128)(2,1)S(1)} %sum_norm.1.refs_0_), channel_id=1, source_target_pairs={{0,8},{8,0},{16,24},{24,16},{1,9},{9,1},{17,25},{25,17},{2,10},{10... | collective-permute-start | bytes 307208 | tf_op jit(solution)/shard_map/ppermute | solution.py:248
  16.2 5.4 %collective-permute-start.6 = (bf16[200,256]{1,0:T(8,128)(2,1)S(1)}, bf16[200,256]{1,0:T(8,128)(2,1)S(1)}, u32[]{:S(2)}, u32[]{:S(2)}) collective-permute-start(bf16[200,256]{1,0:T(8,128)(2,1)S(1)} %sum_norm.1.refs_0_), channel_id=1, source_target_pairs={{0,16},{8,24},{16,0},{24,8},{1,17},{9,25},{17,1},{25,9},{2,18},{10... | collective-permute-start | bytes 307208 | tf_op jit(solution)/shard_map/ppermute | solution.py:248
  17.7 5.1 %collective-permute-start.4 = (bf16[1,200,256]{2,1,0:T(8,128)(2,1)S(1)}, bf16[1,200,256]{2,1,0:T(8,128)(2,1)S(1)}, u32[]{:S(2)}, u32[]{:S(2)}) collective-permute-start(bf16[1,200,256]{2,1,0:T(8,128)(2,1)S(1)} %collective-permute-done.3.refs_0_), channel_id=1, source_target_pairs={{0,1},{1,0},{2,3},{3,2},{4,5},{5,4},{6,7},{7,6},{8,9},{9,8},{10,11... | collective-permute-start | bytes 307208 | tf_op jit(solution)/shard_map/ppermute | solution.py:248
